TPU v7x, 32 devices: a whole 2x2x4 slice. The times are simulated.
32 devices in a mesh: groups: 2 (over x), blk: 16 (over z, y, core).
Axes of the slice: x: 2, y: 2, z: 4, core: 2. Of those that a mesh axis runs over, the one named last changes fastest.
Arguments:
- cache_kv: bfloat16 [32768, 2, 1536], P(('groups', 'blk')), parts along dimension 0, may hold values from -6 to 6
- fresh_qkv: bfloat16 [2, 192, 3, 1536], P(None, ('groups', 'blk')), parts along dimension 1, may hold values from -100 to 100
- list_rows: int32 [2, 192], P(None, ('groups', 'blk')), parts along dimension 1, may hold values from 0 to 1023, as said below
- counts: int32 [2, 32], P(None, 'groups'), parts along dimension 1, may hold values from 1 to 6, 64 in all within a row
Outputs:
- attended: bfloat16 [2, 128, 1536], P(None, ('groups', 'blk')), parts along dimension 1
There are 2 independent parts, one for each index of `groups`. A program takes and returns all parts, laid end to end along the dimension named above; each array names one. Nothing has to cross between parts.
Inputs may be any that keep to these rules, and one draw needn't show every extreme that they name: `list_rows`: the entries of one device and one step are distinct rows of that device. The counts of each step sum to 64.
All inputs are finite; a program needn't handle non-finite values.
Results may differ from a plain program's by a relative error of at most 0.005.
Values may be sent and summed in bfloat16 or wider, within the bound.
No kernel may reach another device: no remote copies, remote signals or barrier semaphores. Data moves between devices by JAX's collectives and lax.ppermute only.
A program may use at most 128 MiB of HBM per device.

v0:
```python
import jax
import jax.numpy as jnp
from jax import lax
from jax.sharding import PartitionSpec as P

HEAD = 128
SLOT = 4
STEPS = 2


def compact_order(step_counts, query_count, slot_count):
    count_ends = jnp.cumsum(step_counts)
    rank_order = jnp.arange(query_count, dtype=jnp.int32)
    before = count_ends[None, :] <= rank_order[:, None]
    home_dev = jnp.sum(before.astype(jnp.int32), axis=1)
    home_start = jnp.sum(jnp.where(before, step_counts[None, :], 0), axis=1)
    return home_dev * slot_count + rank_order - home_start


def refresh_cache(kv_cache, step_fresh, step_rows, live_count):
    slot_count = step_rows.shape[0]
    is_live = jnp.arange(slot_count, dtype=jnp.int32) < live_count
    target = jnp.where(is_live, step_rows, kv_cache.shape[0])
    return kv_cache.at[target].set(step_fresh[:, 1:3, :], mode="drop")


def local_terms(kv_cache, picked):
    query_count, row_width = picked.shape
    head_count = row_width // HEAD
    row_block = min(512, query_count)
    key_rows = kv_cache[:, 0, :].reshape(kv_cache.shape[0], head_count, HEAD)
    value_rows = kv_cache[:, 1, :].reshape(kv_cache.shape[0], head_count, HEAD)

    def one_block(queries):
        queries = queries.reshape(row_block, head_count, HEAD)
        scores = jnp.einsum(
            "bhd,thd->bht", queries, key_rows, preferred_element_type=jnp.float32
        ) * HEAD ** (-0.5)
        highest = jnp.max(scores, axis=2)
        weights = jnp.exp(scores - highest[:, :, None])
        total_weight = jnp.sum(weights, axis=2)
        weighted = jnp.einsum(
            "bht,thd->bhd",
            weights.astype(jnp.bfloat16),
            value_rows,
            preferred_element_type=jnp.float32,
        )
        return (highest, total_weight, weighted)

    highest, total_weight, weighted = lax.map(
        one_block, picked.reshape(query_count // row_block, row_block, row_width)
    )
    return (
        highest.reshape(query_count, head_count),
        total_weight.reshape(query_count, head_count),
        weighted.reshape(query_count, head_count, HEAD),
    )


def combine_rows(highest, total_weight, weighted):
    step_count, query_count, head_count = highest.shape
    overall = lax.pmax(highest, "blk")
    factor = jnp.exp(highest - overall)
    scaled = (weighted * factor[..., None]).reshape(step_count, query_count, head_count * HEAD)
    numer, denom = (
        lax.psum_scatter(scaled, "blk", scatter_dimension=1, tiled=True),
        lax.psum_scatter(total_weight * factor, "blk", scatter_dimension=1, tiled=True),
    )
    numer = numer.reshape(step_count, numer.shape[1], head_count, HEAD)
    shaped = numer / denom[..., None]
    return shaped.reshape(step_count, shaped.shape[1], head_count * HEAD).astype(jnp.bfloat16)


def body(cache_kv, fresh_qkv, list_rows, counts):
    device_count = lax.axis_size("blk")
    my_index = lax.axis_index("blk")
    query_count = device_count * SLOT
    slot_count = list_rows.shape[1]
    kv_cache = cache_kv
    results = []
    for step_index in range(STEPS):
        live_count = lax.dynamic_index_in_dim(counts[step_index], my_index, keepdims=False)
        kv_cache = refresh_cache(kv_cache, fresh_qkv[step_index], list_rows[step_index], live_count)
        gathered = lax.all_gather(fresh_qkv[step_index, :, 0, :], "blk", axis=0, tiled=True)
        picked = gathered[compact_order(counts[step_index], query_count, slot_count)]
        highest, total_weight, weighted = local_terms(kv_cache, picked)
        results.append(combine_rows(highest[None], total_weight[None], weighted[None])[0])
    return jnp.stack(results)


def solution(mesh):
    in_specs = (
        P(("groups", "blk"), None, None),
        P(None, ("groups", "blk"), None, None),
        P(None, ("groups", "blk")),
        P(None, "groups"),
    )
    out_specs = P(None, ("groups", "blk"), None)
    return jax.shard_map(body, mesh=mesh, in_specs=in_specs, out_specs=out_specs, check_vma=False)
```

profile of v0, /device:TPU:0, one launch (start us, length us, event | category | flops | bytes accessed | tf_op | source)
XLA Modules:
  0.0 330.0 jit_solution(16323669545119489735)
XLA Ops:
  6.5 6.8 %copy.171 = bf16[1024,2,1536]{2,1,0:T(2,128)(2,1)} copy(bf16[1024,2,1536]{2,1,0:T(2,128)(2,1)} %param.4) | data formatting | bytes 12582912
  14.4 24.8 %all-gather = bf16[1,96,1,1536]{3,2,0,1:T(2,128)(2,1)S(1)} all-gather(bf16[1,6,1,1536]{3,2,0,1:T(2,128)(2,1)S(1)} %get-tuple-element.61), channel_id=2, replica_groups=mesh['groups'=2,'blk'=16] {'blk'}, dimensions={1}, use_global_device_ids=true | all-gather | bytes 313344 | tf_op jit(solution)/shard_map/all_gather | solution.py:84
  39.3 19.1 %all-gather.1 = bf16[1,96,1,1536]{3,2,0,1:T(2,128)(2,1)S(1)} all-gather(bf16[1,6,1,1536]{3,2,0,1:T(2,128)(2,1)S(1)} %get-tuple-element.62), channel_id=3, replica_groups=mesh['groups'=2,'blk'=16] {'blk'}, dimensions={1}, use_global_device_ids=true | all-gather | bytes 313344 | tf_op jit(solution)/shard_map/all_gather | solution.py:84
  59.7 1.2 fusion.38
  61.0 2.1 scatter_fusion
  63.0 13.5 %fusion.42 = (bf16[1024,1,1536]{2,1,0:T(2,128)(2,1)}, bf16[1024,1,1536]{2,1,0:T(2,128)(2,1)}) fusion(bf16[1024,2,1536]{2,1,0:T(2,128)(2,1)} %scatter_fusion), kind=kLoop, calls=%fused_computation.79 | loop fusion | bytes 12582912 | tf_op jit(solution)/shard_map/slice | solution.py:32
  76.5 15.3 %copy.108 = bf16[1024,1,1536]{0,2,1:T(8,128)(2,1)} copy(bf16[1024,1,1536]{2,1,0:T(2,128)(2,1)} %get-tuple-element.48) | data formatting | bytes 6291456 | tf_op jit(solution)/shard_map/slice | solution.py:32
  91.8 13.4 %copy.109 = bf16[1024,1,1536]{0,2,1:T(8,128)(2,1)S(1)} copy(bf16[1024,1,1536]{2,1,0:T(2,128)(2,1)} %get-tuple-element.56) | data formatting | bytes 6291456 | tf_op jit(solution)/shard_map/slice | solution.py:31
  105.2 2.1 scatter_fusion.1
  107.3 13.5 %fusion.43 = (bf16[1024,1,1536]{2,1,0:T(2,128)(2,1)}, bf16[1024,1,1536]{2,1,0:T(2,128)(2,1)}) fusion(bf16[1024,2,1536]{2,1,0:T(2,128)(2,1)} %scatter_fusion.1), kind=kLoop, calls=%fused_computation.80 | loop fusion | bytes 12582912 | tf_op jit(solution)/shard_map/slice | solution.py:32
  120.8 15.3 %copy.119 = bf16[1024,1,1536]{0,2,1:T(8,128)(2,1)} copy(bf16[1024,1,1536]{2,1,0:T(2,128)(2,1)} %get-tuple-element.58) | data formatting | bytes 6291456 | tf_op jit(solution)/shard_map/slice | solution.py:32
  136.1 15.3 %copy.120 = bf16[1024,1,1536]{0,2,1:T(8,128)(2,1)} copy(bf16[1024,1,1536]{2,1,0:T(2,128)(2,1)} %get-tuple-element.60) | data formatting | bytes 6291456 | tf_op jit(solution)/shard_map/slice | solution.py:31
  151.4 1.4 gather_fusion
  152.8 1.9 gather_fusion.1
  154.7 1.7 bitcast_reduce_fusion.1
  157.1 2.3 copy-done.1
  160.8 59.1 %all-reduce.6 = (f32[1,64,12]{1,2,0:T(8,128)S(1)}, f32[1,64,12]{1,2,0:T(8,128)S(1)}) all-reduce(f32[1,64,12]{1,2,0:T(8,128)S(1)} %bitcast.153, f32[1,64,12]{1,2,0:T(8,128)S(1)} %bitcast.154), channel_id=1, replica_groups=mesh['groups'=2,'blk'=16] {'blk'}, use_global_device_ids=true, to_apply=%region_14.15 | all-reduce | flops 1536 | bytes 12288 | tf_op jit(solution)/shard_map/pmax | solution.py:62
  219.9 4.1 %fusion.23 = f32[64,12,128]{2,0,1:T(8,128)S(1)} fusion(bf16[1024,12,128]{0,2,1:T(8,128)(2,1)} %bitcast.148, f32[12,1024,64]{1,2,0:T(8,128)} %copy-done, f32[64,12]{0,1:T(8,128)S(1)} %get-tuple-element.79, f32[64,12]{0,1:T(8,128)S(1)} %get-tuple-element.65), kind=kOutput, calls=%fused_computation.23 | convolution fusion | flops 203784192 | bytes 6690816 | tf_op jit(solution)/shard_map/while/body/eval_jaxpr/bht,thd->bhd/dot_general | solution.py:42
  224.0 1.0 copy.115
  225.0 1.8 reshape.231
  226.9 3.1 fusion.20
  232.6 58.0 %all-reduce.4 = (f32[1,64,12]{2,1,0:T(8,128)S(1)}, f32[1,64,12]{2,1,0:T(8,128)S(1)}) all-reduce(f32[1,64,12]{2,1,0:T(8,128)S(1)} %copy.127, f32[1,64,12]{2,1,0:T(8,128)S(1)} %copy.116), channel_id=7, replica_groups=mesh['groups'=2,'blk'=16] {'blk'}, use_global_device_ids=true, to_apply=%region_17.18.clone | all-reduce | flops 1536 | bytes 12288
  290.7 30.2 %all-reduce.9.cloned.1.call-done = (f32[1,64,1536]{2,1,0:T(8,128)}, f32[1,64,1536]{2,1,0:T(8,128)}) async-done(((f32[1,64,1536]{2,1,0:T(8,128)}, f32[1,64,1536]{2,1,0:T(8,128)}), (f32[1,64,1536]{2,1,0:T(8,128)}, f32[1,64,1536]{2,1,0:T(8,128)})) %all-reduce.9.cloned.1.call-update) | async-done | bytes 786448
  321.8 0.8 fusion.33
  (53 shorter events, 7.9 us)
Async XLA Ops:
  6.5 6.9 %copy-start.2 = (bf16[2,6,3,1536]{3,0,2,1:T(2,128)(2,1)S(1)}, bf16[2,6,3,1536]{3,0,2,1:T(2,128)(2,1)}, u32[]{:S(2)}) copy-start(bf16[2,6,3,1536]{3,0,2,1:T(2,128)(2,1)} %param.5) | copy-start | bytes 331780
  6.5 7.1 %copy-start.4 = (s32[2,16]{1,0:T(2,128)S(1)}, s32[2,16]{1,0:T(2,128)}, u32[]{:S(2)}) copy-start(s32[2,16]{1,0:T(2,128)} %param.7) | copy-start | bytes 388
  6.5 314.4 %all-reduce.9.cloned.1.call-start = ((), (), s32[]{:S(2)}) async-start(), calls=%async_computation | async-start | bytes 1572864
  13.4 46.3 %copy-start.3 = (s32[2,6]{1,0:T(2,128)S(1)}, s32[2,6]{1,0:T(2,128)}, u32[]{:S(2)}) copy-start(s32[2,6]{1,0:T(2,128)} %param.6) | copy-start | bytes 148
  156.3 3.8 %copy-start = (f32[12,1024,64]{1,2,0:T(8,128)}, f32[12,1024,64]{1,2,0:T(8,128)S(1)}, u32[]{:S(2)}) copy-start(f32[12,1024,64]{1,2,0:T(8,128)S(1)} %get-tuple-element.80) | copy-start | bytes 9437188
  156.3 3.0 copy-start.1
  226.9 4.4 %copy-start.5 = (u32[32]{0:T(128)S(1)}, u32[32]{0:T(128)}, u32[]{:S(2)}) copy-start(u32[32]{0:T(128)} %constant.68) | copy-start | bytes 388
Sparse Core Ops, SparseCore 0:
  231.3 89.6 all-reduce.8
where the time goes:
time: 332 us; the launch traced here: 330 us
  blocking collectives  161 us (48%)
  local copies, waits for them, and re-layouts  110 us (33%)
  waiting for transfers between devices  30.2 us (9%)
  between operations  14.3 us (4%)
  matrix products  9.63 us (3%)
  other arithmetic  5.33 us (2%)
    pmax x1, blocking collectives, combine_rows(): overall = lax.pmax(highest, 'blk')  59.1 us
    unnamed x1, blocking collectives  58 us
    slice x4, local copies, waits for them, and re-layouts, local_terms(): value_rows = kv_cache[:, 1, :].reshape(kv_cache.shape[0], head_count, HEAD)  57.5 us
    all_gather x2, blocking collectives, body(): lax.all_gather(fresh_qkv[step_index, :, 0, :], 'blk', axis=0, tiled=True)  43.9 us
    unnamed x2, waiting for transfers between devices  30.2 us
    slice x2, local copies, waits for them, and re-layouts, local_terms(): key_rows = kv_cache[:, 0, :].reshape(kv_cache.shape[0], head_count, HEAD)  28.7 us
    unnamed x17, local copies, waits for them, and re-layouts  10.6 us
    dot_general x2, matrix products, one_block(): jnp.einsum('bht,thd->bhd', weights.astype(jnp.bfloat16), value_rows, pref...  7.26 us
  transfers between devices with their start and end apart: 1, of which 1 were waited for; matrix products, arithmetic and copies ran while one was open for 0% of the time, Pallas kernels for 0%

commit v1 on v0

v1 whole, which is shorter than its diff:
```python
import functools

import jax
import jax.numpy as jnp
from jax import lax
from jax.experimental import pallas as pl
from jax.experimental.pallas import tpu as pltpu
from jax.sharding import PartitionSpec as P

HEAD = 128
SLOT = 4
STEPS = 2
PAIR = STEPS * SLOT
LOG2E = 1.4426950408889634
SCALE = HEAD ** -0.5 * LOG2E
FAR = -1e30
LANES = 128


def split_kernel(kv_ref, key_ref, value_ref):
    rows = kv_ref.shape[0]
    half = rows // 2
    out = lax.broadcasted_iota(jnp.int32, (rows, rows), 0)
    src = lax.broadcasted_iota(jnp.int32, (rows, rows), 1)
    want = jnp.where(out < half, 2 * out, 2 * (out - half) + 1)
    order = (src == want).astype(jnp.bfloat16)
    for c in range(0, kv_ref.shape[1], 256):
        part = jnp.dot(order, kv_ref[:, c:c + 256], preferred_element_type=jnp.float32)
        key_ref[:, c:c + 256] = part[:half].astype(jnp.bfloat16)
        value_ref[:, c:c + 256] = part[half:].astype(jnp.bfloat16)


def split_cache(cache):
    tokens, _, width = cache.shape
    block = min(128, tokens)
    shape = jax.ShapeDtypeStruct((tokens, width), jnp.bfloat16)
    spec = pl.BlockSpec((block, width), lambda i: (i, 0))
    return pl.pallas_call(
        split_kernel,
        grid=(tokens // block,),
        out_shape=(shape, shape),
        in_specs=[pl.BlockSpec((2 * block, width), lambda i: (i, 0))],
        out_specs=(spec, spec),
        compiler_params=pltpu.CompilerParams(vmem_limit_bytes=32 << 20),
        cost_estimate=pl.CostEstimate(
            flops=4 * block * 2 * tokens * width, bytes_accessed=8 * tokens * width, transcendentals=0
        ),
        name="split_cache",
    )(cache.reshape(2 * tokens, width))


def two_parts(x):
    high = x.astype(jnp.bfloat16).astype(jnp.float32)
    return high, x - high


def attend_kernel(target_ref, bias_ref, fresh_bias_ref, fresh_key_ref, fresh_value_ref, key_ref, value_ref, *rest):
    gathered_refs, out_ref = rest[:-1], rest[-1]
    heads = key_ref.shape[1] // HEAD
    chunk = 128
    chunks = out_ref.shape[0] * PAIR // chunk
    nt = (((1,), (1,)), ((), ()))

    def one_chunk(i):
        base = i * chunk
        want = target_ref[0:1, :] - base
        row = lax.broadcasted_iota(jnp.int32, (chunk, want.shape[1]), 0)
        pick = (row == want).astype(jnp.bfloat16)
        slots = jnp.concatenate([g[...] for g in gathered_refs], axis=0)
        queries = jnp.dot(pick, slots, preferred_element_type=jnp.float32).astype(jnp.bfloat16)
        bias = bias_ref[...]
        fresh_bias = fresh_bias_ref[...]
        lane = lax.broadcasted_iota(jnp.int32, (chunk, LANES), 1)
        highs = jnp.zeros((chunk, LANES), jnp.float32)
        totals = jnp.zeros((chunk, LANES), jnp.float32)
        for h in range(heads):
            cols = slice(h * HEAD, (h + 1) * HEAD)
            q = queries[:, cols]
            s = lax.dot_general(q, key_ref[:, cols], nt, preferred_element_type=jnp.float32)
            sf = lax.dot_general(q, fresh_key_ref[:, cols], nt, preferred_element_type=jnp.float32)
            s = (s.reshape(chunk // PAIR, PAIR, -1) + bias[None]).reshape(chunk, -1)
            sf = (sf.reshape(chunk // PAIR, PAIR, -1) + fresh_bias[None]).reshape(chunk, -1)
            high = jnp.maximum(jnp.max(s, axis=1, keepdims=True), jnp.max(sf, axis=1, keepdims=True))
            w = jnp.exp2((s - high) * SCALE)
            wf = jnp.exp2((sf - high) * SCALE)
            total = jnp.sum(w, axis=1, keepdims=True) + jnp.sum(wf, axis=1, keepdims=True)
            o = jnp.dot(w.astype(jnp.bfloat16), value_ref[:, cols], preferred_element_type=jnp.float32)
            o += jnp.dot(wf.astype(jnp.bfloat16), fresh_value_ref[:, cols], preferred_element_type=jnp.float32)
            o = (o / total).astype(jnp.bfloat16)
            out_ref[pl.ds(i * (chunk // PAIR), chunk // PAIR), :, cols] = o.reshape(chunk // PAIR, PAIR, HEAD)
            highs = jnp.where(lane == h, high, highs)
            totals = jnp.where(lane == h, total, totals)
        h1, r = two_parts(highs)
        h2, h3 = two_parts(r)
        t1, t2 = two_parts(totals)
        stats = h1
        for n, part in enumerate((h2, h3, t1, t2)):
            stats = stats + pltpu.roll(part, 16 * (n + 1), 1)
        stats = stats.astype(jnp.bfloat16)
        width = heads * HEAD
        out_ref[pl.ds(i * (chunk // PAIR), chunk // PAIR), :, width:] = stats.reshape(chunk // PAIR, PAIR, LANES)

    if chunks == 1:
        one_chunk(0)
    else:
        pl.loop(0, chunks)(one_chunk)


def attend(target, bias, fresh_bias, fresh_key, fresh_value, key, value, gathered):
    device_count = target.shape[1] // fresh_key.shape[0]
    tokens, width = key.shape
    rows = device_count * PAIR
    vmem = pl.BlockSpec(memory_space=pltpu.VMEM)
    return pl.pallas_call(
        attend_kernel,
        out_shape=jax.ShapeDtypeStruct((device_count, PAIR, width + LANES), jnp.bfloat16),
        in_specs=[vmem] * (7 + len(gathered)),
        out_specs=vmem,
        compiler_params=pltpu.CompilerParams(vmem_limit_bytes=48 << 20),
        cost_estimate=pl.CostEstimate(
            flops=4 * rows * tokens * width, bytes_accessed=4 * tokens * width,
            transcendentals=rows * tokens * width // HEAD,
        ),
        name="attend",
    )(target, bias, fresh_bias, fresh_key, fresh_value, key, value, *gathered)


def combine_kernel(parts_ref, out_ref):
    width = out_ref.shape[1]
    heads = width // HEAD
    stats = parts_ref[:, :, width:].astype(jnp.float32)

    def part(n):
        return stats[:, :, 16 * n:16 * n + heads]

    high = part(0) + part(1) + part(2)
    total = part(3) + part(4)
    top = jnp.max(high, axis=0, keepdims=True)
    weight = total * jnp.exp2((high - top) * SCALE)
    weight = weight / jnp.sum(weight, axis=0, keepdims=True)
    for h in range(heads):
        cols = slice(h * HEAD, (h + 1) * HEAD)
        o = parts_ref[:, :, cols].astype(jnp.float32) * weight[:, :, h:h + 1]
        out_ref[:, cols] = jnp.sum(o, axis=0).astype(jnp.bfloat16)


def combine(parts):
    vmem = pl.BlockSpec(memory_space=pltpu.VMEM)
    width = parts.shape[2] - LANES
    return pl.pallas_call(
        combine_kernel,
        out_shape=jax.ShapeDtypeStruct((PAIR, width), jnp.bfloat16),
        in_specs=[vmem],
        out_specs=vmem,
        compiler_params=pltpu.CompilerParams(vmem_limit_bytes=32 << 20),
        name="combine",
    )(parts)


def plan_rows(counts, list_rows, my_index, token_count, slot_rows):
    device_count = counts.shape[1]
    slot_count = list_rows.shape[1]
    before = jnp.arange(device_count)[:, None] < jnp.arange(device_count)[None, :]
    starts = jnp.sum(jnp.where(before[None], counts[:, :, None], 0), axis=1)
    device = (my_index - jnp.arange(device_count)) % device_count
    chosen = device[:, None] == jnp.arange(device_count)[None, :]
    start = jnp.sum(jnp.where(chosen[None], starts[:, None, :], 0), axis=2)
    count = jnp.sum(jnp.where(chosen[None], counts[:, None, :], 0), axis=2)
    at = jnp.arange(slot_rows)
    slot, step = at // STEPS, at % STEPS
    start = jnp.where(step[None, :] == 0, start[0][:, None], start[1][:, None])
    count = jnp.where(step[None, :] == 0, count[0][:, None], count[1][:, None])
    rank = start + slot[None, :]
    row = (rank // SLOT) * PAIR + step[None, :] * SLOT + rank % SLOT
    target = jnp.where(slot[None, :] < count, row, -1).reshape(1, -1).astype(jnp.int32)

    mine = jnp.sum(jnp.where(jnp.arange(device_count)[None, :] == my_index, counts, 0), axis=1)
    live = jnp.arange(slot_count)[None, :] < mine[:, None]
    place = jnp.where(live, list_rows, -1)
    hit = jnp.any(place[:, :, None] == jnp.arange(token_count)[None, None, :], axis=1)
    gone = jnp.stack([hit[0], hit[0] | hit[1]])
    bias = jnp.where(gone, FAR, 0.0).astype(jnp.float32)
    bias = jnp.repeat(bias, SLOT, axis=0)
    again = jnp.any(place[0][:, None] == place[1][None, :], axis=1)
    none = jnp.zeros_like(live[0])
    first = jnp.stack([live[0], none], axis=1).reshape(-1)
    second = jnp.stack([live[0] & ~again, live[1]], axis=1).reshape(-1)
    seen = jnp.stack([first, second])
    seen = jnp.pad(seen, ((0, 0), (0, slot_rows - seen.shape[1])))
    fresh_bias = jnp.repeat(jnp.where(seen, 0.0, FAR).astype(jnp.float32), SLOT, axis=0)
    return target, bias, fresh_bias


def body(cache_kv, fresh_qkv, list_rows, counts):
    device_count = lax.axis_size("blk")
    my_index = lax.axis_index("blk")
    slot_count = list_rows.shape[1]
    width = cache_kv.shape[2]
    slot_rows = -(-slot_count * STEPS // 16) * 16
    fresh = fresh_qkv.transpose(2, 1, 0, 3).reshape(3, slot_count * STEPS, width)
    fresh = jnp.pad(fresh, ((0, 0), (0, slot_rows - slot_count * STEPS), (0, 0)))
    mine = fresh[0]
    gathered = [mine]
    for k in range(1, device_count):
        pairs = [(i, (i + k) % device_count) for i in range(device_count)]
        gathered.append(lax.ppermute(mine, "blk", pairs))
    if device_count > 16:
        gathered = [jnp.concatenate(gathered)]
    target, bias, fresh_bias = plan_rows(counts, list_rows, my_index, cache_kv.shape[0], slot_rows)
    key, value = split_cache(cache_kv)
    parts = attend(target, bias, fresh_bias, fresh[1], fresh[2], key, value, gathered)
    parts = lax.all_to_all(parts, "blk", split_axis=0, concat_axis=0, tiled=True)
    return combine(parts).reshape(STEPS, SLOT, width)


def solution(mesh):
    in_specs = (
        P(("groups", "blk"), None, None),
        P(None, ("groups", "blk"), None, None),
        P(None, ("groups", "blk")),
        P(None, "groups"),
    )
    out_specs = P(None, ("groups", "blk"), None)
    return jax.shard_map(body, mesh=mesh, in_specs=in_specs, out_specs=out_specs, check_vma=False)
```

time: 332 us -> 87.5 us (0.26)
  blocking collectives: 161 us -> 18.5 us
  local copies, waits for them, and re-layouts: 110 us -> 28.8 us
  waiting for transfers between devices: 30.2 us -> 0.36 us
  starting transfers between devices: 0.01 us -> 24.2 us
  between operations: 14.3 us -> 0.2 us
  Pallas kernels: 0 us -> 10.7 us
  matrix products: 9.63 us -> 0 us
    slice x11 -> x0, local copies, waits for them, and re-layouts: 86.4 us -> none  [the longest x4 57.5 us: local_terms(): value_rows = kv_cache[:, 1, :].reshape(kv_cache.shape[0], head_count, HEAD)]
    pmax x1 -> x0, blocking collectives: 59.1 us -> none  [combine_rows(): overall = lax.pmax(highest, 'blk')]
    unnamed x1 -> x0, blocking collectives: 58 us -> none
    all_gather x2 -> x0, blocking collectives: 43.9 us -> none  [body(): lax.all_gather(fresh_qkv[step_index, :, 0, :], 'blk', axis=0, tiled=True)]
    unnamed x2 -> x0, waiting for transfers between devices: 30.2 us -> none
    ppermute x0 -> x15, starting transfers between devices: none -> 24.2 us  [body(): gathered.append(lax.ppermute(mine, 'blk', pairs))]
    all_to_all x0 -> x1, blocking collectives: none -> 18.5 us  [body(): lax.all_to_all(parts, 'blk', split_axis=0, concat_axis=0, tiled=True)]
    reshape x2 -> x4, local copies, waits for them, and re-layouts: 2.64 us -> 15.1 us  [the longest x1 13.6 us: split_cache(): cache.reshape(2 * tokens, width)]
  transfers between devices with their start and end apart: 1 -> 15, of which waited for: 1 -> 1; matrix products, arithmetic and copies ran while one was open for 0% -> 23% of each run, Pallas kernels for 0% -> 4%
where the time goes in v1:
time: 87.5 us; the launch traced here: 86.6 us
  local copies, waits for them, and re-layouts  28.8 us (33%)
  starting transfers between devices  24.2 us (28%)
  blocking collectives  18.5 us (21%)
  Pallas kernels  10.7 us (12%)
  other arithmetic  3.85 us (4%)
    ppermute x15, starting transfers between devices, body(): gathered.append(lax.ppermute(mine, 'blk', pairs))  24.2 us
    all_to_all x1, blocking collectives, body(): lax.all_to_all(parts, 'blk', split_axis=0, concat_axis=0, tiled=True)  18.5 us
    reshape x1, local copies, waits for them, and re-layouts, split_cache(): cache.reshape(2 * tokens, width)  13.6 us
    unnamed x25, local copies, waits for them, and re-layouts  11.6 us
    pallas_call x1, Pallas kernels, attend(): pl.pallas_call(attend_kernel, out_shape=jax.ShapeDtypeStruct((device_coun...  7.21 us
    pallas_call x1, Pallas kernels, split_cache(): pl.pallas_call(split_kernel, grid=(tokens // block,), out_shape=(shape, s...  3.04 us
  transfers between devices with their start and end apart: 15, of which 1 were waited for; matrix products, arithmetic and copies ran while one was open for 23% of the time, Pallas kernels for 4%

profile of v1, /device:TPU:0, one launch (start us, length us, event | category | flops | bytes accessed | tf_op | source)
XLA Modules:
  0.0 86.6 jit_solution(14089816110205381382)
XLA Ops:
  0.0 1.0 %copy.13 = bf16[3,6,2,1536]{3,2,1,0:T(2,128)(2,1)S(1)} copy(bf16[3,6,2,1536]{3,2,0,1:T(2,128)(2,1)} %bitcast.29) | data formatting | bytes 221184 | tf_op jit(solution)/shard_map/transpose | solution.py:200
  1.6 2.6 %collective-permute-start.1 = (bf16[16,1536]{1,0:T(8,128)(2,1)S(1)}, bf16[16,1536]{1,0:T(8,128)(2,1)S(1)}, u32[]{:S(2)}, u32[]{:S(2)}) collective-permute-start(bf16[16,1536]{1,0:T(8,128)(2,1)S(1)} %get-tuple-element.11.rest_0_), channel_id=1, source_target_pairs={{0,2},{1,3},{2,4},{3,5},{4,6},{5,7},{6,8},{7,9},{8,10},{9,11},{10,... | collective-permute-start | bytes 147464 | tf_op jit(solution)/shard_map/ppermute | solution.py:206
  4.1 2.4 %collective-permute-start.2 = (bf16[16,1536]{1,0:T(8,128)(2,1)S(1)}, bf16[16,1536]{1,0:T(8,128)(2,1)S(1)}, u32[]{:S(2)}, u32[]{:S(2)}) collective-permute-start(bf16[16,1536]{1,0:T(8,128)(2,1)S(1)} %get-tuple-element.11.rest_0_), channel_id=1, source_target_pairs={{0,3},{1,4},{2,5},{3,6},{4,7},{5,8},{6,9},{7,10},{8,11},{9,12},{10... | collective-permute-start | bytes 147464 | tf_op jit(solution)/shard_map/ppermute | solution.py:206
  6.6 1.6 %collective-permute-start.3 = (bf16[16,1536]{1,0:T(8,128)(2,1)S(1)}, bf16[16,1536]{1,0:T(8,128)(2,1)S(1)}, u32[]{:S(2)}, u32[]{:S(2)}) collective-permute-start(bf16[16,1536]{1,0:T(8,128)(2,1)S(1)} %get-tuple-element.11.rest_0_), channel_id=1, source_target_pairs={{0,4},{1,5},{2,6},{3,7},{4,8},{5,9},{6,10},{7,11},{8,12},{9,13},{1... | collective-permute-start | bytes 147464 | tf_op jit(solution)/shard_map/ppermute | solution.py:206
  8.4 0.8 select_reduce_fusion.3
  11.0 0.8 select_reduce_fusion
  12.4 13.6 %reshape.299.kv_ref = bf16[2048,1536]{1,0:T(8,128)(2,1)} reshape(bf16[1024,2,1536]{2,1,0:T(2,128)(2,1)} %param.4) | data formatting | bytes 12582912 | tf_op jit(solution)/shard_map/reshape | solution.py:49
  26.1 2.8 %copy-done = bf16[2048,1536]{1,0:T(8,128)(2,1)S(1)} copy-done((bf16[2048,1536]{1,0:T(8,128)(2,1)S(1)}, bf16[2048,1536]{1,0:T(8,128)(2,1)}, u32[]{:S(2)}) %copy-start) | copy-done | bytes 6291480
  28.9 3.0 %split_cache.1 = (bf16[1024,1536]{1,0:T(8,128)(2,1)S(1)}, bf16[1024,1536]{1,0:T(8,128)(2,1)S(1)}) custom-call(bf16[2048,1536]{1,0:T(8,128)(2,1)S(1)} %copy-done), custom_call_target="tpu_custom_call" | custom-call | flops 1610612736 | bytes 12582912 | tf_op jit(solution)/shard_map/split_cache/pallas_call | solution.py:38
  31.9 1.6 %copy-done.1 = bf16[1024,1536]{1,0:T(8,128)(2,1)} copy-done((bf16[1024,1536]{1,0:T(8,128)(2,1)}, bf16[1024,1536]{1,0:T(8,128)(2,1)S(1)}, u32[]{:S(2)}) %copy-start.1) | copy-done | bytes 3145752
  34.0 1.2 %collective-permute-start.5 = (bf16[16,1536]{1,0:T(8,128)(2,1)S(1)}, bf16[16,1536]{1,0:T(8,128)(2,1)S(1)}, u32[]{:S(2)}, u32[]{:S(2)}) collective-permute-start(bf16[16,1536]{1,0:T(8,128)(2,1)S(1)} %get-tuple-element.11.rest_0_), channel_id=1, source_target_pairs={{0,6},{1,7},{2,8},{3,9},{4,10},{5,11},{6,12},{7,13},{8,14},{9,15},... | collective-permute-start | bytes 147464 | tf_op jit(solution)/shard_map/ppermute | solution.py:206
  35.3 4.3 %collective-permute-start.6 = (bf16[16,1536]{1,0:T(8,128)(2,1)S(1)}, bf16[16,1536]{1,0:T(8,128)(2,1)S(1)}, u32[]{:S(2)}, u32[]{:S(2)}) collective-permute-start(bf16[16,1536]{1,0:T(8,128)(2,1)S(1)} %get-tuple-element.11.rest_0_), channel_id=1, source_target_pairs={{0,7},{1,8},{2,9},{3,10},{4,11},{5,12},{6,13},{7,14},{8,15},{9,0},... | collective-permute-start | bytes 147464 | tf_op jit(solution)/shard_map/ppermute | solution.py:206
  40.2 2.4 %collective-permute-start.9 = (bf16[16,1536]{1,0:T(8,128)(2,1)S(1)}, bf16[16,1536]{1,0:T(8,128)(2,1)S(1)}, u32[]{:S(2)}, u32[]{:S(2)}) collective-permute-start(bf16[16,1536]{1,0:T(8,128)(2,1)S(1)} %get-tuple-element.11.rest_0_), channel_id=1, source_target_pairs={{0,10},{1,11},{2,12},{3,13},{4,14},{5,15},{6,0},{7,1},{8,2},{9,3},... | collective-permute-start | bytes 147464 | tf_op jit(solution)/shard_map/ppermute | solution.py:206
  43.3 2.9 %collective-permute-start.10 = (bf16[16,1536]{1,0:T(8,128)(2,1)S(1)}, bf16[16,1536]{1,0:T(8,128)(2,1)}, u32[]{:S(2)}, u32[]{:S(2)}) collective-permute-start(bf16[16,1536]{1,0:T(8,128)(2,1)S(1)} %get-tuple-element.11.rest_0_), channel_id=1, source_target_pairs={{0,11},{1,12},{2,13},{3,14},{4,15},{5,0},{6,1},{7,2},{8,3},{9,4},{... | collective-permute-start | bytes 147464 | tf_op jit(solution)/shard_map/ppermute | solution.py:206
  46.8 1.8 %collective-permute-start.11 = (bf16[16,1536]{1,0:T(8,128)(2,1)S(1)}, bf16[16,1536]{1,0:T(8,128)(2,1)}, u32[]{:S(2)}, u32[]{:S(2)}) collective-permute-start(bf16[16,1536]{1,0:T(8,128)(2,1)S(1)} %get-tuple-element.11.rest_0_), channel_id=1, source_target_pairs={{0,12},{1,13},{2,14},{3,15},{4,0},{5,1},{6,2},{7,3},{8,4},{9,5},{1... | collective-permute-start | bytes 147464 | tf_op jit(solution)/shard_map/ppermute | solution.py:206
  49.8 1.4 %collective-permute-start.13 = (bf16[16,1536]{1,0:T(8,128)(2,1)S(1)}, bf16[16,1536]{1,0:T(8,128)(2,1)}, u32[]{:S(2)}, u32[]{:S(2)}) collective-permute-start(bf16[16,1536]{1,0:T(8,128)(2,1)S(1)} %get-tuple-element.11.rest_0_), channel_id=1, source_target_pairs={{0,14},{1,15},{2,0},{3,1},{4,2},{5,3},{6,4},{7,5},{8,6},{9,7},{10,... | collective-permute-start | bytes 147464 | tf_op jit(solution)/shard_map/ppermute | solution.py:206
  51.9 2.2 %collective-permute-start.14 = (bf16[16,1536]{1,0:T(8,128)(2,1)S(1)}, bf16[16,1536]{1,0:T(8,128)(2,1)}, u32[]{:S(2)}, u32[]{:S(2)}) collective-permute-start(bf16[16,1536]{1,0:T(8,128)(2,1)S(1)} %get-tuple-element.11.rest_0_), channel_id=1, source_target_pairs={{0,15},{1,0},{2,1},{3,2},{4,3},{5,4},{6,5},{7,6},{8,7},{9,8},{10,9... | collective-permute-start | bytes 147464 | tf_op jit(solution)/shard_map/ppermute | solution.py:206
  55.8 0.8 copy-done.3
  56.6 0.8 copy-done.5
  57.4 0.8 copy-done.7
  58.2 0.8 copy-done.9
  59.0 0.8 copy-done.11
  59.8 7.2 %attend.1 = bf16[16,8,1664]{2,1,0:T(8,128)(2,1)S(1)} custom-call(s32[1,256]{1,0:T(1,128)S(1)} %fusion.5.target_ref, f32[8,1024]{1,0:T(8,128)S(1)} %reshape.296.bias_ref, f32[8,16]{1,0:T(8,128)S(1)} %bitcast.28, bf16[16,1536]{1,0:T(8,128)(2,1)S(1)} %get-tuple-element.13.fresh_key_ref, bf16[16,1536]{1,0:T(8,128)(2,1)S(1)} %get-tuple-element.12.fresh_value_ref, ...), custom_call_target="tpu_custom_call" | custom-call | flops 805306368 | bytes 6291456 | tf_op jit(solution)/shard_map/attend/pallas_call | solution.py:114
  67.0 18.5 %all_to_all.5.parts_ref = bf16[16,8,1664]{2,1,0:T(8,128)(2,1)S(1)} all-to-all(bf16[16,8,1664]{2,1,0:T(8,128)(2,1)S(1)} %attend.1), channel_id=1, replica_groups=mesh['groups'=2,'blk'=16] {'blk'}, dimensions={0} | all-to-all | bytes 851968 | tf_op jit(solution)/shard_map/all_to_all | solution.py:212
  (77 shorter events, 10.2 us)
Async XLA Ops:
  1.1 33.0 %collective-permute-start = (bf16[16,1536]{1,0:T(8,128)(2,1)S(1)}, bf16[16,1536]{1,0:T(8,128)(2,1)S(1)}, u32[]{:S(2)}, u32[]{:S(2)}) collective-permute-start(bf16[16,1536]{1,0:T(8,128)(2,1)S(1)} %get-tuple-element.11.rest_0_), channel_id=1, source_target_pairs={{0,1},{1,2},{2,3},{3,4},{4,5},{5,6},{6,7},{7,8},{8,9},{9,10},{10,1... | collective-permute-start | bytes 147464 | tf_op jit(solution)/shard_map/ppermute | solution.py:206
  1.6 33.7 %collective-permute-start.1 = (bf16[16,1536]{1,0:T(8,128)(2,1)S(1)}, bf16[16,1536]{1,0:T(8,128)(2,1)S(1)}, u32[]{:S(2)}, u32[]{:S(2)}) collective-permute-start(bf16[16,1536]{1,0:T(8,128)(2,1)S(1)} %get-tuple-element.11.rest_0_), channel_id=1, source_target_pairs={{0,2},{1,3},{2,4},{3,5},{4,6},{5,7},{6,8},{7,9},{8,10},{9,11},{10,... | collective-permute-start | bytes 147464 | tf_op jit(solution)/shard_map/ppermute | solution.py:206
  4.1 35.4 %collective-permute-start.2 = (bf16[16,1536]{1,0:T(8,128)(2,1)S(1)}, bf16[16,1536]{1,0:T(8,128)(2,1)S(1)}, u32[]{:S(2)}, u32[]{:S(2)}) collective-permute-start(bf16[16,1536]{1,0:T(8,128)(2,1)S(1)} %get-tuple-element.11.rest_0_), channel_id=1, source_target_pairs={{0,3},{1,4},{2,5},{3,6},{4,7},{5,8},{6,9},{7,10},{8,11},{9,12},{10... | collective-permute-start | bytes 147464 | tf_op jit(solution)/shard_map/ppermute | solution.py:206
  6.6 33.4 %collective-permute-start.3 = (bf16[16,1536]{1,0:T(8,128)(2,1)S(1)}, bf16[16,1536]{1,0:T(8,128)(2,1)S(1)}, u32[]{:S(2)}, u32[]{:S(2)}) collective-permute-start(bf16[16,1536]{1,0:T(8,128)(2,1)S(1)} %get-tuple-element.11.rest_0_), channel_id=1, source_target_pairs={{0,4},{1,5},{2,6},{3,7},{4,8},{5,9},{6,10},{7,11},{8,12},{9,13},{1... | collective-permute-start | bytes 147464 | tf_op jit(solution)/shard_map/ppermute | solution.py:206
  8.1 32.1 %collective-permute-start.4 = (bf16[16,1536]{1,0:T(8,128)(2,1)S(1)}, bf16[16,1536]{1,0:T(8,128)(2,1)}, u32[]{:S(2)}, u32[]{:S(2)}) collective-permute-start(bf16[16,1536]{1,0:T(8,128)(2,1)S(1)} %get-tuple-element.11.rest_0_), channel_id=1, source_target_pairs={{0,5},{1,6},{2,7},{3,8},{4,9},{5,10},{6,11},{7,12},{8,13},{9,14},{... | collective-permute-start | bytes 147464 | tf_op jit(solution)/shard_map/ppermute | solution.py:206
  26.1 2.8 %copy-start = (bf16[2048,1536]{1,0:T(8,128)(2,1)S(1)}, bf16[2048,1536]{1,0:T(8,128)(2,1)}, u32[]{:S(2)}) copy-start(bf16[2048,1536]{1,0:T(8,128)(2,1)} %reshape.299.kv_ref) | copy-start | bytes 18874372
  31.9 1.7 %copy-start.1 = (bf16[1024,1536]{1,0:T(8,128)(2,1)}, bf16[1024,1536]{1,0:T(8,128)(2,1)S(1)}, u32[]{:S(2)}) copy-start(bf16[1024,1536]{1,0:T(8,128)(2,1)S(1)} %get-tuple-element.8.value_ref) | copy-start | bytes 9437188
  34.0 8.6 %collective-permute-start.5 = (bf16[16,1536]{1,0:T(8,128)(2,1)S(1)}, bf16[16,1536]{1,0:T(8,128)(2,1)S(1)}, u32[]{:S(2)}, u32[]{:S(2)}) collective-permute-start(bf16[16,1536]{1,0:T(8,128)(2,1)S(1)} %get-tuple-element.11.rest_0_), channel_id=1, source_target_pairs={{0,6},{1,7},{2,8},{3,9},{4,10},{5,11},{6,12},{7,13},{8,14},{9,15},... | collective-permute-start | bytes 147464 | tf_op jit(solution)/shard_map/ppermute | solution.py:206
  35.3 10.9 %collective-permute-start.6 = (bf16[16,1536]{1,0:T(8,128)(2,1)S(1)}, bf16[16,1536]{1,0:T(8,128)(2,1)S(1)}, u32[]{:S(2)}, u32[]{:S(2)}) collective-permute-start(bf16[16,1536]{1,0:T(8,128)(2,1)S(1)} %get-tuple-element.11.rest_0_), channel_id=1, source_target_pairs={{0,7},{1,8},{2,9},{3,10},{4,11},{5,12},{6,13},{7,14},{8,15},{9,0},... | collective-permute-start | bytes 147464 | tf_op jit(solution)/shard_map/ppermute | solution.py:206
  39.6 9.0 %collective-permute-start.7 = (bf16[16,1536]{1,0:T(8,128)(2,1)S(1)}, bf16[16,1536]{1,0:T(8,128)(2,1)S(1)}, u32[]{:S(2)}, u32[]{:S(2)}) collective-permute-start(bf16[16,1536]{1,0:T(8,128)(2,1)S(1)} %get-tuple-element.11.rest_0_), channel_id=1, source_target_pairs={{0,8},{1,9},{2,10},{3,11},{4,12},{5,13},{6,14},{7,15},{8,0},{9,1},... | collective-permute-start | bytes 147464 | tf_op jit(solution)/shard_map/ppermute | solution.py:206
  39.9 9.3 %collective-permute-start.8 = (bf16[16,1536]{1,0:T(8,128)(2,1)S(1)}, bf16[16,1536]{1,0:T(8,128)(2,1)S(1)}, u32[]{:S(2)}, u32[]{:S(2)}) collective-permute-start(bf16[16,1536]{1,0:T(8,128)(2,1)S(1)} %get-tuple-element.11.rest_0_), channel_id=1, source_target_pairs={{0,9},{1,10},{2,11},{3,12},{4,13},{5,14},{6,15},{7,0},{8,1},{9,2},... | collective-permute-start | bytes 147464 | tf_op jit(solution)/shard_map/ppermute | solution.py:206
  40.2 11.0 %collective-permute-start.9 = (bf16[16,1536]{1,0:T(8,128)(2,1)S(1)}, bf16[16,1536]{1,0:T(8,128)(2,1)S(1)}, u32[]{:S(2)}, u32[]{:S(2)}) collective-permute-start(bf16[16,1536]{1,0:T(8,128)(2,1)S(1)} %get-tuple-element.11.rest_0_), channel_id=1, source_target_pairs={{0,10},{1,11},{2,12},{3,13},{4,14},{5,15},{6,0},{7,1},{8,2},{9,3},... | collective-permute-start | bytes 147464 | tf_op jit(solution)/shard_map/ppermute | solution.py:206
  43.3 12.2 %collective-permute-start.10 = (bf16[16,1536]{1,0:T(8,128)(2,1)S(1)}, bf16[16,1536]{1,0:T(8,128)(2,1)}, u32[]{:S(2)}, u32[]{:S(2)}) collective-permute-start(bf16[16,1536]{1,0:T(8,128)(2,1)S(1)} %get-tuple-element.11.rest_0_), channel_id=1, source_target_pairs={{0,11},{1,12},{2,13},{3,14},{4,15},{5,0},{6,1},{7,2},{8,3},{9,4},{... | collective-permute-start | bytes 147464 | tf_op jit(solution)/shard_map/ppermute | solution.py:206
  46.1 0.6 copy-start.4
  46.8 8.7 %collective-permute-start.11 = (bf16[16,1536]{1,0:T(8,128)(2,1)S(1)}, bf16[16,1536]{1,0:T(8,128)(2,1)}, u32[]{:S(2)}, u32[]{:S(2)}) collective-permute-start(bf16[16,1536]{1,0:T(8,128)(2,1)S(1)} %get-tuple-element.11.rest_0_), channel_id=1, source_target_pairs={{0,12},{1,13},{2,14},{3,15},{4,0},{5,1},{6,2},{7,3},{8,4},{9,5},{1... | collective-permute-start | bytes 147464 | tf_op jit(solution)/shard_map/ppermute | solution.py:206
  49.2 6.3 %collective-permute-start.12 = (bf16[16,1536]{1,0:T(8,128)(2,1)S(1)}, bf16[16,1536]{1,0:T(8,128)(2,1)}, u32[]{:S(2)}, u32[]{:S(2)}) collective-permute-start(bf16[16,1536]{1,0:T(8,128)(2,1)S(1)} %get-tuple-element.11.rest_0_), channel_id=1, source_target_pairs={{0,13},{1,14},{2,15},{3,0},{4,1},{5,2},{6,3},{7,4},{8,5},{9,6},{10... | collective-permute-start | bytes 147464 | tf_op jit(solution)/shard_map/ppermute | solution.py:206
  49.2 0.6 copy-start.8
  49.8 5.7 %collective-permute-start.13 = (bf16[16,1536]{1,0:T(8,128)(2,1)S(1)}, bf16[16,1536]{1,0:T(8,128)(2,1)}, u32[]{:S(2)}, u32[]{:S(2)}) collective-permute-start(bf16[16,1536]{1,0:T(8,128)(2,1)S(1)} %get-tuple-element.11.rest_0_), channel_id=1, source_target_pairs={{0,14},{1,15},{2,0},{3,1},{4,2},{5,3},{6,4},{7,5},{8,6},{9,7},{10,... | collective-permute-start | bytes 147464 | tf_op jit(solution)/shard_map/ppermute | solution.py:206
  51.9 4.0 %collective-permute-start.14 = (bf16[16,1536]{1,0:T(8,128)(2,1)S(1)}, bf16[16,1536]{1,0:T(8,128)(2,1)}, u32[]{:S(2)}, u32[]{:S(2)}) collective-permute-start(bf16[16,1536]{1,0:T(8,128)(2,1)S(1)} %get-tuple-element.11.rest_0_), channel_id=1, source_target_pairs={{0,15},{1,0},{2,1},{3,2},{4,3},{5,4},{6,5},{7,6},{8,7},{9,8},{10,9... | collective-permute-start | bytes 147464 | tf_op jit(solution)/shard_map/ppermute | solution.py:206
  55.8 0.8 copy-start.3
  56.6 0.8 copy-start.5
  57.4 0.8 copy-start.7
  58.2 0.8 copy-start.9
  59.0 0.8 copy-start.11
  (3 other events, 1.8 us)

commit v2 on v0

v2 whole, which is shorter than its diff:
```python
import jax
import jax.numpy as jnp
from jax import lax
from jax.experimental import pallas as pl
from jax.experimental.pallas import tpu as pltpu
from jax.sharding import PartitionSpec as P

HEAD = 128
SLOT = 4
STEPS = 2
PAIR = STEPS * SLOT
LOG2E = 1.4426950408889634
SCALE = HEAD ** -0.5 * LOG2E
FAR = -1e30
LANES = 128
PART = 16
SLOT_BITS = 2
VMEM = pl.BlockSpec(memory_space=pltpu.VMEM)
SMEM = pl.BlockSpec(memory_space=pltpu.SMEM)
ANY = pl.BlockSpec(memory_space=pl.ANY)


def mesh_digits(device_count):
    bits = (device_count // 2).bit_length() - 1
    far_bits = (bits + 1) // 2
    return 1 << far_bits, 1 << (bits - far_bits)


def place_of(mask, far, near):
    near_bits = near.bit_length() - 1
    core = mask & 1
    near_digit = (mask >> 1) & (near - 1)
    far_digit = mask >> (1 + near_bits)
    return (core * near + near_digit) * far + far_digit


def prepare_kernel(me_ref, counts_ref, rows_ref, cache_ref, fresh_ref,
                   key_ref, value_ref, fresh_key_ref, fresh_value_ref, target_ref, bias_ref, fresh_bias_ref,
                   held, fresh_held, sems):
    tokens, _, width = cache_ref.shape
    slots = fresh_ref.shape[0]
    device_count = counts_ref.shape[1]
    far, near = mesh_digits(device_count)
    block = min(128, tokens)
    blocks = tokens // block

    def fetch(i):
        part = pl.ds(i * block, block)
        return pltpu.make_async_copy(cache_ref.at[part], held.at[part], sems.at[i])

    def fetch_fresh(i):
        return pltpu.make_async_copy(fresh_ref.at[:, 1 + i], fresh_held.at[i], sems.at[blocks + i])

    for i in range(blocks):
        fetch(i).start()
    for i in range(2):
        fetch_fresh(i).start()

    me = me_ref[0]
    col = lax.broadcasted_iota(jnp.int32, target_ref.shape, 1)

    def one_device(dev, carry):
        start0, start1, target = carry
        count0, count1 = counts_ref[0, dev], counts_ref[1, dev]
        local = col - place_of(dev ^ me, far, near) * (STEPS * slots)
        slot, step = local >> 1, local & 1
        rank = slot + jnp.where(step == 0, start0, start1)
        row = place_of((rank >> SLOT_BITS) ^ me, far, near) * PAIR + step * SLOT + (rank & (SLOT - 1))
        good = (local >= 0) & (slot < jnp.where(step == 0, count0, count1))
        return start0 + count0, start1 + count1, jnp.where(good, row, target)

    carry = (jnp.int32(0), jnp.int32(0), jnp.full(target_ref.shape, -1, jnp.int32))
    if device_count <= 16:
        for dev in range(device_count):
            carry = one_device(dev, carry)
    else:
        carry = lax.fori_loop(0, device_count, one_device, carry)
    target_ref[...] = carry[2]

    live0 = [i < counts_ref[0, me] for i in range(slots)]
    live1 = [i < counts_ref[1, me] for i in range(slots)]
    row0 = [jnp.where(live0[i], rows_ref[0, i], -1) for i in range(slots)]
    row1 = [jnp.where(live1[i], rows_ref[1, i], -2) for i in range(slots)]
    token = lax.broadcasted_iota(jnp.int32, bias_ref.shape, 1)
    second = lax.broadcasted_iota(jnp.int32, bias_ref.shape, 0) >= SLOT
    gone = token == row0[0]
    for i in range(1, slots):
        gone = gone | (token == row0[i])
    later = token == row1[0]
    for i in range(1, slots):
        later = later | (token == row1[i])
    bias_ref[...] = jnp.where(gone | (second & later), FAR, 0.0)
    col = lax.broadcasted_iota(jnp.int32, fresh_bias_ref.shape, 1)
    second = (lax.broadcasted_iota(jnp.int32, fresh_bias_ref.shape, 0) >= SLOT).astype(jnp.int32)
    seen = jnp.zeros(fresh_bias_ref.shape, jnp.int32)
    for i in range(slots):
        again = row1[0] == row0[i]
        for j in range(1, slots):
            again = again | (row1[j] == row0[i])
        kept = (live0[i] & jnp.logical_not(again)).astype(jnp.int32)
        early = jnp.where(second == 1, kept, live0[i].astype(jnp.int32))
        seen = jnp.where(col == 2 * i, early, seen)
        seen = jnp.where(col == 2 * i + 1, second * live1[i].astype(jnp.int32), seen)
    fresh_bias_ref[...] = jnp.where(seen == 1, 0.0, FAR)

    out = lax.broadcasted_iota(jnp.int32, (2 * block, 2 * block), 0)
    src = lax.broadcasted_iota(jnp.int32, (2 * block, 2 * block), 1)
    order = (src == jnp.where(out < block, 2 * out, 2 * (out - block) + 1)).astype(jnp.bfloat16)
    pairs = held.reshape(2 * tokens, width)
    for i in range(blocks):
        fetch(i).wait()
        rows = slice(i * block, (i + 1) * block)
        for c in range(0, width, 256):
            part = pairs[2 * i * block:2 * (i + 1) * block, c:c + 256]
            part = jnp.dot(order, part, preferred_element_type=jnp.float32).astype(jnp.bfloat16)
            key_ref[rows, c:c + 256] = part[:block]
            value_ref[rows, c:c + 256] = part[block:]
    for i, ref in enumerate((fresh_key_ref, fresh_value_ref)):
        fetch_fresh(i).wait()
        ref[...] = jnp.zeros_like(ref)
        ref[0:STEPS * slots, :] = fresh_held.at[i].reshape(STEPS * slots, width)[...]


def prepare(me, counts, list_rows, cache, fresh):
    tokens, _, width = cache.shape
    slots = fresh.shape[0]
    fresh_rows = -(-STEPS * slots // 16) * 16
    f32, bf16 = jnp.float32, jnp.bfloat16
    shapes = (
        jax.ShapeDtypeStruct((tokens, width), bf16),
        jax.ShapeDtypeStruct((tokens, width), bf16),
        jax.ShapeDtypeStruct((fresh_rows, width), bf16),
        jax.ShapeDtypeStruct((fresh_rows, width), bf16),
        jax.ShapeDtypeStruct((1, counts.shape[1] * STEPS * slots), jnp.int32),
        jax.ShapeDtypeStruct((PAIR, tokens), f32),
        jax.ShapeDtypeStruct((PAIR, fresh_rows), f32),
    )
    blocks = tokens // min(128, tokens)
    return pl.pallas_call(
        prepare_kernel,
        out_shape=shapes,
        in_specs=[SMEM, SMEM, SMEM, ANY, ANY],
        out_specs=(VMEM,) * len(shapes),
        scratch_shapes=[
            pltpu.VMEM((tokens, 2, width), bf16),
            pltpu.VMEM((2, slots, STEPS, width), bf16),
            pltpu.SemaphoreType.DMA((blocks + 2,)),
        ],
        compiler_params=pltpu.CompilerParams(vmem_limit_bytes=22 << 20),
        cost_estimate=pl.CostEstimate(
            flops=8 * 128 * tokens * width, bytes_accessed=8 * tokens * width, transcendentals=0
        ),
        name="prepare",
    )(me, counts, list_rows, cache, fresh)


def two_parts(x):
    high = x.astype(jnp.bfloat16).astype(jnp.float32)
    return high, x - high


def pack_stats(high, total):
    lane = lax.broadcasted_iota(jnp.int32, high.shape, 1)
    high = jnp.where(lane < PART, high, 0.0)
    total = jnp.where(lane < PART, total, 0.0)
    stats, rest = two_parts(high)
    second, third = two_parts(rest)
    for n, part in enumerate((second, third) + two_parts(total)):
        stats = stats + pltpu.roll(part, PART * (n + 1), 1)
    return stats


def unpack_stats(stats):
    def part(n):
        return pltpu.roll(stats, LANES - PART * n, 1)

    return stats + part(1) + part(2), part(3) + part(4)


def attend_kernel(target_ref, bias_ref, fresh_bias_ref, fresh_key_ref, fresh_value_ref, key_ref, value_ref, *rest):
    gathered_refs, (keep_ref, send_ref) = rest[:-2], rest[-2:]
    width = key_ref.shape[1]
    heads = width // HEAD
    half = keep_ref.shape[0]
    nt = (((1,), (1,)), ((), ()))

    def attend_rows(base, chunk, stores):
        row = lax.broadcasted_iota(jnp.int32, (chunk, target_ref.shape[1]), 0)
        pick = (row == target_ref[...] - base).astype(jnp.bfloat16)
        queries, at = None, 0
        for ref in gathered_refs:
            count = ref.shape[0] * STEPS
            slots = ref.reshape(count, width)[...]
            part = jnp.dot(pick[:, at:at + count], slots, preferred_element_type=jnp.float32)
            queries = part if queries is None else queries + part
            at += count
        queries = queries.astype(jnp.bfloat16)
        bias = bias_ref[...]
        fresh_bias = fresh_bias_ref[...]
        lane = lax.broadcasted_iota(jnp.int32, (chunk, LANES), 1)
        highs = jnp.zeros((chunk, LANES), jnp.float32)
        totals = jnp.zeros((chunk, LANES), jnp.float32)
        for h in range(heads):
            cols = slice(h * HEAD, (h + 1) * HEAD)
            q = queries[:, cols]
            s = lax.dot_general(q, key_ref[:, cols], nt, preferred_element_type=jnp.float32)
            sf = lax.dot_general(q, fresh_key_ref[:, cols], nt, preferred_element_type=jnp.float32)
            s = (s.reshape(chunk // PAIR, PAIR, -1) + bias[None]).reshape(chunk, -1)
            sf = (sf.reshape(chunk // PAIR, PAIR, -1) + fresh_bias[None]).reshape(chunk, -1)
            high = jnp.maximum(jnp.max(s, axis=1, keepdims=True), jnp.max(sf, axis=1, keepdims=True))
            w = jnp.exp2((s - high) * SCALE)
            wf = jnp.exp2((sf - high) * SCALE)
            total = jnp.sum(w, axis=1, keepdims=True) + jnp.sum(wf, axis=1, keepdims=True)
            o = jnp.dot(w.astype(jnp.bfloat16), value_ref[:, cols], preferred_element_type=jnp.float32)
            o += jnp.dot(wf.astype(jnp.bfloat16), fresh_value_ref[:, cols], preferred_element_type=jnp.float32)
            o = o * (1.0 / total)
            for ref, to, start, count in stores:
                ref[pl.ds(to, count), cols] = o[start:start + count].astype(ref.dtype)
            highs = jnp.where(lane == h, high, highs)
            totals = jnp.where(lane == h, total, totals)
        stats = pack_stats(highs, totals)
        for ref, to, start, count in stores:
            ref[pl.ds(to, count), width:] = stats[start:start + count].astype(ref.dtype)

    if 2 * half <= 128:
        attend_rows(0, 2 * half, [(keep_ref, 0, 0, half), (send_ref, 0, half, half)])
    else:
        for ref, base in ((keep_ref, 0), (send_ref, half)):
            @pl.loop(0, half // 128)
            def _(i, ref=ref, base=base):
                to = pl.multiple_of(i * 128, 128)
                attend_rows(base + to, 128, [(ref, to, 0, 128)])


def attend(slots, target, bias, fresh_bias, fresh_key, fresh_value, key, value, gathered):
    tokens, width = key.shape
    rows = target.shape[1] * SLOT // slots
    shape = (rows // 2, width + LANES)
    return pl.pallas_call(
        attend_kernel,
        out_shape=(jax.ShapeDtypeStruct(shape, jnp.float32), jax.ShapeDtypeStruct(shape, jnp.bfloat16)),
        in_specs=[VMEM] * (7 + len(gathered)),
        out_specs=(VMEM, VMEM),
        compiler_params=pltpu.CompilerParams(vmem_limit_bytes=24 << 20),
        cost_estimate=pl.CostEstimate(
            flops=4 * rows * tokens * width, bytes_accessed=4 * tokens * width,
            transcendentals=rows * tokens * width // HEAD,
        ),
        name="attend",
    )(target, bias, fresh_bias, fresh_key, fresh_value, key, value, *gathered)


def merge_kernel(count, last, *refs):
    parts, outs = refs[:count], refs[count:]
    rows, width = parts[0].shape
    width -= LANES
    stats = [unpack_stats(ref[:, width:].astype(jnp.float32)) for ref in parts]
    top = stats[0][0]
    for high, _ in stats[1:]:
        top = jnp.maximum(top, high)
    weights = [total * jnp.exp2((high - top) * SCALE) for high, total in stats]
    total = weights[0]
    for w in weights[1:]:
        total = total + w
    used = lax.broadcasted_iota(jnp.int32, total.shape, 1) < width // HEAD
    share = 1.0 / jnp.where(used, total, 1.0)
    weights = [w * share for w in weights]
    for h in range(width // HEAD):
        cols = slice(h * HEAD, (h + 1) * HEAD)
        o = parts[0][:, cols].astype(jnp.float32) * weights[0][:, h:h + 1]
        for ref, w in zip(parts[1:], weights[1:]):
            o = o + ref[:, cols].astype(jnp.float32) * w[:, h:h + 1]
        if last:
            for s in range(STEPS):
                outs[0][s, :, cols] = o[s * SLOT:(s + 1) * SLOT].astype(jnp.bfloat16)
        else:
            step = rows // len(outs)
            for n, ref in enumerate(outs):
                ref[:, cols] = o[n * step:(n + 1) * step].astype(ref.dtype)
    if not last:
        packed = pack_stats(jnp.where(used, top, 0.0), jnp.where(used, total, 0.0))
        for n, ref in enumerate(outs):
            ref[:, width:] = packed[n * step:(n + 1) * step].astype(ref.dtype)


def merge(parts, out_count, name):
    rows, width = parts[0].shape
    last = out_count == 0
    if last:
        shapes = (jax.ShapeDtypeStruct((STEPS, SLOT, width - LANES), jnp.bfloat16),)
    else:
        shapes = tuple(
            jax.ShapeDtypeStruct((rows // out_count, width), jnp.bfloat16 if n else jnp.float32)
            for n in range(out_count)
        )

    def kernel(*refs):
        merge_kernel(len(parts), last, *refs)

    return pl.pallas_call(
        kernel,
        out_shape=shapes,
        in_specs=[VMEM] * len(parts),
        out_specs=(VMEM,) * len(shapes),
        compiler_params=pltpu.CompilerParams(vmem_limit_bytes=16 << 20),
        name=name,
    )(*parts)


def body(cache_kv, fresh_qkv, list_rows, counts):
    device_count = lax.axis_size("blk")
    me = lax.axis_index("blk")
    far, near = mesh_digits(device_count)

    def swap(x, mask):
        return lax.ppermute(x, "blk", [(i, i ^ mask) for i in range(device_count)])

    fresh = fresh_qkv.transpose(1, 2, 0, 3)
    mine = fresh[:, 0]
    column = jnp.concatenate([mine] + [swap(mine, k * near * 2) for k in range(1, far)])
    plane = [column] + [swap(column, k * 2) for k in range(1, near)]
    gathered = plane + [swap(x, 1) for x in plane]
    ready = prepare(me.reshape(1), counts, list_rows, cache_kv, fresh)
    key, value, fresh_key, fresh_value, target, bias, fresh_bias = ready
    keep, send = attend(list_rows.shape[1], target, bias, fresh_bias, fresh_key, fresh_value, key, value, gathered)
    keep, *sends = merge([keep, swap(send, 1)], near, "merge_core")
    sends = [swap(x, (k + 1) * 2) for k, x in enumerate(sends)]
    keep, *sends = merge([keep] + sends, far, "merge_near")
    sends = [swap(x, (k + 1) * near * 2) for k, x in enumerate(sends)]
    return merge([keep] + sends, 0, "merge_far")[0]


def solution(mesh):
    in_specs = (
        P(("groups", "blk"), None, None),
        P(None, ("groups", "blk"), None, None),
        P(None, ("groups", "blk")),
        P(None, "groups"),
    )
    out_specs = P(None, ("groups", "blk"), None)
    return jax.shard_map(body, mesh=mesh, in_specs=in_specs, out_specs=out_specs, check_vma=False)
```

time: 332 us -> 48.5 us (0.15)
  blocking collectives: 161 us -> 0 us
  local copies, waits for them, and re-layouts: 110 us -> 6.04 us
  between operations: 14.3 us -> 0.07 us
  waiting for transfers between devices: 30.2 us -> 16 us
  starting transfers between devices: 0.01 us -> 14 us
  Pallas kernels: 0 us -> 11.9 us
  matrix products: 9.63 us -> 0 us
  other arithmetic: 5.33 us -> 0.22 us
    slice x11 -> x0, local copies, waits for them, and re-layouts: 86.4 us -> none  [the longest x4 57.5 us: local_terms(): value_rows = kv_cache[:, 1, :].reshape(kv_cache.shape[0], head_count, HEAD)]
    pmax x1 -> x0, blocking collectives: 59.1 us -> none  [combine_rows(): overall = lax.pmax(highest, 'blk')]
    unnamed x1 -> x0, blocking collectives: 58 us -> none
    all_gather x2 -> x0, blocking collectives: 43.9 us -> none  [body(): lax.all_gather(fresh_qkv[step_index, :, 0, :], 'blk', axis=0, tiled=True)]
    unnamed x2 -> x0, waiting for transfers between devices: 30.2 us -> none
    ppermute x0 -> x11, waiting for transfers between devices: none -> 16 us  [swap(): return lax.ppermute(x, 'blk', [(i, i ^ mask) for i in range(device_count)])]
    ppermute x0 -> x11, starting transfers between devices: none -> 14 us  [swap(): return lax.ppermute(x, 'blk', [(i, i ^ mask) for i in range(device_count)])]
    pallas_call x0 -> x5, Pallas kernels: none -> 11.9 us  [the longest x1 5.4 us: attend(): pl.pallas_call(attend_kernel, out_shape=(jax.ShapeDtypeStruct(shape, jnp....]
  transfers between devices with their start and end apart: 1 -> 11, of which waited for: 1 -> 7; matrix products, arithmetic and copies ran while one was open for 0% -> 0% of each run, Pallas kernels for 0% -> 10%
where the time goes in v2:
time: 48.5 us; the launch traced here: 48.2 us
  waiting for transfers between devices  16 us (33%)
  starting transfers between devices  14 us (29%)
  Pallas kernels  11.9 us (25%)
  local copies, waits for them, and re-layouts  6.04 us (12%)
    ppermute x11, waiting for transfers between devices, swap(): return lax.ppermute(x, 'blk', [(i, i ^ mask) for i in range(device_count)])  16 us
    ppermute x11, starting transfers between devices, swap(): return lax.ppermute(x, 'blk', [(i, i ^ mask) for i in range(device_count)])  14 us
    unnamed x9, local copies, waits for them, and re-layouts  6.01 us
    pallas_call x1, Pallas kernels, attend(): pl.pallas_call(attend_kernel, out_shape=(jax.ShapeDtypeStruct(shape, jnp....  5.4 us
    pallas_call x1, Pallas kernels, prepare(): pl.pallas_call(prepare_kernel, out_shape=shapes, in_specs=[SMEM, SMEM, SM...  4.95 us
    pallas_call x3, Pallas kernels, merge(): pl.pallas_call(kernel, out_shape=shapes, in_specs=[VMEM] * len(parts), ou...  1.6 us
  transfers between devices with their start and end apart: 11, of which 7 were waited for; matrix products, arithmetic and copies ran while one was open for 0% of the time, Pallas kernels for 10%

profile of v2, /device:TPU:0, one launch (start us, length us, event | category | flops | bytes accessed | tf_op | source)
XLA Modules:
  0.0 48.2 jit_solution(6694383151583760137)
XLA Ops:
  0.0 1.0 %copy.9 = bf16[2,6,3,1536]{3,0,1,2:T(2,128)(2,1)S(1)} copy(bf16[2,6,3,1536]{3,0,2,1:T(2,128)(2,1)} %param.5) | data formatting | bytes 221184 | tf_op args[1]
  1.0 5.1 %collective-permute-start.2 = (bf16[6,2,1536]{2,1,0:T(2,128)(2,1)S(1)}, bf16[6,2,1536]{2,1,0:T(2,128)(2,1)S(1)}, u32[]{:S(2)}, u32[]{:S(2)}) collective-permute-start(bf16[6,2,1536]{2,1,0:T(2,128)(2,1)S(1)} %slice_bitcast_fusion), channel_id=1, source_target_pairs={{0,12},{1,13},{2,14},{3,15},{4,8},{5,9},{6,10},{7,11},{8,4},{9,5},... | collective-permute-start | bytes 110600 | tf_op jit(solution)/shard_map/ppermute | solution.py:316
  6.1 0.6 %collective-permute-start = (bf16[6,2,1536]{2,1,0:T(2,128)(2,1)S(1)}, bf16[6,2,1536]{2,1,0:T(2,128)(2,1)S(1)}, u32[]{:S(2)}, u32[]{:S(2)}) collective-permute-start(bf16[6,2,1536]{2,1,0:T(2,128)(2,1)S(1)} %slice_bitcast_fusion), channel_id=1, source_target_pairs={{0,4},{1,5},{2,6},{3,7},{4,0},{5,1},{6,2},{7,3},{8,12},{9,13},{10,... | collective-permute-start | bytes 110600 | tf_op jit(solution)/shard_map/ppermute | solution.py:316
  6.8 1.3 %collective-permute-done.2 = bf16[6,2,1536]{2,1,0:T(2,128)(2,1)S(1)} collective-permute-done((bf16[6,2,1536]{2,1,0:T(2,128)(2,1)S(1)}, bf16[6,2,1536]{2,1,0:T(2,128)(2,1)S(1)}, u32[]{:S(2)}, u32[]{:S(2)}) %collective-permute-start.2) | collective-permute-done | bytes 36896 | tf_op jit(solution)/shard_map/ppermute | solution.py:316
  8.1 2.9 %collective-permute-done.1 = bf16[6,2,1536]{2,1,0:T(2,128)(2,1)S(1)} collective-permute-done((bf16[6,2,1536]{2,1,0:T(2,128)(2,1)S(1)}, bf16[6,2,1536]{2,1,0:T(2,128)(2,1)S(1)}, u32[]{:S(2)}, u32[]{:S(2)}) %collective-permute-start.1) | collective-permute-done | bytes 36896 | tf_op jit(solution)/shard_map/ppermute | solution.py:316
  11.2 1.6 %collective-permute-start.3 = (bf16[24,2,1536]{2,1,0:T(2,128)(2,1)S(1)}, bf16[24,2,1536]{2,1,0:T(2,128)(2,1)S(1)}, u32[]{:S(2)}, u32[]{:S(2)}) collective-permute-start(bf16[24,2,1536]{2,1,0:T(2,128)(2,1)S(1)} %pad_maximum_fusion.rest_0_), channel_id=1, source_target_pairs={{0,2},{1,3},{2,0},{3,1},{4,6},{5,7},{6,4},{7,5},{8,10},{9,11},{10,... | collective-permute-start | bytes 442376 | tf_op jit(solution)/shard_map/ppermute | solution.py:316
  12.8 3.6 %collective-permute-done.3.rest_1_ = bf16[24,2,1536]{2,1,0:T(2,128)(2,1)S(1)} collective-permute-done((bf16[24,2,1536]{2,1,0:T(2,128)(2,1)S(1)}, bf16[24,2,1536]{2,1,0:T(2,128)(2,1)S(1)}, u32[]{:S(2)}, u32[]{:S(2)}) %collective-permute-start.3) | collective-permute-done | bytes 147488 | tf_op jit(solution)/shard_map/ppermute | solution.py:316
  16.4 2.8 %copy-done = bf16[1024,2,1536]{2,1,0:T(2,128)(2,1)S(1)} copy-done((bf16[1024,2,1536]{2,1,0:T(2,128)(2,1)S(1)}, bf16[1024,2,1536]{2,1,0:T(2,128)(2,1)}, u32[]{:S(2)}) %copy-start) | copy-done | bytes 6291480
  19.2 0.9 %copy-done.1 = bf16[2,6,3,1536]{3,0,2,1:T(2,128)(2,1)S(1)} copy-done((bf16[2,6,3,1536]{3,0,2,1:T(2,128)(2,1)S(1)}, bf16[2,6,3,1536]{3,0,2,1:T(2,128)(2,1)}, u32[]{:S(2)}) %copy-start.1) | copy-done | bytes 110616
  20.1 0.7 %copy-done.2 = s32[2,16]{1,0:T(2,128)S(1)} copy-done((s32[2,16]{1,0:T(2,128)S(1)}, s32[2,16]{1,0:T(2,128)}, u32[]{:S(2)}) %copy-start.2) | copy-done | bytes 152
  20.8 0.7 %copy-done.3 = s32[2,6]{1,0:T(2,128)S(1)} copy-done((s32[2,6]{1,0:T(2,128)S(1)}, s32[2,6]{1,0:T(2,128)}, u32[]{:S(2)}) %copy-start.3) | copy-done | bytes 72
  21.5 5.0 %prepare.1 = (bf16[1024,1536]{1,0:T(8,128)(2,1)S(1)}, bf16[1024,1536]{1,0:T(8,128)(2,1)S(1)}, bf16[16,1536]{1,0:T(8,128)(2,1)S(1)}, bf16[16,1536]{1,0:T(8,128)(2...) custom-call(s32[1]{0:T(128)} %bitcast.me_ref, s32[2,16]{1,0:T(2,128)S(1)} %copy-done.2, ...), custom_call_target="tpu_custom_call" | custom-call | flops 1610612736 | bytes 12582912 | tf_op jit(solution)/shard_map/prepare/pallas_call | solution.py:139
  26.4 5.4 %attend.1 = (f32[64,1664]{1,0:T(8,128)S(1)}, bf16[64,1664]{1,0:T(8,128)(2,1)S(1)}) custom-call(s32[1,192]{1,0:T(1,128)S(1)} %get-tuple-element.20.target_ref, f32[8,1024]{1,0:T(8,128)S(1)} %get-tuple-element.21.bias_ref, f32[8,16]{1,0:T(8,128)S(1)} %get-tuple-element.22.fresh_bias_ref, bf16[16,1536]{1,0:T(8,128)(2,1)S(1)} %get-tuple-element.23.fresh_key_ref, ...), custom_call_target="tpu_custom_call" | custom-call | flops 805306368 | bytes 6291456 | tf_op jit(solution)/shard_map/attend/pallas_call | solution.py:239
  31.8 0.6 %collective-permute-start.6 = (bf16[64,1664]{1,0:T(8,128)(2,1)S(1)}, bf16[64,1664]{1,0:T(8,128)(2,1)S(1)}, u32[]{:S(2)}, u32[]{:S(2)}) collective-permute-start(bf16[64,1664]{1,0:T(8,128)(2,1)S(1)} %get-tuple-element.28), channel_id=1, source_target_pairs={{0,1},{1,0},{2,3},{3,2},{4,5},{5,4},{6,7},{7,6},{8,9},{9,8},{10,11... | collective-permute-start | bytes 638984 | tf_op jit(solution)/shard_map/ppermute | solution.py:316
  32.4 1.1 %collective-permute-done.6.refs_1_ = bf16[64,1664]{1,0:T(8,128)(2,1)S(1)} collective-permute-done((bf16[64,1664]{1,0:T(8,128)(2,1)S(1)}, bf16[64,1664]{1,0:T(8,128)(2,1)S(1)}, u32[]{:S(2)}, u32[]{:S(2)}) %collective-permute-start.6) | collective-permute-done | bytes 213024 | tf_op jit(solution)/shard_map/ppermute | solution.py:316
  33.5 0.4 merge_core.1
  33.9 1.6 %collective-permute-start.7 = (bf16[32,1664]{1,0:T(8,128)(2,1)S(1)}, bf16[32,1664]{1,0:T(8,128)(2,1)S(1)}, u32[]{:S(2)}, u32[]{:S(2)}) collective-permute-start(bf16[32,1664]{1,0:T(8,128)(2,1)S(1)} %get-tuple-element.30), channel_id=1, source_target_pairs={{0,2},{1,3},{2,0},{3,1},{4,6},{5,7},{6,4},{7,5},{8,10},{9,11},{10,... | collective-permute-start | bytes 319496 | tf_op jit(solution)/shard_map/ppermute | solution.py:316
  35.5 3.7 %collective-permute-done.7.refs_1_ = bf16[32,1664]{1,0:T(8,128)(2,1)S(1)} collective-permute-done((bf16[32,1664]{1,0:T(8,128)(2,1)S(1)}, bf16[32,1664]{1,0:T(8,128)(2,1)S(1)}, u32[]{:S(2)}, u32[]{:S(2)}) %collective-permute-start.7) | collective-permute-done | bytes 106528 | tf_op jit(solution)/shard_map/ppermute | solution.py:316
  39.3 0.3 merge_near.1
  39.6 2.1 %collective-permute-start.9 = (bf16[8,1664]{1,0:T(8,128)(2,1)S(1)}, bf16[8,1664]{1,0:T(8,128)(2,1)S(1)}, u32[]{:S(2)}, u32[]{:S(2)}) collective-permute-start(bf16[8,1664]{1,0:T(8,128)(2,1)S(1)} %get-tuple-element.33), channel_id=1, source_target_pairs={{0,8},{1,9},{2,10},{3,11},{4,12},{5,13},{6,14},{7,15},{8,0},{9,1},... | collective-permute-start | bytes 79880 | tf_op jit(solution)/shard_map/ppermute | solution.py:316
  41.7 2.3 %collective-permute-start.10 = (bf16[8,1664]{1,0:T(8,128)(2,1)S(1)}, bf16[8,1664]{1,0:T(8,128)(2,1)S(1)}, u32[]{:S(2)}, u32[]{:S(2)}) collective-permute-start(bf16[8,1664]{1,0:T(8,128)(2,1)S(1)} %get-tuple-element.34), channel_id=1, source_target_pairs={{0,12},{1,13},{2,14},{3,15},{4,8},{5,9},{6,10},{7,11},{8,4},{9,5},... | collective-permute-start | bytes 79880 | tf_op jit(solution)/shard_map/ppermute | solution.py:316
  44.0 0.4 collective-permute-done.9.refs_2_
  44.5 2.9 %collective-permute-done.10.refs_3_ = bf16[8,1664]{1,0:T(8,128)(2,1)S(1)} collective-permute-done((bf16[8,1664]{1,0:T(8,128)(2,1)S(1)}, bf16[8,1664]{1,0:T(8,128)(2,1)S(1)}, u32[]{:S(2)}, u32[]{:S(2)}) %collective-permute-start.10) | collective-permute-done | bytes 26656 | tf_op jit(solution)/shard_map/ppermute | solution.py:316
  47.4 0.9 %merge_far.1 = bf16[2,4,1536]{2,1,0:T(4,128)(2,1)} custom-call(f32[8,1664]{1,0:T(8,128)S(1)} %get-tuple-element.31.refs_0_, bf16[8,1664]{1,0:T(8,128)(2,1)S(1)} %collective-permute-done.8.refs_1_, bf16[8,1664]{1,0:T(8,128)(2,1)S(1)} %collective-permute-done.9.refs_2_, bf16[8,1664]{1,0:T(8,128)(2,1)S(1)} %collective-permute-done.10.refs_3_), custom_call_target="tpu_custom_call" | custom-call | tf_op jit(solution)/shard_map/merge_far/pallas_call | solution.py:300
  (14 shorter events, 0.3 us)
Async XLA Ops:
  1.0 7.1 %collective-permute-start.2 = (bf16[6,2,1536]{2,1,0:T(2,128)(2,1)S(1)}, bf16[6,2,1536]{2,1,0:T(2,128)(2,1)S(1)}, u32[]{:S(2)}, u32[]{:S(2)}) collective-permute-start(bf16[6,2,1536]{2,1,0:T(2,128)(2,1)S(1)} %slice_bitcast_fusion), channel_id=1, source_target_pairs={{0,12},{1,13},{2,14},{3,15},{4,8},{5,9},{6,10},{7,11},{8,4},{9,5},... | collective-permute-start | bytes 110600 | tf_op jit(solution)/shard_map/ppermute | solution.py:316
  6.1 4.9 %collective-permute-start.1 = (bf16[6,2,1536]{2,1,0:T(2,128)(2,1)S(1)}, bf16[6,2,1536]{2,1,0:T(2,128)(2,1)S(1)}, u32[]{:S(2)}, u32[]{:S(2)}) collective-permute-start(bf16[6,2,1536]{2,1,0:T(2,128)(2,1)S(1)} %slice_bitcast_fusion), channel_id=1, source_target_pairs={{0,8},{1,9},{2,10},{3,11},{4,12},{5,13},{6,14},{7,15},{8,0},{9,1},... | collective-permute-start | bytes 110600 | tf_op jit(solution)/shard_map/ppermute | solution.py:316
  6.1 4.9 %collective-permute-start = (bf16[6,2,1536]{2,1,0:T(2,128)(2,1)S(1)}, bf16[6,2,1536]{2,1,0:T(2,128)(2,1)S(1)}, u32[]{:S(2)}, u32[]{:S(2)}) collective-permute-start(bf16[6,2,1536]{2,1,0:T(2,128)(2,1)S(1)} %slice_bitcast_fusion), channel_id=1, source_target_pairs={{0,4},{1,5},{2,6},{3,7},{4,0},{5,1},{6,2},{7,3},{8,12},{9,13},{10,... | collective-permute-start | bytes 110600 | tf_op jit(solution)/shard_map/ppermute | solution.py:316
  11.2 5.2 %collective-permute-start.3 = (bf16[24,2,1536]{2,1,0:T(2,128)(2,1)S(1)}, bf16[24,2,1536]{2,1,0:T(2,128)(2,1)S(1)}, u32[]{:S(2)}, u32[]{:S(2)}) collective-permute-start(bf16[24,2,1536]{2,1,0:T(2,128)(2,1)S(1)} %pad_maximum_fusion.rest_0_), channel_id=1, source_target_pairs={{0,2},{1,3},{2,0},{3,1},{4,6},{5,7},{6,4},{7,5},{8,10},{9,11},{10,... | collective-permute-start | bytes 442376 | tf_op jit(solution)/shard_map/ppermute | solution.py:316
  12.8 13.6 %collective-permute-start.4 = (bf16[24,2,1536]{2,1,0:T(2,128)(2,1)S(1)}, bf16[24,2,1536]{2,1,0:T(2,128)(2,1)S(1)}, u32[]{:S(2)}, u32[]{:S(2)}) collective-permute-start(bf16[24,2,1536]{2,1,0:T(2,128)(2,1)S(1)} %pad_maximum_fusion.rest_0_), channel_id=1, source_target_pairs={{0,1},{1,0},{2,3},{3,2},{4,5},{5,4},{6,7},{7,6},{8,9},{9,8},{10,11... | collective-permute-start | bytes 442376 | tf_op jit(solution)/shard_map/ppermute | solution.py:316
  16.4 10.0 %collective-permute-start.5 = (bf16[24,2,1536]{2,1,0:T(2,128)(2,1)S(1)}, bf16[24,2,1536]{2,1,0:T(2,128)(2,1)S(1)}, u32[]{:S(2)}, u32[]{:S(2)}) collective-permute-start(bf16[24,2,1536]{2,1,0:T(2,128)(2,1)S(1)} %collective-permute-done.3.rest_1_), channel_id=1, source_target_pairs={{0,1},{1,0},{2,3},{3,2},{4,5},{5,4},{6,7},{7,6},{8,9},{9,8},{10,11... | collective-permute-start | bytes 442376 | tf_op jit(solution)/shard_map/ppermute | solution.py:316
  16.4 2.8 %copy-start = (bf16[1024,2,1536]{2,1,0:T(2,128)(2,1)S(1)}, bf16[1024,2,1536]{2,1,0:T(2,128)(2,1)}, u32[]{:S(2)}) copy-start(bf16[1024,2,1536]{2,1,0:T(2,128)(2,1)} %cache_ref.1) | copy-start | bytes 18874372
  19.2 0.9 %copy-start.1 = (bf16[2,6,3,1536]{3,0,2,1:T(2,128)(2,1)S(1)}, bf16[2,6,3,1536]{3,0,2,1:T(2,128)(2,1)}, u32[]{:S(2)}) copy-start(bf16[2,6,3,1536]{3,0,2,1:T(2,128)(2,1)} %param.5) | copy-start | bytes 331780
  20.1 0.7 %copy-start.2 = (s32[2,16]{1,0:T(2,128)S(1)}, s32[2,16]{1,0:T(2,128)}, u32[]{:S(2)}) copy-start(s32[2,16]{1,0:T(2,128)} %counts_ref.1) | copy-start | bytes 388
  20.8 0.7 %copy-start.3 = (s32[2,6]{1,0:T(2,128)S(1)}, s32[2,6]{1,0:T(2,128)}, u32[]{:S(2)}) copy-start(s32[2,6]{1,0:T(2,128)} %rows_ref.1) | copy-start | bytes 148
  31.8 1.7 %collective-permute-start.6 = (bf16[64,1664]{1,0:T(8,128)(2,1)S(1)}, bf16[64,1664]{1,0:T(8,128)(2,1)S(1)}, u32[]{:S(2)}, u32[]{:S(2)}) collective-permute-start(bf16[64,1664]{1,0:T(8,128)(2,1)S(1)} %get-tuple-element.28), channel_id=1, source_target_pairs={{0,1},{1,0},{2,3},{3,2},{4,5},{5,4},{6,7},{7,6},{8,9},{9,8},{10,11... | collective-permute-start | bytes 638984 | tf_op jit(solution)/shard_map/ppermute | solution.py:316
  33.9 5.3 %collective-permute-start.7 = (bf16[32,1664]{1,0:T(8,128)(2,1)S(1)}, bf16[32,1664]{1,0:T(8,128)(2,1)S(1)}, u32[]{:S(2)}, u32[]{:S(2)}) collective-permute-start(bf16[32,1664]{1,0:T(8,128)(2,1)S(1)} %get-tuple-element.30), channel_id=1, source_target_pairs={{0,2},{1,3},{2,0},{3,1},{4,6},{5,7},{6,4},{7,5},{8,10},{9,11},{10,... | collective-permute-start | bytes 319496 | tf_op jit(solution)/shard_map/ppermute | solution.py:316
  39.6 4.5 %collective-permute-start.8 = (bf16[8,1664]{1,0:T(8,128)(2,1)S(1)}, bf16[8,1664]{1,0:T(8,128)(2,1)S(1)}, u32[]{:S(2)}, u32[]{:S(2)}) collective-permute-start(bf16[8,1664]{1,0:T(8,128)(2,1)S(1)} %get-tuple-element.32), channel_id=1, source_target_pairs={{0,4},{1,5},{2,6},{3,7},{4,0},{5,1},{6,2},{7,3},{8,12},{9,13},{10,... | collective-permute-start | bytes 79880 | tf_op jit(solution)/shard_map/ppermute | solution.py:316
  39.6 4.8 %collective-permute-start.9 = (bf16[8,1664]{1,0:T(8,128)(2,1)S(1)}, bf16[8,1664]{1,0:T(8,128)(2,1)S(1)}, u32[]{:S(2)}, u32[]{:S(2)}) collective-permute-start(bf16[8,1664]{1,0:T(8,128)(2,1)S(1)} %get-tuple-element.33), channel_id=1, source_target_pairs={{0,8},{1,9},{2,10},{3,11},{4,12},{5,13},{6,14},{7,15},{8,0},{9,1},... | collective-permute-start | bytes 79880 | tf_op jit(solution)/shard_map/ppermute | solution.py:316
  41.7 5.6 %collective-permute-start.10 = (bf16[8,1664]{1,0:T(8,128)(2,1)S(1)}, bf16[8,1664]{1,0:T(8,128)(2,1)S(1)}, u32[]{:S(2)}, u32[]{:S(2)}) collective-permute-start(bf16[8,1664]{1,0:T(8,128)(2,1)S(1)} %get-tuple-element.34), channel_id=1, source_target_pairs={{0,12},{1,13},{2,14},{3,15},{4,8},{5,9},{6,10},{7,11},{8,4},{9,5},... | collective-permute-start | bytes 79880 | tf_op jit(solution)/shard_map/ppermute | solution.py:316

commit v3 on v2

--- a/solution.py
+++ b/solution.py
@@ -17,7 +17,7 @@
 SLOT_BITS = 2
 VMEM = pl.BlockSpec(memory_space=pltpu.VMEM)
 SMEM = pl.BlockSpec(memory_space=pltpu.SMEM)
-ANY = pl.BlockSpec(memory_space=pl.ANY)
+HBM = pl.BlockSpec(memory_space=pltpu.HBM)
 
 
 def mesh_digits(device_count):
@@ -34,12 +34,12 @@
     return (core * near + near_digit) * far + far_digit
 
 
-def prepare_kernel(me_ref, counts_ref, rows_ref, cache_ref, fresh_ref,
+def prepare_kernel(table_ref, cache_ref, new_key_ref, new_value_ref,
                    key_ref, value_ref, fresh_key_ref, fresh_value_ref, target_ref, bias_ref, fresh_bias_ref,
-                   held, fresh_held, sems):
+                   held, sems):
     tokens, _, width = cache_ref.shape
-    slots = fresh_ref.shape[0]
-    device_count = counts_ref.shape[1]
+    slots = new_key_ref.shape[0]
+    device_count = table_ref.shape[1] - slots - 1
     far, near = mesh_digits(device_count)
     block = min(128, tokens)
     blocks = tokens // block
@@ -48,20 +48,15 @@
         part = pl.ds(i * block, block)
         return pltpu.make_async_copy(cache_ref.at[part], held.at[part], sems.at[i])
 
-    def fetch_fresh(i):
-        return pltpu.make_async_copy(fresh_ref.at[:, 1 + i], fresh_held.at[i], sems.at[blocks + i])
-
     for i in range(blocks):
         fetch(i).start()
-    for i in range(2):
-        fetch_fresh(i).start()
-
-    me = me_ref[0]
+
+    me = table_ref[0, device_count + slots]
     col = lax.broadcasted_iota(jnp.int32, target_ref.shape, 1)
 
     def one_device(dev, carry):
         start0, start1, target = carry
-        count0, count1 = counts_ref[0, dev], counts_ref[1, dev]
+        count0, count1 = table_ref[0, dev], table_ref[1, dev]
         local = col - place_of(dev ^ me, far, near) * (STEPS * slots)
         slot, step = local >> 1, local & 1
         rank = slot + jnp.where(step == 0, start0, start1)
@@ -77,10 +72,10 @@
         carry = lax.fori_loop(0, device_count, one_device, carry)
     target_ref[...] = carry[2]
 
-    live0 = [i < counts_ref[0, me] for i in range(slots)]
-    live1 = [i < counts_ref[1, me] for i in range(slots)]
-    row0 = [jnp.where(live0[i], rows_ref[0, i], -1) for i in range(slots)]
-    row1 = [jnp.where(live1[i], rows_ref[1, i], -2) for i in range(slots)]
+    live0 = [i < table_ref[0, me] for i in range(slots)]
+    live1 = [i < table_ref[1, me] for i in range(slots)]
+    row0 = [jnp.where(live0[i], table_ref[0, device_count + i], -1) for i in range(slots)]
+    row1 = [jnp.where(live1[i], table_ref[1, device_count + i], -2) for i in range(slots)]
     token = lax.broadcasted_iota(jnp.int32, bias_ref.shape, 1)
     second = lax.broadcasted_iota(jnp.int32, bias_ref.shape, 0) >= SLOT
     gone = token == row0[0]
@@ -115,15 +110,15 @@
             part = jnp.dot(order, part, preferred_element_type=jnp.float32).astype(jnp.bfloat16)
             key_ref[rows, c:c + 256] = part[:block]
             value_ref[rows, c:c + 256] = part[block:]
-    for i, ref in enumerate((fresh_key_ref, fresh_value_ref)):
-        fetch_fresh(i).wait()
+    for ref, new_ref in ((fresh_key_ref, new_key_ref), (fresh_value_ref, new_value_ref)):
         ref[...] = jnp.zeros_like(ref)
-        ref[0:STEPS * slots, :] = fresh_held.at[i].reshape(STEPS * slots, width)[...]
-
-
-def prepare(me, counts, list_rows, cache, fresh):
+        ref[0:STEPS * slots, :] = new_ref.reshape(STEPS * slots, width)[...]
+
+
+def prepare(table, cache, fresh_key, fresh_value):
     tokens, _, width = cache.shape
-    slots = fresh.shape[0]
+    slots = fresh_key.shape[0]
+    device_count = table.shape[1] - slots - 1
     fresh_rows = -(-STEPS * slots // 16) * 16
     f32, bf16 = jnp.float32, jnp.bfloat16
     shapes = (
@@ -131,7 +126,7 @@
         jax.ShapeDtypeStruct((tokens, width), bf16),
         jax.ShapeDtypeStruct((fresh_rows, width), bf16),
         jax.ShapeDtypeStruct((fresh_rows, width), bf16),
-        jax.ShapeDtypeStruct((1, counts.shape[1] * STEPS * slots), jnp.int32),
+        jax.ShapeDtypeStruct((1, device_count * STEPS * slots), jnp.int32),
         jax.ShapeDtypeStruct((PAIR, tokens), f32),
         jax.ShapeDtypeStruct((PAIR, fresh_rows), f32),
     )
@@ -139,19 +134,18 @@
     return pl.pallas_call(
         prepare_kernel,
         out_shape=shapes,
-        in_specs=[SMEM, SMEM, SMEM, ANY, ANY],
+        in_specs=[SMEM, HBM, VMEM, VMEM],
         out_specs=(VMEM,) * len(shapes),
         scratch_shapes=[
             pltpu.VMEM((tokens, 2, width), bf16),
-            pltpu.VMEM((2, slots, STEPS, width), bf16),
-            pltpu.SemaphoreType.DMA((blocks + 2,)),
+            pltpu.SemaphoreType.DMA((blocks,)),
         ],
-        compiler_params=pltpu.CompilerParams(vmem_limit_bytes=22 << 20),
+        compiler_params=pltpu.CompilerParams(vmem_limit_bytes=45 << 20),
         cost_estimate=pl.CostEstimate(
             flops=8 * 128 * tokens * width, bytes_accessed=8 * tokens * width, transcendentals=0
         ),
         name="prepare",
-    )(me, counts, list_rows, cache, fresh)
+    )(table, cache, fresh_key, fresh_value)
 
 
 def two_parts(x):
@@ -316,18 +310,20 @@
         return lax.ppermute(x, "blk", [(i, i ^ mask) for i in range(device_count)])
 
     fresh = fresh_qkv.transpose(1, 2, 0, 3)
-    mine = fresh[:, 0]
-    column = jnp.concatenate([mine] + [swap(mine, k * near * 2) for k in range(1, far)])
+    mine, fresh_key, fresh_value = (fresh[:, i] for i in range(3))
+    table = jnp.concatenate([counts, list_rows, jnp.full((STEPS, 1), me, jnp.int32)], axis=1)
+    ready = prepare(table, cache_kv, fresh_key, fresh_value)
+    column = [swap(mine, k * near * 2) for k in range(1, far)]
+    column, ready = lax.optimization_barrier((column, ready))
+    column = jnp.concatenate([mine] + column)
     plane = [column] + [swap(column, k * 2) for k in range(1, near)]
     gathered = plane + [swap(x, 1) for x in plane]
-    ready = prepare(me.reshape(1), counts, list_rows, cache_kv, fresh)
     key, value, fresh_key, fresh_value, target, bias, fresh_bias = ready
     keep, send = attend(list_rows.shape[1], target, bias, fresh_bias, fresh_key, fresh_value, key, value, gathered)
-    keep, *sends = merge([keep, swap(send, 1)], near, "merge_core")
-    sends = [swap(x, (k + 1) * 2) for k, x in enumerate(sends)]
-    keep, *sends = merge([keep] + sends, far, "merge_near")
-    sends = [swap(x, (k + 1) * near * 2) for k, x in enumerate(sends)]
-    return merge([keep] + sends, 0, "merge_far")[0]
+    chips = near * far
+    keep, *sends = merge([keep, swap(send, 1)], chips, "merge_core")
+    sends = [swap(x, ((n % far) * near + n // far) * 2) for n, x in enumerate(sends, 1)]
+    return merge([keep] + sends, 0, "merge_chips")[0]
 
 
 def solution(mesh):

time: 48.5 us -> 46.3 us (0.955)
  local copies, waits for them, and re-layouts: 6.04 us -> 1.13 us
  starting transfers between devices: 14 us -> 18.9 us
  waiting for transfers between devices: 16 us -> 12.7 us
  other arithmetic: 0.22 us -> 0.99 us
    unnamed x9 -> x1, local copies, waits for them, and re-layouts: 6.01 us -> 0.97 us
    ppermute x11 -> x14, starting transfers between devices: 14 us -> 18.9 us  [swap(): return lax.ppermute(x, 'blk', [(i, i ^ mask) for i in range(device_count)])]
    ppermute x11 -> x14, waiting for transfers between devices: 16 us -> 12.7 us  [swap(): return lax.ppermute(x, 'blk', [(i, i ^ mask) for i in range(device_count)])]
    concatenate x1 -> x2, other arithmetic: 0.22 us -> 0.99 us  [the longest x1 0.77 us: body(): jnp.concatenate([counts, list_rows, jnp.full((STEPS, 1), me, jnp.int32)],...]
    pallas_call x3 -> x2, Pallas kernels: 1.6 us -> 1.36 us  [merge(): pl.pallas_call(kernel, out_shape=shapes, in_specs=[VMEM] * len(parts), ou...]
  transfers between devices with their start and end apart: 11 -> 14, of which waited for: 7 -> 5; matrix products, arithmetic and copies ran while one was open for 0% -> 2% of each run, Pallas kernels for 10% -> 12%
where the time goes in v3:
time: 46.3 us; the launch traced here: 46.1 us
  starting transfers between devices  18.9 us (41%)
  waiting for transfers between devices  12.7 us (27%)
  Pallas kernels  12.3 us (27%)
  local copies, waits for them, and re-layouts  1.13 us (2%)
  other arithmetic  0.99 us (2%)
    ppermute x14, starting transfers between devices, swap(): return lax.ppermute(x, 'blk', [(i, i ^ mask) for i in range(device_count)])  18.9 us
    ppermute x14, waiting for transfers between devices, swap(): return lax.ppermute(x, 'blk', [(i, i ^ mask) for i in range(device_count)])  12.7 us
    pallas_call x1, Pallas kernels, attend(): pl.pallas_call(attend_kernel, out_shape=(jax.ShapeDtypeStruct(shape, jnp....  5.55 us
    pallas_call x1, Pallas kernels, prepare(): pl.pallas_call(prepare_kernel, out_shape=shapes, in_specs=[SMEM, HBM, VME...  5.39 us
    pallas_call x2, Pallas kernels, merge(): pl.pallas_call(kernel, out_shape=shapes, in_specs=[VMEM] * len(parts), ou...  1.36 us
    unnamed x1, local copies, waits for them, and re-layouts  0.97 us
  transfers between devices with their start and end apart: 14, of which 5 were waited for; matrix products, arithmetic and copies ran while one was open for 2% of the time, Pallas kernels for 12%

profile of v3, /device:TPU:0, one launch (start us, length us, event | category | flops | bytes accessed | tf_op | source)
XLA Modules:
  0.0 46.1 jit_solution(4577196346069627685)
XLA Ops:
  0.0 1.0 %copy.7 = bf16[2,6,3,1536]{3,0,1,2:T(2,128)(2,1)S(1)} copy(bf16[2,6,3,1536]{3,0,2,1:T(2,128)(2,1)} %param.5) | data formatting | bytes 221184 | tf_op args[1]
  1.0 0.1 slice_bitcast_fusion
  1.1 5.1 %collective-permute-start.2 = (bf16[6,2,1536]{2,1,0:T(2,128)(2,1)S(1)}, bf16[6,2,1536]{2,1,0:T(2,128)(2,1)S(1)}, u32[]{:S(2)}, u32[]{:S(2)}) collective-permute-start(bf16[6,2,1536]{2,1,0:T(2,128)(2,1)S(1)} %get-tuple-element.61), channel_id=1, source_target_pairs={{0,12},{1,13},{2,14},{3,15},{4,8},{5,9},{6,10},{7,11},{8,4},{9,5},... | collective-permute-start | bytes 110600 | tf_op jit(solution)/shard_map/ppermute | solution.py:310
  6.2 0.6 %collective-permute-start = (bf16[6,2,1536]{2,1,0:T(2,128)(2,1)S(1)}, bf16[6,2,1536]{2,1,0:T(2,128)(2,1)S(1)}, u32[]{:S(2)}, u32[]{:S(2)}) collective-permute-start(bf16[6,2,1536]{2,1,0:T(2,128)(2,1)S(1)} %get-tuple-element.61), channel_id=1, source_target_pairs={{0,4},{1,5},{2,6},{3,7},{4,0},{5,1},{6,2},{7,3},{8,12},{9,13},{10,... | collective-permute-start | bytes 110600 | tf_op jit(solution)/shard_map/ppermute | solution.py:310
  6.8 0.1 pad.6.clone
  6.9 0.8 %add_add_fusion.table_ref = s32[2,23]{1,0:T(2,128)S(1)} fusion(s32[2,6]{1,0:T(2,128)} %param.6, s32[2,16]{1,0:T(2,128)} %param.7, s32[23]{0:T(128)S(1)} %pad.6.clone), kind=kLoop, calls=%fused_computation.5 | loop fusion | flops 92 | bytes 452 | tf_op jit(solution)/shard_map/concatenate | solution.py:314
  7.7 5.4 %prepare.1 = (bf16[1024,1536]{1,0:T(8,128)(2,1)S(1)}, bf16[1024,1536]{1,0:T(8,128)(2,1)S(1)}, bf16[16,1536]{1,0:T(8,128)(2,1)S(1)}, bf16[16,1536]{1,0:T(8,128)(2...) custom-call(s32[2,23]{1,0:T(2,128)S(1)} %add_add_fusion.table_ref, ...), custom_call_target="tpu_custom_call" | custom-call | flops 1610612736 | bytes 12582912 | tf_op jit(solution)/shard_map/prepare/pallas_call | solution.py:134
  13.1 0.2 pad_maximum_fusion.rest_0_
  13.3 1.7 %collective-permute-start.3 = (bf16[24,2,1536]{2,1,0:T(2,128)(2,1)S(1)}, bf16[24,2,1536]{2,1,0:T(2,128)(2,1)S(1)}, u32[]{:S(2)}, u32[]{:S(2)}) collective-permute-start(bf16[24,2,1536]{2,1,0:T(2,128)(2,1)S(1)} %pad_maximum_fusion.rest_0_), channel_id=1, source_target_pairs={{0,2},{1,3},{2,0},{3,1},{4,6},{5,7},{6,4},{7,5},{8,10},{9,11},{10,... | collective-permute-start | bytes 442376 | tf_op jit(solution)/shard_map/ppermute | solution.py:310
  15.1 3.5 %collective-permute-done.3.rest_1_ = bf16[24,2,1536]{2,1,0:T(2,128)(2,1)S(1)} collective-permute-done((bf16[24,2,1536]{2,1,0:T(2,128)(2,1)S(1)}, bf16[24,2,1536]{2,1,0:T(2,128)(2,1)S(1)}, u32[]{:S(2)}, u32[]{:S(2)}) %collective-permute-start.3) | collective-permute-done | bytes 147488 | tf_op jit(solution)/shard_map/ppermute | solution.py:310
  18.5 1.4 %collective-permute-done.5.rest_3_ = bf16[24,2,1536]{2,1,0:T(2,128)(2,1)S(1)} collective-permute-done((bf16[24,2,1536]{2,1,0:T(2,128)(2,1)S(1)}, bf16[24,2,1536]{2,1,0:T(2,128)(2,1)S(1)}, u32[]{:S(2)}, u32[]{:S(2)}) %collective-permute-start.5) | collective-permute-done | bytes 147488 | tf_op jit(solution)/shard_map/ppermute | solution.py:310
  19.9 5.6 %attend.1 = (f32[64,1664]{1,0:T(8,128)S(1)}, bf16[64,1664]{1,0:T(8,128)(2,1)S(1)}) custom-call(s32[1,192]{1,0:T(1,128)S(1)} %get-tuple-element.39.target_ref, f32[8,1024]{1,0:T(8,128)S(1)} %get-tuple-element.40.bias_ref, f32[8,16]{1,0:T(8,128)S(1)} %get-tuple-element.41.fresh_bias_ref, bf16[16,1536]{1,0:T(8,128)(2,1)S(1)} %get-tuple-element.42.fresh_key_ref, ...), custom_call_target="tpu_custom_call" | custom-call | flops 805306368 | bytes 6291456 | tf_op jit(solution)/shard_map/attend/pallas_call | solution.py:233
  25.5 0.2 collective-permute-start.6
  25.6 1.3 %collective-permute-done.6.refs_1_ = bf16[64,1664]{1,0:T(8,128)(2,1)S(1)} collective-permute-done((bf16[64,1664]{1,0:T(8,128)(2,1)S(1)}, bf16[64,1664]{1,0:T(8,128)(2,1)S(1)}, u32[]{:S(2)}, u32[]{:S(2)}) %collective-permute-start.6) | collective-permute-done | bytes 213024 | tf_op jit(solution)/shard_map/ppermute | solution.py:310
  27.0 0.4 merge_core.1
  27.4 1.5 %collective-permute-start.7 = (bf16[8,1664]{1,0:T(8,128)(2,1)S(1)}, bf16[8,1664]{1,0:T(8,128)(2,1)S(1)}, u32[]{:S(2)}, u32[]{:S(2)}) collective-permute-start(bf16[8,1664]{1,0:T(8,128)(2,1)S(1)} %get-tuple-element.52), channel_id=1, source_target_pairs={{0,4},{1,5},{2,6},{3,7},{4,0},{5,1},{6,2},{7,3},{8,12},{9,13},{10,... | collective-permute-start | bytes 79880 | tf_op jit(solution)/shard_map/ppermute | solution.py:310
  28.9 2.9 %collective-permute-start.8 = (bf16[8,1664]{1,0:T(8,128)(2,1)S(1)}, bf16[8,1664]{1,0:T(8,128)(2,1)S(1)}, u32[]{:S(2)}, u32[]{:S(2)}) collective-permute-start(bf16[8,1664]{1,0:T(8,128)(2,1)S(1)} %get-tuple-element.53), channel_id=1, source_target_pairs={{0,8},{1,9},{2,10},{3,11},{4,12},{5,13},{6,14},{7,15},{8,0},{9,1},... | collective-permute-start | bytes 79880 | tf_op jit(solution)/shard_map/ppermute | solution.py:310
  31.8 0.1 collective-permute-start.9
  31.9 1.7 %collective-permute-start.10 = (bf16[8,1664]{1,0:T(8,128)(2,1)S(1)}, bf16[8,1664]{1,0:T(8,128)(2,1)S(1)}, u32[]{:S(2)}, u32[]{:S(2)}) collective-permute-start(bf16[8,1664]{1,0:T(8,128)(2,1)S(1)} %get-tuple-element.55), channel_id=1, source_target_pairs={{0,2},{1,3},{2,0},{3,1},{4,6},{5,7},{6,4},{7,5},{8,10},{9,11},{10,... | collective-permute-start | bytes 79880 | tf_op jit(solution)/shard_map/ppermute | solution.py:310
  33.5 0.3 collective-permute-start.11
  33.8 4.8 %collective-permute-start.12 = (bf16[8,1664]{1,0:T(8,128)(2,1)S(1)}, bf16[8,1664]{1,0:T(8,128)(2,1)S(1)}, u32[]{:S(2)}, u32[]{:S(2)}) collective-permute-start(bf16[8,1664]{1,0:T(8,128)(2,1)S(1)} %get-tuple-element.57), channel_id=1, source_target_pairs={{0,10},{1,11},{2,8},{3,9},{4,14},{5,15},{6,12},{7,13},{8,2},{9,3},... | collective-permute-start | bytes 79880 | tf_op jit(solution)/shard_map/ppermute | solution.py:310
  38.6 2.1 %collective-permute-done.12.refs_6_ = bf16[8,1664]{1,0:T(8,128)(2,1)S(1)} collective-permute-done((bf16[8,1664]{1,0:T(8,128)(2,1)S(1)}, bf16[8,1664]{1,0:T(8,128)(2,1)S(1)}, u32[]{:S(2)}, u32[]{:S(2)}) %collective-permute-start.12) | collective-permute-done | bytes 26656 | tf_op jit(solution)/shard_map/ppermute | solution.py:310
  40.7 4.4 %collective-permute-done.13.refs_7_ = bf16[8,1664]{1,0:T(8,128)(2,1)S(1)} collective-permute-done((bf16[8,1664]{1,0:T(8,128)(2,1)S(1)}, bf16[8,1664]{1,0:T(8,128)(2,1)S(1)}, u32[]{:S(2)}, u32[]{:S(2)}) %collective-permute-start.13) | collective-permute-done | bytes 26656 | tf_op jit(solution)/shard_map/ppermute | solution.py:310
  45.2 0.9 %merge_chips.1 = bf16[2,4,1536]{2,1,0:T(4,128)(2,1)} custom-call(f32[8,1664]{1,0:T(8,128)S(1)} %get-tuple-element.51.refs_0_, bf16[8,1664]{1,0:T(8,128)(2,1)S(1)} %collective-permute-done.7.refs_1_, bf16[8,1664]{1,0:T(8,128)(2,1)S(1)} %collective-permute-done.8.refs_2_, bf16[8,1664]{1,0:T(8,128)(2,1)S(1)} %collective-permute-done.9.refs_3_, ...), custom_call_target="tpu_custom_call" | custom-call | tf_op jit(solution)/shard_map/merge_chips/pallas_call | solution.py:294
  (13 shorter events, 0.1 us)
Async XLA Ops:
  1.1 12.0 %collective-permute-start.2 = (bf16[6,2,1536]{2,1,0:T(2,128)(2,1)S(1)}, bf16[6,2,1536]{2,1,0:T(2,128)(2,1)S(1)}, u32[]{:S(2)}, u32[]{:S(2)}) collective-permute-start(bf16[6,2,1536]{2,1,0:T(2,128)(2,1)S(1)} %get-tuple-element.61), channel_id=1, source_target_pairs={{0,12},{1,13},{2,14},{3,15},{4,8},{5,9},{6,10},{7,11},{8,4},{9,5},... | collective-permute-start | bytes 110600 | tf_op jit(solution)/shard_map/ppermute | solution.py:310
  6.2 6.9 %collective-permute-start.1 = (bf16[6,2,1536]{2,1,0:T(2,128)(2,1)S(1)}, bf16[6,2,1536]{2,1,0:T(2,128)(2,1)S(1)}, u32[]{:S(2)}, u32[]{:S(2)}) collective-permute-start(bf16[6,2,1536]{2,1,0:T(2,128)(2,1)S(1)} %get-tuple-element.61), channel_id=1, source_target_pairs={{0,8},{1,9},{2,10},{3,11},{4,12},{5,13},{6,14},{7,15},{8,0},{9,1},... | collective-permute-start | bytes 110600 | tf_op jit(solution)/shard_map/ppermute | solution.py:310
  6.2 6.9 %collective-permute-start = (bf16[6,2,1536]{2,1,0:T(2,128)(2,1)S(1)}, bf16[6,2,1536]{2,1,0:T(2,128)(2,1)S(1)}, u32[]{:S(2)}, u32[]{:S(2)}) collective-permute-start(bf16[6,2,1536]{2,1,0:T(2,128)(2,1)S(1)} %get-tuple-element.61), channel_id=1, source_target_pairs={{0,4},{1,5},{2,6},{3,7},{4,0},{5,1},{6,2},{7,3},{8,12},{9,13},{10,... | collective-permute-start | bytes 110600 | tf_op jit(solution)/shard_map/ppermute | solution.py:310
  13.3 5.2 %collective-permute-start.3 = (bf16[24,2,1536]{2,1,0:T(2,128)(2,1)S(1)}, bf16[24,2,1536]{2,1,0:T(2,128)(2,1)S(1)}, u32[]{:S(2)}, u32[]{:S(2)}) collective-permute-start(bf16[24,2,1536]{2,1,0:T(2,128)(2,1)S(1)} %pad_maximum_fusion.rest_0_), channel_id=1, source_target_pairs={{0,2},{1,3},{2,0},{3,1},{4,6},{5,7},{6,4},{7,5},{8,10},{9,11},{10,... | collective-permute-start | bytes 442376 | tf_op jit(solution)/shard_map/ppermute | solution.py:310
  15.1 3.5 %collective-permute-start.4 = (bf16[24,2,1536]{2,1,0:T(2,128)(2,1)S(1)}, bf16[24,2,1536]{2,1,0:T(2,128)(2,1)S(1)}, u32[]{:S(2)}, u32[]{:S(2)}) collective-permute-start(bf16[24,2,1536]{2,1,0:T(2,128)(2,1)S(1)} %pad_maximum_fusion.rest_0_), channel_id=1, source_target_pairs={{0,1},{1,0},{2,3},{3,2},{4,5},{5,4},{6,7},{7,6},{8,9},{9,8},{10,11... | collective-permute-start | bytes 442376 | tf_op jit(solution)/shard_map/ppermute | solution.py:310
  18.5 1.4 %collective-permute-start.5 = (bf16[24,2,1536]{2,1,0:T(2,128)(2,1)S(1)}, bf16[24,2,1536]{2,1,0:T(2,128)(2,1)S(1)}, u32[]{:S(2)}, u32[]{:S(2)}) collective-permute-start(bf16[24,2,1536]{2,1,0:T(2,128)(2,1)S(1)} %collective-permute-done.3.rest_1_), channel_id=1, source_target_pairs={{0,1},{1,0},{2,3},{3,2},{4,5},{5,4},{6,7},{7,6},{8,9},{9,8},{10,11... | collective-permute-start | bytes 442376 | tf_op jit(solution)/shard_map/ppermute | solution.py:310
  25.5 1.5 %collective-permute-start.6 = (bf16[64,1664]{1,0:T(8,128)(2,1)S(1)}, bf16[64,1664]{1,0:T(8,128)(2,1)S(1)}, u32[]{:S(2)}, u32[]{:S(2)}) collective-permute-start(bf16[64,1664]{1,0:T(8,128)(2,1)S(1)} %get-tuple-element.50), channel_id=1, source_target_pairs={{0,1},{1,0},{2,3},{3,2},{4,5},{5,4},{6,7},{7,6},{8,9},{9,8},{10,11... | collective-permute-start | bytes 638984 | tf_op jit(solution)/shard_map/ppermute | solution.py:310
  27.4 6.4 %collective-permute-start.7 = (bf16[8,1664]{1,0:T(8,128)(2,1)S(1)}, bf16[8,1664]{1,0:T(8,128)(2,1)S(1)}, u32[]{:S(2)}, u32[]{:S(2)}) collective-permute-start(bf16[8,1664]{1,0:T(8,128)(2,1)S(1)} %get-tuple-element.52), channel_id=1, source_target_pairs={{0,4},{1,5},{2,6},{3,7},{4,0},{5,1},{6,2},{7,3},{8,12},{9,13},{10,... | collective-permute-start | bytes 79880 | tf_op jit(solution)/shard_map/ppermute | solution.py:310
  28.9 9.7 %collective-permute-start.8 = (bf16[8,1664]{1,0:T(8,128)(2,1)S(1)}, bf16[8,1664]{1,0:T(8,128)(2,1)S(1)}, u32[]{:S(2)}, u32[]{:S(2)}) collective-permute-start(bf16[8,1664]{1,0:T(8,128)(2,1)S(1)} %get-tuple-element.53), channel_id=1, source_target_pairs={{0,8},{1,9},{2,10},{3,11},{4,12},{5,13},{6,14},{7,15},{8,0},{9,1},... | collective-permute-start | bytes 79880 | tf_op jit(solution)/shard_map/ppermute | solution.py:310
  31.8 6.8 %collective-permute-start.9 = (bf16[8,1664]{1,0:T(8,128)(2,1)S(1)}, bf16[8,1664]{1,0:T(8,128)(2,1)S(1)}, u32[]{:S(2)}, u32[]{:S(2)}) collective-permute-start(bf16[8,1664]{1,0:T(8,128)(2,1)S(1)} %get-tuple-element.54), channel_id=1, source_target_pairs={{0,12},{1,13},{2,14},{3,15},{4,8},{5,9},{6,10},{7,11},{8,4},{9,5},... | collective-permute-start | bytes 79880 | tf_op jit(solution)/shard_map/ppermute | solution.py:310
  31.9 6.8 %collective-permute-start.10 = (bf16[8,1664]{1,0:T(8,128)(2,1)S(1)}, bf16[8,1664]{1,0:T(8,128)(2,1)S(1)}, u32[]{:S(2)}, u32[]{:S(2)}) collective-permute-start(bf16[8,1664]{1,0:T(8,128)(2,1)S(1)} %get-tuple-element.55), channel_id=1, source_target_pairs={{0,2},{1,3},{2,0},{3,1},{4,6},{5,7},{6,4},{7,5},{8,10},{9,11},{10,... | collective-permute-start | bytes 79880 | tf_op jit(solution)/shard_map/ppermute | solution.py:310
  33.5 5.1 %collective-permute-start.11 = (bf16[8,1664]{1,0:T(8,128)(2,1)S(1)}, bf16[8,1664]{1,0:T(8,128)(2,1)S(1)}, u32[]{:S(2)}, u32[]{:S(2)}) collective-permute-start(bf16[8,1664]{1,0:T(8,128)(2,1)S(1)} %get-tuple-element.56), channel_id=1, source_target_pairs={{0,6},{1,7},{2,4},{3,5},{4,2},{5,3},{6,0},{7,1},{8,14},{9,15},{10,... | collective-permute-start | bytes 79880 | tf_op jit(solution)/shard_map/ppermute | solution.py:310
  33.8 6.9 %collective-permute-start.12 = (bf16[8,1664]{1,0:T(8,128)(2,1)S(1)}, bf16[8,1664]{1,0:T(8,128)(2,1)S(1)}, u32[]{:S(2)}, u32[]{:S(2)}) collective-permute-start(bf16[8,1664]{1,0:T(8,128)(2,1)S(1)} %get-tuple-element.57), channel_id=1, source_target_pairs={{0,10},{1,11},{2,8},{3,9},{4,14},{5,15},{6,12},{7,13},{8,2},{9,3},... | collective-permute-start | bytes 79880 | tf_op jit(solution)/shard_map/ppermute | solution.py:310
  38.6 6.5 %collective-permute-start.13 = (bf16[8,1664]{1,0:T(8,128)(2,1)S(1)}, bf16[8,1664]{1,0:T(8,128)(2,1)S(1)}, u32[]{:S(2)}, u32[]{:S(2)}) collective-permute-start(bf16[8,1664]{1,0:T(8,128)(2,1)S(1)} %get-tuple-element.58), channel_id=1, source_target_pairs={{0,14},{1,15},{2,12},{3,13},{4,10},{5,11},{6,8},{7,9},{8,6},{9,7},... | collective-permute-start | bytes 79880 | tf_op jit(solution)/shard_map/ppermute | solution.py:310

commit v4 on v3

--- a/solution.py
+++ b/solution.py
@@ -20,18 +20,11 @@
 HBM = pl.BlockSpec(memory_space=pltpu.HBM)
 
 
-def mesh_digits(device_count):
-    bits = (device_count // 2).bit_length() - 1
-    far_bits = (bits + 1) // 2
-    return 1 << far_bits, 1 << (bits - far_bits)
-
-
-def place_of(mask, far, near):
-    near_bits = near.bit_length() - 1
-    core = mask & 1
-    near_digit = (mask >> 1) & (near - 1)
-    far_digit = mask >> (1 + near_bits)
-    return (core * near + near_digit) * far + far_digit
+def place_of(mask, bits):
+    place = 0
+    for n in range(bits):
+        place = place + (((mask >> n) & 1) << (bits - 1 - n))
+    return place
 
 
 def prepare_kernel(table_ref, cache_ref, new_key_ref, new_value_ref,
@@ -40,7 +33,7 @@
     tokens, _, width = cache_ref.shape
     slots = new_key_ref.shape[0]
     device_count = table_ref.shape[1] - slots - 1
-    far, near = mesh_digits(device_count)
+    bits = device_count.bit_length() - 1
     block = min(128, tokens)
     blocks = tokens // block
 
@@ -57,10 +50,10 @@
     def one_device(dev, carry):
         start0, start1, target = carry
         count0, count1 = table_ref[0, dev], table_ref[1, dev]
-        local = col - place_of(dev ^ me, far, near) * (STEPS * slots)
+        local = col - place_of(dev ^ me, bits) * (STEPS * slots)
         slot, step = local >> 1, local & 1
         rank = slot + jnp.where(step == 0, start0, start1)
-        row = place_of((rank >> SLOT_BITS) ^ me, far, near) * PAIR + step * SLOT + (rank & (SLOT - 1))
+        row = place_of((rank >> SLOT_BITS) ^ me, bits) * PAIR + step * SLOT + (rank & (SLOT - 1))
         good = (local >= 0) & (slot < jnp.where(step == 0, count0, count1))
         return start0 + count0, start1 + count1, jnp.where(good, row, target)
 
@@ -304,7 +297,8 @@
 def body(cache_kv, fresh_qkv, list_rows, counts):
     device_count = lax.axis_size("blk")
     me = lax.axis_index("blk")
-    far, near = mesh_digits(device_count)
+    slot_count = list_rows.shape[1]
+    bits = device_count.bit_length() - 1
 
     def swap(x, mask):
         return lax.ppermute(x, "blk", [(i, i ^ mask) for i in range(device_count)])
@@ -313,17 +307,17 @@
     mine, fresh_key, fresh_value = (fresh[:, i] for i in range(3))
     table = jnp.concatenate([counts, list_rows, jnp.full((STEPS, 1), me, jnp.int32)], axis=1)
     ready = prepare(table, cache_kv, fresh_key, fresh_value)
-    column = [swap(mine, k * near * 2) for k in range(1, far)]
-    column, ready = lax.optimization_barrier((column, ready))
-    column = jnp.concatenate([mine] + column)
-    plane = [column] + [swap(column, k * 2) for k in range(1, near)]
-    gathered = plane + [swap(x, 1) for x in plane]
+    held = mine
+    for n in range(bits - 1, 1, -1):
+        held = jnp.concatenate([held, swap(held, 1 << n)])
+    across, beside = swap(held, 2), swap(held, 1)
+    across, ready = lax.optimization_barrier((across, ready))
+    gathered = [held, across, beside, swap(across, 1)]
     key, value, fresh_key, fresh_value, target, bias, fresh_bias = ready
-    keep, send = attend(list_rows.shape[1], target, bias, fresh_bias, fresh_key, fresh_value, key, value, gathered)
-    chips = near * far
-    keep, *sends = merge([keep, swap(send, 1)], chips, "merge_core")
-    sends = [swap(x, ((n % far) * near + n // far) * 2) for n, x in enumerate(sends, 1)]
-    return merge([keep] + sends, 0, "merge_chips")[0]
+    keep, send = attend(slot_count, target, bias, fresh_bias, fresh_key, fresh_value, key, value, gathered)
+    for n in range(bits - 1):
+        keep, send = merge([keep, swap(send, 1 << n)], 2, "merge_%d" % n)
+    return merge([keep, swap(send, 1 << (bits - 1))], 0, "merge_last")[0]
 
 
 def solution(mesh):

time: 46.3 us -> 44.4 us (0.959)
  starting transfers between devices: 18.9 us -> 12.5 us
  waiting for transfers between devices: 12.7 us -> 16.7 us
    ppermute x14 -> x9, starting transfers between devices: 18.9 us -> 12.5 us  [swap(): return lax.ppermute(x, 'blk', [(i, i ^ mask) for i in range(device_count)])]
    ppermute x14 -> x9, waiting for transfers between devices: 12.7 us -> 16.7 us  [swap(): return lax.ppermute(x, 'blk', [(i, i ^ mask) for i in range(device_count)])]
    pallas_call x2 -> x4, Pallas kernels: 1.36 us -> 1.79 us  [merge(): pl.pallas_call(kernel, out_shape=shapes, in_specs=[VMEM] * len(parts), ou...]
  transfers between devices with their start and end apart: 14 -> 9, of which waited for: 5 -> 8; matrix products, arithmetic and copies ran while one was open for 2% -> 2% of each run, Pallas kernels for 12% -> 12%
where the time goes in v4:
time: 44.4 us; the launch traced here: 44.2 us
  waiting for transfers between devices  16.7 us (38%)
  Pallas kernels  12.7 us (29%)
  starting transfers between devices  12.5 us (28%)
  local copies, waits for them, and re-layouts  1.13 us (3%)
  other arithmetic  1.07 us (2%)
    ppermute x9, waiting for transfers between devices, swap(): return lax.ppermute(x, 'blk', [(i, i ^ mask) for i in range(device_count)])  16.7 us
    ppermute x9, starting transfers between devices, swap(): return lax.ppermute(x, 'blk', [(i, i ^ mask) for i in range(device_count)])  12.5 us
    pallas_call x1, Pallas kernels, attend(): pl.pallas_call(attend_kernel, out_shape=(jax.ShapeDtypeStruct(shape, jnp....  5.55 us
    pallas_call x1, Pallas kernels, prepare(): pl.pallas_call(prepare_kernel, out_shape=shapes, in_specs=[SMEM, HBM, VME...  5.4 us
    pallas_call x4, Pallas kernels, merge(): pl.pallas_call(kernel, out_shape=shapes, in_specs=[VMEM] * len(parts), ou...  1.79 us
    unnamed x1, local copies, waits for them, and re-layouts  0.97 us
  transfers between devices with their start and end apart: 9, of which 8 were waited for; matrix products, arithmetic and copies ran while one was open for 2% of the time, Pallas kernels for 12%

profile of v4, /device:TPU:0, one launch (start us, length us, event | category | flops | bytes accessed | tf_op | source)
XLA Modules:
  0.0 44.2 jit_solution(17065852393809744484)
XLA Ops:
  0.0 1.0 %copy.7 = bf16[2,6,3,1536]{3,0,1,2:T(2,128)(2,1)S(1)} copy(bf16[2,6,3,1536]{3,0,2,1:T(2,128)(2,1)} %param.5) | data formatting | bytes 221184 | tf_op args[1]
  1.1 4.1 %collective-permute-start = (bf16[6,2,1536]{2,1,0:T(2,128)(2,1)S(1)}, bf16[6,2,1536]{2,1,0:T(2,128)(2,1)S(1)}, u32[]{:S(2)}, u32[]{:S(2)}) collective-permute-start(bf16[6,2,1536]{2,1,0:T(2,128)(2,1)S(1)} %get-tuple-element.53), channel_id=1, source_target_pairs={{0,8},{1,9},{2,10},{3,11},{4,12},{5,13},{6,14},{7,15},{8,0},{9,1},... | collective-permute-start | bytes 110600 | tf_op jit(solution)/shard_map/ppermute | solution.py:304
  5.2 2.3 %collective-permute-done = bf16[6,2,1536]{2,1,0:T(2,128)(2,1)S(1)} collective-permute-done((bf16[6,2,1536]{2,1,0:T(2,128)(2,1)S(1)}, bf16[6,2,1536]{2,1,0:T(2,128)(2,1)S(1)}, u32[]{:S(2)}, u32[]{:S(2)}) %collective-permute-start) | collective-permute-done | bytes 36896 | tf_op jit(solution)/shard_map/ppermute | solution.py:304
  7.6 1.6 %collective-permute-start.1 = (bf16[12,2,1536]{2,1,0:T(2,128)(2,1)S(1)}, bf16[12,2,1536]{2,1,0:T(2,128)(2,1)S(1)}, u32[]{:S(2)}, u32[]{:S(2)}) collective-permute-start(bf16[12,2,1536]{2,1,0:T(2,128)(2,1)S(1)} %pad_maximum_fusion.1), channel_id=1, source_target_pairs={{0,4},{1,5},{2,6},{3,7},{4,0},{5,1},{6,2},{7,3},{8,12},{9,13},{10,... | collective-permute-start | bytes 221192 | tf_op jit(solution)/shard_map/ppermute | solution.py:304
  9.2 0.8 %add_add_fusion.table_ref = s32[2,23]{1,0:T(2,128)S(1)} fusion(s32[2,6]{1,0:T(2,128)} %param.6, s32[2,16]{1,0:T(2,128)} %param.7, s32[23]{0:T(128)S(1)} %pad.2.clone), kind=kLoop, calls=%fused_computation.6 | loop fusion | flops 92 | bytes 452 | tf_op jit(solution)/shard_map/concatenate | solution.py:308
  9.9 2.1 %collective-permute-done.1 = bf16[12,2,1536]{2,1,0:T(2,128)(2,1)S(1)} collective-permute-done((bf16[12,2,1536]{2,1,0:T(2,128)(2,1)S(1)}, bf16[12,2,1536]{2,1,0:T(2,128)(2,1)S(1)}, u32[]{:S(2)}, u32[]{:S(2)}) %collective-permute-start.1) | collective-permute-done | bytes 73760 | tf_op jit(solution)/shard_map/ppermute | solution.py:304
  12.2 1.8 %collective-permute-start.2 = (bf16[24,2,1536]{2,1,0:T(2,128)(2,1)S(1)}, bf16[24,2,1536]{2,1,0:T(2,128)(2,1)S(1)}, u32[]{:S(2)}, u32[]{:S(2)}) collective-permute-start(bf16[24,2,1536]{2,1,0:T(2,128)(2,1)S(1)} %pad_maximum_fusion.rest_0_), channel_id=1, source_target_pairs={{0,2},{1,3},{2,0},{3,1},{4,6},{5,7},{6,4},{7,5},{8,10},{9,11},{10,... | collective-permute-start | bytes 442376 | tf_op jit(solution)/shard_map/ppermute | solution.py:304
  14.0 5.4 %prepare.1 = (bf16[1024,1536]{1,0:T(8,128)(2,1)S(1)}, bf16[1024,1536]{1,0:T(8,128)(2,1)S(1)}, bf16[16,1536]{1,0:T(8,128)(2,1)S(1)}, bf16[16,1536]{1,0:T(8,128)(2...) custom-call(s32[2,23]{1,0:T(2,128)S(1)} %add_add_fusion.table_ref, ...), custom_call_target="tpu_custom_call" | custom-call | flops 1610612736 | bytes 12582912 | tf_op jit(solution)/shard_map/prepare/pallas_call | solution.py:127
  19.5 0.5 %collective-permute-start.4 = (bf16[24,2,1536]{2,1,0:T(2,128)(2,1)S(1)}, bf16[24,2,1536]{2,1,0:T(2,128)(2,1)S(1)}, u32[]{:S(2)}, u32[]{:S(2)}) collective-permute-start(bf16[24,2,1536]{2,1,0:T(2,128)(2,1)S(1)} %collective-permute-done.2.rest_1_), channel_id=1, source_target_pairs={{0,1},{1,0},{2,3},{3,2},{4,5},{5,4},{6,7},{7,6},{8,9},{9,8},{10,11... | collective-permute-start | bytes 442376 | tf_op jit(solution)/shard_map/ppermute | solution.py:304
  20.0 0.9 %collective-permute-done.3.rest_2_ = bf16[24,2,1536]{2,1,0:T(2,128)(2,1)S(1)} collective-permute-done((bf16[24,2,1536]{2,1,0:T(2,128)(2,1)S(1)}, bf16[24,2,1536]{2,1,0:T(2,128)(2,1)S(1)}, u32[]{:S(2)}, u32[]{:S(2)}) %collective-permute-start.3) | collective-permute-done | bytes 147488 | tf_op jit(solution)/shard_map/ppermute | solution.py:304
  20.9 0.2 collective-permute-done.4.rest_3_
  21.1 5.5 %attend.1 = (f32[64,1664]{1,0:T(8,128)S(1)}, bf16[64,1664]{1,0:T(8,128)(2,1)S(1)}) custom-call(s32[1,192]{1,0:T(1,128)S(1)} %get-tuple-element.35.target_ref, f32[8,1024]{1,0:T(8,128)S(1)} %get-tuple-element.36.bias_ref, f32[8,16]{1,0:T(8,128)S(1)} %get-tuple-element.37.fresh_bias_ref, bf16[16,1536]{1,0:T(8,128)(2,1)S(1)} %get-tuple-element.38.fresh_key_ref, ...), custom_call_target="tpu_custom_call" | custom-call | flops 805306368 | bytes 6291456 | tf_op jit(solution)/shard_map/attend/pallas_call | solution.py:226
  26.6 0.4 collective-permute-start.5
  27.0 1.2 %collective-permute-done.5.refs_1_ = bf16[64,1664]{1,0:T(8,128)(2,1)S(1)} collective-permute-done((bf16[64,1664]{1,0:T(8,128)(2,1)S(1)}, bf16[64,1664]{1,0:T(8,128)(2,1)S(1)}, u32[]{:S(2)}, u32[]{:S(2)}) %collective-permute-start.5) | collective-permute-done | bytes 213024 | tf_op jit(solution)/shard_map/ppermute | solution.py:304
  28.1 0.4 merge_0.1
  28.6 0.4 collective-permute-start.6
  29.0 4.9 %collective-permute-done.6.refs_1_ = bf16[32,1664]{1,0:T(8,128)(2,1)S(1)} collective-permute-done((bf16[32,1664]{1,0:T(8,128)(2,1)S(1)}, bf16[32,1664]{1,0:T(8,128)(2,1)S(1)}, u32[]{:S(2)}, u32[]{:S(2)}) %collective-permute-start.6) | collective-permute-done | bytes 106528 | tf_op jit(solution)/shard_map/ppermute | solution.py:304
  33.8 0.3 merge_1.1
  34.1 1.4 %collective-permute-start.7 = (bf16[16,1664]{1,0:T(8,128)(2,1)S(1)}, bf16[16,1664]{1,0:T(8,128)(2,1)S(1)}, u32[]{:S(2)}, u32[]{:S(2)}) collective-permute-start(bf16[16,1664]{1,0:T(8,128)(2,1)S(1)} %get-tuple-element.48), channel_id=1, source_target_pairs={{0,4},{1,5},{2,6},{3,7},{4,0},{5,1},{6,2},{7,3},{8,12},{9,13},{10,... | collective-permute-start | bytes 159752 | tf_op jit(solution)/shard_map/ppermute | solution.py:304
  35.5 2.8 %collective-permute-done.7.refs_1_ = bf16[16,1664]{1,0:T(8,128)(2,1)S(1)} collective-permute-done((bf16[16,1664]{1,0:T(8,128)(2,1)S(1)}, bf16[16,1664]{1,0:T(8,128)(2,1)S(1)}, u32[]{:S(2)}, u32[]{:S(2)}) %collective-permute-start.7) | collective-permute-done | bytes 53280 | tf_op jit(solution)/shard_map/ppermute | solution.py:304
  38.3 0.2 merge_2.1
  38.6 2.4 %collective-permute-start.8 = (bf16[8,1664]{1,0:T(8,128)(2,1)S(1)}, bf16[8,1664]{1,0:T(8,128)(2,1)S(1)}, u32[]{:S(2)}, u32[]{:S(2)}) collective-permute-start(bf16[8,1664]{1,0:T(8,128)(2,1)S(1)} %get-tuple-element.50), channel_id=1, source_target_pairs={{0,8},{1,9},{2,10},{3,11},{4,12},{5,13},{6,14},{7,15},{8,0},{9,1},... | collective-permute-start | bytes 79880 | tf_op jit(solution)/shard_map/ppermute | solution.py:304
  41.0 2.4 %collective-permute-done.8.refs_1_ = bf16[8,1664]{1,0:T(8,128)(2,1)S(1)} collective-permute-done((bf16[8,1664]{1,0:T(8,128)(2,1)S(1)}, bf16[8,1664]{1,0:T(8,128)(2,1)S(1)}, u32[]{:S(2)}, u32[]{:S(2)}) %collective-permute-start.8) | collective-permute-done | bytes 26656 | tf_op jit(solution)/shard_map/ppermute | solution.py:304
  43.4 0.8 %merge_last.1 = bf16[2,4,1536]{2,1,0:T(4,128)(2,1)} custom-call(f32[8,1664]{1,0:T(8,128)S(1)} %get-tuple-element.49.refs_0_, bf16[8,1664]{1,0:T(8,128)(2,1)S(1)} %collective-permute-done.8.refs_1_), custom_call_target="tpu_custom_call" | custom-call | tf_op jit(solution)/shard_map/merge_last/pallas_call | solution.py:287
  (6 shorter events, 0.5 us)
Async XLA Ops:
  1.1 6.4 %collective-permute-start = (bf16[6,2,1536]{2,1,0:T(2,128)(2,1)S(1)}, bf16[6,2,1536]{2,1,0:T(2,128)(2,1)S(1)}, u32[]{:S(2)}, u32[]{:S(2)}) collective-permute-start(bf16[6,2,1536]{2,1,0:T(2,128)(2,1)S(1)} %get-tuple-element.53), channel_id=1, source_target_pairs={{0,8},{1,9},{2,10},{3,11},{4,12},{5,13},{6,14},{7,15},{8,0},{9,1},... | collective-permute-start | bytes 110600 | tf_op jit(solution)/shard_map/ppermute | solution.py:304
  7.6 4.4 %collective-permute-start.1 = (bf16[12,2,1536]{2,1,0:T(2,128)(2,1)S(1)}, bf16[12,2,1536]{2,1,0:T(2,128)(2,1)S(1)}, u32[]{:S(2)}, u32[]{:S(2)}) collective-permute-start(bf16[12,2,1536]{2,1,0:T(2,128)(2,1)S(1)} %pad_maximum_fusion.1), channel_id=1, source_target_pairs={{0,4},{1,5},{2,6},{3,7},{4,0},{5,1},{6,2},{7,3},{8,12},{9,13},{10,... | collective-permute-start | bytes 221192 | tf_op jit(solution)/shard_map/ppermute | solution.py:304
  12.2 7.3 %collective-permute-start.2 = (bf16[24,2,1536]{2,1,0:T(2,128)(2,1)S(1)}, bf16[24,2,1536]{2,1,0:T(2,128)(2,1)S(1)}, u32[]{:S(2)}, u32[]{:S(2)}) collective-permute-start(bf16[24,2,1536]{2,1,0:T(2,128)(2,1)S(1)} %pad_maximum_fusion.rest_0_), channel_id=1, source_target_pairs={{0,2},{1,3},{2,0},{3,1},{4,6},{5,7},{6,4},{7,5},{8,10},{9,11},{10,... | collective-permute-start | bytes 442376 | tf_op jit(solution)/shard_map/ppermute | solution.py:304
  19.4 1.4 %collective-permute-start.3 = (bf16[24,2,1536]{2,1,0:T(2,128)(2,1)S(1)}, bf16[24,2,1536]{2,1,0:T(2,128)(2,1)S(1)}, u32[]{:S(2)}, u32[]{:S(2)}) collective-permute-start(bf16[24,2,1536]{2,1,0:T(2,128)(2,1)S(1)} %pad_maximum_fusion.rest_0_), channel_id=1, source_target_pairs={{0,1},{1,0},{2,3},{3,2},{4,5},{5,4},{6,7},{7,6},{8,9},{9,8},{10,11... | collective-permute-start | bytes 442376 | tf_op jit(solution)/shard_map/ppermute | solution.py:304
  19.5 1.6 %collective-permute-start.4 = (bf16[24,2,1536]{2,1,0:T(2,128)(2,1)S(1)}, bf16[24,2,1536]{2,1,0:T(2,128)(2,1)S(1)}, u32[]{:S(2)}, u32[]{:S(2)}) collective-permute-start(bf16[24,2,1536]{2,1,0:T(2,128)(2,1)S(1)} %collective-permute-done.2.rest_1_), channel_id=1, source_target_pairs={{0,1},{1,0},{2,3},{3,2},{4,5},{5,4},{6,7},{7,6},{8,9},{9,8},{10,11... | collective-permute-start | bytes 442376 | tf_op jit(solution)/shard_map/ppermute | solution.py:304
  26.6 1.5 %collective-permute-start.5 = (bf16[64,1664]{1,0:T(8,128)(2,1)S(1)}, bf16[64,1664]{1,0:T(8,128)(2,1)S(1)}, u32[]{:S(2)}, u32[]{:S(2)}) collective-permute-start(bf16[64,1664]{1,0:T(8,128)(2,1)S(1)} %get-tuple-element.44), channel_id=1, source_target_pairs={{0,1},{1,0},{2,3},{3,2},{4,5},{5,4},{6,7},{7,6},{8,9},{9,8},{10,11... | collective-permute-start | bytes 638984 | tf_op jit(solution)/shard_map/ppermute | solution.py:304
  28.6 5.2 %collective-permute-start.6 = (bf16[32,1664]{1,0:T(8,128)(2,1)S(1)}, bf16[32,1664]{1,0:T(8,128)(2,1)S(1)}, u32[]{:S(2)}, u32[]{:S(2)}) collective-permute-start(bf16[32,1664]{1,0:T(8,128)(2,1)S(1)} %get-tuple-element.46), channel_id=1, source_target_pairs={{0,2},{1,3},{2,0},{3,1},{4,6},{5,7},{6,4},{7,5},{8,10},{9,11},{10,... | collective-permute-start | bytes 319496 | tf_op jit(solution)/shard_map/ppermute | solution.py:304
  34.1 4.2 %collective-permute-start.7 = (bf16[16,1664]{1,0:T(8,128)(2,1)S(1)}, bf16[16,1664]{1,0:T(8,128)(2,1)S(1)}, u32[]{:S(2)}, u32[]{:S(2)}) collective-permute-start(bf16[16,1664]{1,0:T(8,128)(2,1)S(1)} %get-tuple-element.48), channel_id=1, source_target_pairs={{0,4},{1,5},{2,6},{3,7},{4,0},{5,1},{6,2},{7,3},{8,12},{9,13},{10,... | collective-permute-start | bytes 159752 | tf_op jit(solution)/shard_map/ppermute | solution.py:304
  38.6 4.8 %collective-permute-start.8 = (bf16[8,1664]{1,0:T(8,128)(2,1)S(1)}, bf16[8,1664]{1,0:T(8,128)(2,1)S(1)}, u32[]{:S(2)}, u32[]{:S(2)}) collective-permute-start(bf16[8,1664]{1,0:T(8,128)(2,1)S(1)} %get-tuple-element.50), channel_id=1, source_target_pairs={{0,8},{1,9},{2,10},{3,11},{4,12},{5,13},{6,14},{7,15},{8,0},{9,1},... | collective-permute-start | bytes 79880 | tf_op jit(solution)/shard_map/ppermute | solution.py:304

commit v5 on v3

--- a/solution.py
+++ b/solution.py
@@ -28,10 +28,7 @@
 
 def place_of(mask, far, near):
     near_bits = near.bit_length() - 1
-    core = mask & 1
-    near_digit = (mask >> 1) & (near - 1)
-    far_digit = mask >> (1 + near_bits)
-    return (core * near + near_digit) * far + far_digit
+    return ((mask & 1) * near + ((mask >> 1) & (near - 1))) * far + (mask >> (1 + near_bits))
 
 
 def prepare_kernel(table_ref, cache_ref, new_key_ref, new_value_ref,
@@ -60,7 +57,9 @@
         local = col - place_of(dev ^ me, far, near) * (STEPS * slots)
         slot, step = local >> 1, local & 1
         rank = slot + jnp.where(step == 0, start0, start1)
-        row = place_of((rank >> SLOT_BITS) ^ me, far, near) * PAIR + step * SLOT + (rank & (SLOT - 1))
+        home = rank >> SLOT_BITS
+        home = ((home ^ me) & 1) * (device_count // 2) + (home >> 1)
+        row = home * PAIR + step * SLOT + (rank & (SLOT - 1))
         good = (local >= 0) & (slot < jnp.where(step == 0, count0, count1))
         return start0 + count0, start1 + count1, jnp.where(good, row, target)
 
@@ -244,11 +243,9 @@
     )(target, bias, fresh_bias, fresh_key, fresh_value, key, value, *gathered)
 
 
-def merge_kernel(count, last, *refs):
-    parts, outs = refs[:count], refs[count:]
-    rows, width = parts[0].shape
-    width -= LANES
-    stats = [unpack_stats(ref[:, width:].astype(jnp.float32)) for ref in parts]
+def merged(parts):
+    width = parts[0].shape[1] - LANES
+    stats = [unpack_stats(part[:, width:].astype(jnp.float32)) for part in parts]
     top = stats[0][0]
     for high, _ in stats[1:]:
         top = jnp.maximum(top, high)
@@ -262,40 +259,31 @@
     for h in range(width // HEAD):
         cols = slice(h * HEAD, (h + 1) * HEAD)
         o = parts[0][:, cols].astype(jnp.float32) * weights[0][:, h:h + 1]
-        for ref, w in zip(parts[1:], weights[1:]):
-            o = o + ref[:, cols].astype(jnp.float32) * w[:, h:h + 1]
-        if last:
+        for part, w in zip(parts[1:], weights[1:]):
+            o = o + part[:, cols].astype(jnp.float32) * w[:, h:h + 1]
+        yield cols, o
+    yield slice(width, width + LANES), pack_stats(jnp.where(used, top, 0.0), jnp.where(used, total, 0.0))
+
+
+def merge_cores_kernel(keep_ref, other_ref, out_ref):
+    for cols, o in merged([keep_ref, other_ref]):
+        out_ref[:, :, cols] = o.reshape(o.shape[0] // PAIR, PAIR, -1).astype(jnp.bfloat16)
+
+
+def merge_chips_kernel(parts_ref, out_ref):
+    width = out_ref.shape[2]
+    for cols, o in merged([parts_ref.at[n] for n in range(parts_ref.shape[0])]):
+        if cols.start < width:
             for s in range(STEPS):
-                outs[0][s, :, cols] = o[s * SLOT:(s + 1) * SLOT].astype(jnp.bfloat16)
-        else:
-            step = rows // len(outs)
-            for n, ref in enumerate(outs):
-                ref[:, cols] = o[n * step:(n + 1) * step].astype(ref.dtype)
-    if not last:
-        packed = pack_stats(jnp.where(used, top, 0.0), jnp.where(used, total, 0.0))
-        for n, ref in enumerate(outs):
-            ref[:, width:] = packed[n * step:(n + 1) * step].astype(ref.dtype)
-
-
-def merge(parts, out_count, name):
-    rows, width = parts[0].shape
-    last = out_count == 0
-    if last:
-        shapes = (jax.ShapeDtypeStruct((STEPS, SLOT, width - LANES), jnp.bfloat16),)
-    else:
-        shapes = tuple(
-            jax.ShapeDtypeStruct((rows // out_count, width), jnp.bfloat16 if n else jnp.float32)
-            for n in range(out_count)
-        )
-
-    def kernel(*refs):
-        merge_kernel(len(parts), last, *refs)
-
+                out_ref[s, :, cols] = o[s * SLOT:(s + 1) * SLOT].astype(jnp.bfloat16)
+
+
+def merge(kernel, parts, shape, name):
     return pl.pallas_call(
         kernel,
-        out_shape=shapes,
+        out_shape=jax.ShapeDtypeStruct(shape, jnp.bfloat16),
         in_specs=[VMEM] * len(parts),
-        out_specs=(VMEM,) * len(shapes),
+        out_specs=VMEM,
         compiler_params=pltpu.CompilerParams(vmem_limit_bytes=16 << 20),
         name=name,
     )(*parts)
@@ -304,7 +292,9 @@
 def body(cache_kv, fresh_qkv, list_rows, counts):
     device_count = lax.axis_size("blk")
     me = lax.axis_index("blk")
+    slot_count = list_rows.shape[1]
     far, near = mesh_digits(device_count)
+    width = cache_kv.shape[2]
 
     def swap(x, mask):
         return lax.ppermute(x, "blk", [(i, i ^ mask) for i in range(device_count)])
@@ -313,17 +303,18 @@
     mine, fresh_key, fresh_value = (fresh[:, i] for i in range(3))
     table = jnp.concatenate([counts, list_rows, jnp.full((STEPS, 1), me, jnp.int32)], axis=1)
     ready = prepare(table, cache_kv, fresh_key, fresh_value)
-    column = [swap(mine, k * near * 2) for k in range(1, far)]
-    column, ready = lax.optimization_barrier((column, ready))
-    column = jnp.concatenate([mine] + column)
-    plane = [column] + [swap(column, k * 2) for k in range(1, near)]
-    gathered = plane + [swap(x, 1) for x in plane]
+    plane = [jnp.concatenate([mine] + [swap(mine, k * near * 2) for k in range(1, far)])]
+    across = [swap(plane[0], k * 2) for k in range(1, near)]
+    beside = swap(plane[0], 1)
+    across, ready = lax.optimization_barrier((across, ready))
+    gathered = plane + across + [beside] + [swap(x, 1) for x in across]
     key, value, fresh_key, fresh_value, target, bias, fresh_bias = ready
-    keep, send = attend(list_rows.shape[1], target, bias, fresh_bias, fresh_key, fresh_value, key, value, gathered)
-    chips = near * far
-    keep, *sends = merge([keep, swap(send, 1)], chips, "merge_core")
-    sends = [swap(x, ((n % far) * near + n // far) * 2) for n, x in enumerate(sends, 1)]
-    return merge([keep] + sends, 0, "merge_chips")[0]
+    keep, send = attend(slot_count, target, bias, fresh_bias, fresh_key, fresh_value, key, value, gathered)
+    chips = device_count // 2
+    parts = merge(merge_cores_kernel, [keep, swap(send, 1)], (chips, PAIR, width + LANES), "merge_cores")
+    groups = [[chip * 2 + core for chip in range(chips)] for core in range(2)]
+    parts = lax.all_to_all(parts, "blk", split_axis=0, concat_axis=0, axis_index_groups=groups, tiled=True)
+    return merge(merge_chips_kernel, [parts], (STEPS, SLOT, width), "merge_chips")
 
 
 def solution(mesh):

time: 46.3 us -> 40.3 us (0.87)
  blocking collectives: 0 us -> 11.8 us
  starting transfers between devices: 18.9 us -> 8.25 us
  waiting for transfers between devices: 12.7 us -> 5.61 us
    all_to_all x0 -> x1, blocking collectives: none -> 11.8 us  [body(): lax.all_to_all(parts, 'blk', split_axis=0, concat_axis=0, axis_index_grou...]
    ppermute x14 -> x7, starting transfers between devices: 18.9 us -> 8.25 us  [swap(): return lax.ppermute(x, 'blk', [(i, i ^ mask) for i in range(device_count)])]
    ppermute x14 -> x7, waiting for transfers between devices: 12.7 us -> 5.61 us  [swap(): return lax.ppermute(x, 'blk', [(i, i ^ mask) for i in range(device_count)])]
  transfers between devices with their start and end apart: 14 -> 7, of which waited for: 5 -> 5; matrix products, arithmetic and copies ran while one was open for 2% -> 2% of each run, Pallas kernels for 12% -> 13%
where the time goes in v5:
time: 40.3 us; the launch traced here: 40.1 us
  Pallas kernels  12.3 us (31%)
  blocking collectives  11.8 us (29%)
  starting transfers between devices  8.25 us (20%)
  waiting for transfers between devices  5.61 us (14%)
  local copies, waits for them, and re-layouts  1.13 us (3%)
  other arithmetic  0.99 us (2%)
    all_to_all x1, blocking collectives, body(): lax.all_to_all(parts, 'blk', split_axis=0, concat_axis=0, axis_index_grou...  11.8 us
    ppermute x7, starting transfers between devices, swap(): return lax.ppermute(x, 'blk', [(i, i ^ mask) for i in range(device_count)])  8.25 us
    ppermute x7, waiting for transfers between devices, swap(): return lax.ppermute(x, 'blk', [(i, i ^ mask) for i in range(device_count)])  5.61 us
    pallas_call x1, Pallas kernels, attend(): pl.pallas_call(attend_kernel, out_shape=(jax.ShapeDtypeStruct(shape, jnp....  5.55 us
    pallas_call x1, Pallas kernels, prepare(): pl.pallas_call(prepare_kernel, out_shape=shapes, in_specs=[SMEM, HBM, VME...  5.4 us
    pallas_call x2, Pallas kernels, merge(): pl.pallas_call(kernel, out_shape=jax.ShapeDtypeStruct(shape, jnp.bfloat16...  1.36 us
    unnamed x1, local copies, waits for them, and re-layouts  0.97 us
  transfers between devices with their start and end apart: 7, of which 5 were waited for; matrix products, arithmetic and copies ran while one was open for 2% of the time, Pallas kernels for 13%

profile of v5, /device:TPU:0, one launch (start us, length us, event | category | flops | bytes accessed | tf_op | source)
XLA Modules:
  0.0 40.1 jit_solution(12229351021705884973)
XLA Ops:
  0.0 1.0 %copy.7 = bf16[2,6,3,1536]{3,0,1,2:T(2,128)(2,1)S(1)} copy(bf16[2,6,3,1536]{3,0,2,1:T(2,128)(2,1)} %param.5) | data formatting | bytes 221184 | tf_op args[1]
  1.0 0.1 slice_bitcast_fusion
  1.1 5.1 %collective-permute-start.2 = (bf16[6,2,1536]{2,1,0:T(2,128)(2,1)S(1)}, bf16[6,2,1536]{2,1,0:T(2,128)(2,1)S(1)}, u32[]{:S(2)}, u32[]{:S(2)}) collective-permute-start(bf16[6,2,1536]{2,1,0:T(2,128)(2,1)S(1)} %get-tuple-element.41), channel_id=1, source_target_pairs={{0,12},{1,13},{2,14},{3,15},{4,8},{5,9},{6,10},{7,11},{8,4},{9,5},... | collective-permute-start | bytes 110600 | tf_op jit(solution)/shard_map/ppermute | solution.py:300
  6.2 0.0 collective-permute-start.1
  6.2 0.6 %collective-permute-start = (bf16[6,2,1536]{2,1,0:T(2,128)(2,1)S(1)}, bf16[6,2,1536]{2,1,0:T(2,128)(2,1)S(1)}, u32[]{:S(2)}, u32[]{:S(2)}) collective-permute-start(bf16[6,2,1536]{2,1,0:T(2,128)(2,1)S(1)} %get-tuple-element.41), channel_id=1, source_target_pairs={{0,4},{1,5},{2,6},{3,7},{4,0},{5,1},{6,2},{7,3},{8,12},{9,13},{10,... | collective-permute-start | bytes 110600 | tf_op jit(solution)/shard_map/ppermute | solution.py:300
  6.8 0.1 pad.2.clone
  6.9 0.8 %add_add_fusion.table_ref = s32[2,23]{1,0:T(2,128)S(1)} fusion(s32[2,6]{1,0:T(2,128)} %param.6, s32[2,16]{1,0:T(2,128)} %param.7, s32[23]{0:T(128)S(1)} %pad.2.clone), kind=kLoop, calls=%fused_computation.5 | loop fusion | flops 92 | bytes 452 | tf_op jit(solution)/shard_map/concatenate | solution.py:304
  7.7 0.5 %collective-permute-done.2 = bf16[6,2,1536]{2,1,0:T(2,128)(2,1)S(1)} collective-permute-done((bf16[6,2,1536]{2,1,0:T(2,128)(2,1)S(1)}, bf16[6,2,1536]{2,1,0:T(2,128)(2,1)S(1)}, u32[]{:S(2)}, u32[]{:S(2)}) %collective-permute-start.2) | collective-permute-done | bytes 36896 | tf_op jit(solution)/shard_map/ppermute | solution.py:300
  8.1 2.9 %collective-permute-done.1 = bf16[6,2,1536]{2,1,0:T(2,128)(2,1)S(1)} collective-permute-done((bf16[6,2,1536]{2,1,0:T(2,128)(2,1)S(1)}, bf16[6,2,1536]{2,1,0:T(2,128)(2,1)S(1)}, u32[]{:S(2)}, u32[]{:S(2)}) %collective-permute-start.1) | collective-permute-done | bytes 36896 | tf_op jit(solution)/shard_map/ppermute | solution.py:300
  11.0 0.0 collective-permute-done
  11.0 0.2 pad_maximum_fusion.rest_0_
  11.3 1.6 %collective-permute-start.3 = (bf16[24,2,1536]{2,1,0:T(2,128)(2,1)S(1)}, bf16[24,2,1536]{2,1,0:T(2,128)(2,1)S(1)}, u32[]{:S(2)}, u32[]{:S(2)}) collective-permute-start(bf16[24,2,1536]{2,1,0:T(2,128)(2,1)S(1)} %pad_maximum_fusion.rest_0_), channel_id=1, source_target_pairs={{0,2},{1,3},{2,0},{3,1},{4,6},{5,7},{6,4},{7,5},{8,10},{9,11},{10,... | collective-permute-start | bytes 442376 | tf_op jit(solution)/shard_map/ppermute | solution.py:300
  12.8 5.4 %prepare.1 = (bf16[1024,1536]{1,0:T(8,128)(2,1)S(1)}, bf16[1024,1536]{1,0:T(8,128)(2,1)S(1)}, bf16[16,1536]{1,0:T(8,128)(2,1)S(1)}, bf16[16,1536]{1,0:T(8,128)(2...) custom-call(s32[2,23]{1,0:T(2,128)S(1)} %add_add_fusion.table_ref, ...), custom_call_target="tpu_custom_call" | custom-call | flops 1610612736 | bytes 12582912 | tf_op jit(solution)/shard_map/prepare/pallas_call | solution.py:133
  18.3 0.1 collective-permute-start.4
  18.3 0.0 collective-permute-done.3.rest_1_
  18.4 0.5 %collective-permute-start.5 = (bf16[24,2,1536]{2,1,0:T(2,128)(2,1)S(1)}, bf16[24,2,1536]{2,1,0:T(2,128)(2,1)S(1)}, u32[]{:S(2)}, u32[]{:S(2)}) collective-permute-start(bf16[24,2,1536]{2,1,0:T(2,128)(2,1)S(1)} %collective-permute-done.3.rest_1_), channel_id=1, source_target_pairs={{0,1},{1,0},{2,3},{3,2},{4,5},{5,4},{6,7},{7,6},{8,9},{9,8},{10,11... | collective-permute-start | bytes 442376 | tf_op jit(solution)/shard_map/ppermute | solution.py:300
  18.8 0.9 %collective-permute-done.4.rest_2_ = bf16[24,2,1536]{2,1,0:T(2,128)(2,1)S(1)} collective-permute-done((bf16[24,2,1536]{2,1,0:T(2,128)(2,1)S(1)}, bf16[24,2,1536]{2,1,0:T(2,128)(2,1)S(1)}, u32[]{:S(2)}, u32[]{:S(2)}) %collective-permute-start.4) | collective-permute-done | bytes 147488 | tf_op jit(solution)/shard_map/ppermute | solution.py:300
  19.7 0.2 collective-permute-done.5.rest_3_
  19.9 5.6 %attend.1 = (f32[64,1664]{1,0:T(8,128)S(1)}, bf16[64,1664]{1,0:T(8,128)(2,1)S(1)}) custom-call(s32[1,192]{1,0:T(1,128)S(1)} %get-tuple-element.29.target_ref, f32[8,1024]{1,0:T(8,128)S(1)} %get-tuple-element.30.bias_ref, f32[8,16]{1,0:T(8,128)S(1)} %get-tuple-element.31.fresh_bias_ref, bf16[16,1536]{1,0:T(8,128)(2,1)S(1)} %get-tuple-element.32.fresh_key_ref, ...), custom_call_target="tpu_custom_call" | custom-call | flops 805306368 | bytes 6291456 | tf_op jit(solution)/shard_map/attend/pallas_call | solution.py:232
  25.5 0.4 collective-permute-start.6
  25.8 1.2 %collective-permute-done.6.other_ref = bf16[64,1664]{1,0:T(8,128)(2,1)S(1)} collective-permute-done((bf16[64,1664]{1,0:T(8,128)(2,1)S(1)}, bf16[64,1664]{1,0:T(8,128)(2,1)S(1)}, u32[]{:S(2)}, u32[]{:S(2)}) %collective-permute-start.6) | collective-permute-done | bytes 213024 | tf_op jit(solution)/shard_map/ppermute | solution.py:300
  27.0 0.4 %merge_cores.1 = bf16[8,8,1664]{2,1,0:T(8,128)(2,1)S(1)} custom-call(f32[64,1664]{1,0:T(8,128)S(1)} %get-tuple-element.37.keep_ref, bf16[64,1664]{1,0:T(8,128)(2,1)S(1)} %collective-permute-done.6.other_ref), custom_call_target="tpu_custom_call" | custom-call | tf_op jit(solution)/shard_map/merge_cores/pallas_call | solution.py:282
  27.4 11.8 %all_to_all.5.parts_ref = bf16[8,8,1664]{2,1,0:T(8,128)(2,1)S(1)} all-to-all(bf16[8,8,1664]{2,1,0:T(8,128)(2,1)S(1)} %merge_cores.1), channel_id=1, replica_groups={{0,2,4,6,8,10,12,14},{1,3,5,7,9,11,13,15},{16,18,20,22,24,26,28,30},{17..., dimensions={0} | all-to-all | bytes 425984 | tf_op jit(solution)/shard_map/all_to_all | solution.py:316
  39.2 0.9 %merge_chips.1 = bf16[2,4,1536]{2,1,0:T(4,128)(2,1)} custom-call(bf16[8,8,1664]{2,1,0:T(8,128)(2,1)S(1)} %all_to_all.5.parts_ref), custom_call_target="tpu_custom_call" | custom-call | tf_op jit(solution)/shard_map/merge_chips/pallas_call | solution.py:282
Async XLA Ops:
  1.1 7.1 %collective-permute-start.2 = (bf16[6,2,1536]{2,1,0:T(2,128)(2,1)S(1)}, bf16[6,2,1536]{2,1,0:T(2,128)(2,1)S(1)}, u32[]{:S(2)}, u32[]{:S(2)}) collective-permute-start(bf16[6,2,1536]{2,1,0:T(2,128)(2,1)S(1)} %get-tuple-element.41), channel_id=1, source_target_pairs={{0,12},{1,13},{2,14},{3,15},{4,8},{5,9},{6,10},{7,11},{8,4},{9,5},... | collective-permute-start | bytes 110600 | tf_op jit(solution)/shard_map/ppermute | solution.py:300
  6.2 4.9 %collective-permute-start.1 = (bf16[6,2,1536]{2,1,0:T(2,128)(2,1)S(1)}, bf16[6,2,1536]{2,1,0:T(2,128)(2,1)S(1)}, u32[]{:S(2)}, u32[]{:S(2)}) collective-permute-start(bf16[6,2,1536]{2,1,0:T(2,128)(2,1)S(1)} %get-tuple-element.41), channel_id=1, source_target_pairs={{0,8},{1,9},{2,10},{3,11},{4,12},{5,13},{6,14},{7,15},{8,0},{9,1},... | collective-permute-start | bytes 110600 | tf_op jit(solution)/shard_map/ppermute | solution.py:300
  6.2 4.9 %collective-permute-start = (bf16[6,2,1536]{2,1,0:T(2,128)(2,1)S(1)}, bf16[6,2,1536]{2,1,0:T(2,128)(2,1)S(1)}, u32[]{:S(2)}, u32[]{:S(2)}) collective-permute-start(bf16[6,2,1536]{2,1,0:T(2,128)(2,1)S(1)} %get-tuple-element.41), channel_id=1, source_target_pairs={{0,4},{1,5},{2,6},{3,7},{4,0},{5,1},{6,2},{7,3},{8,12},{9,13},{10,... | collective-permute-start | bytes 110600 | tf_op jit(solution)/shard_map/ppermute | solution.py:300
  11.3 7.1 %collective-permute-start.3 = (bf16[24,2,1536]{2,1,0:T(2,128)(2,1)S(1)}, bf16[24,2,1536]{2,1,0:T(2,128)(2,1)S(1)}, u32[]{:S(2)}, u32[]{:S(2)}) collective-permute-start(bf16[24,2,1536]{2,1,0:T(2,128)(2,1)S(1)} %pad_maximum_fusion.rest_0_), channel_id=1, source_target_pairs={{0,2},{1,3},{2,0},{3,1},{4,6},{5,7},{6,4},{7,5},{8,10},{9,11},{10,... | collective-permute-start | bytes 442376 | tf_op jit(solution)/shard_map/ppermute | solution.py:300
  18.3 1.4 %collective-permute-start.4 = (bf16[24,2,1536]{2,1,0:T(2,128)(2,1)S(1)}, bf16[24,2,1536]{2,1,0:T(2,128)(2,1)S(1)}, u32[]{:S(2)}, u32[]{:S(2)}) collective-permute-start(bf16[24,2,1536]{2,1,0:T(2,128)(2,1)S(1)} %pad_maximum_fusion.rest_0_), channel_id=1, source_target_pairs={{0,1},{1,0},{2,3},{3,2},{4,5},{5,4},{6,7},{7,6},{8,9},{9,8},{10,11... | collective-permute-start | bytes 442376 | tf_op jit(solution)/shard_map/ppermute | solution.py:300
  18.4 1.6 %collective-permute-start.5 = (bf16[24,2,1536]{2,1,0:T(2,128)(2,1)S(1)}, bf16[24,2,1536]{2,1,0:T(2,128)(2,1)S(1)}, u32[]{:S(2)}, u32[]{:S(2)}) collective-permute-start(bf16[24,2,1536]{2,1,0:T(2,128)(2,1)S(1)} %collective-permute-done.3.rest_1_), channel_id=1, source_target_pairs={{0,1},{1,0},{2,3},{3,2},{4,5},{5,4},{6,7},{7,6},{8,9},{9,8},{10,11... | collective-permute-start | bytes 442376 | tf_op jit(solution)/shard_map/ppermute | solution.py:300
  25.5 1.5 %collective-permute-start.6 = (bf16[64,1664]{1,0:T(8,128)(2,1)S(1)}, bf16[64,1664]{1,0:T(8,128)(2,1)S(1)}, u32[]{:S(2)}, u32[]{:S(2)}) collective-permute-start(bf16[64,1664]{1,0:T(8,128)(2,1)S(1)} %get-tuple-element.38), channel_id=1, source_target_pairs={{0,1},{1,0},{2,3},{3,2},{4,5},{5,4},{6,7},{7,6},{8,9},{9,8},{10,11... | collective-permute-start | bytes 638984 | tf_op jit(solution)/shard_map/ppermute | solution.py:300

commit v6 on v5

--- a/solution.py
+++ b/solution.py
@@ -43,7 +43,7 @@
 
     def fetch(i):
         part = pl.ds(i * block, block)
-        return pltpu.make_async_copy(cache_ref.at[part], held.at[part], sems.at[i])
+        return pltpu.make_async_copy(cache_ref.at[part], held.at[part, :, pl.ds(0, width)], sems.at[i])
 
     for i in range(blocks):
         fetch(i).start()
@@ -100,7 +100,7 @@
     out = lax.broadcasted_iota(jnp.int32, (2 * block, 2 * block), 0)
     src = lax.broadcasted_iota(jnp.int32, (2 * block, 2 * block), 1)
     order = (src == jnp.where(out < block, 2 * out, 2 * (out - block) + 1)).astype(jnp.bfloat16)
-    pairs = held.reshape(2 * tokens, width)
+    pairs = held.reshape(2 * tokens, held.shape[2])
     for i in range(blocks):
         fetch(i).wait()
         rows = slice(i * block, (i + 1) * block)
@@ -136,7 +136,7 @@
         in_specs=[SMEM, HBM, VMEM, VMEM],
         out_specs=(VMEM,) * len(shapes),
         scratch_shapes=[
-            pltpu.VMEM((tokens, 2, width), bf16),
+            pltpu.VMEM((tokens, 2, width + LANES), bf16),
             pltpu.SemaphoreType.DMA((blocks,)),
         ],
         compiler_params=pltpu.CompilerParams(vmem_limit_bytes=45 << 20),
@@ -193,20 +193,32 @@
         lane = lax.broadcasted_iota(jnp.int32, (chunk, LANES), 1)
         highs = jnp.zeros((chunk, LANES), jnp.float32)
         totals = jnp.zeros((chunk, LANES), jnp.float32)
-        for h in range(heads):
+        ones = jnp.ones((key_ref.shape[0], LANES), jnp.bfloat16)
+
+        def score(h):
             cols = slice(h * HEAD, (h + 1) * HEAD)
             q = queries[:, cols]
             s = lax.dot_general(q, key_ref[:, cols], nt, preferred_element_type=jnp.float32)
             sf = lax.dot_general(q, fresh_key_ref[:, cols], nt, preferred_element_type=jnp.float32)
             s = (s.reshape(chunk // PAIR, PAIR, -1) + bias[None]).reshape(chunk, -1)
             sf = (sf.reshape(chunk // PAIR, PAIR, -1) + fresh_bias[None]).reshape(chunk, -1)
+            return s, sf
+
+        following = score(0)
+        for h in range(heads):
+            cols = slice(h * HEAD, (h + 1) * HEAD)
+            s, sf = following
+            if h + 1 < heads:
+                following = score(h + 1)
             high = jnp.maximum(jnp.max(s, axis=1, keepdims=True), jnp.max(sf, axis=1, keepdims=True))
-            w = jnp.exp2((s - high) * SCALE)
-            wf = jnp.exp2((sf - high) * SCALE)
-            total = jnp.sum(w, axis=1, keepdims=True) + jnp.sum(wf, axis=1, keepdims=True)
-            o = jnp.dot(w.astype(jnp.bfloat16), value_ref[:, cols], preferred_element_type=jnp.float32)
-            o += jnp.dot(wf.astype(jnp.bfloat16), fresh_value_ref[:, cols], preferred_element_type=jnp.float32)
-            o = o * (1.0 / total)
+            w = jnp.exp2((s - high) * SCALE).astype(jnp.bfloat16)
+            wf = jnp.exp2((sf - high) * SCALE).astype(jnp.bfloat16)
+            value = jnp.concatenate([value_ref[:, cols], ones], axis=1)
+            fresh_value = jnp.concatenate([fresh_value_ref[:, cols], ones[:fresh_value_ref.shape[0]]], axis=1)
+            o = jnp.dot(w, value, preferred_element_type=jnp.float32)
+            o += jnp.dot(wf, fresh_value, preferred_element_type=jnp.float32)
+            total = o[:, HEAD:]
+            o = o[:, :HEAD] * (1.0 / total)
             for ref, to, start, count in stores:
                 ref[pl.ds(to, count), cols] = o[start:start + count].astype(ref.dtype)
             highs = jnp.where(lane == h, high, highs)

time: 40.3 us -> 38.2 us (0.948)
  Pallas kernels: 12.3 us -> 10.2 us
    pallas_call x1, Pallas kernels: 5.55 us -> 3.43 us  [attend(): pl.pallas_call(attend_kernel, out_shape=(jax.ShapeDtypeStruct(shape, jnp....]
  transfers between devices with their start and end apart: 7 -> 7, of which waited for: 5 -> 5; matrix products, arithmetic and copies ran while one was open for 2% -> 2% of each run, Pallas kernels for 13% -> 14%
where the time goes in v6:
time: 38.2 us; the launch traced here: 38 us
  blocking collectives  11.8 us (31%)
  Pallas kernels  10.2 us (27%)
  starting transfers between devices  8.28 us (22%)
  waiting for transfers between devices  5.6 us (15%)
  local copies, waits for them, and re-layouts  1.13 us (3%)
  other arithmetic  0.99 us (3%)
    all_to_all x1, blocking collectives, body(): lax.all_to_all(parts, 'blk', split_axis=0, concat_axis=0, axis_index_grou...  11.8 us
    ppermute x7, starting transfers between devices, swap(): return lax.ppermute(x, 'blk', [(i, i ^ mask) for i in range(device_count)])  8.28 us
    ppermute x7, waiting for transfers between devices, swap(): return lax.ppermute(x, 'blk', [(i, i ^ mask) for i in range(device_count)])  5.6 us
    pallas_call x1, Pallas kernels, prepare(): pl.pallas_call(prepare_kernel, out_shape=shapes, in_specs=[SMEM, HBM, VME...  5.39 us
    pallas_call x1, Pallas kernels, attend(): pl.pallas_call(attend_kernel, out_shape=(jax.ShapeDtypeStruct(shape, jnp....  3.43 us
    pallas_call x2, Pallas kernels, merge(): pl.pallas_call(kernel, out_shape=jax.ShapeDtypeStruct(shape, jnp.bfloat16...  1.36 us
    unnamed x1, local copies, waits for them, and re-layouts  0.97 us
    concatenate x1, other arithmetic, body(): jnp.concatenate([counts, list_rows, jnp.full((STEPS, 1), me, jnp.int32)],...  0.77 us
  transfers between devices with their start and end apart: 7, of which 5 were waited for; matrix products, arithmetic and copies ran while one was open for 2% of the time, Pallas kernels for 14%

profile of v6, /device:TPU:0, one launch (start us, length us, event | category | flops | bytes accessed | tf_op | source)
XLA Modules:
  0.0 38.0 jit_solution(5086190927568800465)
XLA Ops:
  0.0 1.0 %copy.7 = bf16[2,6,3,1536]{3,0,1,2:T(2,128)(2,1)S(1)} copy(bf16[2,6,3,1536]{3,0,2,1:T(2,128)(2,1)} %param.5) | data formatting | bytes 221184 | tf_op args[1]
  1.0 0.1 slice_bitcast_fusion
  1.1 5.1 %collective-permute-start.2 = (bf16[6,2,1536]{2,1,0:T(2,128)(2,1)S(1)}, bf16[6,2,1536]{2,1,0:T(2,128)(2,1)S(1)}, u32[]{:S(2)}, u32[]{:S(2)}) collective-permute-start(bf16[6,2,1536]{2,1,0:T(2,128)(2,1)S(1)} %get-tuple-element.41), channel_id=1, source_target_pairs={{0,12},{1,13},{2,14},{3,15},{4,8},{5,9},{6,10},{7,11},{8,4},{9,5},... | collective-permute-start | bytes 110600 | tf_op jit(solution)/shard_map/ppermute | solution.py:312
  6.2 0.0 collective-permute-start.1
  6.2 0.6 %collective-permute-start = (bf16[6,2,1536]{2,1,0:T(2,128)(2,1)S(1)}, bf16[6,2,1536]{2,1,0:T(2,128)(2,1)S(1)}, u32[]{:S(2)}, u32[]{:S(2)}) collective-permute-start(bf16[6,2,1536]{2,1,0:T(2,128)(2,1)S(1)} %get-tuple-element.41), channel_id=1, source_target_pairs={{0,4},{1,5},{2,6},{3,7},{4,0},{5,1},{6,2},{7,3},{8,12},{9,13},{10,... | collective-permute-start | bytes 110600 | tf_op jit(solution)/shard_map/ppermute | solution.py:312
  6.8 0.1 pad.2.clone
  6.9 0.8 %add_add_fusion.table_ref = s32[2,23]{1,0:T(2,128)S(1)} fusion(s32[2,6]{1,0:T(2,128)} %param.6, s32[2,16]{1,0:T(2,128)} %param.7, s32[23]{0:T(128)S(1)} %pad.2.clone), kind=kLoop, calls=%fused_computation.5 | loop fusion | flops 92 | bytes 452 | tf_op jit(solution)/shard_map/concatenate | solution.py:316
  7.7 0.5 %collective-permute-done.2 = bf16[6,2,1536]{2,1,0:T(2,128)(2,1)S(1)} collective-permute-done((bf16[6,2,1536]{2,1,0:T(2,128)(2,1)S(1)}, bf16[6,2,1536]{2,1,0:T(2,128)(2,1)S(1)}, u32[]{:S(2)}, u32[]{:S(2)}) %collective-permute-start.2) | collective-permute-done | bytes 36896 | tf_op jit(solution)/shard_map/ppermute | solution.py:312
  8.1 2.9 %collective-permute-done.1 = bf16[6,2,1536]{2,1,0:T(2,128)(2,1)S(1)} collective-permute-done((bf16[6,2,1536]{2,1,0:T(2,128)(2,1)S(1)}, bf16[6,2,1536]{2,1,0:T(2,128)(2,1)S(1)}, u32[]{:S(2)}, u32[]{:S(2)}) %collective-permute-start.1) | collective-permute-done | bytes 36896 | tf_op jit(solution)/shard_map/ppermute | solution.py:312
  11.0 0.0 collective-permute-done
  11.0 0.2 pad_maximum_fusion.rest_0_
  11.3 1.6 %collective-permute-start.3 = (bf16[24,2,1536]{2,1,0:T(2,128)(2,1)S(1)}, bf16[24,2,1536]{2,1,0:T(2,128)(2,1)S(1)}, u32[]{:S(2)}, u32[]{:S(2)}) collective-permute-start(bf16[24,2,1536]{2,1,0:T(2,128)(2,1)S(1)} %pad_maximum_fusion.rest_0_), channel_id=1, source_target_pairs={{0,2},{1,3},{2,0},{3,1},{4,6},{5,7},{6,4},{7,5},{8,10},{9,11},{10,... | collective-permute-start | bytes 442376 | tf_op jit(solution)/shard_map/ppermute | solution.py:312
  12.8 5.4 %prepare.1 = (bf16[1024,1536]{1,0:T(8,128)(2,1)S(1)}, bf16[1024,1536]{1,0:T(8,128)(2,1)S(1)}, bf16[16,1536]{1,0:T(8,128)(2,1)S(1)}, bf16[16,1536]{1,0:T(8,128)(2...) custom-call(s32[2,23]{1,0:T(2,128)S(1)} %add_add_fusion.table_ref, ...), custom_call_target="tpu_custom_call" | custom-call | flops 1610612736 | bytes 12582912 | tf_op jit(solution)/shard_map/prepare/pallas_call | solution.py:133
  18.2 0.1 collective-permute-start.4
  18.3 0.0 collective-permute-done.3.rest_1_
  18.3 0.5 %collective-permute-start.5 = (bf16[24,2,1536]{2,1,0:T(2,128)(2,1)S(1)}, bf16[24,2,1536]{2,1,0:T(2,128)(2,1)S(1)}, u32[]{:S(2)}, u32[]{:S(2)}) collective-permute-start(bf16[24,2,1536]{2,1,0:T(2,128)(2,1)S(1)} %collective-permute-done.3.rest_1_), channel_id=1, source_target_pairs={{0,1},{1,0},{2,3},{3,2},{4,5},{5,4},{6,7},{7,6},{8,9},{9,8},{10,11... | collective-permute-start | bytes 442376 | tf_op jit(solution)/shard_map/ppermute | solution.py:312
  18.8 0.9 %collective-permute-done.4.rest_2_ = bf16[24,2,1536]{2,1,0:T(2,128)(2,1)S(1)} collective-permute-done((bf16[24,2,1536]{2,1,0:T(2,128)(2,1)S(1)}, bf16[24,2,1536]{2,1,0:T(2,128)(2,1)S(1)}, u32[]{:S(2)}, u32[]{:S(2)}) %collective-permute-start.4) | collective-permute-done | bytes 147488 | tf_op jit(solution)/shard_map/ppermute | solution.py:312
  19.7 0.2 collective-permute-done.5.rest_3_
  19.9 3.4 %attend.1 = (f32[64,1664]{1,0:T(8,128)S(1)}, bf16[64,1664]{1,0:T(8,128)(2,1)S(1)}) custom-call(s32[1,192]{1,0:T(1,128)S(1)} %get-tuple-element.29.target_ref, f32[8,1024]{1,0:T(8,128)S(1)} %get-tuple-element.30.bias_ref, f32[8,16]{1,0:T(8,128)S(1)} %get-tuple-element.31.fresh_bias_ref, bf16[16,1536]{1,0:T(8,128)(2,1)S(1)} %get-tuple-element.32.fresh_key_ref, ...), custom_call_target="tpu_custom_call" | custom-call | flops 805306368 | bytes 6291456 | tf_op jit(solution)/shard_map/attend/pallas_call | solution.py:244
  23.3 0.4 collective-permute-start.6
  23.7 1.2 %collective-permute-done.6.other_ref = bf16[64,1664]{1,0:T(8,128)(2,1)S(1)} collective-permute-done((bf16[64,1664]{1,0:T(8,128)(2,1)S(1)}, bf16[64,1664]{1,0:T(8,128)(2,1)S(1)}, u32[]{:S(2)}, u32[]{:S(2)}) %collective-permute-start.6) | collective-permute-done | bytes 213024 | tf_op jit(solution)/shard_map/ppermute | solution.py:312
  24.9 0.4 %merge_cores.1 = bf16[8,8,1664]{2,1,0:T(8,128)(2,1)S(1)} custom-call(f32[64,1664]{1,0:T(8,128)S(1)} %get-tuple-element.37.keep_ref, bf16[64,1664]{1,0:T(8,128)(2,1)S(1)} %collective-permute-done.6.other_ref), custom_call_target="tpu_custom_call" | custom-call | tf_op jit(solution)/shard_map/merge_cores/pallas_call | solution.py:294
  25.3 11.8 %all_to_all.5.parts_ref = bf16[8,8,1664]{2,1,0:T(8,128)(2,1)S(1)} all-to-all(bf16[8,8,1664]{2,1,0:T(8,128)(2,1)S(1)} %merge_cores.1), channel_id=1, replica_groups={{0,2,4,6,8,10,12,14},{1,3,5,7,9,11,13,15},{16,18,20,22,24,26,28,30},{17..., dimensions={0} | all-to-all | bytes 425984 | tf_op jit(solution)/shard_map/all_to_all | solution.py:328
  37.1 0.9 %merge_chips.1 = bf16[2,4,1536]{2,1,0:T(4,128)(2,1)} custom-call(bf16[8,8,1664]{2,1,0:T(8,128)(2,1)S(1)} %all_to_all.5.parts_ref), custom_call_target="tpu_custom_call" | custom-call | tf_op jit(solution)/shard_map/merge_chips/pallas_call | solution.py:294
Async XLA Ops:
  1.1 7.1 %collective-permute-start.2 = (bf16[6,2,1536]{2,1,0:T(2,128)(2,1)S(1)}, bf16[6,2,1536]{2,1,0:T(2,128)(2,1)S(1)}, u32[]{:S(2)}, u32[]{:S(2)}) collective-permute-start(bf16[6,2,1536]{2,1,0:T(2,128)(2,1)S(1)} %get-tuple-element.41), channel_id=1, source_target_pairs={{0,12},{1,13},{2,14},{3,15},{4,8},{5,9},{6,10},{7,11},{8,4},{9,5},... | collective-permute-start | bytes 110600 | tf_op jit(solution)/shard_map/ppermute | solution.py:312
  6.2 4.9 %collective-permute-start.1 = (bf16[6,2,1536]{2,1,0:T(2,128)(2,1)S(1)}, bf16[6,2,1536]{2,1,0:T(2,128)(2,1)S(1)}, u32[]{:S(2)}, u32[]{:S(2)}) collective-permute-start(bf16[6,2,1536]{2,1,0:T(2,128)(2,1)S(1)} %get-tuple-element.41), channel_id=1, source_target_pairs={{0,8},{1,9},{2,10},{3,11},{4,12},{5,13},{6,14},{7,15},{8,0},{9,1},... | collective-permute-start | bytes 110600 | tf_op jit(solution)/shard_map/ppermute | solution.py:312
  6.2 4.9 %collective-permute-start = (bf16[6,2,1536]{2,1,0:T(2,128)(2,1)S(1)}, bf16[6,2,1536]{2,1,0:T(2,128)(2,1)S(1)}, u32[]{:S(2)}, u32[]{:S(2)}) collective-permute-start(bf16[6,2,1536]{2,1,0:T(2,128)(2,1)S(1)} %get-tuple-element.41), channel_id=1, source_target_pairs={{0,4},{1,5},{2,6},{3,7},{4,0},{5,1},{6,2},{7,3},{8,12},{9,13},{10,... | collective-permute-start | bytes 110600 | tf_op jit(solution)/shard_map/ppermute | solution.py:312
  11.3 7.1 %collective-permute-start.3 = (bf16[24,2,1536]{2,1,0:T(2,128)(2,1)S(1)}, bf16[24,2,1536]{2,1,0:T(2,128)(2,1)S(1)}, u32[]{:S(2)}, u32[]{:S(2)}) collective-permute-start(bf16[24,2,1536]{2,1,0:T(2,128)(2,1)S(1)} %pad_maximum_fusion.rest_0_), channel_id=1, source_target_pairs={{0,2},{1,3},{2,0},{3,1},{4,6},{5,7},{6,4},{7,5},{8,10},{9,11},{10,... | collective-permute-start | bytes 442376 | tf_op jit(solution)/shard_map/ppermute | solution.py:312
  18.2 1.4 %collective-permute-start.4 = (bf16[24,2,1536]{2,1,0:T(2,128)(2,1)S(1)}, bf16[24,2,1536]{2,1,0:T(2,128)(2,1)S(1)}, u32[]{:S(2)}, u32[]{:S(2)}) collective-permute-start(bf16[24,2,1536]{2,1,0:T(2,128)(2,1)S(1)} %pad_maximum_fusion.rest_0_), channel_id=1, source_target_pairs={{0,1},{1,0},{2,3},{3,2},{4,5},{5,4},{6,7},{7,6},{8,9},{9,8},{10,11... | collective-permute-start | bytes 442376 | tf_op jit(solution)/shard_map/ppermute | solution.py:312
  18.3 1.6 %collective-permute-start.5 = (bf16[24,2,1536]{2,1,0:T(2,128)(2,1)S(1)}, bf16[24,2,1536]{2,1,0:T(2,128)(2,1)S(1)}, u32[]{:S(2)}, u32[]{:S(2)}) collective-permute-start(bf16[24,2,1536]{2,1,0:T(2,128)(2,1)S(1)} %collective-permute-done.3.rest_1_), channel_id=1, source_target_pairs={{0,1},{1,0},{2,3},{3,2},{4,5},{5,4},{6,7},{7,6},{8,9},{9,8},{10,11... | collective-permute-start | bytes 442376 | tf_op jit(solution)/shard_map/ppermute | solution.py:312
  23.3 1.5 %collective-permute-start.6 = (bf16[64,1664]{1,0:T(8,128)(2,1)S(1)}, bf16[64,1664]{1,0:T(8,128)(2,1)S(1)}, u32[]{:S(2)}, u32[]{:S(2)}) collective-permute-start(bf16[64,1664]{1,0:T(8,128)(2,1)S(1)} %get-tuple-element.38), channel_id=1, source_target_pairs={{0,1},{1,0},{2,3},{3,2},{4,5},{5,4},{6,7},{7,6},{8,9},{9,8},{10,11... | collective-permute-start | bytes 638984 | tf_op jit(solution)/shard_map/ppermute | solution.py:312

commit v7 on v6

--- a/solution.py
+++ b/solution.py
@@ -15,20 +15,17 @@
 LANES = 128
 PART = 16
 SLOT_BITS = 2
+WAITS = 4
 VMEM = pl.BlockSpec(memory_space=pltpu.VMEM)
 SMEM = pl.BlockSpec(memory_space=pltpu.SMEM)
 HBM = pl.BlockSpec(memory_space=pltpu.HBM)
 
 
-def mesh_digits(device_count):
-    bits = (device_count // 2).bit_length() - 1
-    far_bits = (bits + 1) // 2
-    return 1 << far_bits, 1 << (bits - far_bits)
-
-
-def place_of(mask, far, near):
-    near_bits = near.bit_length() - 1
-    return ((mask & 1) * near + ((mask >> 1) & (near - 1))) * far + (mask >> (1 + near_bits))
+def turned(mask, bits):
+    place = 0
+    for n in range(bits):
+        place = place + (((mask >> n) & 1) << (bits - 1 - n))
+    return place
 
 
 def prepare_kernel(table_ref, cache_ref, new_key_ref, new_value_ref,
@@ -37,7 +34,7 @@
     tokens, _, width = cache_ref.shape
     slots = new_key_ref.shape[0]
     device_count = table_ref.shape[1] - slots - 1
-    far, near = mesh_digits(device_count)
+    bits = device_count.bit_length() - 1
     block = min(128, tokens)
     blocks = tokens // block
 
@@ -54,11 +51,11 @@
     def one_device(dev, carry):
         start0, start1, target = carry
         count0, count1 = table_ref[0, dev], table_ref[1, dev]
-        local = col - place_of(dev ^ me, far, near) * (STEPS * slots)
+        local = col - turned(dev ^ me, bits) * (STEPS * slots)
         slot, step = local >> 1, local & 1
         rank = slot + jnp.where(step == 0, start0, start1)
         home = rank >> SLOT_BITS
-        home = ((home ^ me) & 1) * (device_count // 2) + (home >> 1)
+        home = (((home ^ me) & 1) * 4 + ((home >> 1) & 3)) * (device_count // 8) + turned((home ^ me) >> 3, bits - 3)
         row = home * PAIR + step * SLOT + (rank & (SLOT - 1))
         good = (local >= 0) & (slot < jnp.where(step == 0, count0, count1))
         return start0 + count0, start1 + count1, jnp.where(good, row, target)
@@ -102,7 +99,9 @@
     order = (src == jnp.where(out < block, 2 * out, 2 * (out - block) + 1)).astype(jnp.bfloat16)
     pairs = held.reshape(2 * tokens, held.shape[2])
     for i in range(blocks):
-        fetch(i).wait()
+        if i % WAITS == 0:
+            for j in range(i, min(i + WAITS, blocks)):
+                fetch(j).wait()
         rows = slice(i * block, (i + 1) * block)
         for c in range(0, width, 256):
             part = pairs[2 * i * block:2 * (i + 1) * block, c:c + 256]
@@ -180,14 +179,9 @@
     def attend_rows(base, chunk, stores):
         row = lax.broadcasted_iota(jnp.int32, (chunk, target_ref.shape[1]), 0)
         pick = (row == target_ref[...] - base).astype(jnp.bfloat16)
-        queries, at = None, 0
-        for ref in gathered_refs:
-            count = ref.shape[0] * STEPS
-            slots = ref.reshape(count, width)[...]
-            part = jnp.dot(pick[:, at:at + count], slots, preferred_element_type=jnp.float32)
-            queries = part if queries is None else queries + part
-            at += count
-        queries = queries.astype(jnp.bfloat16)
+        slots = [ref.reshape(ref.shape[0] * STEPS, width)[...].astype(jnp.float32) for ref in gathered_refs]
+        slots = jnp.concatenate(slots).astype(jnp.bfloat16)
+        queries = jnp.dot(pick, slots, preferred_element_type=jnp.float32).astype(jnp.bfloat16)
         bias = bias_ref[...]
         fresh_bias = fresh_bias_ref[...]
         lane = lax.broadcasted_iota(jnp.int32, (chunk, LANES), 1)
@@ -279,23 +273,34 @@
 
 def merge_cores_kernel(keep_ref, other_ref, out_ref):
     for cols, o in merged([keep_ref, other_ref]):
-        out_ref[:, :, cols] = o.reshape(o.shape[0] // PAIR, PAIR, -1).astype(jnp.bfloat16)
-
-
-def merge_chips_kernel(parts_ref, out_ref):
-    width = out_ref.shape[2]
-    for cols, o in merged([parts_ref.at[n] for n in range(parts_ref.shape[0])]):
-        if cols.start < width:
+        out_ref[:, :, cols] = o.reshape(out_ref.shape[0], out_ref.shape[1], -1).astype(jnp.bfloat16)
+
+
+def merge_four_kernel(parts_ref, *out_refs):
+    store_merged([parts_ref.at[n] for n in range(parts_ref.shape[0])], out_refs)
+
+
+def merge_two_kernel(keep_ref, other_ref, *out_refs):
+    store_merged([keep_ref, other_ref], out_refs)
+
+
+def store_merged(parts, out_refs):
+    rows, width = parts[0].shape
+    for cols, o in merged(parts):
+        if len(out_refs) == 2:
+            for n, ref in enumerate(out_refs):
+                ref[:, cols] = o[n * rows // 2:(n + 1) * rows // 2].astype(ref.dtype)
+        elif cols.start < width - LANES:
             for s in range(STEPS):
-                out_ref[s, :, cols] = o[s * SLOT:(s + 1) * SLOT].astype(jnp.bfloat16)
-
-
-def merge(kernel, parts, shape, name):
+                out_refs[0][s, :, cols] = o[s * SLOT:(s + 1) * SLOT].astype(jnp.bfloat16)
+
+
+def merge(kernel, parts, shapes, name):
     return pl.pallas_call(
         kernel,
-        out_shape=jax.ShapeDtypeStruct(shape, jnp.bfloat16),
+        out_shape=shapes,
         in_specs=[VMEM] * len(parts),
-        out_specs=VMEM,
+        out_specs=jax.tree.map(lambda _: VMEM, shapes),
         compiler_params=pltpu.CompilerParams(vmem_limit_bytes=16 << 20),
         name=name,
     )(*parts)
@@ -305,7 +310,7 @@
     device_count = lax.axis_size("blk")
     me = lax.axis_index("blk")
     slot_count = list_rows.shape[1]
-    far, near = mesh_digits(device_count)
+    bits = device_count.bit_length() - 1
     width = cache_kv.shape[2]
 
     def swap(x, mask):
@@ -315,18 +320,30 @@
     mine, fresh_key, fresh_value = (fresh[:, i] for i in range(3))
     table = jnp.concatenate([counts, list_rows, jnp.full((STEPS, 1), me, jnp.int32)], axis=1)
     ready = prepare(table, cache_kv, fresh_key, fresh_value)
-    plane = [jnp.concatenate([mine] + [swap(mine, k * near * 2) for k in range(1, far)])]
-    across = [swap(plane[0], k * 2) for k in range(1, near)]
-    beside = swap(plane[0], 1)
-    across, ready = lax.optimization_barrier((across, ready))
-    gathered = plane + across + [beside] + [swap(x, 1) for x in across]
+    column = mine
+    for n in range(bits - 1, 2, -1):
+        column = jnp.concatenate([column, swap(column, 1 << n)])
+    others = [swap(column, mask) for mask in (4, 2, 6)]
+    beside = swap(column, 1)
+    others, beside, ready = lax.optimization_barrier((others, beside, ready))
+    others = jnp.concatenate(others)
+    gathered = [column, others, beside, swap(others, 1)]
     key, value, fresh_key, fresh_value, target, bias, fresh_bias = ready
     keep, send = attend(slot_count, target, bias, fresh_bias, fresh_key, fresh_value, key, value, gathered)
-    chips = device_count // 2
-    parts = merge(merge_cores_kernel, [keep, swap(send, 1)], (chips, PAIR, width + LANES), "merge_cores")
-    groups = [[chip * 2 + core for chip in range(chips)] for core in range(2)]
-    parts = lax.all_to_all(parts, "blk", split_axis=0, concat_axis=0, axis_index_groups=groups, tiled=True)
-    return merge(merge_chips_kernel, [parts], (STEPS, SLOT, width), "merge_chips")
+    rows = device_count // 8 * PAIR
+    lanes = width + LANES
+    bf16 = jnp.bfloat16
+    parts = merge(merge_cores_kernel, [keep, swap(send, 1)], jax.ShapeDtypeStruct((4, rows, lanes), bf16), "merge_cores")
+    fours = [[(first * 4 + chip) * 2 + core for chip in range(4)] for first in range(device_count // 8) for core in range(2)]
+    parts = [lax.all_to_all(parts, "blk", split_axis=0, concat_axis=0, axis_index_groups=fours, tiled=True)]
+    kernel, name = merge_four_kernel, "merge_four"
+    for n in range(3, bits):
+        rows //= 2
+        shapes = (jax.ShapeDtypeStruct((rows, lanes), jnp.float32), jax.ShapeDtypeStruct((rows, lanes), bf16))
+        keep, send = merge(kernel, parts, shapes, name)
+        parts = [keep, swap(send, 1 << n)]
+        kernel, name = merge_two_kernel, "merge_two"
+    return merge(kernel, parts, jax.ShapeDtypeStruct((STEPS, SLOT, width), bf16), name)
 
 
 def solution(mesh):

time: 38.2 us -> 38.7 us (1.013)
  blocking collectives: 11.8 us -> 9.15 us
  starting transfers between devices: 8.28 us -> 10.9 us
  waiting for transfers between devices: 5.6 us -> 6.18 us
    ppermute x7 -> x8, starting transfers between devices: 8.28 us -> 10.9 us  [swap(): return lax.ppermute(x, 'blk', [(i, i ^ mask) for i in range(device_count)])]
    all_to_all x1, blocking collectives: 11.8 us -> 9.15 us  [body(): lax.all_to_all(parts, 'blk', split_axis=0, concat_axis=0, axis_index_grou...]
    ppermute x7 -> x8, waiting for transfers between devices: 5.6 us -> 6.18 us  [swap(): return lax.ppermute(x, 'blk', [(i, i ^ mask) for i in range(device_count)])]
    pallas_call x2 -> x3, Pallas kernels: 1.36 us -> 1.56 us  [merge(): pl.pallas_call(kernel, out_shape=shapes, in_specs=[VMEM] * len(parts), ou...]
    unnamed x1 -> x3, local copies, waits for them, and re-layouts: 0.97 us -> 1.09 us
  transfers between devices with their start and end apart: 7 -> 8, of which waited for: 5 -> 4; matrix products, arithmetic and copies ran while one was open for 2% -> 2% of each run, Pallas kernels for 14% -> 14%
where the time goes in v7:
time: 38.7 us; the launch traced here: 38.5 us
  starting transfers between devices  10.9 us (28%)
  Pallas kernels  9.98 us (26%)
  blocking collectives  9.15 us (24%)
  waiting for transfers between devices  6.18 us (16%)
  local copies, waits for them, and re-layouts  1.31 us (3%)
  other arithmetic  0.87 us (2%)
    ppermute x8, starting transfers between devices, swap(): return lax.ppermute(x, 'blk', [(i, i ^ mask) for i in range(device_count)])  10.9 us
    all_to_all x1, blocking collectives, body(): lax.all_to_all(parts, 'blk', split_axis=0, concat_axis=0, axis_index_grou...  9.15 us
    ppermute x8, waiting for transfers between devices, swap(): return lax.ppermute(x, 'blk', [(i, i ^ mask) for i in range(device_count)])  6.18 us
    pallas_call x1, Pallas kernels, prepare(): pl.pallas_call(prepare_kernel, out_shape=shapes, in_specs=[SMEM, HBM, VME...  5.21 us
    pallas_call x1, Pallas kernels, attend(): pl.pallas_call(attend_kernel, out_shape=(jax.ShapeDtypeStruct(shape, jnp....  3.22 us
    pallas_call x3, Pallas kernels, merge(): pl.pallas_call(kernel, out_shape=shapes, in_specs=[VMEM] * len(parts), ou...  1.56 us
    unnamed x3, local copies, waits for them, and re-layouts  1.09 us
  transfers between devices with their start and end apart: 8, of which 4 were waited for; matrix products, arithmetic and copies ran while one was open for 2% of the time, Pallas kernels for 14%

profile of v7, /device:TPU:0, one launch (start us, length us, event | category | flops | bytes accessed | tf_op | source)
XLA Modules:
  0.0 38.5 jit_solution(12631688760939944373)
XLA Ops:
  0.0 1.0 %copy.7 = bf16[2,6,3,1536]{3,0,1,2:T(2,128)(2,1)S(1)} copy(bf16[2,6,3,1536]{3,0,2,1:T(2,128)(2,1)} %param.5) | data formatting | bytes 221184 | tf_op args[1]
  1.0 0.1 slice_bitcast_fusion
  1.1 4.1 %collective-permute-start = (bf16[6,2,1536]{2,1,0:T(2,128)(2,1)S(1)}, bf16[6,2,1536]{2,1,0:T(2,128)(2,1)S(1)}, u32[]{:S(2)}, u32[]{:S(2)}) collective-permute-start(bf16[6,2,1536]{2,1,0:T(2,128)(2,1)S(1)} %get-tuple-element.51), channel_id=1, source_target_pairs={{0,8},{1,9},{2,10},{3,11},{4,12},{5,13},{6,14},{7,15},{8,0},{9,1},... | collective-permute-start | bytes 110600 | tf_op jit(solution)/shard_map/ppermute | solution.py:317
  5.2 0.1 pad.2.clone
  5.2 0.8 %add_add_fusion.table_ref = s32[2,23]{1,0:T(2,128)S(1)} fusion(s32[2,6]{1,0:T(2,128)} %param.6, s32[2,16]{1,0:T(2,128)} %param.7, s32[23]{0:T(128)S(1)} %pad.2.clone), kind=kLoop, calls=%fused_computation.8 | loop fusion | flops 92 | bytes 452 | tf_op jit(solution)/shard_map/concatenate | solution.py:321
  6.0 1.5 %collective-permute-done = bf16[6,2,1536]{2,1,0:T(2,128)(2,1)S(1)} collective-permute-done((bf16[6,2,1536]{2,1,0:T(2,128)(2,1)S(1)}, bf16[6,2,1536]{2,1,0:T(2,128)(2,1)S(1)}, u32[]{:S(2)}, u32[]{:S(2)}) %collective-permute-start) | collective-permute-done | bytes 36896 | tf_op jit(solution)/shard_map/ppermute | solution.py:317
  7.5 0.1 pad_maximum_fusion.rest_0_
  7.6 0.1 collective-permute-start.4
  7.7 2.5 %collective-permute-start.3 = (bf16[12,2,1536]{2,1,0:T(2,128)(2,1)S(1)}, bf16[12,2,1536]{2,1,0:T(2,128)(2,1)S(1)}, u32[]{:S(2)}, u32[]{:S(2)}) collective-permute-start(bf16[12,2,1536]{2,1,0:T(2,128)(2,1)S(1)} %pad_maximum_fusion.rest_0_), channel_id=1, source_target_pairs={{0,6},{1,7},{2,4},{3,5},{4,2},{5,3},{6,0},{7,1},{8,14},{9,15},{10,... | collective-permute-start | bytes 221192 | tf_op jit(solution)/shard_map/ppermute | solution.py:317
  10.2 0.5 %collective-permute-start.2 = (bf16[12,2,1536]{2,1,0:T(2,128)(2,1)S(1)}, bf16[12,2,1536]{2,1,0:T(2,128)(2,1)S(1)}, u32[]{:S(2)}, u32[]{:S(2)}) collective-permute-start(bf16[12,2,1536]{2,1,0:T(2,128)(2,1)S(1)} %pad_maximum_fusion.rest_0_), channel_id=1, source_target_pairs={{0,2},{1,3},{2,0},{3,1},{4,6},{5,7},{6,4},{7,5},{8,10},{9,11},{10,... | collective-permute-start | bytes 221192 | tf_op jit(solution)/shard_map/ppermute | solution.py:317
  10.7 0.5 %collective-permute-start.1 = (bf16[12,2,1536]{2,1,0:T(2,128)(2,1)S(1)}, bf16[12,2,1536]{2,1,0:T(2,128)(2,1)S(1)}, u32[]{:S(2)}, u32[]{:S(2)}) collective-permute-start(bf16[12,2,1536]{2,1,0:T(2,128)(2,1)S(1)} %pad_maximum_fusion.rest_0_), channel_id=1, source_target_pairs={{0,4},{1,5},{2,6},{3,7},{4,0},{5,1},{6,2},{7,3},{8,12},{9,13},{10,... | collective-permute-start | bytes 221192 | tf_op jit(solution)/shard_map/ppermute | solution.py:317
  11.2 5.2 %prepare.1 = (bf16[1024,1536]{1,0:T(8,128)(2,1)S(1)}, bf16[1024,1536]{1,0:T(8,128)(2,1)S(1)}, bf16[16,1536]{1,0:T(8,128)(2,1)S(1)}, bf16[16,1536]{1,0:T(8,128)(2...) custom-call(s32[2,23]{1,0:T(2,128)S(1)} %add_add_fusion.table_ref, ...), custom_call_target="tpu_custom_call" | custom-call | flops 1610612736 | bytes 12582912 | tf_op jit(solution)/shard_map/prepare/pallas_call | solution.py:132
  16.6 0.1 constant_dynamic-update-slice_fusion.rest_1_
  16.7 0.1 collective-permute-start.5
  16.8 1.5 %collective-permute-done.5.rest_3_ = bf16[36,2,1536]{2,1,0:T(2,128)(2,1)S(1)} collective-permute-done((bf16[36,2,1536]{2,1,0:T(2,128)(2,1)S(1)}, bf16[36,2,1536]{2,1,0:T(2,128)(2,1)S(1)}, u32[]{:S(2)}, u32[]{:S(2)}) %collective-permute-start.5) | collective-permute-done | bytes 221216 | tf_op jit(solution)/shard_map/ppermute | solution.py:317
  18.2 3.2 %attend.1 = (f32[64,1664]{1,0:T(8,128)S(1)}, bf16[64,1664]{1,0:T(8,128)(2,1)S(1)}) custom-call(s32[1,192]{1,0:T(1,128)S(1)} %get-tuple-element.34.target_ref, f32[8,1024]{1,0:T(8,128)S(1)} %get-tuple-element.35.bias_ref, f32[8,16]{1,0:T(8,128)S(1)} %get-tuple-element.36.fresh_bias_ref, bf16[16,1536]{1,0:T(8,128)(2,1)S(1)} %get-tuple-element.37.fresh_key_ref, ...), custom_call_target="tpu_custom_call" | custom-call | flops 805306368 | bytes 6291456 | tf_op jit(solution)/shard_map/attend/pallas_call | solution.py:238
  21.5 0.2 collective-permute-start.6
  21.7 1.3 %collective-permute-done.6.other_ref = bf16[64,1664]{1,0:T(8,128)(2,1)S(1)} collective-permute-done((bf16[64,1664]{1,0:T(8,128)(2,1)S(1)}, bf16[64,1664]{1,0:T(8,128)(2,1)S(1)}, u32[]{:S(2)}, u32[]{:S(2)}) %collective-permute-start.6) | collective-permute-done | bytes 213024 | tf_op jit(solution)/shard_map/ppermute | solution.py:317
  23.0 0.4 %merge_cores.1 = bf16[4,16,1664]{2,1,0:T(8,128)(2,1)S(1)} custom-call(f32[64,1664]{1,0:T(8,128)S(1)} %get-tuple-element.45.keep_ref, bf16[64,1664]{1,0:T(8,128)(2,1)S(1)} %collective-permute-done.6.other_ref), custom_call_target="tpu_custom_call" | custom-call | tf_op jit(solution)/shard_map/merge_cores/pallas_call | solution.py:299
  23.4 9.2 %all_to_all.5.parts_ref = bf16[4,16,1664]{2,1,0:T(8,128)(2,1)S(1)} all-to-all(bf16[4,16,1664]{2,1,0:T(8,128)(2,1)S(1)} %merge_cores.1), channel_id=1, replica_groups={{0,2,4,6},{1,3,5,7},{8,10,12,14},{9,11,13,15},{16,18,20,22},{17,19,21,2..., dimensions={0} | all-to-all | bytes 425984 | tf_op jit(solution)/shard_map/all_to_all | solution.py:338
  32.6 0.3 merge_four.1
  32.9 2.9 %collective-permute-start.7 = (bf16[8,1664]{1,0:T(8,128)(2,1)S(1)}, bf16[8,1664]{1,0:T(8,128)(2,1)S(1)}, u32[]{:S(2)}, u32[]{:S(2)}) collective-permute-start(bf16[8,1664]{1,0:T(8,128)(2,1)S(1)} %get-tuple-element.48), channel_id=1, source_target_pairs={{0,8},{1,9},{2,10},{3,11},{4,12},{5,13},{6,14},{7,15},{8,0},{9,1},... | collective-permute-start | bytes 79880 | tf_op jit(solution)/shard_map/ppermute | solution.py:317
  35.8 1.9 %collective-permute-done.7.other_ref = bf16[8,1664]{1,0:T(8,128)(2,1)S(1)} collective-permute-done((bf16[8,1664]{1,0:T(8,128)(2,1)S(1)}, bf16[8,1664]{1,0:T(8,128)(2,1)S(1)}, u32[]{:S(2)}, u32[]{:S(2)}) %collective-permute-start.7) | collective-permute-done | bytes 26656 | tf_op jit(solution)/shard_map/ppermute | solution.py:317
  37.7 0.8 %merge_two.1 = bf16[2,4,1536]{2,1,0:T(4,128)(2,1)} custom-call(f32[8,1664]{1,0:T(8,128)S(1)} %get-tuple-element.47.keep_ref, bf16[8,1664]{1,0:T(8,128)(2,1)S(1)} %collective-permute-done.7.other_ref), custom_call_target="tpu_custom_call" | custom-call | tf_op jit(solution)/shard_map/merge_two/pallas_call | solution.py:299
  (6 shorter events, 0.1 us)
Async XLA Ops:
  1.1 6.4 %collective-permute-start = (bf16[6,2,1536]{2,1,0:T(2,128)(2,1)S(1)}, bf16[6,2,1536]{2,1,0:T(2,128)(2,1)S(1)}, u32[]{:S(2)}, u32[]{:S(2)}) collective-permute-start(bf16[6,2,1536]{2,1,0:T(2,128)(2,1)S(1)} %get-tuple-element.51), channel_id=1, source_target_pairs={{0,8},{1,9},{2,10},{3,11},{4,12},{5,13},{6,14},{7,15},{8,0},{9,1},... | collective-permute-start | bytes 110600 | tf_op jit(solution)/shard_map/ppermute | solution.py:317
  7.6 8.9 %collective-permute-start.4 = (bf16[12,2,1536]{2,1,0:T(2,128)(2,1)S(1)}, bf16[12,2,1536]{2,1,0:T(2,128)(2,1)S(1)}, u32[]{:S(2)}, u32[]{:S(2)}) collective-permute-start(bf16[12,2,1536]{2,1,0:T(2,128)(2,1)S(1)} %pad_maximum_fusion.rest_0_), channel_id=1, source_target_pairs={{0,1},{1,0},{2,3},{3,2},{4,5},{5,4},{6,7},{7,6},{8,9},{9,8},{10,11... | collective-permute-start | bytes 221192 | tf_op jit(solution)/shard_map/ppermute | solution.py:317
  7.7 8.8 %collective-permute-start.3 = (bf16[12,2,1536]{2,1,0:T(2,128)(2,1)S(1)}, bf16[12,2,1536]{2,1,0:T(2,128)(2,1)S(1)}, u32[]{:S(2)}, u32[]{:S(2)}) collective-permute-start(bf16[12,2,1536]{2,1,0:T(2,128)(2,1)S(1)} %pad_maximum_fusion.rest_0_), channel_id=1, source_target_pairs={{0,6},{1,7},{2,4},{3,5},{4,2},{5,3},{6,0},{7,1},{8,14},{9,15},{10,... | collective-permute-start | bytes 221192 | tf_op jit(solution)/shard_map/ppermute | solution.py:317
  10.2 6.3 %collective-permute-start.2 = (bf16[12,2,1536]{2,1,0:T(2,128)(2,1)S(1)}, bf16[12,2,1536]{2,1,0:T(2,128)(2,1)S(1)}, u32[]{:S(2)}, u32[]{:S(2)}) collective-permute-start(bf16[12,2,1536]{2,1,0:T(2,128)(2,1)S(1)} %pad_maximum_fusion.rest_0_), channel_id=1, source_target_pairs={{0,2},{1,3},{2,0},{3,1},{4,6},{5,7},{6,4},{7,5},{8,10},{9,11},{10,... | collective-permute-start | bytes 221192 | tf_op jit(solution)/shard_map/ppermute | solution.py:317
  10.7 5.8 %collective-permute-start.1 = (bf16[12,2,1536]{2,1,0:T(2,128)(2,1)S(1)}, bf16[12,2,1536]{2,1,0:T(2,128)(2,1)S(1)}, u32[]{:S(2)}, u32[]{:S(2)}) collective-permute-start(bf16[12,2,1536]{2,1,0:T(2,128)(2,1)S(1)} %pad_maximum_fusion.rest_0_), channel_id=1, source_target_pairs={{0,4},{1,5},{2,6},{3,7},{4,0},{5,1},{6,2},{7,3},{8,12},{9,13},{10,... | collective-permute-start | bytes 221192 | tf_op jit(solution)/shard_map/ppermute | solution.py:317
  16.7 1.5 %collective-permute-start.5 = (bf16[36,2,1536]{2,1,0:T(2,128)(2,1)S(1)}, bf16[36,2,1536]{2,1,0:T(2,128)(2,1)S(1)}, u32[]{:S(2)}, u32[]{:S(2)}) collective-permute-start(bf16[36,2,1536]{2,1,0:T(2,128)(2,1)S(1)} %constant_dynamic-update-slice_fusion.rest_1_), channel_id=1, source_target_pairs={{0,1},{1,0},{2,3},{3,2},{4,5},{5,4},{6,7},{7,6},{8,9},{9,8},{10,11... | collective-permute-start | bytes 663560 | tf_op jit(solution)/shard_map/ppermute | solution.py:317
  21.5 1.5 %collective-permute-start.6 = (bf16[64,1664]{1,0:T(8,128)(2,1)S(1)}, bf16[64,1664]{1,0:T(8,128)(2,1)S(1)}, u32[]{:S(2)}, u32[]{:S(2)}) collective-permute-start(bf16[64,1664]{1,0:T(8,128)(2,1)S(1)} %get-tuple-element.46), channel_id=1, source_target_pairs={{0,1},{1,0},{2,3},{3,2},{4,5},{5,4},{6,7},{7,6},{8,9},{9,8},{10,11... | collective-permute-start | bytes 638984 | tf_op jit(solution)/shard_map/ppermute | solution.py:317
  32.9 4.8 %collective-permute-start.7 = (bf16[8,1664]{1,0:T(8,128)(2,1)S(1)}, bf16[8,1664]{1,0:T(8,128)(2,1)S(1)}, u32[]{:S(2)}, u32[]{:S(2)}) collective-permute-start(bf16[8,1664]{1,0:T(8,128)(2,1)S(1)} %get-tuple-element.48), channel_id=1, source_target_pairs={{0,8},{1,9},{2,10},{3,11},{4,12},{5,13},{6,14},{7,15},{8,0},{9,1},... | collective-permute-start | bytes 79880 | tf_op jit(solution)/shard_map/ppermute | solution.py:317

commit v8 on v6

--- a/solution.py
+++ b/solution.py
@@ -15,46 +15,30 @@
 LANES = 128
 PART = 16
 SLOT_BITS = 2
+WAITS = 4
+SORT_VMEM = 48
 VMEM = pl.BlockSpec(memory_space=pltpu.VMEM)
 SMEM = pl.BlockSpec(memory_space=pltpu.SMEM)
 HBM = pl.BlockSpec(memory_space=pltpu.HBM)
 
 
-def mesh_digits(device_count):
-    bits = (device_count // 2).bit_length() - 1
-    far_bits = (bits + 1) // 2
-    return 1 << far_bits, 1 << (bits - far_bits)
-
-
-def place_of(mask, far, near):
-    near_bits = near.bit_length() - 1
-    return ((mask & 1) * near + ((mask >> 1) & (near - 1))) * far + (mask >> (1 + near_bits))
-
-
-def prepare_kernel(table_ref, cache_ref, new_key_ref, new_value_ref,
-                   key_ref, value_ref, fresh_key_ref, fresh_value_ref, target_ref, bias_ref, fresh_bias_ref,
-                   held, sems):
-    tokens, _, width = cache_ref.shape
-    slots = new_key_ref.shape[0]
+def turned(mask, bits):
+    place = 0
+    for n in range(bits):
+        place = place + (((mask >> n) & 1) << (bits - 1 - n))
+    return place
+
+
+def plan_kernel_part(table_ref, slots, target_ref, bias_ref, fresh_bias_ref):
     device_count = table_ref.shape[1] - slots - 1
-    far, near = mesh_digits(device_count)
-    block = min(128, tokens)
-    blocks = tokens // block
-
-    def fetch(i):
-        part = pl.ds(i * block, block)
-        return pltpu.make_async_copy(cache_ref.at[part], held.at[part, :, pl.ds(0, width)], sems.at[i])
-
-    for i in range(blocks):
-        fetch(i).start()
-
+    bits = device_count.bit_length() - 1
     me = table_ref[0, device_count + slots]
     col = lax.broadcasted_iota(jnp.int32, target_ref.shape, 1)
 
     def one_device(dev, carry):
         start0, start1, target = carry
         count0, count1 = table_ref[0, dev], table_ref[1, dev]
-        local = col - place_of(dev ^ me, far, near) * (STEPS * slots)
+        local = col - turned(dev ^ me, bits) * (STEPS * slots)
         slot, step = local >> 1, local & 1
         rank = slot + jnp.where(step == 0, start0, start1)
         home = rank >> SLOT_BITS
@@ -97,54 +81,84 @@
         seen = jnp.where(col == 2 * i + 1, second * live1[i].astype(jnp.int32), seen)
     fresh_bias_ref[...] = jnp.where(seen == 1, 0.0, FAR)
 
+
+def sort_kernel(first, planned, *refs):
+    refs = list(refs)
+    table_ref = refs.pop(0) if planned else None
+    cache_ref = refs.pop(0)
+    new_refs = [refs.pop(0) for _ in range(2)] if planned else []
+    key_ref, value_ref, *small_refs, held, sems = refs
+    tokens, width = key_ref.shape
+    block = min(128, tokens)
+    blocks = tokens // block
+
+    def fetch(i):
+        part = pl.ds(i * block, block)
+        return pltpu.make_async_copy(
+            cache_ref.at[part, :, pl.ds(first, width)], held.at[part, :, pl.ds(0, width)], sems.at[i]
+        )
+
+    for i in range(blocks):
+        fetch(i).start()
+    if planned:
+        slots = new_refs[0].shape[0]
+        for ref, new_ref in zip(small_refs[:2], new_refs):
+            ref[...] = jnp.zeros_like(ref)
+            ref[0:STEPS * slots, :] = new_ref.reshape(STEPS * slots, ref.shape[1])[...]
+        plan_kernel_part(table_ref, slots, *small_refs[2:])
     out = lax.broadcasted_iota(jnp.int32, (2 * block, 2 * block), 0)
     src = lax.broadcasted_iota(jnp.int32, (2 * block, 2 * block), 1)
     order = (src == jnp.where(out < block, 2 * out, 2 * (out - block) + 1)).astype(jnp.bfloat16)
     pairs = held.reshape(2 * tokens, held.shape[2])
     for i in range(blocks):
-        fetch(i).wait()
+        if i % WAITS == 0:
+            for j in range(i, min(i + WAITS, blocks)):
+                fetch(j).wait()
         rows = slice(i * block, (i + 1) * block)
         for c in range(0, width, 256):
             part = pairs[2 * i * block:2 * (i + 1) * block, c:c + 256]
             part = jnp.dot(order, part, preferred_element_type=jnp.float32).astype(jnp.bfloat16)
             key_ref[rows, c:c + 256] = part[:block]
             value_ref[rows, c:c + 256] = part[block:]
-    for ref, new_ref in ((fresh_key_ref, new_key_ref), (fresh_value_ref, new_value_ref)):
-        ref[...] = jnp.zeros_like(ref)
-        ref[0:STEPS * slots, :] = new_ref.reshape(STEPS * slots, width)[...]
-
-
-def prepare(table, cache, fresh_key, fresh_value):
-    tokens, _, width = cache.shape
-    slots = fresh_key.shape[0]
-    device_count = table.shape[1] - slots - 1
-    fresh_rows = -(-STEPS * slots // 16) * 16
+
+
+def sort_cache(cache, first, width, plan, name):
+    tokens, _, full = cache.shape
     f32, bf16 = jnp.float32, jnp.bfloat16
-    shapes = (
-        jax.ShapeDtypeStruct((tokens, width), bf16),
-        jax.ShapeDtypeStruct((tokens, width), bf16),
-        jax.ShapeDtypeStruct((fresh_rows, width), bf16),
-        jax.ShapeDtypeStruct((fresh_rows, width), bf16),
-        jax.ShapeDtypeStruct((1, device_count * STEPS * slots), jnp.int32),
-        jax.ShapeDtypeStruct((PAIR, tokens), f32),
-        jax.ShapeDtypeStruct((PAIR, fresh_rows), f32),
-    )
+    shapes = [jax.ShapeDtypeStruct((tokens, width), bf16)] * 2
+    inputs, specs = [cache], [HBM]
+    if plan:
+        table, fresh_key, fresh_value = plan
+        slots = fresh_key.shape[0]
+        device_count = table.shape[1] - slots - 1
+        fresh_rows = -(-STEPS * slots // 16) * 16
+        shapes += [jax.ShapeDtypeStruct((fresh_rows, full), bf16)] * 2
+        shapes += [
+            jax.ShapeDtypeStruct((1, device_count * STEPS * slots), jnp.int32),
+            jax.ShapeDtypeStruct((PAIR, tokens), f32),
+            jax.ShapeDtypeStruct((PAIR, fresh_rows), f32),
+        ]
+        inputs, specs = [table, cache, fresh_key, fresh_value], [SMEM, HBM, VMEM, VMEM]
+
+    def kernel(*refs):
+        sort_kernel(first, bool(plan), *refs)
+
     blocks = tokens // min(128, tokens)
     return pl.pallas_call(
-        prepare_kernel,
-        out_shape=shapes,
-        in_specs=[SMEM, HBM, VMEM, VMEM],
+        kernel,
+        out_shape=tuple(shapes),
+        in_specs=specs,
         out_specs=(VMEM,) * len(shapes),
         scratch_shapes=[
             pltpu.VMEM((tokens, 2, width + LANES), bf16),
             pltpu.SemaphoreType.DMA((blocks,)),
         ],
-        compiler_params=pltpu.CompilerParams(vmem_limit_bytes=45 << 20),
+        compiler_params=pltpu.CompilerParams(vmem_limit_bytes=SORT_VMEM << 20),
         cost_estimate=pl.CostEstimate(
             flops=8 * 128 * tokens * width, bytes_accessed=8 * tokens * width, transcendentals=0
         ),
-        name="prepare",
-    )(table, cache, fresh_key, fresh_value)
+        name=name,
+    )(*inputs)
 
 
 def two_parts(x):
@@ -170,9 +184,11 @@
     return stats + part(1) + part(2), part(3) + part(4)
 
 
-def attend_kernel(target_ref, bias_ref, fresh_bias_ref, fresh_key_ref, fresh_value_ref, key_ref, value_ref, *rest):
-    gathered_refs, (keep_ref, send_ref) = rest[:-2], rest[-2:]
-    width = key_ref.shape[1]
+def attend_kernel(target_ref, bias_ref, fresh_bias_ref, fresh_key_ref, fresh_value_ref, *rest):
+    key_refs, value_refs, gathered_refs, (keep_ref, send_ref) = rest[0:4:2], rest[1:4:2], rest[4:-2], rest[-2:]
+    width = fresh_key_ref.shape[1]
+    part_heads = key_refs[0].shape[1] // HEAD
+    tokens = key_refs[0].shape[0]
     heads = width // HEAD
     half = keep_ref.shape[0]
     nt = (((1,), (1,)), ((), ()))
@@ -180,25 +196,24 @@
     def attend_rows(base, chunk, stores):
         row = lax.broadcasted_iota(jnp.int32, (chunk, target_ref.shape[1]), 0)
         pick = (row == target_ref[...] - base).astype(jnp.bfloat16)
-        queries, at = None, 0
-        for ref in gathered_refs:
-            count = ref.shape[0] * STEPS
-            slots = ref.reshape(count, width)[...]
-            part = jnp.dot(pick[:, at:at + count], slots, preferred_element_type=jnp.float32)
-            queries = part if queries is None else queries + part
-            at += count
-        queries = queries.astype(jnp.bfloat16)
+        slots = [ref.reshape(ref.shape[0] * STEPS, width)[...].astype(jnp.float32) for ref in gathered_refs]
+        slots = jnp.concatenate(slots).astype(jnp.bfloat16)
+        queries = jnp.dot(pick, slots, preferred_element_type=jnp.float32).astype(jnp.bfloat16)
         bias = bias_ref[...]
         fresh_bias = fresh_bias_ref[...]
         lane = lax.broadcasted_iota(jnp.int32, (chunk, LANES), 1)
         highs = jnp.zeros((chunk, LANES), jnp.float32)
         totals = jnp.zeros((chunk, LANES), jnp.float32)
-        ones = jnp.ones((key_ref.shape[0], LANES), jnp.bfloat16)
+        ones = jnp.ones((tokens, LANES), jnp.bfloat16)
+
+        def block_of(refs, h):
+            at = h % part_heads * HEAD
+            return refs[h // part_heads][:, at:at + HEAD]
 
         def score(h):
             cols = slice(h * HEAD, (h + 1) * HEAD)
             q = queries[:, cols]
-            s = lax.dot_general(q, key_ref[:, cols], nt, preferred_element_type=jnp.float32)
+            s = lax.dot_general(q, block_of(key_refs, h), nt, preferred_element_type=jnp.float32)
             sf = lax.dot_general(q, fresh_key_ref[:, cols], nt, preferred_element_type=jnp.float32)
             s = (s.reshape(chunk // PAIR, PAIR, -1) + bias[None]).reshape(chunk, -1)
             sf = (sf.reshape(chunk // PAIR, PAIR, -1) + fresh_bias[None]).reshape(chunk, -1)
@@ -213,7 +228,7 @@
             high = jnp.maximum(jnp.max(s, axis=1, keepdims=True), jnp.max(sf, axis=1, keepdims=True))
             w = jnp.exp2((s - high) * SCALE).astype(jnp.bfloat16)
             wf = jnp.exp2((sf - high) * SCALE).astype(jnp.bfloat16)
-            value = jnp.concatenate([value_ref[:, cols], ones], axis=1)
+            value = jnp.concatenate([block_of(value_refs, h), ones], axis=1)
             fresh_value = jnp.concatenate([fresh_value_ref[:, cols], ones[:fresh_value_ref.shape[0]]], axis=1)
             o = jnp.dot(w, value, preferred_element_type=jnp.float32)
             o += jnp.dot(wf, fresh_value, preferred_element_type=jnp.float32)
@@ -237,14 +252,14 @@
                 attend_rows(base + to, 128, [(ref, to, 0, 128)])
 
 
-def attend(slots, target, bias, fresh_bias, fresh_key, fresh_value, key, value, gathered):
-    tokens, width = key.shape
+def attend(slots, target, bias, fresh_bias, fresh_key, fresh_value, sorted_parts, gathered):
+    tokens, width = sorted_parts[0].shape[0], fresh_key.shape[1]
     rows = target.shape[1] * SLOT // slots
     shape = (rows // 2, width + LANES)
     return pl.pallas_call(
         attend_kernel,
         out_shape=(jax.ShapeDtypeStruct(shape, jnp.float32), jax.ShapeDtypeStruct(shape, jnp.bfloat16)),
-        in_specs=[VMEM] * (7 + len(gathered)),
+        in_specs=[VMEM] * (5 + len(sorted_parts) + len(gathered)),
         out_specs=(VMEM, VMEM),
         compiler_params=pltpu.CompilerParams(vmem_limit_bytes=24 << 20),
         cost_estimate=pl.CostEstimate(
@@ -252,7 +267,7 @@
             transcendentals=rows * tokens * width // HEAD,
         ),
         name="attend",
-    )(target, bias, fresh_bias, fresh_key, fresh_value, key, value, *gathered)
+    )(target, bias, fresh_bias, fresh_key, fresh_value, *sorted_parts, *gathered)
 
 
 def merged(parts):
@@ -305,7 +320,7 @@
     device_count = lax.axis_size("blk")
     me = lax.axis_index("blk")
     slot_count = list_rows.shape[1]
-    far, near = mesh_digits(device_count)
+    bits = device_count.bit_length() - 1
     width = cache_kv.shape[2]
 
     def swap(x, mask):
@@ -313,15 +328,23 @@
 
     fresh = fresh_qkv.transpose(1, 2, 0, 3)
     mine, fresh_key, fresh_value = (fresh[:, i] for i in range(3))
+    half = width // 2
+    early = sort_cache(cache_kv, 0, half, None, "sort_first")
+    column = mine
+    for n in range(bits - 1, 2, -1):
+        other = swap(column, 1 << n)
+        if n == bits - 1:
+            other, early, counts, list_rows = lax.optimization_barrier((other, early, counts, list_rows))
+        column = jnp.concatenate([column, other])
     table = jnp.concatenate([counts, list_rows, jnp.full((STEPS, 1), me, jnp.int32)], axis=1)
-    ready = prepare(table, cache_kv, fresh_key, fresh_value)
-    plane = [jnp.concatenate([mine] + [swap(mine, k * near * 2) for k in range(1, far)])]
-    across = [swap(plane[0], k * 2) for k in range(1, near)]
-    beside = swap(plane[0], 1)
-    across, ready = lax.optimization_barrier((across, ready))
-    gathered = plane + across + [beside] + [swap(x, 1) for x in across]
-    key, value, fresh_key, fresh_value, target, bias, fresh_bias = ready
-    keep, send = attend(slot_count, target, bias, fresh_bias, fresh_key, fresh_value, key, value, gathered)
+    late = sort_cache(cache_kv, half, half, (table, fresh_key, fresh_value), "sort_second")
+    others = [swap(column, mask) for mask in (4, 2, 6)]
+    beside = swap(column, 1)
+    others, beside, late = lax.optimization_barrier((others, beside, late))
+    others = jnp.concatenate(others)
+    gathered = [column, others, beside, swap(others, 1)]
+    key, value, fresh_key, fresh_value, target, bias, fresh_bias = late
+    keep, send = attend(slot_count, target, bias, fresh_bias, fresh_key, fresh_value, [*early, key, value], gathered)
     chips = device_count // 2
     parts = merge(merge_cores_kernel, [keep, swap(send, 1)], (chips, PAIR, width + LANES), "merge_cores")
     groups = [[chip * 2 + core for chip in range(chips)] for core in range(2)]

time: 38.2 us -> 37.1 us (0.971)
  waiting for transfers between devices: 5.6 us -> 3.12 us
  blocking collectives: 11.8 us -> 13.3 us
  other arithmetic: 0.99 us -> 0.18 us
  Pallas kernels: 10.2 us -> 10.8 us
    ppermute x7, waiting for transfers between devices: 5.6 us -> 3.12 us  [swap(): return lax.ppermute(x, 'blk', [(i, i ^ mask) for i in range(device_count)])]
    all_to_all x1, blocking collectives: 11.8 us -> 13.3 us  [body(): lax.all_to_all(parts, 'blk', split_axis=0, concat_axis=0, axis_index_grou...]
    pallas_call x1 -> x2, Pallas kernels: 5.39 us -> 6.42 us  [sort_cache(): pl.pallas_call(kernel, out_shape=tuple(shapes), in_specs=specs, out_specs...]
    concatenate x1, other arithmetic: 0.77 us -> 0.08 us  [body(): jnp.concatenate([counts, list_rows, jnp.full((STEPS, 1), me, jnp.int32)],...]
    unnamed x1 -> x7, local copies, waits for them, and re-layouts: 0.97 us -> 1.1 us
  transfers between devices with their start and end apart: 7 -> 7, of which waited for: 5 -> 3; matrix products, arithmetic and copies ran while one was open for 2% -> 0% of each run, Pallas kernels for 14% -> 17%
where the time goes in v8:
time: 37.1 us; the launch traced here: 36.9 us
  blocking collectives  13.3 us (36%)
  Pallas kernels  10.8 us (29%)
  starting transfers between devices  8 us (22%)
  waiting for transfers between devices  3.12 us (8%)
  local copies, waits for them, and re-layouts  1.32 us (4%)
    all_to_all x1, blocking collectives, body(): lax.all_to_all(parts, 'blk', split_axis=0, concat_axis=0, axis_index_grou...  13.3 us
    ppermute x7, starting transfers between devices, swap(): return lax.ppermute(x, 'blk', [(i, i ^ mask) for i in range(device_count)])  8 us
    pallas_call x2, Pallas kernels, sort_cache(): pl.pallas_call(kernel, out_shape=tuple(shapes), in_specs=specs, out_specs...  6.42 us
    ppermute x7, waiting for transfers between devices, swap(): return lax.ppermute(x, 'blk', [(i, i ^ mask) for i in range(device_count)])  3.12 us
    pallas_call x1, Pallas kernels, attend(): pl.pallas_call(attend_kernel, out_shape=(jax.ShapeDtypeStruct(shape, jnp....  3.06 us
    pallas_call x2, Pallas kernels, merge(): pl.pallas_call(kernel, out_shape=jax.ShapeDtypeStruct(shape, jnp.bfloat16...  1.36 us
    unnamed x7, local copies, waits for them, and re-layouts  1.1 us
  transfers between devices with their start and end apart: 7, of which 3 were waited for; matrix products, arithmetic and copies ran while one was open for 0% of the time, Pallas kernels for 17%

profile of v8, /device:TPU:0, one launch (start us, length us, event | category | flops | bytes accessed | tf_op | source)
XLA Modules:
  0.0 36.9 jit_solution(5720552024593673030)
XLA Ops:
  0.0 1.0 %copy.7 = bf16[2,6,3,1536]{3,0,1,2:T(2,128)(2,1)S(1)} copy(bf16[2,6,3,1536]{3,0,2,1:T(2,128)(2,1)} %param.5) | data formatting | bytes 221184 | tf_op args[1]
  1.0 0.1 slice_bitcast_fusion
  1.1 4.1 %collective-permute-start = (bf16[6,2,1536]{2,1,0:T(2,128)(2,1)S(1)}, bf16[6,2,1536]{2,1,0:T(2,128)(2,1)S(1)}, u32[]{:S(2)}, u32[]{:S(2)}) collective-permute-start(bf16[6,2,1536]{2,1,0:T(2,128)(2,1)S(1)} %get-tuple-element.61), channel_id=1, source_target_pairs={{0,8},{1,9},{2,10},{3,11},{4,12},{5,13},{6,14},{7,15},{8,0},{9,1},... | collective-permute-start | bytes 110600 | tf_op jit(solution)/shard_map/ppermute | solution.py:327
  5.2 2.9 %sort_first.1 = (bf16[1024,768]{1,0:T(8,128)(2,1)S(1)}, bf16[1024,768]{1,0:T(8,128)(2,1)S(1)}) custom-call(bf16[1024,2,1536]{2,1,0:T(2,128)(2,1)} %refs_1_.1), custom_call_target="tpu_custom_call" | custom-call | flops 805306368 | bytes 6291456 | tf_op jit(solution)/shard_map/sort_first/pallas_call | solution.py:147
  8.1 0.1 pad.2.clone
  8.2 0.1 pad_maximum_fusion.rest_4_
  8.3 0.1 collective-permute-start.4
  8.4 2.6 %collective-permute-start.3 = (bf16[12,2,1536]{2,1,0:T(2,128)(2,1)S(1)}, bf16[12,2,1536]{2,1,0:T(2,128)(2,1)S(1)}, u32[]{:S(2)}, u32[]{:S(2)}) collective-permute-start(bf16[12,2,1536]{2,1,0:T(2,128)(2,1)S(1)} %pad_maximum_fusion.rest_4_), channel_id=1, source_target_pairs={{0,6},{1,7},{2,4},{3,5},{4,2},{5,3},{6,0},{7,1},{8,14},{9,15},{10,... | collective-permute-start | bytes 221192 | tf_op jit(solution)/shard_map/ppermute | solution.py:327
  11.0 0.5 %collective-permute-start.2 = (bf16[12,2,1536]{2,1,0:T(2,128)(2,1)S(1)}, bf16[12,2,1536]{2,1,0:T(2,128)(2,1)S(1)}, u32[]{:S(2)}, u32[]{:S(2)}) collective-permute-start(bf16[12,2,1536]{2,1,0:T(2,128)(2,1)S(1)} %pad_maximum_fusion.rest_4_), channel_id=1, source_target_pairs={{0,2},{1,3},{2,0},{3,1},{4,6},{5,7},{6,4},{7,5},{8,10},{9,11},{10,... | collective-permute-start | bytes 221192 | tf_op jit(solution)/shard_map/ppermute | solution.py:327
  11.5 0.4 %collective-permute-start.1 = (bf16[12,2,1536]{2,1,0:T(2,128)(2,1)S(1)}, bf16[12,2,1536]{2,1,0:T(2,128)(2,1)S(1)}, u32[]{:S(2)}, u32[]{:S(2)}) collective-permute-start(bf16[12,2,1536]{2,1,0:T(2,128)(2,1)S(1)} %pad_maximum_fusion.rest_4_), channel_id=1, source_target_pairs={{0,4},{1,5},{2,6},{3,7},{4,0},{5,1},{6,2},{7,3},{8,12},{9,13},{10,... | collective-permute-start | bytes 221192 | tf_op jit(solution)/shard_map/ppermute | solution.py:327
  12.0 0.1 add_add_fusion.refs_0_
  12.0 3.5 %sort_second.1 = (bf16[1024,768]{1,0:T(8,128)(2,1)S(1)}, bf16[1024,768]{1,0:T(8,128)(2,1)S(1)}, bf16[16,1536]{1,0:T(8,128)(2,1)S(1)}, bf16[16,1536]{1,0:T(8,128)...) custom-call(s32[2,23]{1,0:T(2,128)S(1)} %add_add_fusion.refs_0_, ...), custom_call_target="tpu_custom_call" | custom-call | flops 805306368 | bytes 6291456 | tf_op jit(solution)/shard_map/sort_second/pallas_call | solution.py:147
  15.6 0.3 collective-permute-done.1
  15.9 0.1 constant_dynamic-update-slice_fusion.2
  15.9 0.1 constant_dynamic-update-slice_fusion.1
  16.0 0.1 constant_dynamic-update-slice_fusion.rest_5_
  16.1 0.1 collective-permute-start.5
  16.1 1.5 %collective-permute-done.5.rest_7_ = bf16[36,2,1536]{2,1,0:T(2,128)(2,1)S(1)} collective-permute-done((bf16[36,2,1536]{2,1,0:T(2,128)(2,1)S(1)}, bf16[36,2,1536]{2,1,0:T(2,128)(2,1)S(1)}, u32[]{:S(2)}, u32[]{:S(2)}) %collective-permute-start.5) | collective-permute-done | bytes 221216 | tf_op jit(solution)/shard_map/ppermute | solution.py:327
  17.6 3.1 %attend.1 = (f32[64,1664]{1,0:T(8,128)S(1)}, bf16[64,1664]{1,0:T(8,128)(2,1)S(1)}) custom-call(s32[1,192]{1,0:T(1,128)S(1)} %get-tuple-element.44.target_ref, f32[8,1024]{1,0:T(8,128)S(1)} %get-tuple-element.45.bias_ref, f32[8,16]{1,0:T(8,128)S(1)} %get-tuple-element.46.fresh_bias_ref, bf16[16,1536]{1,0:T(8,128)(2,1)S(1)} %get-tuple-element.47.fresh_key_ref, ...), custom_call_target="tpu_custom_call" | custom-call | flops 805306368 | bytes 6291456 | tf_op jit(solution)/shard_map/attend/pallas_call | solution.py:259
  20.7 0.2 collective-permute-start.6
  20.9 1.3 %collective-permute-done.6.other_ref = bf16[64,1664]{1,0:T(8,128)(2,1)S(1)} collective-permute-done((bf16[64,1664]{1,0:T(8,128)(2,1)S(1)}, bf16[64,1664]{1,0:T(8,128)(2,1)S(1)}, u32[]{:S(2)}, u32[]{:S(2)}) %collective-permute-start.6) | collective-permute-done | bytes 213024 | tf_op jit(solution)/shard_map/ppermute | solution.py:327
  22.2 0.4 %merge_cores.1 = bf16[8,8,1664]{2,1,0:T(8,128)(2,1)S(1)} custom-call(f32[64,1664]{1,0:T(8,128)S(1)} %get-tuple-element.57.keep_ref, bf16[64,1664]{1,0:T(8,128)(2,1)S(1)} %collective-permute-done.6.other_ref), custom_call_target="tpu_custom_call" | custom-call | tf_op jit(solution)/shard_map/merge_cores/pallas_call | solution.py:309
  22.7 13.3 %all_to_all.5.parts_ref = bf16[8,8,1664]{2,1,0:T(8,128)(2,1)S(1)} all-to-all(bf16[8,8,1664]{2,1,0:T(8,128)(2,1)S(1)} %merge_cores.1), channel_id=1, replica_groups={{0,2,4,6,8,10,12,14},{1,3,5,7,9,11,13,15},{16,18,20,22,24,26,28,30},{17..., dimensions={0} | all-to-all | bytes 425984 | tf_op jit(solution)/shard_map/all_to_all | solution.py:351
  36.0 0.9 %merge_chips.1 = bf16[2,4,1536]{2,1,0:T(4,128)(2,1)} custom-call(bf16[8,8,1664]{2,1,0:T(8,128)(2,1)S(1)} %all_to_all.5.parts_ref), custom_call_target="tpu_custom_call" | custom-call | tf_op jit(solution)/shard_map/merge_chips/pallas_call | solution.py:309
  (8 shorter events, 0.0 us)
Async XLA Ops:
  1.1 10.9 %copy-start = (s32[2,6]{1,0:T(2,128)S(1)}, s32[2,6]{1,0:T(2,128)}, u32[]{:S(2)}) copy-start(s32[2,6]{1,0:T(2,128)} %param.6) | copy-start | bytes 148
  1.1 10.9 %copy-start.1 = (s32[2,16]{1,0:T(2,128)S(1)}, s32[2,16]{1,0:T(2,128)}, u32[]{:S(2)}) copy-start(s32[2,16]{1,0:T(2,128)} %param.7) | copy-start | bytes 388
  1.1 7.1 %collective-permute-start = (bf16[6,2,1536]{2,1,0:T(2,128)(2,1)S(1)}, bf16[6,2,1536]{2,1,0:T(2,128)(2,1)S(1)}, u32[]{:S(2)}, u32[]{:S(2)}) collective-permute-start(bf16[6,2,1536]{2,1,0:T(2,128)(2,1)S(1)} %get-tuple-element.61), channel_id=1, source_target_pairs={{0,8},{1,9},{2,10},{3,11},{4,12},{5,13},{6,14},{7,15},{8,0},{9,1},... | collective-permute-start | bytes 110600 | tf_op jit(solution)/shard_map/ppermute | solution.py:327
  8.3 7.2 %collective-permute-start.4 = (bf16[12,2,1536]{2,1,0:T(2,128)(2,1)S(1)}, bf16[12,2,1536]{2,1,0:T(2,128)(2,1)S(1)}, u32[]{:S(2)}, u32[]{:S(2)}) collective-permute-start(bf16[12,2,1536]{2,1,0:T(2,128)(2,1)S(1)} %pad_maximum_fusion.rest_4_), channel_id=1, source_target_pairs={{0,1},{1,0},{2,3},{3,2},{4,5},{5,4},{6,7},{7,6},{8,9},{9,8},{10,11... | collective-permute-start | bytes 221192 | tf_op jit(solution)/shard_map/ppermute | solution.py:327
  8.4 7.1 %collective-permute-start.3 = (bf16[12,2,1536]{2,1,0:T(2,128)(2,1)S(1)}, bf16[12,2,1536]{2,1,0:T(2,128)(2,1)S(1)}, u32[]{:S(2)}, u32[]{:S(2)}) collective-permute-start(bf16[12,2,1536]{2,1,0:T(2,128)(2,1)S(1)} %pad_maximum_fusion.rest_4_), channel_id=1, source_target_pairs={{0,6},{1,7},{2,4},{3,5},{4,2},{5,3},{6,0},{7,1},{8,14},{9,15},{10,... | collective-permute-start | bytes 221192 | tf_op jit(solution)/shard_map/ppermute | solution.py:327
  11.0 4.6 %collective-permute-start.2 = (bf16[12,2,1536]{2,1,0:T(2,128)(2,1)S(1)}, bf16[12,2,1536]{2,1,0:T(2,128)(2,1)S(1)}, u32[]{:S(2)}, u32[]{:S(2)}) collective-permute-start(bf16[12,2,1536]{2,1,0:T(2,128)(2,1)S(1)} %pad_maximum_fusion.rest_4_), channel_id=1, source_target_pairs={{0,2},{1,3},{2,0},{3,1},{4,6},{5,7},{6,4},{7,5},{8,10},{9,11},{10,... | collective-permute-start | bytes 221192 | tf_op jit(solution)/shard_map/ppermute | solution.py:327
  11.5 4.4 %collective-permute-start.1 = (bf16[12,2,1536]{2,1,0:T(2,128)(2,1)S(1)}, bf16[12,2,1536]{2,1,0:T(2,128)(2,1)S(1)}, u32[]{:S(2)}, u32[]{:S(2)}) collective-permute-start(bf16[12,2,1536]{2,1,0:T(2,128)(2,1)S(1)} %pad_maximum_fusion.rest_4_), channel_id=1, source_target_pairs={{0,4},{1,5},{2,6},{3,7},{4,0},{5,1},{6,2},{7,3},{8,12},{9,13},{10,... | collective-permute-start | bytes 221192 | tf_op jit(solution)/shard_map/ppermute | solution.py:327
  16.1 1.5 %collective-permute-start.5 = (bf16[36,2,1536]{2,1,0:T(2,128)(2,1)S(1)}, bf16[36,2,1536]{2,1,0:T(2,128)(2,1)S(1)}, u32[]{:S(2)}, u32[]{:S(2)}) collective-permute-start(bf16[36,2,1536]{2,1,0:T(2,128)(2,1)S(1)} %constant_dynamic-update-slice_fusion.rest_5_), channel_id=1, source_target_pairs={{0,1},{1,0},{2,3},{3,2},{4,5},{5,4},{6,7},{7,6},{8,9},{9,8},{10,11... | collective-permute-start | bytes 663560 | tf_op jit(solution)/shard_map/ppermute | solution.py:327
  20.7 1.5 %collective-permute-start.6 = (bf16[64,1664]{1,0:T(8,128)(2,1)S(1)}, bf16[64,1664]{1,0:T(8,128)(2,1)S(1)}, u32[]{:S(2)}, u32[]{:S(2)}) collective-permute-start(bf16[64,1664]{1,0:T(8,128)(2,1)S(1)} %get-tuple-element.58), channel_id=1, source_target_pairs={{0,1},{1,0},{2,3},{3,2},{4,5},{5,4},{6,7},{7,6},{8,9},{9,8},{10,11... | collective-permute-start | bytes 638984 | tf_op jit(solution)/shard_map/ppermute | solution.py:327

commit v9 on v8

--- a/solution.py
+++ b/solution.py
@@ -339,8 +339,8 @@
     table = jnp.concatenate([counts, list_rows, jnp.full((STEPS, 1), me, jnp.int32)], axis=1)
     late = sort_cache(cache_kv, half, half, (table, fresh_key, fresh_value), "sort_second")
     others = [swap(column, mask) for mask in (4, 2, 6)]
+    others, column, late = lax.optimization_barrier((others, column, late))
     beside = swap(column, 1)
-    others, beside, late = lax.optimization_barrier((others, beside, late))
     others = jnp.concatenate(others)
     gathered = [column, others, beside, swap(others, 1)]
     key, value, fresh_key, fresh_value, target, bias, fresh_bias = late

time: 37.1 us -> 37.2 us (level)
  starting transfers between devices: 8 us -> 8.48 us
  waiting for transfers between devices: 3.12 us -> 2.69 us
    ppermute x7, starting transfers between devices: 8 us -> 8.48 us  [swap(): return lax.ppermute(x, 'blk', [(i, i ^ mask) for i in range(device_count)])]
    ppermute x7, waiting for transfers between devices: 3.12 us -> 2.69 us  [swap(): return lax.ppermute(x, 'blk', [(i, i ^ mask) for i in range(device_count)])]
where the time goes in v9:
time: 37.2 us; the launch traced here: 37 us
  blocking collectives  13.4 us (36%)
  Pallas kernels  10.8 us (29%)
  starting transfers between devices  8.48 us (23%)
  waiting for transfers between devices  2.69 us (7%)
  local copies, waits for them, and re-layouts  1.32 us (4%)
    all_to_all x1, blocking collectives, body(): lax.all_to_all(parts, 'blk', split_axis=0, concat_axis=0, axis_index_grou...  13.4 us
    ppermute x7, starting transfers between devices, swap(): return lax.ppermute(x, 'blk', [(i, i ^ mask) for i in range(device_count)])  8.48 us
    pallas_call x2, Pallas kernels, sort_cache(): pl.pallas_call(kernel, out_shape=tuple(shapes), in_specs=specs, out_specs...  6.4 us
    pallas_call x1, Pallas kernels, attend(): pl.pallas_call(attend_kernel, out_shape=(jax.ShapeDtypeStruct(shape, jnp....  3.06 us
    ppermute x7, waiting for transfers between devices, swap(): return lax.ppermute(x, 'blk', [(i, i ^ mask) for i in range(device_count)])  2.69 us
    pallas_call x2, Pallas kernels, merge(): pl.pallas_call(kernel, out_shape=jax.ShapeDtypeStruct(shape, jnp.bfloat16...  1.36 us
    unnamed x7, local copies, waits for them, and re-layouts  1.1 us
  transfers between devices with their start and end apart: 7, of which 3 were waited for; matrix products, arithmetic and copies ran while one was open for 0% of the time, Pallas kernels for 17%

profile of v9, /device:TPU:0, one launch (start us, length us, event | category | flops | bytes accessed | tf_op | source)
XLA Modules:
  0.0 37.0 jit_solution(3770555019934652018)
XLA Ops:
  0.0 1.0 %copy.7 = bf16[2,6,3,1536]{3,0,1,2:T(2,128)(2,1)S(1)} copy(bf16[2,6,3,1536]{3,0,2,1:T(2,128)(2,1)} %param.5) | data formatting | bytes 221184 | tf_op args[1]
  1.0 0.1 slice_bitcast_fusion
  1.1 4.1 %collective-permute-start = (bf16[6,2,1536]{2,1,0:T(2,128)(2,1)S(1)}, bf16[6,2,1536]{2,1,0:T(2,128)(2,1)S(1)}, u32[]{:S(2)}, u32[]{:S(2)}) collective-permute-start(bf16[6,2,1536]{2,1,0:T(2,128)(2,1)S(1)} %get-tuple-element.61), channel_id=1, source_target_pairs={{0,8},{1,9},{2,10},{3,11},{4,12},{5,13},{6,14},{7,15},{8,0},{9,1},... | collective-permute-start | bytes 110600 | tf_op jit(solution)/shard_map/ppermute | solution.py:327
  5.2 2.9 %sort_first.1 = (bf16[1024,768]{1,0:T(8,128)(2,1)S(1)}, bf16[1024,768]{1,0:T(8,128)(2,1)S(1)}) custom-call(bf16[1024,2,1536]{2,1,0:T(2,128)(2,1)} %refs_1_.1), custom_call_target="tpu_custom_call" | custom-call | flops 805306368 | bytes 6291456 | tf_op jit(solution)/shard_map/sort_first/pallas_call | solution.py:147
  8.1 0.1 pad.2.clone
  8.2 0.1 pad_maximum_fusion.rest_4_
  8.3 2.6 %collective-permute-start.3 = (bf16[12,2,1536]{2,1,0:T(2,128)(2,1)S(1)}, bf16[12,2,1536]{2,1,0:T(2,128)(2,1)S(1)}, u32[]{:S(2)}, u32[]{:S(2)}) collective-permute-start(bf16[12,2,1536]{2,1,0:T(2,128)(2,1)S(1)} %pad_maximum_fusion.rest_4_), channel_id=1, source_target_pairs={{0,6},{1,7},{2,4},{3,5},{4,2},{5,3},{6,0},{7,1},{8,14},{9,15},{10,... | collective-permute-start | bytes 221192 | tf_op jit(solution)/shard_map/ppermute | solution.py:327
  10.9 0.5 %collective-permute-start.2 = (bf16[12,2,1536]{2,1,0:T(2,128)(2,1)S(1)}, bf16[12,2,1536]{2,1,0:T(2,128)(2,1)S(1)}, u32[]{:S(2)}, u32[]{:S(2)}) collective-permute-start(bf16[12,2,1536]{2,1,0:T(2,128)(2,1)S(1)} %pad_maximum_fusion.rest_4_), channel_id=1, source_target_pairs={{0,2},{1,3},{2,0},{3,1},{4,6},{5,7},{6,4},{7,5},{8,10},{9,11},{10,... | collective-permute-start | bytes 221192 | tf_op jit(solution)/shard_map/ppermute | solution.py:327
  11.4 0.4 %collective-permute-start.1 = (bf16[12,2,1536]{2,1,0:T(2,128)(2,1)S(1)}, bf16[12,2,1536]{2,1,0:T(2,128)(2,1)S(1)}, u32[]{:S(2)}, u32[]{:S(2)}) collective-permute-start(bf16[12,2,1536]{2,1,0:T(2,128)(2,1)S(1)} %pad_maximum_fusion.rest_4_), channel_id=1, source_target_pairs={{0,4},{1,5},{2,6},{3,7},{4,0},{5,1},{6,2},{7,3},{8,12},{9,13},{10,... | collective-permute-start | bytes 221192 | tf_op jit(solution)/shard_map/ppermute | solution.py:327
  11.9 0.1 add_add_fusion.refs_0_
  12.0 3.5 %sort_second.1 = (bf16[1024,768]{1,0:T(8,128)(2,1)S(1)}, bf16[1024,768]{1,0:T(8,128)(2,1)S(1)}, bf16[16,1536]{1,0:T(8,128)(2,1)S(1)}, bf16[16,1536]{1,0:T(8,128)...) custom-call(s32[2,23]{1,0:T(2,128)S(1)} %add_add_fusion.refs_0_, ...), custom_call_target="tpu_custom_call" | custom-call | flops 805306368 | bytes 6291456 | tf_op jit(solution)/shard_map/sort_second/pallas_call | solution.py:147
  15.5 0.3 collective-permute-done.1
  15.8 0.1 constant_dynamic-update-slice_fusion.2
  15.8 0.1 constant_dynamic-update-slice_fusion.1
  15.9 0.1 constant_dynamic-update-slice_fusion.rest_5_
  16.0 0.1 collective-permute-start.5
  16.1 0.5 %collective-permute-start.4 = (bf16[12,2,1536]{2,1,0:T(2,128)(2,1)S(1)}, bf16[12,2,1536]{2,1,0:T(2,128)(2,1)S(1)}, u32[]{:S(2)}, u32[]{:S(2)}) collective-permute-start(bf16[12,2,1536]{2,1,0:T(2,128)(2,1)S(1)} %pad_maximum_fusion.rest_4_), channel_id=1, source_target_pairs={{0,1},{1,0},{2,3},{3,2},{4,5},{5,4},{6,7},{7,6},{8,9},{9,8},{10,11... | collective-permute-start | bytes 221192 | tf_op jit(solution)/shard_map/ppermute | solution.py:327
  16.6 1.1 %collective-permute-done.4.rest_6_ = bf16[12,2,1536]{2,1,0:T(2,128)(2,1)S(1)} collective-permute-done((bf16[12,2,1536]{2,1,0:T(2,128)(2,1)S(1)}, bf16[12,2,1536]{2,1,0:T(2,128)(2,1)S(1)}, u32[]{:S(2)}, u32[]{:S(2)}) %collective-permute-start.4) | collective-permute-done | bytes 73760 | tf_op jit(solution)/shard_map/ppermute | solution.py:327
  17.6 3.1 %attend.1 = (f32[64,1664]{1,0:T(8,128)S(1)}, bf16[64,1664]{1,0:T(8,128)(2,1)S(1)}) custom-call(s32[1,192]{1,0:T(1,128)S(1)} %get-tuple-element.44.target_ref, f32[8,1024]{1,0:T(8,128)S(1)} %get-tuple-element.45.bias_ref, f32[8,16]{1,0:T(8,128)S(1)} %get-tuple-element.46.fresh_bias_ref, bf16[16,1536]{1,0:T(8,128)(2,1)S(1)} %get-tuple-element.47.fresh_key_ref, ...), custom_call_target="tpu_custom_call" | custom-call | flops 805306368 | bytes 6291456 | tf_op jit(solution)/shard_map/attend/pallas_call | solution.py:259
  20.7 0.3 collective-permute-start.6
  21.0 1.3 %collective-permute-done.6.other_ref = bf16[64,1664]{1,0:T(8,128)(2,1)S(1)} collective-permute-done((bf16[64,1664]{1,0:T(8,128)(2,1)S(1)}, bf16[64,1664]{1,0:T(8,128)(2,1)S(1)}, u32[]{:S(2)}, u32[]{:S(2)}) %collective-permute-start.6) | collective-permute-done | bytes 213024 | tf_op jit(solution)/shard_map/ppermute | solution.py:327
  22.2 0.4 %merge_cores.1 = bf16[8,8,1664]{2,1,0:T(8,128)(2,1)S(1)} custom-call(f32[64,1664]{1,0:T(8,128)S(1)} %get-tuple-element.57.keep_ref, bf16[64,1664]{1,0:T(8,128)(2,1)S(1)} %collective-permute-done.6.other_ref), custom_call_target="tpu_custom_call" | custom-call | tf_op jit(solution)/shard_map/merge_cores/pallas_call | solution.py:309
  22.7 13.4 %all_to_all.5.parts_ref = bf16[8,8,1664]{2,1,0:T(8,128)(2,1)S(1)} all-to-all(bf16[8,8,1664]{2,1,0:T(8,128)(2,1)S(1)} %merge_cores.1), channel_id=1, replica_groups={{0,2,4,6,8,10,12,14},{1,3,5,7,9,11,13,15},{16,18,20,22,24,26,28,30},{17..., dimensions={0} | all-to-all | bytes 425984 | tf_op jit(solution)/shard_map/all_to_all | solution.py:351
  36.1 0.9 %merge_chips.1 = bf16[2,4,1536]{2,1,0:T(4,128)(2,1)} custom-call(bf16[8,8,1664]{2,1,0:T(8,128)(2,1)S(1)} %all_to_all.5.parts_ref), custom_call_target="tpu_custom_call" | custom-call | tf_op jit(solution)/shard_map/merge_chips/pallas_call | solution.py:309
  (8 shorter events, 0.0 us)
Async XLA Ops:
  1.1 10.8 %copy-start = (s32[2,6]{1,0:T(2,128)S(1)}, s32[2,6]{1,0:T(2,128)}, u32[]{:S(2)}) copy-start(s32[2,6]{1,0:T(2,128)} %param.6) | copy-start | bytes 148
  1.1 10.8 %copy-start.1 = (s32[2,16]{1,0:T(2,128)S(1)}, s32[2,16]{1,0:T(2,128)}, u32[]{:S(2)}) copy-start(s32[2,16]{1,0:T(2,128)} %param.7) | copy-start | bytes 388
  1.1 7.1 %collective-permute-start = (bf16[6,2,1536]{2,1,0:T(2,128)(2,1)S(1)}, bf16[6,2,1536]{2,1,0:T(2,128)(2,1)S(1)}, u32[]{:S(2)}, u32[]{:S(2)}) collective-permute-start(bf16[6,2,1536]{2,1,0:T(2,128)(2,1)S(1)} %get-tuple-element.61), channel_id=1, source_target_pairs={{0,8},{1,9},{2,10},{3,11},{4,12},{5,13},{6,14},{7,15},{8,0},{9,1},... | collective-permute-start | bytes 110600 | tf_op jit(solution)/shard_map/ppermute | solution.py:327
  8.3 7.1 %collective-permute-start.3 = (bf16[12,2,1536]{2,1,0:T(2,128)(2,1)S(1)}, bf16[12,2,1536]{2,1,0:T(2,128)(2,1)S(1)}, u32[]{:S(2)}, u32[]{:S(2)}) collective-permute-start(bf16[12,2,1536]{2,1,0:T(2,128)(2,1)S(1)} %pad_maximum_fusion.rest_4_), channel_id=1, source_target_pairs={{0,6},{1,7},{2,4},{3,5},{4,2},{5,3},{6,0},{7,1},{8,14},{9,15},{10,... | collective-permute-start | bytes 221192 | tf_op jit(solution)/shard_map/ppermute | solution.py:327
  10.9 4.5 %collective-permute-start.2 = (bf16[12,2,1536]{2,1,0:T(2,128)(2,1)S(1)}, bf16[12,2,1536]{2,1,0:T(2,128)(2,1)S(1)}, u32[]{:S(2)}, u32[]{:S(2)}) collective-permute-start(bf16[12,2,1536]{2,1,0:T(2,128)(2,1)S(1)} %pad_maximum_fusion.rest_4_), channel_id=1, source_target_pairs={{0,2},{1,3},{2,0},{3,1},{4,6},{5,7},{6,4},{7,5},{8,10},{9,11},{10,... | collective-permute-start | bytes 221192 | tf_op jit(solution)/shard_map/ppermute | solution.py:327
  11.4 4.4 %collective-permute-start.1 = (bf16[12,2,1536]{2,1,0:T(2,128)(2,1)S(1)}, bf16[12,2,1536]{2,1,0:T(2,128)(2,1)S(1)}, u32[]{:S(2)}, u32[]{:S(2)}) collective-permute-start(bf16[12,2,1536]{2,1,0:T(2,128)(2,1)S(1)} %pad_maximum_fusion.rest_4_), channel_id=1, source_target_pairs={{0,4},{1,5},{2,6},{3,7},{4,0},{5,1},{6,2},{7,3},{8,12},{9,13},{10,... | collective-permute-start | bytes 221192 | tf_op jit(solution)/shard_map/ppermute | solution.py:327
  16.0 1.7 %collective-permute-start.5 = (bf16[36,2,1536]{2,1,0:T(2,128)(2,1)S(1)}, bf16[36,2,1536]{2,1,0:T(2,128)(2,1)S(1)}, u32[]{:S(2)}, u32[]{:S(2)}) collective-permute-start(bf16[36,2,1536]{2,1,0:T(2,128)(2,1)S(1)} %constant_dynamic-update-slice_fusion.rest_5_), channel_id=1, source_target_pairs={{0,1},{1,0},{2,3},{3,2},{4,5},{5,4},{6,7},{7,6},{8,9},{9,8},{10,11... | collective-permute-start | bytes 663560 | tf_op jit(solution)/shard_map/ppermute | solution.py:327
  16.1 1.6 %collective-permute-start.4 = (bf16[12,2,1536]{2,1,0:T(2,128)(2,1)S(1)}, bf16[12,2,1536]{2,1,0:T(2,128)(2,1)S(1)}, u32[]{:S(2)}, u32[]{:S(2)}) collective-permute-start(bf16[12,2,1536]{2,1,0:T(2,128)(2,1)S(1)} %pad_maximum_fusion.rest_4_), channel_id=1, source_target_pairs={{0,1},{1,0},{2,3},{3,2},{4,5},{5,4},{6,7},{7,6},{8,9},{9,8},{10,11... | collective-permute-start | bytes 221192 | tf_op jit(solution)/shard_map/ppermute | solution.py:327
  20.7 1.5 %collective-permute-start.6 = (bf16[64,1664]{1,0:T(8,128)(2,1)S(1)}, bf16[64,1664]{1,0:T(8,128)(2,1)S(1)}, u32[]{:S(2)}, u32[]{:S(2)}) collective-permute-start(bf16[64,1664]{1,0:T(8,128)(2,1)S(1)} %get-tuple-element.58), channel_id=1, source_target_pairs={{0,1},{1,0},{2,3},{3,2},{4,5},{5,4},{6,7},{7,6},{8,9},{9,8},{10,11... | collective-permute-start | bytes 638984 | tf_op jit(solution)/shard_map/ppermute | solution.py:327

commit v10 on v9

--- a/solution.py
+++ b/solution.py
@@ -22,11 +22,16 @@
 HBM = pl.BlockSpec(memory_space=pltpu.HBM)
 
 
-def turned(mask, bits):
-    place = 0
-    for n in range(bits):
-        place = place + (((mask >> n) & 1) << (bits - 1 - n))
-    return place
+def exchange_order(bits):
+    first = list(range(bits - 1, 0, -1))
+    return first, first[:-3] + [first[-2], first[-1], first[-3]]
+
+
+def place_of(dev, me, bits):
+    mask = dev ^ me
+    first, second = exchange_order(bits)
+    places = [sum(((mask >> n) & 1) << e for e, n in enumerate(order)) for order in (first, second)]
+    return jnp.where((dev & 1) == 1, places[1], places[0]) + ((mask & 1) << (bits - 1))
 
 
 def plan_kernel_part(table_ref, slots, target_ref, bias_ref, fresh_bias_ref):
@@ -38,7 +43,7 @@
     def one_device(dev, carry):
         start0, start1, target = carry
         count0, count1 = table_ref[0, dev], table_ref[1, dev]
-        local = col - turned(dev ^ me, bits) * (STEPS * slots)
+        local = col - place_of(dev, me, bits) * (STEPS * slots)
         slot, step = local >> 1, local & 1
         rank = slot + jnp.where(step == 0, start0, start1)
         home = rank >> SLOT_BITS
@@ -323,22 +328,24 @@
     bits = device_count.bit_length() - 1
     width = cache_kv.shape[2]
 
-    def swap(x, mask):
-        return lax.ppermute(x, "blk", [(i, i ^ mask) for i in range(device_count)])
+    def swap(x, *masks):
+        return lax.ppermute(x, "blk", [(i, i ^ masks[i % len(masks)]) for i in range(device_count)])
 
     fresh = fresh_qkv.transpose(1, 2, 0, 3)
     mine, fresh_key, fresh_value = (fresh[:, i] for i in range(3))
     half = width // 2
     early = sort_cache(cache_kv, 0, half, None, "sort_first")
     column = mine
-    for n in range(bits - 1, 2, -1):
-        other = swap(column, 1 << n)
-        if n == bits - 1:
+    steps = [(1 << m, 1 << n) for m, n in zip(*exchange_order(bits))]
+    for e, masks in enumerate(steps[:-2]):
+        other = swap(column, *masks)
+        if e == 0:
             other, early, counts, list_rows = lax.optimization_barrier((other, early, counts, list_rows))
         column = jnp.concatenate([column, other])
     table = jnp.concatenate([counts, list_rows, jnp.full((STEPS, 1), me, jnp.int32)], axis=1)
     late = sort_cache(cache_kv, half, half, (table, fresh_key, fresh_value), "sort_second")
-    others = [swap(column, mask) for mask in (4, 2, 6)]
+    both = [m | n for m, n in zip(*steps[-2:])]
+    others = [swap(column, *masks) for masks in (*steps[-2:], both)]
     others, column, late = lax.optimization_barrier((others, column, late))
     beside = swap(column, 1)
     others = jnp.concatenate(others)

time: 37.2 us -> 37.2 us (level)
  no operation moved by 1% of the time
where the time goes in v10:
time: 37.2 us; the launch traced here: 37 us
  blocking collectives  13.2 us (35%)
  Pallas kernels  10.8 us (29%)
  starting transfers between devices  8.48 us (23%)
  waiting for transfers between devices  2.86 us (8%)
  local copies, waits for them, and re-layouts  1.32 us (4%)
    all_to_all x1, blocking collectives, body(): lax.all_to_all(parts, 'blk', split_axis=0, concat_axis=0, axis_index_grou...  13.2 us
    ppermute x7, starting transfers between devices, swap(): lax.ppermute(x, 'blk', [(i, i ^ masks[i % len(masks)]) for i in range(dev...  8.48 us
    pallas_call x2, Pallas kernels, sort_cache(): pl.pallas_call(kernel, out_shape=tuple(shapes), in_specs=specs, out_specs...  6.4 us
    pallas_call x1, Pallas kernels, attend(): pl.pallas_call(attend_kernel, out_shape=(jax.ShapeDtypeStruct(shape, jnp....  3.07 us
    ppermute x7, waiting for transfers between devices, swap(): lax.ppermute(x, 'blk', [(i, i ^ masks[i % len(masks)]) for i in range(dev...  2.86 us
    pallas_call x2, Pallas kernels, merge(): pl.pallas_call(kernel, out_shape=jax.ShapeDtypeStruct(shape, jnp.bfloat16...  1.36 us
    unnamed x7, local copies, waits for them, and re-layouts  1.1 us
  transfers between devices with their start and end apart: 7, of which 3 were waited for; matrix products, arithmetic and copies ran while one was open for 0% of the time, Pallas kernels for 17%

profile of v10, /device:TPU:0, one launch (start us, length us, event | category | flops | bytes accessed | tf_op | source)
XLA Modules:
  0.0 37.0 jit_solution(7533795486595202731)
XLA Ops:
  0.0 1.0 %copy.7 = bf16[2,6,3,1536]{3,0,1,2:T(2,128)(2,1)S(1)} copy(bf16[2,6,3,1536]{3,0,2,1:T(2,128)(2,1)} %param.5) | data formatting | bytes 221184 | tf_op args[1]
  1.0 0.1 slice_bitcast_fusion
  1.1 4.1 %collective-permute-start = (bf16[6,2,1536]{2,1,0:T(2,128)(2,1)S(1)}, bf16[6,2,1536]{2,1,0:T(2,128)(2,1)S(1)}, u32[]{:S(2)}, u32[]{:S(2)}) collective-permute-start(bf16[6,2,1536]{2,1,0:T(2,128)(2,1)S(1)} %get-tuple-element.61), channel_id=1, source_target_pairs={{0,8},{1,5},{2,10},{3,7},{4,12},{5,1},{6,14},{7,3},{8,0},{9,13},{1... | collective-permute-start | bytes 110600 | tf_op jit(solution)/shard_map/ppermute | solution.py:332
  5.2 2.9 %sort_first.1 = (bf16[1024,768]{1,0:T(8,128)(2,1)S(1)}, bf16[1024,768]{1,0:T(8,128)(2,1)S(1)}) custom-call(bf16[1024,2,1536]{2,1,0:T(2,128)(2,1)} %refs_1_.1), custom_call_target="tpu_custom_call" | custom-call | flops 805306368 | bytes 6291456 | tf_op jit(solution)/shard_map/sort_first/pallas_call | solution.py:152
  8.1 0.1 pad.2.clone
  8.2 0.1 pad_maximum_fusion.rest_4_
  8.3 2.6 %collective-permute-start.3 = (bf16[12,2,1536]{2,1,0:T(2,128)(2,1)S(1)}, bf16[12,2,1536]{2,1,0:T(2,128)(2,1)S(1)}, u32[]{:S(2)}, u32[]{:S(2)}) collective-permute-start(bf16[12,2,1536]{2,1,0:T(2,128)(2,1)S(1)} %pad_maximum_fusion.rest_4_), channel_id=1, source_target_pairs={{0,6},{1,11},{2,4},{3,9},{4,2},{5,15},{6,0},{7,13},{8,14},{9,3},{1... | collective-permute-start | bytes 221192 | tf_op jit(solution)/shard_map/ppermute | solution.py:332
  10.9 0.5 %collective-permute-start.2 = (bf16[12,2,1536]{2,1,0:T(2,128)(2,1)S(1)}, bf16[12,2,1536]{2,1,0:T(2,128)(2,1)S(1)}, u32[]{:S(2)}, u32[]{:S(2)}) collective-permute-start(bf16[12,2,1536]{2,1,0:T(2,128)(2,1)S(1)} %pad_maximum_fusion.rest_4_), channel_id=1, source_target_pairs={{0,2},{1,9},{2,0},{3,11},{4,6},{5,13},{6,4},{7,15},{8,10},{9,1},{1... | collective-permute-start | bytes 221192 | tf_op jit(solution)/shard_map/ppermute | solution.py:332
  11.4 0.4 %collective-permute-start.1 = (bf16[12,2,1536]{2,1,0:T(2,128)(2,1)S(1)}, bf16[12,2,1536]{2,1,0:T(2,128)(2,1)S(1)}, u32[]{:S(2)}, u32[]{:S(2)}) collective-permute-start(bf16[12,2,1536]{2,1,0:T(2,128)(2,1)S(1)} %pad_maximum_fusion.rest_4_), channel_id=1, source_target_pairs={{0,4},{1,3},{2,6},{3,1},{4,0},{5,7},{6,2},{7,5},{8,12},{9,11},{10,... | collective-permute-start | bytes 221192 | tf_op jit(solution)/shard_map/ppermute | solution.py:332
  11.9 0.1 add_add_fusion.refs_0_
  12.0 3.5 %sort_second.1 = (bf16[1024,768]{1,0:T(8,128)(2,1)S(1)}, bf16[1024,768]{1,0:T(8,128)(2,1)S(1)}, bf16[16,1536]{1,0:T(8,128)(2,1)S(1)}, bf16[16,1536]{1,0:T(8,128)...) custom-call(s32[2,23]{1,0:T(2,128)S(1)} %add_add_fusion.refs_0_, ...), custom_call_target="tpu_custom_call" | custom-call | flops 805306368 | bytes 6291456 | tf_op jit(solution)/shard_map/sort_second/pallas_call | solution.py:152
  15.5 0.5 %collective-permute-done.1 = bf16[12,2,1536]{2,1,0:T(2,128)(2,1)S(1)} collective-permute-done((bf16[12,2,1536]{2,1,0:T(2,128)(2,1)S(1)}, bf16[12,2,1536]{2,1,0:T(2,128)(2,1)S(1)}, u32[]{:S(2)}, u32[]{:S(2)}) %collective-permute-start.1) | collective-permute-done | bytes 73760 | tf_op jit(solution)/shard_map/ppermute | solution.py:332
  16.0 0.1 constant_dynamic-update-slice_fusion.2
  16.0 0.1 constant_dynamic-update-slice_fusion.1
  16.1 0.1 constant_dynamic-update-slice_fusion.rest_5_
  16.1 0.1 collective-permute-start.5
  16.2 0.5 %collective-permute-start.4 = (bf16[12,2,1536]{2,1,0:T(2,128)(2,1)S(1)}, bf16[12,2,1536]{2,1,0:T(2,128)(2,1)S(1)}, u32[]{:S(2)}, u32[]{:S(2)}) collective-permute-start(bf16[12,2,1536]{2,1,0:T(2,128)(2,1)S(1)} %pad_maximum_fusion.rest_4_), channel_id=1, source_target_pairs={{0,1},{1,0},{2,3},{3,2},{4,5},{5,4},{6,7},{7,6},{8,9},{9,8},{10,11... | collective-permute-start | bytes 221192 | tf_op jit(solution)/shard_map/ppermute | solution.py:332
  16.7 1.1 %collective-permute-done.4.rest_6_ = bf16[12,2,1536]{2,1,0:T(2,128)(2,1)S(1)} collective-permute-done((bf16[12,2,1536]{2,1,0:T(2,128)(2,1)S(1)}, bf16[12,2,1536]{2,1,0:T(2,128)(2,1)S(1)}, u32[]{:S(2)}, u32[]{:S(2)}) %collective-permute-start.4) | collective-permute-done | bytes 73760 | tf_op jit(solution)/shard_map/ppermute | solution.py:332
  17.8 3.1 %attend.1 = (f32[64,1664]{1,0:T(8,128)S(1)}, bf16[64,1664]{1,0:T(8,128)(2,1)S(1)}) custom-call(s32[1,192]{1,0:T(1,128)S(1)} %get-tuple-element.44.target_ref, f32[8,1024]{1,0:T(8,128)S(1)} %get-tuple-element.45.bias_ref, f32[8,16]{1,0:T(8,128)S(1)} %get-tuple-element.46.fresh_bias_ref, bf16[16,1536]{1,0:T(8,128)(2,1)S(1)} %get-tuple-element.47.fresh_key_ref, ...), custom_call_target="tpu_custom_call" | custom-call | flops 805306368 | bytes 6291456 | tf_op jit(solution)/shard_map/attend/pallas_call | solution.py:264
  20.9 0.3 collective-permute-start.6
  21.1 1.3 %collective-permute-done.6.other_ref = bf16[64,1664]{1,0:T(8,128)(2,1)S(1)} collective-permute-done((bf16[64,1664]{1,0:T(8,128)(2,1)S(1)}, bf16[64,1664]{1,0:T(8,128)(2,1)S(1)}, u32[]{:S(2)}, u32[]{:S(2)}) %collective-permute-start.6) | collective-permute-done | bytes 213024 | tf_op jit(solution)/shard_map/ppermute | solution.py:332
  22.4 0.4 %merge_cores.1 = bf16[8,8,1664]{2,1,0:T(8,128)(2,1)S(1)} custom-call(f32[64,1664]{1,0:T(8,128)S(1)} %get-tuple-element.57.keep_ref, bf16[64,1664]{1,0:T(8,128)(2,1)S(1)} %collective-permute-done.6.other_ref), custom_call_target="tpu_custom_call" | custom-call | tf_op jit(solution)/shard_map/merge_cores/pallas_call | solution.py:314
  22.8 13.2 %all_to_all.5.parts_ref = bf16[8,8,1664]{2,1,0:T(8,128)(2,1)S(1)} all-to-all(bf16[8,8,1664]{2,1,0:T(8,128)(2,1)S(1)} %merge_cores.1), channel_id=1, replica_groups={{0,2,4,6,8,10,12,14},{1,3,5,7,9,11,13,15},{16,18,20,22,24,26,28,30},{17..., dimensions={0} | all-to-all | bytes 425984 | tf_op jit(solution)/shard_map/all_to_all | solution.py:358
  36.1 0.9 %merge_chips.1 = bf16[2,4,1536]{2,1,0:T(4,128)(2,1)} custom-call(bf16[8,8,1664]{2,1,0:T(8,128)(2,1)S(1)} %all_to_all.5.parts_ref), custom_call_target="tpu_custom_call" | custom-call | tf_op jit(solution)/shard_map/merge_chips/pallas_call | solution.py:314
  (8 shorter events, 0.0 us)
Async XLA Ops:
  1.1 10.8 %copy-start = (s32[2,6]{1,0:T(2,128)S(1)}, s32[2,6]{1,0:T(2,128)}, u32[]{:S(2)}) copy-start(s32[2,6]{1,0:T(2,128)} %param.6) | copy-start | bytes 148
  1.1 10.8 %copy-start.1 = (s32[2,16]{1,0:T(2,128)S(1)}, s32[2,16]{1,0:T(2,128)}, u32[]{:S(2)}) copy-start(s32[2,16]{1,0:T(2,128)} %param.7) | copy-start | bytes 388
  1.1 7.1 %collective-permute-start = (bf16[6,2,1536]{2,1,0:T(2,128)(2,1)S(1)}, bf16[6,2,1536]{2,1,0:T(2,128)(2,1)S(1)}, u32[]{:S(2)}, u32[]{:S(2)}) collective-permute-start(bf16[6,2,1536]{2,1,0:T(2,128)(2,1)S(1)} %get-tuple-element.61), channel_id=1, source_target_pairs={{0,8},{1,5},{2,10},{3,7},{4,12},{5,1},{6,14},{7,3},{8,0},{9,13},{1... | collective-permute-start | bytes 110600 | tf_op jit(solution)/shard_map/ppermute | solution.py:332
  8.3 7.1 %collective-permute-start.3 = (bf16[12,2,1536]{2,1,0:T(2,128)(2,1)S(1)}, bf16[12,2,1536]{2,1,0:T(2,128)(2,1)S(1)}, u32[]{:S(2)}, u32[]{:S(2)}) collective-permute-start(bf16[12,2,1536]{2,1,0:T(2,128)(2,1)S(1)} %pad_maximum_fusion.rest_4_), channel_id=1, source_target_pairs={{0,6},{1,11},{2,4},{3,9},{4,2},{5,15},{6,0},{7,13},{8,14},{9,3},{1... | collective-permute-start | bytes 221192 | tf_op jit(solution)/shard_map/ppermute | solution.py:332
  10.9 4.5 %collective-permute-start.2 = (bf16[12,2,1536]{2,1,0:T(2,128)(2,1)S(1)}, bf16[12,2,1536]{2,1,0:T(2,128)(2,1)S(1)}, u32[]{:S(2)}, u32[]{:S(2)}) collective-permute-start(bf16[12,2,1536]{2,1,0:T(2,128)(2,1)S(1)} %pad_maximum_fusion.rest_4_), channel_id=1, source_target_pairs={{0,2},{1,9},{2,0},{3,11},{4,6},{5,13},{6,4},{7,15},{8,10},{9,1},{1... | collective-permute-start | bytes 221192 | tf_op jit(solution)/shard_map/ppermute | solution.py:332
  11.4 4.5 %collective-permute-start.1 = (bf16[12,2,1536]{2,1,0:T(2,128)(2,1)S(1)}, bf16[12,2,1536]{2,1,0:T(2,128)(2,1)S(1)}, u32[]{:S(2)}, u32[]{:S(2)}) collective-permute-start(bf16[12,2,1536]{2,1,0:T(2,128)(2,1)S(1)} %pad_maximum_fusion.rest_4_), channel_id=1, source_target_pairs={{0,4},{1,3},{2,6},{3,1},{4,0},{5,7},{6,2},{7,5},{8,12},{9,11},{10,... | collective-permute-start | bytes 221192 | tf_op jit(solution)/shard_map/ppermute | solution.py:332
  16.1 1.7 %collective-permute-start.5 = (bf16[36,2,1536]{2,1,0:T(2,128)(2,1)S(1)}, bf16[36,2,1536]{2,1,0:T(2,128)(2,1)S(1)}, u32[]{:S(2)}, u32[]{:S(2)}) collective-permute-start(bf16[36,2,1536]{2,1,0:T(2,128)(2,1)S(1)} %constant_dynamic-update-slice_fusion.rest_5_), channel_id=1, source_target_pairs={{0,1},{1,0},{2,3},{3,2},{4,5},{5,4},{6,7},{7,6},{8,9},{9,8},{10,11... | collective-permute-start | bytes 663560 | tf_op jit(solution)/shard_map/ppermute | solution.py:332
  16.2 1.6 %collective-permute-start.4 = (bf16[12,2,1536]{2,1,0:T(2,128)(2,1)S(1)}, bf16[12,2,1536]{2,1,0:T(2,128)(2,1)S(1)}, u32[]{:S(2)}, u32[]{:S(2)}) collective-permute-start(bf16[12,2,1536]{2,1,0:T(2,128)(2,1)S(1)} %pad_maximum_fusion.rest_4_), channel_id=1, source_target_pairs={{0,1},{1,0},{2,3},{3,2},{4,5},{5,4},{6,7},{7,6},{8,9},{9,8},{10,11... | collective-permute-start | bytes 221192 | tf_op jit(solution)/shard_map/ppermute | solution.py:332
  20.9 1.5 %collective-permute-start.6 = (bf16[64,1664]{1,0:T(8,128)(2,1)S(1)}, bf16[64,1664]{1,0:T(8,128)(2,1)S(1)}, u32[]{:S(2)}, u32[]{:S(2)}) collective-permute-start(bf16[64,1664]{1,0:T(8,128)(2,1)S(1)} %get-tuple-element.58), channel_id=1, source_target_pairs={{0,1},{1,0},{2,3},{3,2},{4,5},{5,4},{6,7},{7,6},{8,9},{9,8},{10,11... | collective-permute-start | bytes 638984 | tf_op jit(solution)/shard_map/ppermute | solution.py:332

commit v11 on v10

--- a/solution.py
+++ b/solution.py
@@ -212,8 +212,8 @@
         ones = jnp.ones((tokens, LANES), jnp.bfloat16)
 
         def block_of(refs, h):
-            at = h % part_heads * HEAD
-            return refs[h // part_heads][:, at:at + HEAD]
+            part, at = (0, h) if h < part_heads else (1, h - part_heads)
+            return refs[part][:, at * HEAD:(at + 1) * HEAD]
 
         def score(h):
             cols = slice(h * HEAD, (h + 1) * HEAD)
@@ -333,8 +333,8 @@
 
     fresh = fresh_qkv.transpose(1, 2, 0, 3)
     mine, fresh_key, fresh_value = (fresh[:, i] for i in range(3))
-    half = width // 2
-    early = sort_cache(cache_kv, 0, half, None, "sort_first")
+    most = width * 2 // 3
+    early = sort_cache(cache_kv, 0, most, None, "sort_first")
     column = mine
     steps = [(1 << m, 1 << n) for m, n in zip(*exchange_order(bits))]
     for e, masks in enumerate(steps[:-2]):
@@ -343,7 +343,7 @@
             other, early, counts, list_rows = lax.optimization_barrier((other, early, counts, list_rows))
         column = jnp.concatenate([column, other])
     table = jnp.concatenate([counts, list_rows, jnp.full((STEPS, 1), me, jnp.int32)], axis=1)
-    late = sort_cache(cache_kv, half, half, (table, fresh_key, fresh_value), "sort_second")
+    late = sort_cache(cache_kv, most, width - most, (table, fresh_key, fresh_value), "sort_second")
     both = [m | n for m, n in zip(*steps[-2:])]
     others = [swap(column, *masks) for masks in (*steps[-2:], both)]
     others, column, late = lax.optimization_barrier((others, column, late))

time: 37.2 us -> 37.4 us (level)
  blocking collectives: 13.2 us -> 11.2 us
  local copies, waits for them, and re-layouts: 1.32 us -> 2.66 us
  waiting for transfers between devices: 2.86 us -> 3.3 us
  Pallas kernels: 10.8 us -> 11.2 us
    all_to_all x1, blocking collectives: 13.2 us -> 11.2 us  [body(): lax.all_to_all(parts, 'blk', split_axis=0, concat_axis=0, axis_index_grou...]
    unnamed x7 -> x11, local copies, waits for them, and re-layouts: 1.1 us -> 2.44 us
    ppermute x7, waiting for transfers between devices: 2.86 us -> 3.3 us  [swap(): lax.ppermute(x, 'blk', [(i, i ^ masks[i % len(masks)]) for i in range(dev...]
  transfers between devices with their start and end apart: 7 -> 7, of which waited for: 3 -> 4; matrix products, arithmetic and copies ran while one was open for 0% -> 0% of each run, Pallas kernels for 17% -> 17%
where the time goes in v11:
time: 37.4 us; the launch traced here: 37.2 us
  Pallas kernels  11.2 us (30%)
  blocking collectives  11.2 us (30%)
  starting transfers between devices  8.49 us (23%)
  waiting for transfers between devices  3.3 us (9%)
  local copies, waits for them, and re-layouts  2.66 us (7%)
    all_to_all x1, blocking collectives, body(): lax.all_to_all(parts, 'blk', split_axis=0, concat_axis=0, axis_index_grou...  11.2 us
    ppermute x7, starting transfers between devices, swap(): lax.ppermute(x, 'blk', [(i, i ^ masks[i % len(masks)]) for i in range(dev...  8.49 us
    pallas_call x2, Pallas kernels, sort_cache(): pl.pallas_call(kernel, out_shape=tuple(shapes), in_specs=specs, out_specs...  6.5 us
    pallas_call x1, Pallas kernels, attend(): pl.pallas_call(attend_kernel, out_shape=(jax.ShapeDtypeStruct(shape, jnp....  3.4 us
    ppermute x7, waiting for transfers between devices, swap(): lax.ppermute(x, 'blk', [(i, i ^ masks[i % len(masks)]) for i in range(dev...  3.3 us
    unnamed x11, local copies, waits for them, and re-layouts  2.44 us
    pallas_call x2, Pallas kernels, merge(): pl.pallas_call(kernel, out_shape=jax.ShapeDtypeStruct(shape, jnp.bfloat16...  1.36 us
  transfers between devices with their start and end apart: 7, of which 4 were waited for; matrix products, arithmetic and copies ran while one was open for 0% of the time, Pallas kernels for 17%

profile of v11, /device:TPU:0, one launch (start us, length us, event | category | flops | bytes accessed | tf_op | source)
XLA Modules:
  0.0 37.2 jit_solution(13338360233261630767)
XLA Ops:
  0.0 1.0 %copy.7 = bf16[2,6,3,1536]{3,0,1,2:T(2,128)(2,1)S(1)} copy(bf16[2,6,3,1536]{3,0,2,1:T(2,128)(2,1)} %param.5) | data formatting | bytes 221184 | tf_op args[1]
  1.0 0.1 slice_bitcast_fusion
  1.1 4.1 %collective-permute-start = (bf16[6,2,1536]{2,1,0:T(2,128)(2,1)S(1)}, bf16[6,2,1536]{2,1,0:T(2,128)(2,1)S(1)}, u32[]{:S(2)}, u32[]{:S(2)}) collective-permute-start(bf16[6,2,1536]{2,1,0:T(2,128)(2,1)S(1)} %get-tuple-element.61), channel_id=1, source_target_pairs={{0,8},{1,5},{2,10},{3,7},{4,12},{5,1},{6,14},{7,3},{8,0},{9,13},{1... | collective-permute-start | bytes 110600 | tf_op jit(solution)/shard_map/ppermute | solution.py:332
  5.2 3.5 %sort_first.1 = (bf16[1024,1024]{1,0:T(8,128)(2,1)S(1)}, bf16[1024,1024]{1,0:T(8,128)(2,1)S(1)}) custom-call(bf16[1024,2,1536]{2,1,0:T(2,128)(2,1)} %refs_1_.1), custom_call_target="tpu_custom_call" | custom-call | flops 1073741824 | bytes 8388608 | tf_op jit(solution)/shard_map/sort_first/pallas_call | solution.py:152
  8.7 1.3 %copy-done = bf16[1024,1024]{1,0:T(8,128)(2,1)} copy-done((bf16[1024,1024]{1,0:T(8,128)(2,1)}, bf16[1024,1024]{1,0:T(8,128)(2,1)S(1)}, u32[]{:S(2)}) %copy-start) | copy-done | bytes 2097176
  10.0 0.1 pad.2.clone
  10.1 0.1 pad_maximum_fusion.rest_4_
  10.2 2.6 %collective-permute-start.3 = (bf16[12,2,1536]{2,1,0:T(2,128)(2,1)S(1)}, bf16[12,2,1536]{2,1,0:T(2,128)(2,1)S(1)}, u32[]{:S(2)}, u32[]{:S(2)}) collective-permute-start(bf16[12,2,1536]{2,1,0:T(2,128)(2,1)S(1)} %pad_maximum_fusion.rest_4_), channel_id=1, source_target_pairs={{0,6},{1,11},{2,4},{3,9},{4,2},{5,15},{6,0},{7,13},{8,14},{9,3},{1... | collective-permute-start | bytes 221192 | tf_op jit(solution)/shard_map/ppermute | solution.py:332
  12.8 0.5 %collective-permute-start.2 = (bf16[12,2,1536]{2,1,0:T(2,128)(2,1)S(1)}, bf16[12,2,1536]{2,1,0:T(2,128)(2,1)S(1)}, u32[]{:S(2)}, u32[]{:S(2)}) collective-permute-start(bf16[12,2,1536]{2,1,0:T(2,128)(2,1)S(1)} %pad_maximum_fusion.rest_4_), channel_id=1, source_target_pairs={{0,2},{1,9},{2,0},{3,11},{4,6},{5,13},{6,4},{7,15},{8,10},{9,1},{1... | collective-permute-start | bytes 221192 | tf_op jit(solution)/shard_map/ppermute | solution.py:332
  13.3 0.5 %collective-permute-start.1 = (bf16[12,2,1536]{2,1,0:T(2,128)(2,1)S(1)}, bf16[12,2,1536]{2,1,0:T(2,128)(2,1)S(1)}, u32[]{:S(2)}, u32[]{:S(2)}) collective-permute-start(bf16[12,2,1536]{2,1,0:T(2,128)(2,1)S(1)} %pad_maximum_fusion.rest_4_), channel_id=1, source_target_pairs={{0,4},{1,3},{2,6},{3,1},{4,0},{5,7},{6,2},{7,5},{8,12},{9,11},{10,... | collective-permute-start | bytes 221192 | tf_op jit(solution)/shard_map/ppermute | solution.py:332
  13.8 0.1 add_add_fusion.refs_0_
  13.9 3.0 %sort_second.1 = (bf16[1024,512]{1,0:T(8,128)(2,1)S(1)}, bf16[1024,512]{1,0:T(8,128)(2,1)S(1)}, bf16[16,1536]{1,0:T(8,128)(2,1)S(1)}, bf16[16,1536]{1,0:T(8,128)...) custom-call(s32[2,23]{1,0:T(2,128)S(1)} %add_add_fusion.refs_0_, ...), custom_call_target="tpu_custom_call" | custom-call | flops 536870912 | bytes 4194304 | tf_op jit(solution)/shard_map/sort_second/pallas_call | solution.py:152
  16.9 0.3 collective-permute-done.2
  17.2 0.6 %collective-permute-done.1 = bf16[12,2,1536]{2,1,0:T(2,128)(2,1)S(1)} collective-permute-done((bf16[12,2,1536]{2,1,0:T(2,128)(2,1)S(1)}, bf16[12,2,1536]{2,1,0:T(2,128)(2,1)S(1)}, u32[]{:S(2)}, u32[]{:S(2)}) %collective-permute-start.1) | collective-permute-done | bytes 73760 | tf_op jit(solution)/shard_map/ppermute | solution.py:332
  17.9 0.1 constant_dynamic-update-slice_fusion.1
  18.0 0.1 collective-permute-start.5
  18.1 0.5 %collective-permute-start.4 = (bf16[12,2,1536]{2,1,0:T(2,128)(2,1)S(1)}, bf16[12,2,1536]{2,1,0:T(2,128)(2,1)S(1)}, u32[]{:S(2)}, u32[]{:S(2)}) collective-permute-start(bf16[12,2,1536]{2,1,0:T(2,128)(2,1)S(1)} %pad_maximum_fusion.rest_4_), channel_id=1, source_target_pairs={{0,1},{1,0},{2,3},{3,2},{4,5},{5,4},{6,7},{7,6},{8,9},{9,8},{10,11... | collective-permute-start | bytes 221192 | tf_op jit(solution)/shard_map/ppermute | solution.py:332
  18.6 1.1 %collective-permute-done.4.rest_6_ = bf16[12,2,1536]{2,1,0:T(2,128)(2,1)S(1)} collective-permute-done((bf16[12,2,1536]{2,1,0:T(2,128)(2,1)S(1)}, bf16[12,2,1536]{2,1,0:T(2,128)(2,1)S(1)}, u32[]{:S(2)}, u32[]{:S(2)}) %collective-permute-start.4) | collective-permute-done | bytes 73760 | tf_op jit(solution)/shard_map/ppermute | solution.py:332
  19.7 3.4 %attend.1 = (f32[64,1664]{1,0:T(8,128)S(1)}, bf16[64,1664]{1,0:T(8,128)(2,1)S(1)}) custom-call(s32[1,192]{1,0:T(1,128)S(1)} %get-tuple-element.44.target_ref, f32[8,1024]{1,0:T(8,128)S(1)} %get-tuple-element.45.bias_ref, f32[8,16]{1,0:T(8,128)S(1)} %get-tuple-element.46.fresh_bias_ref, bf16[16,1536]{1,0:T(8,128)(2,1)S(1)} %get-tuple-element.47.fresh_key_ref, ...), custom_call_target="tpu_custom_call" | custom-call | flops 805306368 | bytes 6291456 | tf_op jit(solution)/shard_map/attend/pallas_call | solution.py:264
  23.1 0.3 collective-permute-start.6
  23.3 1.3 %collective-permute-done.6.other_ref = bf16[64,1664]{1,0:T(8,128)(2,1)S(1)} collective-permute-done((bf16[64,1664]{1,0:T(8,128)(2,1)S(1)}, bf16[64,1664]{1,0:T(8,128)(2,1)S(1)}, u32[]{:S(2)}, u32[]{:S(2)}) %collective-permute-start.6) | collective-permute-done | bytes 213024 | tf_op jit(solution)/shard_map/ppermute | solution.py:332
  24.6 0.4 %merge_cores.1 = bf16[8,8,1664]{2,1,0:T(8,128)(2,1)S(1)} custom-call(f32[64,1664]{1,0:T(8,128)S(1)} %get-tuple-element.57.keep_ref, bf16[64,1664]{1,0:T(8,128)(2,1)S(1)} %collective-permute-done.6.other_ref), custom_call_target="tpu_custom_call" | custom-call | tf_op jit(solution)/shard_map/merge_cores/pallas_call | solution.py:314
  25.1 11.2 %all_to_all.5.parts_ref = bf16[8,8,1664]{2,1,0:T(8,128)(2,1)S(1)} all-to-all(bf16[8,8,1664]{2,1,0:T(8,128)(2,1)S(1)} %merge_cores.1), channel_id=1, replica_groups={{0,2,4,6,8,10,12,14},{1,3,5,7,9,11,13,15},{16,18,20,22,24,26,28,30},{17..., dimensions={0} | all-to-all | bytes 425984 | tf_op jit(solution)/shard_map/all_to_all | solution.py:358
  36.3 0.9 %merge_chips.1 = bf16[2,4,1536]{2,1,0:T(4,128)(2,1)} custom-call(bf16[8,8,1664]{2,1,0:T(8,128)(2,1)S(1)} %all_to_all.5.parts_ref), custom_call_target="tpu_custom_call" | custom-call | tf_op jit(solution)/shard_map/merge_chips/pallas_call | solution.py:314
  (12 shorter events, 0.1 us)
Async XLA Ops:
  1.1 12.7 %copy-start.2 = (s32[2,6]{1,0:T(2,128)S(1)}, s32[2,6]{1,0:T(2,128)}, u32[]{:S(2)}) copy-start(s32[2,6]{1,0:T(2,128)} %param.6) | copy-start | bytes 148
  1.1 12.7 %copy-start.3 = (s32[2,16]{1,0:T(2,128)S(1)}, s32[2,16]{1,0:T(2,128)}, u32[]{:S(2)}) copy-start(s32[2,16]{1,0:T(2,128)} %param.7) | copy-start | bytes 388
  1.1 9.0 %collective-permute-start = (bf16[6,2,1536]{2,1,0:T(2,128)(2,1)S(1)}, bf16[6,2,1536]{2,1,0:T(2,128)(2,1)S(1)}, u32[]{:S(2)}, u32[]{:S(2)}) collective-permute-start(bf16[6,2,1536]{2,1,0:T(2,128)(2,1)S(1)} %get-tuple-element.61), channel_id=1, source_target_pairs={{0,8},{1,5},{2,10},{3,7},{4,12},{5,1},{6,14},{7,3},{8,0},{9,13},{1... | collective-permute-start | bytes 110600 | tf_op jit(solution)/shard_map/ppermute | solution.py:332
  8.7 1.3 %copy-start = (bf16[1024,1024]{1,0:T(8,128)(2,1)}, bf16[1024,1024]{1,0:T(8,128)(2,1)S(1)}, u32[]{:S(2)}) copy-start(bf16[1024,1024]{1,0:T(8,128)(2,1)S(1)} %get-tuple-element.50.rest_1_) | copy-start | bytes 6291460
  10.2 6.6 %collective-permute-start.3 = (bf16[12,2,1536]{2,1,0:T(2,128)(2,1)S(1)}, bf16[12,2,1536]{2,1,0:T(2,128)(2,1)S(1)}, u32[]{:S(2)}, u32[]{:S(2)}) collective-permute-start(bf16[12,2,1536]{2,1,0:T(2,128)(2,1)S(1)} %pad_maximum_fusion.rest_4_), channel_id=1, source_target_pairs={{0,6},{1,11},{2,4},{3,9},{4,2},{5,15},{6,0},{7,13},{8,14},{9,3},{1... | collective-permute-start | bytes 221192 | tf_op jit(solution)/shard_map/ppermute | solution.py:332
  12.8 4.4 %collective-permute-start.2 = (bf16[12,2,1536]{2,1,0:T(2,128)(2,1)S(1)}, bf16[12,2,1536]{2,1,0:T(2,128)(2,1)S(1)}, u32[]{:S(2)}, u32[]{:S(2)}) collective-permute-start(bf16[12,2,1536]{2,1,0:T(2,128)(2,1)S(1)} %pad_maximum_fusion.rest_4_), channel_id=1, source_target_pairs={{0,2},{1,9},{2,0},{3,11},{4,6},{5,13},{6,4},{7,15},{8,10},{9,1},{1... | collective-permute-start | bytes 221192 | tf_op jit(solution)/shard_map/ppermute | solution.py:332
  13.3 4.5 %collective-permute-start.1 = (bf16[12,2,1536]{2,1,0:T(2,128)(2,1)S(1)}, bf16[12,2,1536]{2,1,0:T(2,128)(2,1)S(1)}, u32[]{:S(2)}, u32[]{:S(2)}) collective-permute-start(bf16[12,2,1536]{2,1,0:T(2,128)(2,1)S(1)} %pad_maximum_fusion.rest_4_), channel_id=1, source_target_pairs={{0,4},{1,3},{2,6},{3,1},{4,0},{5,7},{6,2},{7,5},{8,12},{9,11},{10,... | collective-permute-start | bytes 221192 | tf_op jit(solution)/shard_map/ppermute | solution.py:332
  13.9 5.8 %copy-start.1 = (bf16[1024,1024]{1,0:T(8,128)(2,1)S(1)}, bf16[1024,1024]{1,0:T(8,128)(2,1)}, u32[]{:S(2)}) copy-start(bf16[1024,1024]{1,0:T(8,128)(2,1)} %copy-done) | copy-start | bytes 6291460
  18.0 1.7 %collective-permute-start.5 = (bf16[36,2,1536]{2,1,0:T(2,128)(2,1)S(1)}, bf16[36,2,1536]{2,1,0:T(2,128)(2,1)S(1)}, u32[]{:S(2)}, u32[]{:S(2)}) collective-permute-start(bf16[36,2,1536]{2,1,0:T(2,128)(2,1)S(1)} %constant_dynamic-update-slice_fusion.rest_5_), channel_id=1, source_target_pairs={{0,1},{1,0},{2,3},{3,2},{4,5},{5,4},{6,7},{7,6},{8,9},{9,8},{10,11... | collective-permute-start | bytes 663560 | tf_op jit(solution)/shard_map/ppermute | solution.py:332
  18.1 1.6 %collective-permute-start.4 = (bf16[12,2,1536]{2,1,0:T(2,128)(2,1)S(1)}, bf16[12,2,1536]{2,1,0:T(2,128)(2,1)S(1)}, u32[]{:S(2)}, u32[]{:S(2)}) collective-permute-start(bf16[12,2,1536]{2,1,0:T(2,128)(2,1)S(1)} %pad_maximum_fusion.rest_4_), channel_id=1, source_target_pairs={{0,1},{1,0},{2,3},{3,2},{4,5},{5,4},{6,7},{7,6},{8,9},{9,8},{10,11... | collective-permute-start | bytes 221192 | tf_op jit(solution)/shard_map/ppermute | solution.py:332
  23.1 1.5 %collective-permute-start.6 = (bf16[64,1664]{1,0:T(8,128)(2,1)S(1)}, bf16[64,1664]{1,0:T(8,128)(2,1)S(1)}, u32[]{:S(2)}, u32[]{:S(2)}) collective-permute-start(bf16[64,1664]{1,0:T(8,128)(2,1)S(1)} %get-tuple-element.58), channel_id=1, source_target_pairs={{0,1},{1,0},{2,3},{3,2},{4,5},{5,4},{6,7},{7,6},{8,9},{9,8},{10,11... | collective-permute-start | bytes 638984 | tf_op jit(solution)/shard_map/ppermute | solution.py:332

commit v12 on v11

--- a/solution.py
+++ b/solution.py
@@ -16,7 +16,7 @@
 PART = 16
 SLOT_BITS = 2
 WAITS = 4
-SORT_VMEM = 48
+SORT_VMEM = 46
 VMEM = pl.BlockSpec(memory_space=pltpu.VMEM)
 SMEM = pl.BlockSpec(memory_space=pltpu.SMEM)
 HBM = pl.BlockSpec(memory_space=pltpu.HBM)

time: 37.4 us -> 37.4 us (level)
  no operation moved by 1% of the time
where the time goes in v12:
time: 37.4 us; the launch traced here: 37.2 us
  Pallas kernels  11.2 us (30%)
  blocking collectives  11.2 us (30%)
  starting transfers between devices  8.49 us (23%)
  waiting for transfers between devices  3.3 us (9%)
  local copies, waits for them, and re-layouts  2.66 us (7%)
    all_to_all x1, blocking collectives, body(): lax.all_to_all(parts, 'blk', split_axis=0, concat_axis=0, axis_index_grou...  11.2 us
    ppermute x7, starting transfers between devices, swap(): lax.ppermute(x, 'blk', [(i, i ^ masks[i % len(masks)]) for i in range(dev...  8.49 us
    pallas_call x2, Pallas kernels, sort_cache(): pl.pallas_call(kernel, out_shape=tuple(shapes), in_specs=specs, out_specs...  6.5 us
    pallas_call x1, Pallas kernels, attend(): pl.pallas_call(attend_kernel, out_shape=(jax.ShapeDtypeStruct(shape, jnp....  3.4 us
    ppermute x7, waiting for transfers between devices, swap(): lax.ppermute(x, 'blk', [(i, i ^ masks[i % len(masks)]) for i in range(dev...  3.3 us
    unnamed x11, local copies, waits for them, and re-layouts  2.44 us
    pallas_call x2, Pallas kernels, merge(): pl.pallas_call(kernel, out_shape=jax.ShapeDtypeStruct(shape, jnp.bfloat16...  1.36 us
  transfers between devices with their start and end apart: 7, of which 4 were waited for; matrix products, arithmetic and copies ran while one was open for 0% of the time, Pallas kernels for 17%

profile of v12, /device:TPU:0, one launch (start us, length us, event | category | flops | bytes accessed | tf_op | source)
XLA Modules:
  0.0 37.2 jit_solution(4350960158652487047)
XLA Ops:
  0.0 1.0 %copy.7 = bf16[2,6,3,1536]{3,0,1,2:T(2,128)(2,1)S(1)} copy(bf16[2,6,3,1536]{3,0,2,1:T(2,128)(2,1)} %param.5) | data formatting | bytes 221184 | tf_op args[1]
  1.0 0.1 slice_bitcast_fusion
  1.1 4.1 %collective-permute-start = (bf16[6,2,1536]{2,1,0:T(2,128)(2,1)S(1)}, bf16[6,2,1536]{2,1,0:T(2,128)(2,1)S(1)}, u32[]{:S(2)}, u32[]{:S(2)}) collective-permute-start(bf16[6,2,1536]{2,1,0:T(2,128)(2,1)S(1)} %get-tuple-element.61), channel_id=1, source_target_pairs={{0,8},{1,5},{2,10},{3,7},{4,12},{5,1},{6,14},{7,3},{8,0},{9,13},{1... | collective-permute-start | bytes 110600 | tf_op jit(solution)/shard_map/ppermute | solution.py:332
  5.2 3.5 %sort_first.1 = (bf16[1024,1024]{1,0:T(8,128)(2,1)S(1)}, bf16[1024,1024]{1,0:T(8,128)(2,1)S(1)}) custom-call(bf16[1024,2,1536]{2,1,0:T(2,128)(2,1)} %refs_1_.1), custom_call_target="tpu_custom_call" | custom-call | flops 1073741824 | bytes 8388608 | tf_op jit(solution)/shard_map/sort_first/pallas_call | solution.py:152
  8.7 1.3 %copy-done = bf16[1024,1024]{1,0:T(8,128)(2,1)} copy-done((bf16[1024,1024]{1,0:T(8,128)(2,1)}, bf16[1024,1024]{1,0:T(8,128)(2,1)S(1)}, u32[]{:S(2)}) %copy-start) | copy-done | bytes 2097176
  10.0 0.1 pad.2.clone
  10.1 0.1 pad_maximum_fusion.rest_4_
  10.2 2.6 %collective-permute-start.3 = (bf16[12,2,1536]{2,1,0:T(2,128)(2,1)S(1)}, bf16[12,2,1536]{2,1,0:T(2,128)(2,1)S(1)}, u32[]{:S(2)}, u32[]{:S(2)}) collective-permute-start(bf16[12,2,1536]{2,1,0:T(2,128)(2,1)S(1)} %pad_maximum_fusion.rest_4_), channel_id=1, source_target_pairs={{0,6},{1,11},{2,4},{3,9},{4,2},{5,15},{6,0},{7,13},{8,14},{9,3},{1... | collective-permute-start | bytes 221192 | tf_op jit(solution)/shard_map/ppermute | solution.py:332
  12.8 0.5 %collective-permute-start.2 = (bf16[12,2,1536]{2,1,0:T(2,128)(2,1)S(1)}, bf16[12,2,1536]{2,1,0:T(2,128)(2,1)S(1)}, u32[]{:S(2)}, u32[]{:S(2)}) collective-permute-start(bf16[12,2,1536]{2,1,0:T(2,128)(2,1)S(1)} %pad_maximum_fusion.rest_4_), channel_id=1, source_target_pairs={{0,2},{1,9},{2,0},{3,11},{4,6},{5,13},{6,4},{7,15},{8,10},{9,1},{1... | collective-permute-start | bytes 221192 | tf_op jit(solution)/shard_map/ppermute | solution.py:332
  13.3 0.5 %collective-permute-start.1 = (bf16[12,2,1536]{2,1,0:T(2,128)(2,1)S(1)}, bf16[12,2,1536]{2,1,0:T(2,128)(2,1)S(1)}, u32[]{:S(2)}, u32[]{:S(2)}) collective-permute-start(bf16[12,2,1536]{2,1,0:T(2,128)(2,1)S(1)} %pad_maximum_fusion.rest_4_), channel_id=1, source_target_pairs={{0,4},{1,3},{2,6},{3,1},{4,0},{5,7},{6,2},{7,5},{8,12},{9,11},{10,... | collective-permute-start | bytes 221192 | tf_op jit(solution)/shard_map/ppermute | solution.py:332
  13.8 0.1 add_add_fusion.refs_0_
  13.9 3.0 %sort_second.1 = (bf16[1024,512]{1,0:T(8,128)(2,1)S(1)}, bf16[1024,512]{1,0:T(8,128)(2,1)S(1)}, bf16[16,1536]{1,0:T(8,128)(2,1)S(1)}, bf16[16,1536]{1,0:T(8,128)...) custom-call(s32[2,23]{1,0:T(2,128)S(1)} %add_add_fusion.refs_0_, ...), custom_call_target="tpu_custom_call" | custom-call | flops 536870912 | bytes 4194304 | tf_op jit(solution)/shard_map/sort_second/pallas_call | solution.py:152
  16.9 0.3 collective-permute-done.2
  17.2 0.6 %collective-permute-done.1 = bf16[12,2,1536]{2,1,0:T(2,128)(2,1)S(1)} collective-permute-done((bf16[12,2,1536]{2,1,0:T(2,128)(2,1)S(1)}, bf16[12,2,1536]{2,1,0:T(2,128)(2,1)S(1)}, u32[]{:S(2)}, u32[]{:S(2)}) %collective-permute-start.1) | collective-permute-done | bytes 73760 | tf_op jit(solution)/shard_map/ppermute | solution.py:332
  17.9 0.1 constant_dynamic-update-slice_fusion.1
  18.0 0.1 collective-permute-start.5
  18.1 0.5 %collective-permute-start.4 = (bf16[12,2,1536]{2,1,0:T(2,128)(2,1)S(1)}, bf16[12,2,1536]{2,1,0:T(2,128)(2,1)S(1)}, u32[]{:S(2)}, u32[]{:S(2)}) collective-permute-start(bf16[12,2,1536]{2,1,0:T(2,128)(2,1)S(1)} %pad_maximum_fusion.rest_4_), channel_id=1, source_target_pairs={{0,1},{1,0},{2,3},{3,2},{4,5},{5,4},{6,7},{7,6},{8,9},{9,8},{10,11... | collective-permute-start | bytes 221192 | tf_op jit(solution)/shard_map/ppermute | solution.py:332
  18.6 1.1 %collective-permute-done.4.rest_6_ = bf16[12,2,1536]{2,1,0:T(2,128)(2,1)S(1)} collective-permute-done((bf16[12,2,1536]{2,1,0:T(2,128)(2,1)S(1)}, bf16[12,2,1536]{2,1,0:T(2,128)(2,1)S(1)}, u32[]{:S(2)}, u32[]{:S(2)}) %collective-permute-start.4) | collective-permute-done | bytes 73760 | tf_op jit(solution)/shard_map/ppermute | solution.py:332
  19.7 3.4 %attend.1 = (f32[64,1664]{1,0:T(8,128)S(1)}, bf16[64,1664]{1,0:T(8,128)(2,1)S(1)}) custom-call(s32[1,192]{1,0:T(1,128)S(1)} %get-tuple-element.44.target_ref, f32[8,1024]{1,0:T(8,128)S(1)} %get-tuple-element.45.bias_ref, f32[8,16]{1,0:T(8,128)S(1)} %get-tuple-element.46.fresh_bias_ref, bf16[16,1536]{1,0:T(8,128)(2,1)S(1)} %get-tuple-element.47.fresh_key_ref, ...), custom_call_target="tpu_custom_call" | custom-call | flops 805306368 | bytes 6291456 | tf_op jit(solution)/shard_map/attend/pallas_call | solution.py:264
  23.1 0.3 collective-permute-start.6
  23.3 1.3 %collective-permute-done.6.other_ref = bf16[64,1664]{1,0:T(8,128)(2,1)S(1)} collective-permute-done((bf16[64,1664]{1,0:T(8,128)(2,1)S(1)}, bf16[64,1664]{1,0:T(8,128)(2,1)S(1)}, u32[]{:S(2)}, u32[]{:S(2)}) %collective-permute-start.6) | collective-permute-done | bytes 213024 | tf_op jit(solution)/shard_map/ppermute | solution.py:332
  24.6 0.4 %merge_cores.1 = bf16[8,8,1664]{2,1,0:T(8,128)(2,1)S(1)} custom-call(f32[64,1664]{1,0:T(8,128)S(1)} %get-tuple-element.57.keep_ref, bf16[64,1664]{1,0:T(8,128)(2,1)S(1)} %collective-permute-done.6.other_ref), custom_call_target="tpu_custom_call" | custom-call | tf_op jit(solution)/shard_map/merge_cores/pallas_call | solution.py:314
  25.1 11.2 %all_to_all.5.parts_ref = bf16[8,8,1664]{2,1,0:T(8,128)(2,1)S(1)} all-to-all(bf16[8,8,1664]{2,1,0:T(8,128)(2,1)S(1)} %merge_cores.1), channel_id=1, replica_groups={{0,2,4,6,8,10,12,14},{1,3,5,7,9,11,13,15},{16,18,20,22,24,26,28,30},{17..., dimensions={0} | all-to-all | bytes 425984 | tf_op jit(solution)/shard_map/all_to_all | solution.py:358
  36.3 0.9 %merge_chips.1 = bf16[2,4,1536]{2,1,0:T(4,128)(2,1)} custom-call(bf16[8,8,1664]{2,1,0:T(8,128)(2,1)S(1)} %all_to_all.5.parts_ref), custom_call_target="tpu_custom_call" | custom-call | tf_op jit(solution)/shard_map/merge_chips/pallas_call | solution.py:314
  (12 shorter events, 0.1 us)
Async XLA Ops:
  1.1 12.7 %copy-start.2 = (s32[2,6]{1,0:T(2,128)S(1)}, s32[2,6]{1,0:T(2,128)}, u32[]{:S(2)}) copy-start(s32[2,6]{1,0:T(2,128)} %param.6) | copy-start | bytes 148
  1.1 12.7 %copy-start.3 = (s32[2,16]{1,0:T(2,128)S(1)}, s32[2,16]{1,0:T(2,128)}, u32[]{:S(2)}) copy-start(s32[2,16]{1,0:T(2,128)} %param.7) | copy-start | bytes 388
  1.1 9.0 %collective-permute-start = (bf16[6,2,1536]{2,1,0:T(2,128)(2,1)S(1)}, bf16[6,2,1536]{2,1,0:T(2,128)(2,1)S(1)}, u32[]{:S(2)}, u32[]{:S(2)}) collective-permute-start(bf16[6,2,1536]{2,1,0:T(2,128)(2,1)S(1)} %get-tuple-element.61), channel_id=1, source_target_pairs={{0,8},{1,5},{2,10},{3,7},{4,12},{5,1},{6,14},{7,3},{8,0},{9,13},{1... | collective-permute-start | bytes 110600 | tf_op jit(solution)/shard_map/ppermute | solution.py:332
  8.7 1.3 %copy-start = (bf16[1024,1024]{1,0:T(8,128)(2,1)}, bf16[1024,1024]{1,0:T(8,128)(2,1)S(1)}, u32[]{:S(2)}) copy-start(bf16[1024,1024]{1,0:T(8,128)(2,1)S(1)} %get-tuple-element.50.rest_1_) | copy-start | bytes 6291460
  10.2 6.6 %collective-permute-start.3 = (bf16[12,2,1536]{2,1,0:T(2,128)(2,1)S(1)}, bf16[12,2,1536]{2,1,0:T(2,128)(2,1)S(1)}, u32[]{:S(2)}, u32[]{:S(2)}) collective-permute-start(bf16[12,2,1536]{2,1,0:T(2,128)(2,1)S(1)} %pad_maximum_fusion.rest_4_), channel_id=1, source_target_pairs={{0,6},{1,11},{2,4},{3,9},{4,2},{5,15},{6,0},{7,13},{8,14},{9,3},{1... | collective-permute-start | bytes 221192 | tf_op jit(solution)/shard_map/ppermute | solution.py:332
  12.8 4.4 %collective-permute-start.2 = (bf16[12,2,1536]{2,1,0:T(2,128)(2,1)S(1)}, bf16[12,2,1536]{2,1,0:T(2,128)(2,1)S(1)}, u32[]{:S(2)}, u32[]{:S(2)}) collective-permute-start(bf16[12,2,1536]{2,1,0:T(2,128)(2,1)S(1)} %pad_maximum_fusion.rest_4_), channel_id=1, source_target_pairs={{0,2},{1,9},{2,0},{3,11},{4,6},{5,13},{6,4},{7,15},{8,10},{9,1},{1... | collective-permute-start | bytes 221192 | tf_op jit(solution)/shard_map/ppermute | solution.py:332
  13.3 4.5 %collective-permute-start.1 = (bf16[12,2,1536]{2,1,0:T(2,128)(2,1)S(1)}, bf16[12,2,1536]{2,1,0:T(2,128)(2,1)S(1)}, u32[]{:S(2)}, u32[]{:S(2)}) collective-permute-start(bf16[12,2,1536]{2,1,0:T(2,128)(2,1)S(1)} %pad_maximum_fusion.rest_4_), channel_id=1, source_target_pairs={{0,4},{1,3},{2,6},{3,1},{4,0},{5,7},{6,2},{7,5},{8,12},{9,11},{10,... | collective-permute-start | bytes 221192 | tf_op jit(solution)/shard_map/ppermute | solution.py:332
  13.9 5.8 %copy-start.1 = (bf16[1024,1024]{1,0:T(8,128)(2,1)S(1)}, bf16[1024,1024]{1,0:T(8,128)(2,1)}, u32[]{:S(2)}) copy-start(bf16[1024,1024]{1,0:T(8,128)(2,1)} %copy-done) | copy-start | bytes 6291460
  18.0 1.7 %collective-permute-start.5 = (bf16[36,2,1536]{2,1,0:T(2,128)(2,1)S(1)}, bf16[36,2,1536]{2,1,0:T(2,128)(2,1)S(1)}, u32[]{:S(2)}, u32[]{:S(2)}) collective-permute-start(bf16[36,2,1536]{2,1,0:T(2,128)(2,1)S(1)} %constant_dynamic-update-slice_fusion.rest_5_), channel_id=1, source_target_pairs={{0,1},{1,0},{2,3},{3,2},{4,5},{5,4},{6,7},{7,6},{8,9},{9,8},{10,11... | collective-permute-start | bytes 663560 | tf_op jit(solution)/shard_map/ppermute | solution.py:332
  18.1 1.6 %collective-permute-start.4 = (bf16[12,2,1536]{2,1,0:T(2,128)(2,1)S(1)}, bf16[12,2,1536]{2,1,0:T(2,128)(2,1)S(1)}, u32[]{:S(2)}, u32[]{:S(2)}) collective-permute-start(bf16[12,2,1536]{2,1,0:T(2,128)(2,1)S(1)} %pad_maximum_fusion.rest_4_), channel_id=1, source_target_pairs={{0,1},{1,0},{2,3},{3,2},{4,5},{5,4},{6,7},{7,6},{8,9},{9,8},{10,11... | collective-permute-start | bytes 221192 | tf_op jit(solution)/shard_map/ppermute | solution.py:332
  23.1 1.5 %collective-permute-start.6 = (bf16[64,1664]{1,0:T(8,128)(2,1)S(1)}, bf16[64,1664]{1,0:T(8,128)(2,1)S(1)}, u32[]{:S(2)}, u32[]{:S(2)}) collective-permute-start(bf16[64,1664]{1,0:T(8,128)(2,1)S(1)} %get-tuple-element.58), channel_id=1, source_target_pairs={{0,1},{1,0},{2,3},{3,2},{4,5},{5,4},{6,7},{7,6},{8,9},{9,8},{10,11... | collective-permute-start | bytes 638984 | tf_op jit(solution)/shard_map/ppermute | solution.py:332

commit v13 on v12

--- a/solution.py
+++ b/solution.py
@@ -16,7 +16,7 @@
 PART = 16
 SLOT_BITS = 2
 WAITS = 4
-SORT_VMEM = 46
+SORT_VMEM = (46, 38)
 VMEM = pl.BlockSpec(memory_space=pltpu.VMEM)
 SMEM = pl.BlockSpec(memory_space=pltpu.SMEM)
 HBM = pl.BlockSpec(memory_space=pltpu.HBM)
@@ -158,7 +158,7 @@
             pltpu.VMEM((tokens, 2, width + LANES), bf16),
             pltpu.SemaphoreType.DMA((blocks,)),
         ],
-        compiler_params=pltpu.CompilerParams(vmem_limit_bytes=SORT_VMEM << 20),
+        compiler_params=pltpu.CompilerParams(vmem_limit_bytes=SORT_VMEM[bool(plan)] << 20),
         cost_estimate=pl.CostEstimate(
             flops=8 * 128 * tokens * width, bytes_accessed=8 * tokens * width, transcendentals=0
         ),

time: 37.4 us -> 39.5 us (1.056)
  local copies, waits for them, and re-layouts: 2.66 us -> 5.44 us
  blocking collectives: 11.2 us -> 12.2 us
  waiting for transfers between devices: 3.3 us -> 2.35 us
  Pallas kernels: 11.2 us -> 10.5 us
    unnamed x11 -> x13, local copies, waits for them, and re-layouts: 2.44 us -> 5.22 us
    ppermute x7, waiting for transfers between devices: 3.3 us -> 2.35 us  [swap(): lax.ppermute(x, 'blk', [(i, i ^ masks[i % len(masks)]) for i in range(dev...]
    all_to_all x1, blocking collectives: 11.2 us -> 12.2 us  [body(): lax.all_to_all(parts, 'blk', split_axis=0, concat_axis=0, axis_index_grou...]
    pallas_call x2, Pallas kernels: 6.5 us -> 5.79 us  [sort_cache(): pl.pallas_call(kernel, out_shape=tuple(shapes), in_specs=specs, out_specs...]
  transfers between devices with their start and end apart: 7 -> 7, of which waited for: 4 -> 2; matrix products, arithmetic and copies ran while one was open for 0% -> 0% of each run, Pallas kernels for 17% -> 15%
where the time goes in v13:
time: 39.5 us; the launch traced here: 39.3 us
  blocking collectives  12.2 us (31%)
  Pallas kernels  10.5 us (27%)
  starting transfers between devices  8.49 us (21%)
  local copies, waits for them, and re-layouts  5.44 us (14%)
  waiting for transfers between devices  2.35 us (6%)
    all_to_all x1, blocking collectives, body(): lax.all_to_all(parts, 'blk', split_axis=0, concat_axis=0, axis_index_grou...  12.2 us
    ppermute x7, starting transfers between devices, swap(): lax.ppermute(x, 'blk', [(i, i ^ masks[i % len(masks)]) for i in range(dev...  8.49 us
    pallas_call x2, Pallas kernels, sort_cache(): pl.pallas_call(kernel, out_shape=tuple(shapes), in_specs=specs, out_specs...  5.79 us
    unnamed x13, local copies, waits for them, and re-layouts  5.22 us
    pallas_call x1, Pallas kernels, attend(): pl.pallas_call(attend_kernel, out_shape=(jax.ShapeDtypeStruct(shape, jnp....  3.39 us
    ppermute x7, waiting for transfers between devices, swap(): lax.ppermute(x, 'blk', [(i, i ^ masks[i % len(masks)]) for i in range(dev...  2.35 us
    pallas_call x2, Pallas kernels, merge(): pl.pallas_call(kernel, out_shape=jax.ShapeDtypeStruct(shape, jnp.bfloat16...  1.36 us
  transfers between devices with their start and end apart: 7, of which 2 were waited for; matrix products, arithmetic and copies ran while one was open for 0% of the time, Pallas kernels for 15%

profile of v13, /device:TPU:0, one launch (start us, length us, event | category | flops | bytes accessed | tf_op | source)
XLA Modules:
  0.0 39.3 jit_solution(18439217543904850775)
XLA Ops:
  0.0 1.0 %copy.7 = bf16[2,6,3,1536]{3,0,1,2:T(2,128)(2,1)S(1)} copy(bf16[2,6,3,1536]{3,0,2,1:T(2,128)(2,1)} %param.5) | data formatting | bytes 221184 | tf_op args[1]
  1.0 0.1 slice_bitcast_fusion
  1.1 4.1 %collective-permute-start = (bf16[6,2,1536]{2,1,0:T(2,128)(2,1)S(1)}, bf16[6,2,1536]{2,1,0:T(2,128)(2,1)S(1)}, u32[]{:S(2)}, u32[]{:S(2)}) collective-permute-start(bf16[6,2,1536]{2,1,0:T(2,128)(2,1)S(1)} %get-tuple-element.61), channel_id=1, source_target_pairs={{0,8},{1,5},{2,10},{3,7},{4,12},{5,1},{6,14},{7,3},{8,0},{9,13},{1... | collective-permute-start | bytes 110600 | tf_op jit(solution)/shard_map/ppermute | solution.py:332
  5.2 3.5 %sort_first.1 = (bf16[1024,1024]{1,0:T(8,128)(2,1)S(1)}, bf16[1024,1024]{1,0:T(8,128)(2,1)S(1)}) custom-call(bf16[1024,2,1536]{2,1,0:T(2,128)(2,1)} %refs_1_.1), custom_call_target="tpu_custom_call" | custom-call | flops 1073741824 | bytes 8388608 | tf_op jit(solution)/shard_map/sort_first/pallas_call | solution.py:152
  8.7 1.3 %copy-done.1 = bf16[1024,1024]{1,0:T(8,128)(2,1)} copy-done((bf16[1024,1024]{1,0:T(8,128)(2,1)}, bf16[1024,1024]{1,0:T(8,128)(2,1)S(1)}, u32[]{:S(2)}) %copy-start.1) | copy-done | bytes 2097176
  10.0 0.1 pad.2.clone
  10.1 0.1 pad_maximum_fusion.rest_4_
  10.2 2.6 %collective-permute-start.3 = (bf16[12,2,1536]{2,1,0:T(2,128)(2,1)S(1)}, bf16[12,2,1536]{2,1,0:T(2,128)(2,1)S(1)}, u32[]{:S(2)}, u32[]{:S(2)}) collective-permute-start(bf16[12,2,1536]{2,1,0:T(2,128)(2,1)S(1)} %pad_maximum_fusion.rest_4_), channel_id=1, source_target_pairs={{0,6},{1,11},{2,4},{3,9},{4,2},{5,15},{6,0},{7,13},{8,14},{9,3},{1... | collective-permute-start | bytes 221192 | tf_op jit(solution)/shard_map/ppermute | solution.py:332
  12.8 0.5 %collective-permute-start.2 = (bf16[12,2,1536]{2,1,0:T(2,128)(2,1)S(1)}, bf16[12,2,1536]{2,1,0:T(2,128)(2,1)S(1)}, u32[]{:S(2)}, u32[]{:S(2)}) collective-permute-start(bf16[12,2,1536]{2,1,0:T(2,128)(2,1)S(1)} %pad_maximum_fusion.rest_4_), channel_id=1, source_target_pairs={{0,2},{1,9},{2,0},{3,11},{4,6},{5,13},{6,4},{7,15},{8,10},{9,1},{1... | collective-permute-start | bytes 221192 | tf_op jit(solution)/shard_map/ppermute | solution.py:332
  13.3 0.5 %collective-permute-start.1 = (bf16[12,2,1536]{2,1,0:T(2,128)(2,1)S(1)}, bf16[12,2,1536]{2,1,0:T(2,128)(2,1)S(1)}, u32[]{:S(2)}, u32[]{:S(2)}) collective-permute-start(bf16[12,2,1536]{2,1,0:T(2,128)(2,1)S(1)} %pad_maximum_fusion.rest_4_), channel_id=1, source_target_pairs={{0,4},{1,3},{2,6},{3,1},{4,0},{5,7},{6,2},{7,5},{8,12},{9,11},{10,... | collective-permute-start | bytes 221192 | tf_op jit(solution)/shard_map/ppermute | solution.py:332
  13.8 0.1 add_add_fusion.refs_0_
  13.9 2.8 %copy-done = bf16[1024,2,1536]{2,1,0:T(2,128)(2,1)S(1)} copy-done((bf16[1024,2,1536]{2,1,0:T(2,128)(2,1)S(1)}, bf16[1024,2,1536]{2,1,0:T(2,128)(2,1)}, u32[]{:S(2)}) %copy-start) | copy-done | bytes 6291480
  16.6 2.3 %sort_second.1 = (bf16[1024,512]{1,0:T(8,128)(2,1)S(1)}, bf16[1024,512]{1,0:T(8,128)(2,1)S(1)}, bf16[16,1536]{1,0:T(8,128)(2,1)S(1)}, bf16[16,1536]{1,0:T(8,128)...) custom-call(s32[2,23]{1,0:T(2,128)S(1)} %add_add_fusion.refs_0_, ...), custom_call_target="tpu_custom_call" | custom-call | flops 536870912 | bytes 4194304 | tf_op jit(solution)/shard_map/sort_second/pallas_call | solution.py:152
  19.0 0.1 constant_dynamic-update-slice_fusion.1
  19.1 0.1 constant_dynamic-update-slice_fusion.rest_5_
  19.2 0.1 collective-permute-start.5
  19.3 0.5 %collective-permute-start.4 = (bf16[12,2,1536]{2,1,0:T(2,128)(2,1)S(1)}, bf16[12,2,1536]{2,1,0:T(2,128)(2,1)S(1)}, u32[]{:S(2)}, u32[]{:S(2)}) collective-permute-start(bf16[12,2,1536]{2,1,0:T(2,128)(2,1)S(1)} %pad_maximum_fusion.rest_4_), channel_id=1, source_target_pairs={{0,1},{1,0},{2,3},{3,2},{4,5},{5,4},{6,7},{7,6},{8,9},{9,8},{10,11... | collective-permute-start | bytes 221192 | tf_op jit(solution)/shard_map/ppermute | solution.py:332
  19.7 1.1 %collective-permute-done.4.rest_6_ = bf16[12,2,1536]{2,1,0:T(2,128)(2,1)S(1)} collective-permute-done((bf16[12,2,1536]{2,1,0:T(2,128)(2,1)S(1)}, bf16[12,2,1536]{2,1,0:T(2,128)(2,1)S(1)}, u32[]{:S(2)}, u32[]{:S(2)}) %collective-permute-start.4) | collective-permute-done | bytes 73760 | tf_op jit(solution)/shard_map/ppermute | solution.py:332
  20.8 3.4 %attend.1 = (f32[64,1664]{1,0:T(8,128)S(1)}, bf16[64,1664]{1,0:T(8,128)(2,1)S(1)}) custom-call(s32[1,192]{1,0:T(1,128)S(1)} %get-tuple-element.44.target_ref, f32[8,1024]{1,0:T(8,128)S(1)} %get-tuple-element.45.bias_ref, f32[8,16]{1,0:T(8,128)S(1)} %get-tuple-element.46.fresh_bias_ref, bf16[16,1536]{1,0:T(8,128)(2,1)S(1)} %get-tuple-element.47.fresh_key_ref, ...), custom_call_target="tpu_custom_call" | custom-call | flops 805306368 | bytes 6291456 | tf_op jit(solution)/shard_map/attend/pallas_call | solution.py:264
  24.2 0.3 collective-permute-start.6
  24.5 1.3 %collective-permute-done.6.other_ref = bf16[64,1664]{1,0:T(8,128)(2,1)S(1)} collective-permute-done((bf16[64,1664]{1,0:T(8,128)(2,1)S(1)}, bf16[64,1664]{1,0:T(8,128)(2,1)S(1)}, u32[]{:S(2)}, u32[]{:S(2)}) %collective-permute-start.6) | collective-permute-done | bytes 213024 | tf_op jit(solution)/shard_map/ppermute | solution.py:332
  25.8 0.4 %merge_cores.1 = bf16[8,8,1664]{2,1,0:T(8,128)(2,1)S(1)} custom-call(f32[64,1664]{1,0:T(8,128)S(1)} %get-tuple-element.57.keep_ref, bf16[64,1664]{1,0:T(8,128)(2,1)S(1)} %collective-permute-done.6.other_ref), custom_call_target="tpu_custom_call" | custom-call | tf_op jit(solution)/shard_map/merge_cores/pallas_call | solution.py:314
  26.2 12.2 %all_to_all.5.parts_ref = bf16[8,8,1664]{2,1,0:T(8,128)(2,1)S(1)} all-to-all(bf16[8,8,1664]{2,1,0:T(8,128)(2,1)S(1)} %merge_cores.1), channel_id=1, replica_groups={{0,2,4,6,8,10,12,14},{1,3,5,7,9,11,13,15},{16,18,20,22,24,26,28,30},{17..., dimensions={0} | all-to-all | bytes 425984 | tf_op jit(solution)/shard_map/all_to_all | solution.py:358
  38.4 0.9 %merge_chips.1 = bf16[2,4,1536]{2,1,0:T(4,128)(2,1)} custom-call(bf16[8,8,1664]{2,1,0:T(8,128)(2,1)S(1)} %all_to_all.5.parts_ref), custom_call_target="tpu_custom_call" | custom-call | tf_op jit(solution)/shard_map/merge_chips/pallas_call | solution.py:314
  (14 shorter events, 0.1 us)
Async XLA Ops:
  1.1 12.7 %copy-start.3 = (s32[2,6]{1,0:T(2,128)S(1)}, s32[2,6]{1,0:T(2,128)}, u32[]{:S(2)}) copy-start(s32[2,6]{1,0:T(2,128)} %param.6) | copy-start | bytes 148
  1.1 12.7 %copy-start.4 = (s32[2,16]{1,0:T(2,128)S(1)}, s32[2,16]{1,0:T(2,128)}, u32[]{:S(2)}) copy-start(s32[2,16]{1,0:T(2,128)} %param.7) | copy-start | bytes 388
  1.1 9.0 %collective-permute-start = (bf16[6,2,1536]{2,1,0:T(2,128)(2,1)S(1)}, bf16[6,2,1536]{2,1,0:T(2,128)(2,1)S(1)}, u32[]{:S(2)}, u32[]{:S(2)}) collective-permute-start(bf16[6,2,1536]{2,1,0:T(2,128)(2,1)S(1)} %get-tuple-element.61), channel_id=1, source_target_pairs={{0,8},{1,5},{2,10},{3,7},{4,12},{5,1},{6,14},{7,3},{8,0},{9,13},{1... | collective-permute-start | bytes 110600 | tf_op jit(solution)/shard_map/ppermute | solution.py:332
  8.7 1.3 %copy-start.1 = (bf16[1024,1024]{1,0:T(8,128)(2,1)}, bf16[1024,1024]{1,0:T(8,128)(2,1)S(1)}, u32[]{:S(2)}) copy-start(bf16[1024,1024]{1,0:T(8,128)(2,1)S(1)} %get-tuple-element.50.rest_1_) | copy-start | bytes 6291460
  10.2 8.7 %collective-permute-start.3 = (bf16[12,2,1536]{2,1,0:T(2,128)(2,1)S(1)}, bf16[12,2,1536]{2,1,0:T(2,128)(2,1)S(1)}, u32[]{:S(2)}, u32[]{:S(2)}) collective-permute-start(bf16[12,2,1536]{2,1,0:T(2,128)(2,1)S(1)} %pad_maximum_fusion.rest_4_), channel_id=1, source_target_pairs={{0,6},{1,11},{2,4},{3,9},{4,2},{5,15},{6,0},{7,13},{8,14},{9,3},{1... | collective-permute-start | bytes 221192 | tf_op jit(solution)/shard_map/ppermute | solution.py:332
  12.8 6.1 %collective-permute-start.2 = (bf16[12,2,1536]{2,1,0:T(2,128)(2,1)S(1)}, bf16[12,2,1536]{2,1,0:T(2,128)(2,1)S(1)}, u32[]{:S(2)}, u32[]{:S(2)}) collective-permute-start(bf16[12,2,1536]{2,1,0:T(2,128)(2,1)S(1)} %pad_maximum_fusion.rest_4_), channel_id=1, source_target_pairs={{0,2},{1,9},{2,0},{3,11},{4,6},{5,13},{6,4},{7,15},{8,10},{9,1},{1... | collective-permute-start | bytes 221192 | tf_op jit(solution)/shard_map/ppermute | solution.py:332
  13.3 5.6 %collective-permute-start.1 = (bf16[12,2,1536]{2,1,0:T(2,128)(2,1)S(1)}, bf16[12,2,1536]{2,1,0:T(2,128)(2,1)S(1)}, u32[]{:S(2)}, u32[]{:S(2)}) collective-permute-start(bf16[12,2,1536]{2,1,0:T(2,128)(2,1)S(1)} %pad_maximum_fusion.rest_4_), channel_id=1, source_target_pairs={{0,4},{1,3},{2,6},{3,1},{4,0},{5,7},{6,2},{7,5},{8,12},{9,11},{10,... | collective-permute-start | bytes 221192 | tf_op jit(solution)/shard_map/ppermute | solution.py:332
  13.9 2.8 %copy-start = (bf16[1024,2,1536]{2,1,0:T(2,128)(2,1)S(1)}, bf16[1024,2,1536]{2,1,0:T(2,128)(2,1)}, u32[]{:S(2)}) copy-start(bf16[1024,2,1536]{2,1,0:T(2,128)(2,1)} %refs_1_.1) | copy-start | bytes 18874372
  16.6 4.2 %copy-start.2 = (bf16[1024,1024]{1,0:T(8,128)(2,1)S(1)}, bf16[1024,1024]{1,0:T(8,128)(2,1)}, u32[]{:S(2)}) copy-start(bf16[1024,1024]{1,0:T(8,128)(2,1)} %copy-done.1) | copy-start | bytes 6291460
  19.2 1.7 %collective-permute-start.5 = (bf16[36,2,1536]{2,1,0:T(2,128)(2,1)S(1)}, bf16[36,2,1536]{2,1,0:T(2,128)(2,1)S(1)}, u32[]{:S(2)}, u32[]{:S(2)}) collective-permute-start(bf16[36,2,1536]{2,1,0:T(2,128)(2,1)S(1)} %constant_dynamic-update-slice_fusion.rest_5_), channel_id=1, source_target_pairs={{0,1},{1,0},{2,3},{3,2},{4,5},{5,4},{6,7},{7,6},{8,9},{9,8},{10,11... | collective-permute-start | bytes 663560 | tf_op jit(solution)/shard_map/ppermute | solution.py:332
  19.3 1.6 %collective-permute-start.4 = (bf16[12,2,1536]{2,1,0:T(2,128)(2,1)S(1)}, bf16[12,2,1536]{2,1,0:T(2,128)(2,1)S(1)}, u32[]{:S(2)}, u32[]{:S(2)}) collective-permute-start(bf16[12,2,1536]{2,1,0:T(2,128)(2,1)S(1)} %pad_maximum_fusion.rest_4_), channel_id=1, source_target_pairs={{0,1},{1,0},{2,3},{3,2},{4,5},{5,4},{6,7},{7,6},{8,9},{9,8},{10,11... | collective-permute-start | bytes 221192 | tf_op jit(solution)/shard_map/ppermute | solution.py:332
  24.2 1.5 %collective-permute-start.6 = (bf16[64,1664]{1,0:T(8,128)(2,1)S(1)}, bf16[64,1664]{1,0:T(8,128)(2,1)S(1)}, u32[]{:S(2)}, u32[]{:S(2)}) collective-permute-start(bf16[64,1664]{1,0:T(8,128)(2,1)S(1)} %get-tuple-element.58), channel_id=1, source_target_pairs={{0,1},{1,0},{2,3},{3,2},{4,5},{5,4},{6,7},{7,6},{8,9},{9,8},{10,11... | collective-permute-start | bytes 638984 | tf_op jit(solution)/shard_map/ppermute | solution.py:332

commit v14 on v11

--- a/solution.py
+++ b/solution.py
@@ -34,15 +34,33 @@
     return jnp.where((dev & 1) == 1, places[1], places[0]) + ((mask & 1) << (bits - 1))
 
 
-def plan_kernel_part(table_ref, slots, target_ref, bias_ref, fresh_bias_ref):
-    device_count = table_ref.shape[1] - slots - 1
+def join_kernel(first_ref, second_ref, out_ref):
+    count = first_ref.shape[0]
+    out_ref[:count] = first_ref[...]
+    out_ref[count:] = second_ref[...]
+
+
+def join(first, second):
+    shape = (2 * first.shape[0], *first.shape[1:])
+    return pl.pallas_call(
+        join_kernel,
+        out_shape=jax.ShapeDtypeStruct(shape, first.dtype),
+        in_specs=[VMEM, VMEM],
+        out_specs=VMEM,
+        compiler_params=pltpu.CompilerParams(vmem_limit_bytes=16 << 20),
+        name="join",
+    )(first, second)
+
+
+def plan_kernel_part(me_ref, counts_ref, rows_ref, target_ref, bias_ref, fresh_bias_ref):
+    device_count, slots = counts_ref.shape[1], rows_ref.shape[1]
     bits = device_count.bit_length() - 1
-    me = table_ref[0, device_count + slots]
+    me = me_ref[0]
     col = lax.broadcasted_iota(jnp.int32, target_ref.shape, 1)
 
     def one_device(dev, carry):
         start0, start1, target = carry
-        count0, count1 = table_ref[0, dev], table_ref[1, dev]
+        count0, count1 = counts_ref[0, dev], counts_ref[1, dev]
         local = col - place_of(dev, me, bits) * (STEPS * slots)
         slot, step = local >> 1, local & 1
         rank = slot + jnp.where(step == 0, start0, start1)
@@ -60,10 +78,10 @@
         carry = lax.fori_loop(0, device_count, one_device, carry)
     target_ref[...] = carry[2]
 
-    live0 = [i < table_ref[0, me] for i in range(slots)]
-    live1 = [i < table_ref[1, me] for i in range(slots)]
-    row0 = [jnp.where(live0[i], table_ref[0, device_count + i], -1) for i in range(slots)]
-    row1 = [jnp.where(live1[i], table_ref[1, device_count + i], -2) for i in range(slots)]
+    live0 = [i < counts_ref[0, me] for i in range(slots)]
+    live1 = [i < counts_ref[1, me] for i in range(slots)]
+    row0 = [jnp.where(live0[i], rows_ref[0, i], -1) for i in range(slots)]
+    row1 = [jnp.where(live1[i], rows_ref[1, i], -2) for i in range(slots)]
     token = lax.broadcasted_iota(jnp.int32, bias_ref.shape, 1)
     second = lax.broadcasted_iota(jnp.int32, bias_ref.shape, 0) >= SLOT
     gone = token == row0[0]
@@ -89,7 +107,7 @@
 
 def sort_kernel(first, planned, *refs):
     refs = list(refs)
-    table_ref = refs.pop(0) if planned else None
+    table_refs = [refs.pop(0) for _ in range(3)] if planned else []
     cache_ref = refs.pop(0)
     new_refs = [refs.pop(0) for _ in range(2)] if planned else []
     key_ref, value_ref, *small_refs, held, sems = refs
@@ -110,7 +128,7 @@
         for ref, new_ref in zip(small_refs[:2], new_refs):
             ref[...] = jnp.zeros_like(ref)
             ref[0:STEPS * slots, :] = new_ref.reshape(STEPS * slots, ref.shape[1])[...]
-        plan_kernel_part(table_ref, slots, *small_refs[2:])
+        plan_kernel_part(*table_refs, *small_refs[2:])
     out = lax.broadcasted_iota(jnp.int32, (2 * block, 2 * block), 0)
     src = lax.broadcasted_iota(jnp.int32, (2 * block, 2 * block), 1)
     order = (src == jnp.where(out < block, 2 * out, 2 * (out - block) + 1)).astype(jnp.bfloat16)
@@ -133,9 +151,9 @@
     shapes = [jax.ShapeDtypeStruct((tokens, width), bf16)] * 2
     inputs, specs = [cache], [HBM]
     if plan:
-        table, fresh_key, fresh_value = plan
+        tables, fresh_key, fresh_value = plan
         slots = fresh_key.shape[0]
-        device_count = table.shape[1] - slots - 1
+        device_count = tables[1].shape[1]
         fresh_rows = -(-STEPS * slots // 16) * 16
         shapes += [jax.ShapeDtypeStruct((fresh_rows, full), bf16)] * 2
         shapes += [
@@ -143,7 +161,8 @@
             jax.ShapeDtypeStruct((PAIR, tokens), f32),
             jax.ShapeDtypeStruct((PAIR, fresh_rows), f32),
         ]
-        inputs, specs = [table, cache, fresh_key, fresh_value], [SMEM, HBM, VMEM, VMEM]
+        inputs = [*tables, cache, fresh_key, fresh_value]
+        specs = [SMEM, SMEM, SMEM, HBM, VMEM, VMEM]
 
     def kernel(*refs):
         sort_kernel(first, bool(plan), *refs)
@@ -341,9 +360,9 @@
         other = swap(column, *masks)
         if e == 0:
             other, early, counts, list_rows = lax.optimization_barrier((other, early, counts, list_rows))
-        column = jnp.concatenate([column, other])
-    table = jnp.concatenate([counts, list_rows, jnp.full((STEPS, 1), me, jnp.int32)], axis=1)
-    late = sort_cache(cache_kv, most, width - most, (table, fresh_key, fresh_value), "sort_second")
+        column = join(column, other)
+    tables = (me.reshape(1), counts, list_rows)
+    late = sort_cache(cache_kv, most, width - most, (tables, fresh_key, fresh_value), "sort_second")
     both = [m | n for m, n in zip(*steps[-2:])]
     others = [swap(column, *masks) for masks in (*steps[-2:], both)]
     others, column, late = lax.optimization_barrier((others, column, late))

time: 37.4 us -> 37.2 us (level)
  transfers between devices with their start and end apart: 7 -> 7, of which waited for: 4 -> 4; matrix products, arithmetic and copies ran while one was open for 0% -> 0% of each run, Pallas kernels for 17% -> 18%
where the time goes in v14:
time: 37.2 us; the launch traced here: 37 us
  Pallas kernels  11.2 us (30%)
  blocking collectives  11.2 us (30%)
  starting transfers between devices  8.49 us (23%)
  waiting for transfers between devices  3.38 us (9%)
  local copies, waits for them, and re-layouts  2.58 us (7%)
    all_to_all x1, blocking collectives, body(): lax.all_to_all(parts, 'blk', split_axis=0, concat_axis=0, axis_index_grou...  11.2 us
    ppermute x7, starting transfers between devices, swap(): lax.ppermute(x, 'blk', [(i, i ^ masks[i % len(masks)]) for i in range(dev...  8.49 us
    pallas_call x2, Pallas kernels, sort_cache(): pl.pallas_call(kernel, out_shape=tuple(shapes), in_specs=specs, out_specs...  6.49 us
    ppermute x7, waiting for transfers between devices, swap(): lax.ppermute(x, 'blk', [(i, i ^ masks[i % len(masks)]) for i in range(dev...  3.38 us
    pallas_call x1, Pallas kernels, attend(): pl.pallas_call(attend_kernel, out_shape=(jax.ShapeDtypeStruct(shape, jnp....  3.33 us
    unnamed x11, local copies, waits for them, and re-layouts  2.44 us
    pallas_call x2, Pallas kernels, merge(): pl.pallas_call(kernel, out_shape=jax.ShapeDtypeStruct(shape, jnp.bfloat16...  1.36 us
  transfers between devices with their start and end apart: 7, of which 4 were waited for; matrix products, arithmetic and copies ran while one was open for 0% of the time, Pallas kernels for 18%

profile of v14, /device:TPU:0, one launch (start us, length us, event | category | flops | bytes accessed | tf_op | source)
XLA Modules:
  0.0 37.0 jit_solution(10241484025141737103)
XLA Ops:
  0.0 1.0 %copy.7 = bf16[2,6,3,1536]{3,0,1,2:T(2,128)(2,1)S(1)} copy(bf16[2,6,3,1536]{3,0,2,1:T(2,128)(2,1)} %param.5) | data formatting | bytes 221184 | tf_op args[1]
  1.0 0.1 slice_bitcast_fusion
  1.1 0.0 copy-start.3
  1.1 4.1 %collective-permute-start = (bf16[6,2,1536]{2,1,0:T(2,128)(2,1)S(1)}, bf16[6,2,1536]{2,1,0:T(2,128)(2,1)S(1)}, u32[]{:S(2)}, u32[]{:S(2)}) collective-permute-start(bf16[6,2,1536]{2,1,0:T(2,128)(2,1)S(1)} %get-tuple-element.61.first_ref), channel_id=1, source_target_pairs={{0,8},{1,5},{2,10},{3,7},{4,12},{5,1},{6,14},{7,3},{8,0},{9,13},{1... | collective-permute-start | bytes 110600 | tf_op jit(solution)/shard_map/ppermute | solution.py:351
  5.2 3.5 %sort_first.1 = (bf16[1024,1024]{1,0:T(8,128)(2,1)S(1)}, bf16[1024,1024]{1,0:T(8,128)(2,1)S(1)}) custom-call(bf16[1024,2,1536]{2,1,0:T(2,128)(2,1)} %refs_3_.1), custom_call_target="tpu_custom_call" | custom-call | flops 1073741824 | bytes 8388608 | tf_op jit(solution)/shard_map/sort_first/pallas_call | solution.py:171
  8.7 1.3 %copy-done = bf16[1024,1024]{1,0:T(8,128)(2,1)} copy-done((bf16[1024,1024]{1,0:T(8,128)(2,1)}, bf16[1024,1024]{1,0:T(8,128)(2,1)S(1)}, u32[]{:S(2)}) %copy-start) | copy-done | bytes 2097176
  10.1 2.6 %collective-permute-start.3 = (bf16[12,2,1536]{2,1,0:T(2,128)(2,1)S(1)}, bf16[12,2,1536]{2,1,0:T(2,128)(2,1)S(1)}, u32[]{:S(2)}, u32[]{:S(2)}) collective-permute-start(bf16[12,2,1536]{2,1,0:T(2,128)(2,1)S(1)} %join.1.rest_4_), channel_id=1, source_target_pairs={{0,6},{1,11},{2,4},{3,9},{4,2},{5,15},{6,0},{7,13},{8,14},{9,3},{1... | collective-permute-start | bytes 221192 | tf_op jit(solution)/shard_map/ppermute | solution.py:351
  12.7 0.5 %collective-permute-start.2 = (bf16[12,2,1536]{2,1,0:T(2,128)(2,1)S(1)}, bf16[12,2,1536]{2,1,0:T(2,128)(2,1)S(1)}, u32[]{:S(2)}, u32[]{:S(2)}) collective-permute-start(bf16[12,2,1536]{2,1,0:T(2,128)(2,1)S(1)} %join.1.rest_4_), channel_id=1, source_target_pairs={{0,2},{1,9},{2,0},{3,11},{4,6},{5,13},{6,4},{7,15},{8,10},{9,1},{1... | collective-permute-start | bytes 221192 | tf_op jit(solution)/shard_map/ppermute | solution.py:351
  13.2 0.5 %collective-permute-start.1 = (bf16[12,2,1536]{2,1,0:T(2,128)(2,1)S(1)}, bf16[12,2,1536]{2,1,0:T(2,128)(2,1)S(1)}, u32[]{:S(2)}, u32[]{:S(2)}) collective-permute-start(bf16[12,2,1536]{2,1,0:T(2,128)(2,1)S(1)} %join.1.rest_4_), channel_id=1, source_target_pairs={{0,4},{1,3},{2,6},{3,1},{4,0},{5,7},{6,2},{7,5},{8,12},{9,11},{10,... | collective-permute-start | bytes 221192 | tf_op jit(solution)/shard_map/ppermute | solution.py:351
  13.6 3.0 %sort_second.1 = (bf16[1024,512]{1,0:T(8,128)(2,1)S(1)}, bf16[1024,512]{1,0:T(8,128)(2,1)S(1)}, bf16[16,1536]{1,0:T(8,128)(2,1)S(1)}, bf16[16,1536]{1,0:T(8,128)...) custom-call(s32[1]{0:T(128)} %bitcast.2.refs_0_, s32[2,16]{1,0:T(2,128)S(1)} %copy-done.2, ...), custom_call_target="tpu_custom_call" | custom-call | flops 536870912 | bytes 4194304 | tf_op jit(solution)/shard_map/sort_second/pallas_call | solution.py:171
  16.6 0.4 %collective-permute-done.2 = bf16[12,2,1536]{2,1,0:T(2,128)(2,1)S(1)} collective-permute-done((bf16[12,2,1536]{2,1,0:T(2,128)(2,1)S(1)}, bf16[12,2,1536]{2,1,0:T(2,128)(2,1)S(1)}, u32[]{:S(2)}, u32[]{:S(2)}) %collective-permute-start.2) | collective-permute-done | bytes 73760 | tf_op jit(solution)/shard_map/ppermute | solution.py:351
  17.0 0.6 %collective-permute-done.1 = bf16[12,2,1536]{2,1,0:T(2,128)(2,1)S(1)} collective-permute-done((bf16[12,2,1536]{2,1,0:T(2,128)(2,1)S(1)}, bf16[12,2,1536]{2,1,0:T(2,128)(2,1)S(1)}, u32[]{:S(2)}, u32[]{:S(2)}) %collective-permute-start.1) | collective-permute-done | bytes 73760 | tf_op jit(solution)/shard_map/ppermute | solution.py:351
  17.7 0.1 constant_dynamic-update-slice_fusion.2
  17.7 0.1 constant_dynamic-update-slice_fusion.1
  17.8 0.1 constant_dynamic-update-slice_fusion.rest_5_
  17.9 0.1 collective-permute-start.5
  17.9 0.5 %collective-permute-start.4 = (bf16[12,2,1536]{2,1,0:T(2,128)(2,1)S(1)}, bf16[12,2,1536]{2,1,0:T(2,128)(2,1)S(1)}, u32[]{:S(2)}, u32[]{:S(2)}) collective-permute-start(bf16[12,2,1536]{2,1,0:T(2,128)(2,1)S(1)} %join.1.rest_4_), channel_id=1, source_target_pairs={{0,1},{1,0},{2,3},{3,2},{4,5},{5,4},{6,7},{7,6},{8,9},{9,8},{10,11... | collective-permute-start | bytes 221192 | tf_op jit(solution)/shard_map/ppermute | solution.py:351
  18.4 1.1 %collective-permute-done.4.rest_6_ = bf16[12,2,1536]{2,1,0:T(2,128)(2,1)S(1)} collective-permute-done((bf16[12,2,1536]{2,1,0:T(2,128)(2,1)S(1)}, bf16[12,2,1536]{2,1,0:T(2,128)(2,1)S(1)}, u32[]{:S(2)}, u32[]{:S(2)}) %collective-permute-start.4) | collective-permute-done | bytes 73760 | tf_op jit(solution)/shard_map/ppermute | solution.py:351
  19.5 3.3 %attend.1 = (f32[64,1664]{1,0:T(8,128)S(1)}, bf16[64,1664]{1,0:T(8,128)(2,1)S(1)}) custom-call(s32[1,192]{1,0:T(1,128)S(1)} %get-tuple-element.44.target_ref, f32[8,1024]{1,0:T(8,128)S(1)} %get-tuple-element.45.bias_ref, f32[8,16]{1,0:T(8,128)S(1)} %get-tuple-element.46.fresh_bias_ref, bf16[16,1536]{1,0:T(8,128)(2,1)S(1)} %get-tuple-element.47.fresh_key_ref, ...), custom_call_target="tpu_custom_call" | custom-call | flops 805306368 | bytes 6291456 | tf_op jit(solution)/shard_map/attend/pallas_call | solution.py:283
  22.8 0.3 collective-permute-start.6
  23.1 1.3 %collective-permute-done.6.other_ref = bf16[64,1664]{1,0:T(8,128)(2,1)S(1)} collective-permute-done((bf16[64,1664]{1,0:T(8,128)(2,1)S(1)}, bf16[64,1664]{1,0:T(8,128)(2,1)S(1)}, u32[]{:S(2)}, u32[]{:S(2)}) %collective-permute-start.6) | collective-permute-done | bytes 213024 | tf_op jit(solution)/shard_map/ppermute | solution.py:351
  24.4 0.4 %merge_cores.1 = bf16[8,8,1664]{2,1,0:T(8,128)(2,1)S(1)} custom-call(f32[64,1664]{1,0:T(8,128)S(1)} %get-tuple-element.57.keep_ref, bf16[64,1664]{1,0:T(8,128)(2,1)S(1)} %collective-permute-done.6.other_ref), custom_call_target="tpu_custom_call" | custom-call | tf_op jit(solution)/shard_map/merge_cores/pallas_call | solution.py:333
  24.8 11.2 %all_to_all.5.parts_ref = bf16[8,8,1664]{2,1,0:T(8,128)(2,1)S(1)} all-to-all(bf16[8,8,1664]{2,1,0:T(8,128)(2,1)S(1)} %merge_cores.1), channel_id=1, replica_groups={{0,2,4,6,8,10,12,14},{1,3,5,7,9,11,13,15},{16,18,20,22,24,26,28,30},{17..., dimensions={0} | all-to-all | bytes 425984 | tf_op jit(solution)/shard_map/all_to_all | solution.py:377
  36.1 0.9 %merge_chips.1 = bf16[2,4,1536]{2,1,0:T(4,128)(2,1)} custom-call(bf16[8,8,1664]{2,1,0:T(8,128)(2,1)S(1)} %all_to_all.5.parts_ref), custom_call_target="tpu_custom_call" | custom-call | tf_op jit(solution)/shard_map/merge_chips/pallas_call | solution.py:333
  (10 shorter events, 0.0 us)
Async XLA Ops:
  1.1 12.6 %copy-start.2 = (s32[2,16]{1,0:T(2,128)S(1)}, s32[2,16]{1,0:T(2,128)}, u32[]{:S(2)}) copy-start(s32[2,16]{1,0:T(2,128)} %refs_1_) | copy-start | bytes 388
  1.1 12.5 %copy-start.3 = (s32[2,6]{1,0:T(2,128)S(1)}, s32[2,6]{1,0:T(2,128)}, u32[]{:S(2)}) copy-start(s32[2,6]{1,0:T(2,128)} %refs_2_) | copy-start | bytes 148
  1.1 9.0 %collective-permute-start = (bf16[6,2,1536]{2,1,0:T(2,128)(2,1)S(1)}, bf16[6,2,1536]{2,1,0:T(2,128)(2,1)S(1)}, u32[]{:S(2)}, u32[]{:S(2)}) collective-permute-start(bf16[6,2,1536]{2,1,0:T(2,128)(2,1)S(1)} %get-tuple-element.61.first_ref), channel_id=1, source_target_pairs={{0,8},{1,5},{2,10},{3,7},{4,12},{5,1},{6,14},{7,3},{8,0},{9,13},{1... | collective-permute-start | bytes 110600 | tf_op jit(solution)/shard_map/ppermute | solution.py:351
  8.7 1.3 %copy-start = (bf16[1024,1024]{1,0:T(8,128)(2,1)}, bf16[1024,1024]{1,0:T(8,128)(2,1)S(1)}, u32[]{:S(2)}) copy-start(bf16[1024,1024]{1,0:T(8,128)(2,1)S(1)} %get-tuple-element.50.rest_1_) | copy-start | bytes 6291460
  10.1 6.6 %collective-permute-start.3 = (bf16[12,2,1536]{2,1,0:T(2,128)(2,1)S(1)}, bf16[12,2,1536]{2,1,0:T(2,128)(2,1)S(1)}, u32[]{:S(2)}, u32[]{:S(2)}) collective-permute-start(bf16[12,2,1536]{2,1,0:T(2,128)(2,1)S(1)} %join.1.rest_4_), channel_id=1, source_target_pairs={{0,6},{1,11},{2,4},{3,9},{4,2},{5,15},{6,0},{7,13},{8,14},{9,3},{1... | collective-permute-start | bytes 221192 | tf_op jit(solution)/shard_map/ppermute | solution.py:351
  12.7 4.4 %collective-permute-start.2 = (bf16[12,2,1536]{2,1,0:T(2,128)(2,1)S(1)}, bf16[12,2,1536]{2,1,0:T(2,128)(2,1)S(1)}, u32[]{:S(2)}, u32[]{:S(2)}) collective-permute-start(bf16[12,2,1536]{2,1,0:T(2,128)(2,1)S(1)} %join.1.rest_4_), channel_id=1, source_target_pairs={{0,2},{1,9},{2,0},{3,11},{4,6},{5,13},{6,4},{7,15},{8,10},{9,1},{1... | collective-permute-start | bytes 221192 | tf_op jit(solution)/shard_map/ppermute | solution.py:351
  13.2 4.5 %collective-permute-start.1 = (bf16[12,2,1536]{2,1,0:T(2,128)(2,1)S(1)}, bf16[12,2,1536]{2,1,0:T(2,128)(2,1)S(1)}, u32[]{:S(2)}, u32[]{:S(2)}) collective-permute-start(bf16[12,2,1536]{2,1,0:T(2,128)(2,1)S(1)} %join.1.rest_4_), channel_id=1, source_target_pairs={{0,4},{1,3},{2,6},{3,1},{4,0},{5,7},{6,2},{7,5},{8,12},{9,11},{10,... | collective-permute-start | bytes 221192 | tf_op jit(solution)/shard_map/ppermute | solution.py:351
  13.6 5.9 %copy-start.1 = (bf16[1024,1024]{1,0:T(8,128)(2,1)S(1)}, bf16[1024,1024]{1,0:T(8,128)(2,1)}, u32[]{:S(2)}) copy-start(bf16[1024,1024]{1,0:T(8,128)(2,1)} %copy-done) | copy-start | bytes 6291460
  17.9 1.7 %collective-permute-start.5 = (bf16[36,2,1536]{2,1,0:T(2,128)(2,1)S(1)}, bf16[36,2,1536]{2,1,0:T(2,128)(2,1)S(1)}, u32[]{:S(2)}, u32[]{:S(2)}) collective-permute-start(bf16[36,2,1536]{2,1,0:T(2,128)(2,1)S(1)} %constant_dynamic-update-slice_fusion.rest_5_), channel_id=1, source_target_pairs={{0,1},{1,0},{2,3},{3,2},{4,5},{5,4},{6,7},{7,6},{8,9},{9,8},{10,11... | collective-permute-start | bytes 663560 | tf_op jit(solution)/shard_map/ppermute | solution.py:351
  17.9 1.6 %collective-permute-start.4 = (bf16[12,2,1536]{2,1,0:T(2,128)(2,1)S(1)}, bf16[12,2,1536]{2,1,0:T(2,128)(2,1)S(1)}, u32[]{:S(2)}, u32[]{:S(2)}) collective-permute-start(bf16[12,2,1536]{2,1,0:T(2,128)(2,1)S(1)} %join.1.rest_4_), channel_id=1, source_target_pairs={{0,1},{1,0},{2,3},{3,2},{4,5},{5,4},{6,7},{7,6},{8,9},{9,8},{10,11... | collective-permute-start | bytes 221192 | tf_op jit(solution)/shard_map/ppermute | solution.py:351
  22.8 1.5 %collective-permute-start.6 = (bf16[64,1664]{1,0:T(8,128)(2,1)S(1)}, bf16[64,1664]{1,0:T(8,128)(2,1)S(1)}, u32[]{:S(2)}, u32[]{:S(2)}) collective-permute-start(bf16[64,1664]{1,0:T(8,128)(2,1)S(1)} %get-tuple-element.58), channel_id=1, source_target_pairs={{0,1},{1,0},{2,3},{3,2},{4,5},{5,4},{6,7},{7,6},{8,9},{9,8},{10,11... | collective-permute-start | bytes 638984 | tf_op jit(solution)/shard_map/ppermute | solution.py:351

commit v15 on v14

--- a/solution.py
+++ b/solution.py
@@ -34,22 +34,24 @@
     return jnp.where((dev & 1) == 1, places[1], places[0]) + ((mask & 1) << (bits - 1))
 
 
-def join_kernel(first_ref, second_ref, out_ref):
-    count = first_ref.shape[0]
-    out_ref[:count] = first_ref[...]
-    out_ref[count:] = second_ref[...]
-
-
-def join(first, second):
-    shape = (2 * first.shape[0], *first.shape[1:])
+def join_kernel(*refs):
+    *part_refs, out_ref = refs
+    at = 0
+    for ref in part_refs:
+        out_ref[at:at + ref.shape[0]] = ref[...]
+        at += ref.shape[0]
+
+
+def join(*parts):
+    shape = (sum(x.shape[0] for x in parts), *parts[0].shape[1:])
     return pl.pallas_call(
         join_kernel,
-        out_shape=jax.ShapeDtypeStruct(shape, first.dtype),
-        in_specs=[VMEM, VMEM],
+        out_shape=jax.ShapeDtypeStruct(shape, parts[0].dtype),
+        in_specs=[VMEM] * len(parts),
         out_specs=VMEM,
         compiler_params=pltpu.CompilerParams(vmem_limit_bytes=16 << 20),
         name="join",
-    )(first, second)
+    )(*parts)
 
 
 def plan_kernel_part(me_ref, counts_ref, rows_ref, target_ref, bias_ref, fresh_bias_ref):
@@ -352,7 +354,7 @@
 
     fresh = fresh_qkv.transpose(1, 2, 0, 3)
     mine, fresh_key, fresh_value = (fresh[:, i] for i in range(3))
-    most = width * 2 // 3
+    most = width // 2
     early = sort_cache(cache_kv, 0, most, None, "sort_first")
     column = mine
     steps = [(1 << m, 1 << n) for m, n in zip(*exchange_order(bits))]
@@ -367,7 +369,7 @@
     others = [swap(column, *masks) for masks in (*steps[-2:], both)]
     others, column, late = lax.optimization_barrier((others, column, late))
     beside = swap(column, 1)
-    others = jnp.concatenate(others)
+    others = join(*others)
     gathered = [column, others, beside, swap(others, 1)]
     key, value, fresh_key, fresh_value, target, bias, fresh_bias = late
     keep, send = attend(slot_count, target, bias, fresh_bias, fresh_key, fresh_value, [*early, key, value], gathered)

time: 37.2 us -> 36.9 us (level)
  blocking collectives: 11.2 us -> 13.2 us
  local copies, waits for them, and re-layouts: 2.58 us -> 1.07 us
  waiting for transfers between devices: 3.38 us -> 2.92 us
    all_to_all x1, blocking collectives: 11.2 us -> 13.2 us  [body(): lax.all_to_all(parts, 'blk', split_axis=0, concat_axis=0, axis_index_grou...]
    unnamed x11 -> x5, local copies, waits for them, and re-layouts: 2.44 us -> 0.99 us
    ppermute x7, waiting for transfers between devices: 3.38 us -> 2.92 us  [swap(): lax.ppermute(x, 'blk', [(i, i ^ masks[i % len(masks)]) for i in range(dev...]
  transfers between devices with their start and end apart: 7 -> 7, of which waited for: 4 -> 3; matrix products, arithmetic and copies ran while one was open for 0% -> 0% of each run, Pallas kernels for 18% -> 17%
where the time goes in v15:
time: 36.9 us; the launch traced here: 36.7 us
  blocking collectives  13.2 us (36%)
  Pallas kernels  10.9 us (30%)
  starting transfers between devices  8.48 us (23%)
  waiting for transfers between devices  2.92 us (8%)
  local copies, waits for them, and re-layouts  1.07 us (3%)
    all_to_all x1, blocking collectives, body(): lax.all_to_all(parts, 'blk', split_axis=0, concat_axis=0, axis_index_grou...  13.2 us
    ppermute x7, starting transfers between devices, swap(): lax.ppermute(x, 'blk', [(i, i ^ masks[i % len(masks)]) for i in range(dev...  8.48 us
    pallas_call x2, Pallas kernels, sort_cache(): pl.pallas_call(kernel, out_shape=tuple(shapes), in_specs=specs, out_specs...  6.41 us
    pallas_call x1, Pallas kernels, attend(): pl.pallas_call(attend_kernel, out_shape=(jax.ShapeDtypeStruct(shape, jnp....  3.08 us
    ppermute x7, waiting for transfers between devices, swap(): lax.ppermute(x, 'blk', [(i, i ^ masks[i % len(masks)]) for i in range(dev...  2.92 us
    pallas_call x2, Pallas kernels, merge(): pl.pallas_call(kernel, out_shape=jax.ShapeDtypeStruct(shape, jnp.bfloat16...  1.36 us
    unnamed x5, local copies, waits for them, and re-layouts  0.99 us
  transfers between devices with their start and end apart: 7, of which 3 were waited for; matrix products, arithmetic and copies ran while one was open for 0% of the time, Pallas kernels for 17%

profile of v15, /device:TPU:0, one launch (start us, length us, event | category | flops | bytes accessed | tf_op | source)
XLA Modules:
  0.0 36.7 jit_solution(12342066717266030464)
XLA Ops:
  0.0 1.0 %copy.7 = bf16[2,6,3,1536]{3,0,1,2:T(2,128)(2,1)S(1)} copy(bf16[2,6,3,1536]{3,0,2,1:T(2,128)(2,1)} %param.5) | data formatting | bytes 221184 | tf_op args[1]
  1.0 0.1 slice_bitcast_fusion
  1.1 0.0 copy-start
  1.1 0.0 copy-start.1
  1.1 4.1 %collective-permute-start = (bf16[6,2,1536]{2,1,0:T(2,128)(2,1)S(1)}, bf16[6,2,1536]{2,1,0:T(2,128)(2,1)S(1)}, u32[]{:S(2)}, u32[]{:S(2)}) collective-permute-start(bf16[6,2,1536]{2,1,0:T(2,128)(2,1)S(1)} %get-tuple-element.61.refs_0_), channel_id=1, source_target_pairs={{0,8},{1,5},{2,10},{3,7},{4,12},{5,1},{6,14},{7,3},{8,0},{9,13},{1... | collective-permute-start | bytes 110600 | tf_op jit(solution)/shard_map/ppermute | solution.py:353
  5.2 2.9 %sort_first.1 = (bf16[1024,768]{1,0:T(8,128)(2,1)S(1)}, bf16[1024,768]{1,0:T(8,128)(2,1)S(1)}) custom-call(bf16[1024,2,1536]{2,1,0:T(2,128)(2,1)} %refs_3_.1), custom_call_target="tpu_custom_call" | custom-call | flops 805306368 | bytes 6291456 | tf_op jit(solution)/shard_map/sort_first/pallas_call | solution.py:173
  8.1 0.0 collective-permute-done.refs_1_
  8.2 2.6 %collective-permute-start.3 = (bf16[12,2,1536]{2,1,0:T(2,128)(2,1)S(1)}, bf16[12,2,1536]{2,1,0:T(2,128)(2,1)S(1)}, u32[]{:S(2)}, u32[]{:S(2)}) collective-permute-start(bf16[12,2,1536]{2,1,0:T(2,128)(2,1)S(1)} %join.2.rest_4_), channel_id=1, source_target_pairs={{0,6},{1,11},{2,4},{3,9},{4,2},{5,15},{6,0},{7,13},{8,14},{9,3},{1... | collective-permute-start | bytes 221192 | tf_op jit(solution)/shard_map/ppermute | solution.py:353
  10.8 0.5 %collective-permute-start.2 = (bf16[12,2,1536]{2,1,0:T(2,128)(2,1)S(1)}, bf16[12,2,1536]{2,1,0:T(2,128)(2,1)S(1)}, u32[]{:S(2)}, u32[]{:S(2)}) collective-permute-start(bf16[12,2,1536]{2,1,0:T(2,128)(2,1)S(1)} %join.2.rest_4_), channel_id=1, source_target_pairs={{0,2},{1,9},{2,0},{3,11},{4,6},{5,13},{6,4},{7,15},{8,10},{9,1},{1... | collective-permute-start | bytes 221192 | tf_op jit(solution)/shard_map/ppermute | solution.py:353
  11.3 0.4 %collective-permute-start.1 = (bf16[12,2,1536]{2,1,0:T(2,128)(2,1)S(1)}, bf16[12,2,1536]{2,1,0:T(2,128)(2,1)S(1)}, u32[]{:S(2)}, u32[]{:S(2)}) collective-permute-start(bf16[12,2,1536]{2,1,0:T(2,128)(2,1)S(1)} %join.2.rest_4_), channel_id=1, source_target_pairs={{0,4},{1,3},{2,6},{3,1},{4,0},{5,7},{6,2},{7,5},{8,12},{9,11},{10,... | collective-permute-start | bytes 221192 | tf_op jit(solution)/shard_map/ppermute | solution.py:353
  11.7 3.5 %sort_second.1 = (bf16[1024,768]{1,0:T(8,128)(2,1)S(1)}, bf16[1024,768]{1,0:T(8,128)(2,1)S(1)}, bf16[16,1536]{1,0:T(8,128)(2,1)S(1)}, bf16[16,1536]{1,0:T(8,128)...) custom-call(s32[1]{0:T(128)} %bitcast.2.refs_0_, s32[2,16]{1,0:T(2,128)S(1)} %copy-done, ...), custom_call_target="tpu_custom_call" | custom-call | flops 805306368 | bytes 6291456 | tf_op jit(solution)/shard_map/sort_second/pallas_call | solution.py:173
  15.2 0.0 collective-permute-done.3.refs_2_
  15.2 0.0 collective-permute-done.2.refs_1_
  15.2 0.6 %collective-permute-done.1.refs_0_ = bf16[12,2,1536]{2,1,0:T(2,128)(2,1)S(1)} collective-permute-done((bf16[12,2,1536]{2,1,0:T(2,128)(2,1)S(1)}, bf16[12,2,1536]{2,1,0:T(2,128)(2,1)S(1)}, u32[]{:S(2)}, u32[]{:S(2)}) %collective-permute-start.1) | collective-permute-done | bytes 73760 | tf_op jit(solution)/shard_map/ppermute | solution.py:353
  15.8 0.1 collective-permute-start.5
  15.9 0.5 %collective-permute-start.4 = (bf16[12,2,1536]{2,1,0:T(2,128)(2,1)S(1)}, bf16[12,2,1536]{2,1,0:T(2,128)(2,1)S(1)}, u32[]{:S(2)}, u32[]{:S(2)}) collective-permute-start(bf16[12,2,1536]{2,1,0:T(2,128)(2,1)S(1)} %join.2.rest_4_), channel_id=1, source_target_pairs={{0,1},{1,0},{2,3},{3,2},{4,5},{5,4},{6,7},{7,6},{8,9},{9,8},{10,11... | collective-permute-start | bytes 221192 | tf_op jit(solution)/shard_map/ppermute | solution.py:353
  16.4 1.1 %collective-permute-done.4.rest_6_ = bf16[12,2,1536]{2,1,0:T(2,128)(2,1)S(1)} collective-permute-done((bf16[12,2,1536]{2,1,0:T(2,128)(2,1)S(1)}, bf16[12,2,1536]{2,1,0:T(2,128)(2,1)S(1)}, u32[]{:S(2)}, u32[]{:S(2)}) %collective-permute-start.4) | collective-permute-done | bytes 73760 | tf_op jit(solution)/shard_map/ppermute | solution.py:353
  17.5 0.0 collective-permute-done.5.rest_7_
  17.5 3.1 %attend.1 = (f32[64,1664]{1,0:T(8,128)S(1)}, bf16[64,1664]{1,0:T(8,128)(2,1)S(1)}) custom-call(s32[1,192]{1,0:T(1,128)S(1)} %get-tuple-element.44.target_ref, f32[8,1024]{1,0:T(8,128)S(1)} %get-tuple-element.45.bias_ref, f32[8,16]{1,0:T(8,128)S(1)} %get-tuple-element.46.fresh_bias_ref, bf16[16,1536]{1,0:T(8,128)(2,1)S(1)} %get-tuple-element.47.fresh_key_ref, ...), custom_call_target="tpu_custom_call" | custom-call | flops 805306368 | bytes 6291456 | tf_op jit(solution)/shard_map/attend/pallas_call | solution.py:285
  20.6 0.3 collective-permute-start.6
  20.8 1.3 %collective-permute-done.6.other_ref = bf16[64,1664]{1,0:T(8,128)(2,1)S(1)} collective-permute-done((bf16[64,1664]{1,0:T(8,128)(2,1)S(1)}, bf16[64,1664]{1,0:T(8,128)(2,1)S(1)}, u32[]{:S(2)}, u32[]{:S(2)}) %collective-permute-start.6) | collective-permute-done | bytes 213024 | tf_op jit(solution)/shard_map/ppermute | solution.py:353
  22.1 0.4 %merge_cores.1 = bf16[8,8,1664]{2,1,0:T(8,128)(2,1)S(1)} custom-call(f32[64,1664]{1,0:T(8,128)S(1)} %get-tuple-element.57.keep_ref, bf16[64,1664]{1,0:T(8,128)(2,1)S(1)} %collective-permute-done.6.other_ref), custom_call_target="tpu_custom_call" | custom-call | tf_op jit(solution)/shard_map/merge_cores/pallas_call | solution.py:335
  22.5 13.2 %all_to_all.5.parts_ref = bf16[8,8,1664]{2,1,0:T(8,128)(2,1)S(1)} all-to-all(bf16[8,8,1664]{2,1,0:T(8,128)(2,1)S(1)} %merge_cores.1), channel_id=1, replica_groups={{0,2,4,6,8,10,12,14},{1,3,5,7,9,11,13,15},{16,18,20,22,24,26,28,30},{17..., dimensions={0} | all-to-all | bytes 425984 | tf_op jit(solution)/shard_map/all_to_all | solution.py:379
  35.8 0.9 %merge_chips.1 = bf16[2,4,1536]{2,1,0:T(4,128)(2,1)} custom-call(bf16[8,8,1664]{2,1,0:T(8,128)(2,1)S(1)} %all_to_all.5.parts_ref), custom_call_target="tpu_custom_call" | custom-call | tf_op jit(solution)/shard_map/merge_chips/pallas_call | solution.py:335
  (4 shorter events, 0.0 us)
Async XLA Ops:
  1.1 10.7 %copy-start = (s32[2,16]{1,0:T(2,128)S(1)}, s32[2,16]{1,0:T(2,128)}, u32[]{:S(2)}) copy-start(s32[2,16]{1,0:T(2,128)} %refs_1_) | copy-start | bytes 388
  1.1 10.7 %copy-start.1 = (s32[2,6]{1,0:T(2,128)S(1)}, s32[2,6]{1,0:T(2,128)}, u32[]{:S(2)}) copy-start(s32[2,6]{1,0:T(2,128)} %refs_2_) | copy-start | bytes 148
  1.1 7.1 %collective-permute-start = (bf16[6,2,1536]{2,1,0:T(2,128)(2,1)S(1)}, bf16[6,2,1536]{2,1,0:T(2,128)(2,1)S(1)}, u32[]{:S(2)}, u32[]{:S(2)}) collective-permute-start(bf16[6,2,1536]{2,1,0:T(2,128)(2,1)S(1)} %get-tuple-element.61.refs_0_), channel_id=1, source_target_pairs={{0,8},{1,5},{2,10},{3,7},{4,12},{5,1},{6,14},{7,3},{8,0},{9,13},{1... | collective-permute-start | bytes 110600 | tf_op jit(solution)/shard_map/ppermute | solution.py:353
  8.2 7.0 %collective-permute-start.3 = (bf16[12,2,1536]{2,1,0:T(2,128)(2,1)S(1)}, bf16[12,2,1536]{2,1,0:T(2,128)(2,1)S(1)}, u32[]{:S(2)}, u32[]{:S(2)}) collective-permute-start(bf16[12,2,1536]{2,1,0:T(2,128)(2,1)S(1)} %join.2.rest_4_), channel_id=1, source_target_pairs={{0,6},{1,11},{2,4},{3,9},{4,2},{5,15},{6,0},{7,13},{8,14},{9,3},{1... | collective-permute-start | bytes 221192 | tf_op jit(solution)/shard_map/ppermute | solution.py:353
  10.8 4.5 %collective-permute-start.2 = (bf16[12,2,1536]{2,1,0:T(2,128)(2,1)S(1)}, bf16[12,2,1536]{2,1,0:T(2,128)(2,1)S(1)}, u32[]{:S(2)}, u32[]{:S(2)}) collective-permute-start(bf16[12,2,1536]{2,1,0:T(2,128)(2,1)S(1)} %join.2.rest_4_), channel_id=1, source_target_pairs={{0,2},{1,9},{2,0},{3,11},{4,6},{5,13},{6,4},{7,15},{8,10},{9,1},{1... | collective-permute-start | bytes 221192 | tf_op jit(solution)/shard_map/ppermute | solution.py:353
  11.3 4.5 %collective-permute-start.1 = (bf16[12,2,1536]{2,1,0:T(2,128)(2,1)S(1)}, bf16[12,2,1536]{2,1,0:T(2,128)(2,1)S(1)}, u32[]{:S(2)}, u32[]{:S(2)}) collective-permute-start(bf16[12,2,1536]{2,1,0:T(2,128)(2,1)S(1)} %join.2.rest_4_), channel_id=1, source_target_pairs={{0,4},{1,3},{2,6},{3,1},{4,0},{5,7},{6,2},{7,5},{8,12},{9,11},{10,... | collective-permute-start | bytes 221192 | tf_op jit(solution)/shard_map/ppermute | solution.py:353
  15.8 1.7 %collective-permute-start.5 = (bf16[36,2,1536]{2,1,0:T(2,128)(2,1)S(1)}, bf16[36,2,1536]{2,1,0:T(2,128)(2,1)S(1)}, u32[]{:S(2)}, u32[]{:S(2)}) collective-permute-start(bf16[36,2,1536]{2,1,0:T(2,128)(2,1)S(1)} %join.3.rest_5_), channel_id=1, source_target_pairs={{0,1},{1,0},{2,3},{3,2},{4,5},{5,4},{6,7},{7,6},{8,9},{9,8},{10,11... | collective-permute-start | bytes 663560 | tf_op jit(solution)/shard_map/ppermute | solution.py:353
  15.9 1.6 %collective-permute-start.4 = (bf16[12,2,1536]{2,1,0:T(2,128)(2,1)S(1)}, bf16[12,2,1536]{2,1,0:T(2,128)(2,1)S(1)}, u32[]{:S(2)}, u32[]{:S(2)}) collective-permute-start(bf16[12,2,1536]{2,1,0:T(2,128)(2,1)S(1)} %join.2.rest_4_), channel_id=1, source_target_pairs={{0,1},{1,0},{2,3},{3,2},{4,5},{5,4},{6,7},{7,6},{8,9},{9,8},{10,11... | collective-permute-start | bytes 221192 | tf_op jit(solution)/shard_map/ppermute | solution.py:353
  20.6 1.5 %collective-permute-start.6 = (bf16[64,1664]{1,0:T(8,128)(2,1)S(1)}, bf16[64,1664]{1,0:T(8,128)(2,1)S(1)}, u32[]{:S(2)}, u32[]{:S(2)}) collective-permute-start(bf16[64,1664]{1,0:T(8,128)(2,1)S(1)} %get-tuple-element.58), channel_id=1, source_target_pairs={{0,1},{1,0},{2,3},{3,2},{4,5},{5,4},{6,7},{7,6},{8,9},{9,8},{10,11... | collective-permute-start | bytes 638984 | tf_op jit(solution)/shard_map/ppermute | solution.py:353

commit v16 on v15

--- a/solution.py
+++ b/solution.py
@@ -15,7 +15,7 @@
 LANES = 128
 PART = 16
 SLOT_BITS = 2
-WAITS = 4
+WAITS = 2
 SORT_VMEM = 48
 VMEM = pl.BlockSpec(memory_space=pltpu.VMEM)
 SMEM = pl.BlockSpec(memory_space=pltpu.SMEM)

time: 36.9 us -> 36.9 us (level)
  transfers between devices with their start and end apart: 7 -> 7, of which waited for: 3 -> 3; matrix products, arithmetic and copies ran while one was open for 0% -> 0% of each run, Pallas kernels for 17% -> 18%
where the time goes in v16:
time: 36.9 us; the launch traced here: 36.8 us
  blocking collectives  13.2 us (36%)
  Pallas kernels  11.1 us (30%)
  starting transfers between devices  8.48 us (23%)
  waiting for transfers between devices  2.82 us (8%)
  local copies, waits for them, and re-layouts  1.07 us (3%)
    all_to_all x1, blocking collectives, body(): lax.all_to_all(parts, 'blk', split_axis=0, concat_axis=0, axis_index_grou...  13.2 us
    ppermute x7, starting transfers between devices, swap(): lax.ppermute(x, 'blk', [(i, i ^ masks[i % len(masks)]) for i in range(dev...  8.48 us
    pallas_call x2, Pallas kernels, sort_cache(): pl.pallas_call(kernel, out_shape=tuple(shapes), in_specs=specs, out_specs...  6.58 us
    pallas_call x1, Pallas kernels, attend(): pl.pallas_call(attend_kernel, out_shape=(jax.ShapeDtypeStruct(shape, jnp....  3.08 us
    ppermute x7, waiting for transfers between devices, swap(): lax.ppermute(x, 'blk', [(i, i ^ masks[i % len(masks)]) for i in range(dev...  2.82 us
    pallas_call x2, Pallas kernels, merge(): pl.pallas_call(kernel, out_shape=jax.ShapeDtypeStruct(shape, jnp.bfloat16...  1.36 us
    unnamed x5, local copies, waits for them, and re-layouts  0.99 us
  transfers between devices with their start and end apart: 7, of which 3 were waited for; matrix products, arithmetic and copies ran while one was open for 0% of the time, Pallas kernels for 18%

profile of v16, /device:TPU:0, one launch (start us, length us, event | category | flops | bytes accessed | tf_op | source)
XLA Modules:
  0.0 36.8 jit_solution(17965089034667180157)
XLA Ops:
  0.0 1.0 %copy.7 = bf16[2,6,3,1536]{3,0,1,2:T(2,128)(2,1)S(1)} copy(bf16[2,6,3,1536]{3,0,2,1:T(2,128)(2,1)} %param.5) | data formatting | bytes 221184 | tf_op args[1]
  1.0 0.1 slice_bitcast_fusion
  1.1 0.0 copy-start
  1.1 0.0 copy-start.1
  1.1 4.1 %collective-permute-start = (bf16[6,2,1536]{2,1,0:T(2,128)(2,1)S(1)}, bf16[6,2,1536]{2,1,0:T(2,128)(2,1)S(1)}, u32[]{:S(2)}, u32[]{:S(2)}) collective-permute-start(bf16[6,2,1536]{2,1,0:T(2,128)(2,1)S(1)} %get-tuple-element.61.refs_0_), channel_id=1, source_target_pairs={{0,8},{1,5},{2,10},{3,7},{4,12},{5,1},{6,14},{7,3},{8,0},{9,13},{1... | collective-permute-start | bytes 110600 | tf_op jit(solution)/shard_map/ppermute | solution.py:353
  5.2 3.0 %sort_first.1 = (bf16[1024,768]{1,0:T(8,128)(2,1)S(1)}, bf16[1024,768]{1,0:T(8,128)(2,1)S(1)}) custom-call(bf16[1024,2,1536]{2,1,0:T(2,128)(2,1)} %refs_3_.1), custom_call_target="tpu_custom_call" | custom-call | flops 805306368 | bytes 6291456 | tf_op jit(solution)/shard_map/sort_first/pallas_call | solution.py:173
  8.2 0.0 collective-permute-done.refs_1_
  8.2 2.6 %collective-permute-start.3 = (bf16[12,2,1536]{2,1,0:T(2,128)(2,1)S(1)}, bf16[12,2,1536]{2,1,0:T(2,128)(2,1)S(1)}, u32[]{:S(2)}, u32[]{:S(2)}) collective-permute-start(bf16[12,2,1536]{2,1,0:T(2,128)(2,1)S(1)} %join.2.rest_4_), channel_id=1, source_target_pairs={{0,6},{1,11},{2,4},{3,9},{4,2},{5,15},{6,0},{7,13},{8,14},{9,3},{1... | collective-permute-start | bytes 221192 | tf_op jit(solution)/shard_map/ppermute | solution.py:353
  10.8 0.5 %collective-permute-start.2 = (bf16[12,2,1536]{2,1,0:T(2,128)(2,1)S(1)}, bf16[12,2,1536]{2,1,0:T(2,128)(2,1)S(1)}, u32[]{:S(2)}, u32[]{:S(2)}) collective-permute-start(bf16[12,2,1536]{2,1,0:T(2,128)(2,1)S(1)} %join.2.rest_4_), channel_id=1, source_target_pairs={{0,2},{1,9},{2,0},{3,11},{4,6},{5,13},{6,4},{7,15},{8,10},{9,1},{1... | collective-permute-start | bytes 221192 | tf_op jit(solution)/shard_map/ppermute | solution.py:353
  11.4 0.4 %collective-permute-start.1 = (bf16[12,2,1536]{2,1,0:T(2,128)(2,1)S(1)}, bf16[12,2,1536]{2,1,0:T(2,128)(2,1)S(1)}, u32[]{:S(2)}, u32[]{:S(2)}) collective-permute-start(bf16[12,2,1536]{2,1,0:T(2,128)(2,1)S(1)} %join.2.rest_4_), channel_id=1, source_target_pairs={{0,4},{1,3},{2,6},{3,1},{4,0},{5,7},{6,2},{7,5},{8,12},{9,11},{10,... | collective-permute-start | bytes 221192 | tf_op jit(solution)/shard_map/ppermute | solution.py:353
  11.8 3.6 %sort_second.1 = (bf16[1024,768]{1,0:T(8,128)(2,1)S(1)}, bf16[1024,768]{1,0:T(8,128)(2,1)S(1)}, bf16[16,1536]{1,0:T(8,128)(2,1)S(1)}, bf16[16,1536]{1,0:T(8,128)...) custom-call(s32[1]{0:T(128)} %bitcast.2.refs_0_, s32[2,16]{1,0:T(2,128)S(1)} %copy-done, ...), custom_call_target="tpu_custom_call" | custom-call | flops 805306368 | bytes 6291456 | tf_op jit(solution)/shard_map/sort_second/pallas_call | solution.py:173
  15.4 0.0 collective-permute-done.3.refs_2_
  15.4 0.0 collective-permute-done.2.refs_1_
  15.4 0.5 %collective-permute-done.1.refs_0_ = bf16[12,2,1536]{2,1,0:T(2,128)(2,1)S(1)} collective-permute-done((bf16[12,2,1536]{2,1,0:T(2,128)(2,1)S(1)}, bf16[12,2,1536]{2,1,0:T(2,128)(2,1)S(1)}, u32[]{:S(2)}, u32[]{:S(2)}) %collective-permute-start.1) | collective-permute-done | bytes 73760 | tf_op jit(solution)/shard_map/ppermute | solution.py:353
  15.9 0.1 collective-permute-start.5
  16.0 0.5 %collective-permute-start.4 = (bf16[12,2,1536]{2,1,0:T(2,128)(2,1)S(1)}, bf16[12,2,1536]{2,1,0:T(2,128)(2,1)S(1)}, u32[]{:S(2)}, u32[]{:S(2)}) collective-permute-start(bf16[12,2,1536]{2,1,0:T(2,128)(2,1)S(1)} %join.2.rest_4_), channel_id=1, source_target_pairs={{0,1},{1,0},{2,3},{3,2},{4,5},{5,4},{6,7},{7,6},{8,9},{9,8},{10,11... | collective-permute-start | bytes 221192 | tf_op jit(solution)/shard_map/ppermute | solution.py:353
  16.5 1.1 %collective-permute-done.4.rest_6_ = bf16[12,2,1536]{2,1,0:T(2,128)(2,1)S(1)} collective-permute-done((bf16[12,2,1536]{2,1,0:T(2,128)(2,1)S(1)}, bf16[12,2,1536]{2,1,0:T(2,128)(2,1)S(1)}, u32[]{:S(2)}, u32[]{:S(2)}) %collective-permute-start.4) | collective-permute-done | bytes 73760 | tf_op jit(solution)/shard_map/ppermute | solution.py:353
  17.5 0.0 collective-permute-done.5.rest_7_
  17.5 3.1 %attend.1 = (f32[64,1664]{1,0:T(8,128)S(1)}, bf16[64,1664]{1,0:T(8,128)(2,1)S(1)}) custom-call(s32[1,192]{1,0:T(1,128)S(1)} %get-tuple-element.44.target_ref, f32[8,1024]{1,0:T(8,128)S(1)} %get-tuple-element.45.bias_ref, f32[8,16]{1,0:T(8,128)S(1)} %get-tuple-element.46.fresh_bias_ref, bf16[16,1536]{1,0:T(8,128)(2,1)S(1)} %get-tuple-element.47.fresh_key_ref, ...), custom_call_target="tpu_custom_call" | custom-call | flops 805306368 | bytes 6291456 | tf_op jit(solution)/shard_map/attend/pallas_call | solution.py:285
  20.6 0.3 collective-permute-start.6
  20.9 1.3 %collective-permute-done.6.other_ref = bf16[64,1664]{1,0:T(8,128)(2,1)S(1)} collective-permute-done((bf16[64,1664]{1,0:T(8,128)(2,1)S(1)}, bf16[64,1664]{1,0:T(8,128)(2,1)S(1)}, u32[]{:S(2)}, u32[]{:S(2)}) %collective-permute-start.6) | collective-permute-done | bytes 213024 | tf_op jit(solution)/shard_map/ppermute | solution.py:353
  22.2 0.4 %merge_cores.1 = bf16[8,8,1664]{2,1,0:T(8,128)(2,1)S(1)} custom-call(f32[64,1664]{1,0:T(8,128)S(1)} %get-tuple-element.57.keep_ref, bf16[64,1664]{1,0:T(8,128)(2,1)S(1)} %collective-permute-done.6.other_ref), custom_call_target="tpu_custom_call" | custom-call | tf_op jit(solution)/shard_map/merge_cores/pallas_call | solution.py:335
  22.6 13.2 %all_to_all.5.parts_ref = bf16[8,8,1664]{2,1,0:T(8,128)(2,1)S(1)} all-to-all(bf16[8,8,1664]{2,1,0:T(8,128)(2,1)S(1)} %merge_cores.1), channel_id=1, replica_groups={{0,2,4,6,8,10,12,14},{1,3,5,7,9,11,13,15},{16,18,20,22,24,26,28,30},{17..., dimensions={0} | all-to-all | bytes 425984 | tf_op jit(solution)/shard_map/all_to_all | solution.py:379
  35.8 0.9 %merge_chips.1 = bf16[2,4,1536]{2,1,0:T(4,128)(2,1)} custom-call(bf16[8,8,1664]{2,1,0:T(8,128)(2,1)S(1)} %all_to_all.5.parts_ref), custom_call_target="tpu_custom_call" | custom-call | tf_op jit(solution)/shard_map/merge_chips/pallas_call | solution.py:335
  (4 shorter events, 0.0 us)
Async XLA Ops:
  1.1 10.7 %copy-start = (s32[2,16]{1,0:T(2,128)S(1)}, s32[2,16]{1,0:T(2,128)}, u32[]{:S(2)}) copy-start(s32[2,16]{1,0:T(2,128)} %refs_1_) | copy-start | bytes 388
  1.1 10.7 %copy-start.1 = (s32[2,6]{1,0:T(2,128)S(1)}, s32[2,6]{1,0:T(2,128)}, u32[]{:S(2)}) copy-start(s32[2,6]{1,0:T(2,128)} %refs_2_) | copy-start | bytes 148
  1.1 7.1 %collective-permute-start = (bf16[6,2,1536]{2,1,0:T(2,128)(2,1)S(1)}, bf16[6,2,1536]{2,1,0:T(2,128)(2,1)S(1)}, u32[]{:S(2)}, u32[]{:S(2)}) collective-permute-start(bf16[6,2,1536]{2,1,0:T(2,128)(2,1)S(1)} %get-tuple-element.61.refs_0_), channel_id=1, source_target_pairs={{0,8},{1,5},{2,10},{3,7},{4,12},{5,1},{6,14},{7,3},{8,0},{9,13},{1... | collective-permute-start | bytes 110600 | tf_op jit(solution)/shard_map/ppermute | solution.py:353
  8.2 7.1 %collective-permute-start.3 = (bf16[12,2,1536]{2,1,0:T(2,128)(2,1)S(1)}, bf16[12,2,1536]{2,1,0:T(2,128)(2,1)S(1)}, u32[]{:S(2)}, u32[]{:S(2)}) collective-permute-start(bf16[12,2,1536]{2,1,0:T(2,128)(2,1)S(1)} %join.2.rest_4_), channel_id=1, source_target_pairs={{0,6},{1,11},{2,4},{3,9},{4,2},{5,15},{6,0},{7,13},{8,14},{9,3},{1... | collective-permute-start | bytes 221192 | tf_op jit(solution)/shard_map/ppermute | solution.py:353
  10.8 4.6 %collective-permute-start.2 = (bf16[12,2,1536]{2,1,0:T(2,128)(2,1)S(1)}, bf16[12,2,1536]{2,1,0:T(2,128)(2,1)S(1)}, u32[]{:S(2)}, u32[]{:S(2)}) collective-permute-start(bf16[12,2,1536]{2,1,0:T(2,128)(2,1)S(1)} %join.2.rest_4_), channel_id=1, source_target_pairs={{0,2},{1,9},{2,0},{3,11},{4,6},{5,13},{6,4},{7,15},{8,10},{9,1},{1... | collective-permute-start | bytes 221192 | tf_op jit(solution)/shard_map/ppermute | solution.py:353
  11.4 4.5 %collective-permute-start.1 = (bf16[12,2,1536]{2,1,0:T(2,128)(2,1)S(1)}, bf16[12,2,1536]{2,1,0:T(2,128)(2,1)S(1)}, u32[]{:S(2)}, u32[]{:S(2)}) collective-permute-start(bf16[12,2,1536]{2,1,0:T(2,128)(2,1)S(1)} %join.2.rest_4_), channel_id=1, source_target_pairs={{0,4},{1,3},{2,6},{3,1},{4,0},{5,7},{6,2},{7,5},{8,12},{9,11},{10,... | collective-permute-start | bytes 221192 | tf_op jit(solution)/shard_map/ppermute | solution.py:353
  15.9 1.7 %collective-permute-start.5 = (bf16[36,2,1536]{2,1,0:T(2,128)(2,1)S(1)}, bf16[36,2,1536]{2,1,0:T(2,128)(2,1)S(1)}, u32[]{:S(2)}, u32[]{:S(2)}) collective-permute-start(bf16[36,2,1536]{2,1,0:T(2,128)(2,1)S(1)} %join.3.rest_5_), channel_id=1, source_target_pairs={{0,1},{1,0},{2,3},{3,2},{4,5},{5,4},{6,7},{7,6},{8,9},{9,8},{10,11... | collective-permute-start | bytes 663560 | tf_op jit(solution)/shard_map/ppermute | solution.py:353
  16.0 1.6 %collective-permute-start.4 = (bf16[12,2,1536]{2,1,0:T(2,128)(2,1)S(1)}, bf16[12,2,1536]{2,1,0:T(2,128)(2,1)S(1)}, u32[]{:S(2)}, u32[]{:S(2)}) collective-permute-start(bf16[12,2,1536]{2,1,0:T(2,128)(2,1)S(1)} %join.2.rest_4_), channel_id=1, source_target_pairs={{0,1},{1,0},{2,3},{3,2},{4,5},{5,4},{6,7},{7,6},{8,9},{9,8},{10,11... | collective-permute-start | bytes 221192 | tf_op jit(solution)/shard_map/ppermute | solution.py:353
  20.6 1.5 %collective-permute-start.6 = (bf16[64,1664]{1,0:T(8,128)(2,1)S(1)}, bf16[64,1664]{1,0:T(8,128)(2,1)S(1)}, u32[]{:S(2)}, u32[]{:S(2)}) collective-permute-start(bf16[64,1664]{1,0:T(8,128)(2,1)S(1)} %get-tuple-element.58), channel_id=1, source_target_pairs={{0,1},{1,0},{2,3},{3,2},{4,5},{5,4},{6,7},{7,6},{8,9},{9,8},{10,11... | collective-permute-start | bytes 638984 | tf_op jit(solution)/shard_map/ppermute | solution.py:353

commit v17 on v16

--- a/solution.py
+++ b/solution.py
@@ -367,8 +367,8 @@
     late = sort_cache(cache_kv, most, width - most, (tables, fresh_key, fresh_value), "sort_second")
     both = [m | n for m, n in zip(*steps[-2:])]
     others = [swap(column, *masks) for masks in (*steps[-2:], both)]
-    others, column, late = lax.optimization_barrier((others, column, late))
     beside = swap(column, 1)
+    others, beside, late = lax.optimization_barrier((others, beside, late))
     others = join(*others)
     gathered = [column, others, beside, swap(others, 1)]
     key, value, fresh_key, fresh_value, target, bias, fresh_bias = late

time: 36.9 us -> 37.2 us (level)
  waiting for transfers between devices: 2.82 us -> 3.77 us
  starting transfers between devices: 8.48 us -> 8 us
    ppermute x7, waiting for transfers between devices: 2.82 us -> 3.77 us  [swap(): lax.ppermute(x, 'blk', [(i, i ^ masks[i % len(masks)]) for i in range(dev...]
    ppermute x7, starting transfers between devices: 8.48 us -> 8 us  [swap(): lax.ppermute(x, 'blk', [(i, i ^ masks[i % len(masks)]) for i in range(dev...]
  transfers between devices with their start and end apart: 7 -> 7, of which waited for: 3 -> 4; matrix products, arithmetic and copies ran while one was open for 0% -> 0% of each run, Pallas kernels for 18% -> 18%
where the time goes in v17:
time: 37.2 us; the launch traced here: 37 us
  blocking collectives  13 us (35%)
  Pallas kernels  11.1 us (30%)
  starting transfers between devices  8 us (22%)
  waiting for transfers between devices  3.77 us (10%)
  local copies, waits for them, and re-layouts  1.07 us (3%)
    all_to_all x1, blocking collectives, body(): lax.all_to_all(parts, 'blk', split_axis=0, concat_axis=0, axis_index_grou...  13 us
    ppermute x7, starting transfers between devices, swap(): lax.ppermute(x, 'blk', [(i, i ^ masks[i % len(masks)]) for i in range(dev...  8 us
    pallas_call x2, Pallas kernels, sort_cache(): pl.pallas_call(kernel, out_shape=tuple(shapes), in_specs=specs, out_specs...  6.58 us
    ppermute x7, waiting for transfers between devices, swap(): lax.ppermute(x, 'blk', [(i, i ^ masks[i % len(masks)]) for i in range(dev...  3.77 us
    pallas_call x1, Pallas kernels, attend(): pl.pallas_call(attend_kernel, out_shape=(jax.ShapeDtypeStruct(shape, jnp....  3.08 us
    pallas_call x2, Pallas kernels, merge(): pl.pallas_call(kernel, out_shape=jax.ShapeDtypeStruct(shape, jnp.bfloat16...  1.36 us
    unnamed x5, local copies, waits for them, and re-layouts  0.99 us
  transfers between devices with their start and end apart: 7, of which 4 were waited for; matrix products, arithmetic and copies ran while one was open for 0% of the time, Pallas kernels for 18%

profile of v17, /device:TPU:0, one launch (start us, length us, event | category | flops | bytes accessed | tf_op | source)
XLA Modules:
  0.0 37.0 jit_solution(9687559185015573799)
XLA Ops:
  0.0 1.0 %copy.7 = bf16[2,6,3,1536]{3,0,1,2:T(2,128)(2,1)S(1)} copy(bf16[2,6,3,1536]{3,0,2,1:T(2,128)(2,1)} %param.5) | data formatting | bytes 221184 | tf_op args[1]
  1.0 0.1 slice_bitcast_fusion
  1.1 0.0 copy-start
  1.1 0.0 copy-start.1
  1.1 4.1 %collective-permute-start = (bf16[6,2,1536]{2,1,0:T(2,128)(2,1)S(1)}, bf16[6,2,1536]{2,1,0:T(2,128)(2,1)S(1)}, u32[]{:S(2)}, u32[]{:S(2)}) collective-permute-start(bf16[6,2,1536]{2,1,0:T(2,128)(2,1)S(1)} %get-tuple-element.61.refs_0_), channel_id=1, source_target_pairs={{0,8},{1,5},{2,10},{3,7},{4,12},{5,1},{6,14},{7,3},{8,0},{9,13},{1... | collective-permute-start | bytes 110600 | tf_op jit(solution)/shard_map/ppermute | solution.py:353
  5.2 3.0 %sort_first.1 = (bf16[1024,768]{1,0:T(8,128)(2,1)S(1)}, bf16[1024,768]{1,0:T(8,128)(2,1)S(1)}) custom-call(bf16[1024,2,1536]{2,1,0:T(2,128)(2,1)} %refs_3_.1), custom_call_target="tpu_custom_call" | custom-call | flops 805306368 | bytes 6291456 | tf_op jit(solution)/shard_map/sort_first/pallas_call | solution.py:173
  8.2 0.0 collective-permute-done.refs_1_
  8.2 0.1 collective-permute-start.4
  8.3 2.6 %collective-permute-start.3 = (bf16[12,2,1536]{2,1,0:T(2,128)(2,1)S(1)}, bf16[12,2,1536]{2,1,0:T(2,128)(2,1)S(1)}, u32[]{:S(2)}, u32[]{:S(2)}) collective-permute-start(bf16[12,2,1536]{2,1,0:T(2,128)(2,1)S(1)} %join.2.rest_4_), channel_id=1, source_target_pairs={{0,6},{1,11},{2,4},{3,9},{4,2},{5,15},{6,0},{7,13},{8,14},{9,3},{1... | collective-permute-start | bytes 221192 | tf_op jit(solution)/shard_map/ppermute | solution.py:353
  10.9 0.5 %collective-permute-start.2 = (bf16[12,2,1536]{2,1,0:T(2,128)(2,1)S(1)}, bf16[12,2,1536]{2,1,0:T(2,128)(2,1)S(1)}, u32[]{:S(2)}, u32[]{:S(2)}) collective-permute-start(bf16[12,2,1536]{2,1,0:T(2,128)(2,1)S(1)} %join.2.rest_4_), channel_id=1, source_target_pairs={{0,2},{1,9},{2,0},{3,11},{4,6},{5,13},{6,4},{7,15},{8,10},{9,1},{1... | collective-permute-start | bytes 221192 | tf_op jit(solution)/shard_map/ppermute | solution.py:353
  11.4 0.4 %collective-permute-start.1 = (bf16[12,2,1536]{2,1,0:T(2,128)(2,1)S(1)}, bf16[12,2,1536]{2,1,0:T(2,128)(2,1)S(1)}, u32[]{:S(2)}, u32[]{:S(2)}) collective-permute-start(bf16[12,2,1536]{2,1,0:T(2,128)(2,1)S(1)} %join.2.rest_4_), channel_id=1, source_target_pairs={{0,4},{1,3},{2,6},{3,1},{4,0},{5,7},{6,2},{7,5},{8,12},{9,11},{10,... | collective-permute-start | bytes 221192 | tf_op jit(solution)/shard_map/ppermute | solution.py:353
  11.9 3.6 %sort_second.1 = (bf16[1024,768]{1,0:T(8,128)(2,1)S(1)}, bf16[1024,768]{1,0:T(8,128)(2,1)S(1)}, bf16[16,1536]{1,0:T(8,128)(2,1)S(1)}, bf16[16,1536]{1,0:T(8,128)...) custom-call(s32[1]{0:T(128)} %bitcast.2.refs_0_, s32[2,16]{1,0:T(2,128)S(1)} %copy-done, ...), custom_call_target="tpu_custom_call" | custom-call | flops 805306368 | bytes 6291456 | tf_op jit(solution)/shard_map/sort_second/pallas_call | solution.py:173
  15.5 0.0 collective-permute-done.4.rest_6_
  15.5 0.0 collective-permute-done.3.refs_2_
  15.5 0.3 collective-permute-done.2.refs_1_
  15.8 0.6 %collective-permute-done.1.refs_0_ = bf16[12,2,1536]{2,1,0:T(2,128)(2,1)S(1)} collective-permute-done((bf16[12,2,1536]{2,1,0:T(2,128)(2,1)S(1)}, bf16[12,2,1536]{2,1,0:T(2,128)(2,1)S(1)}, u32[]{:S(2)}, u32[]{:S(2)}) %collective-permute-start.1) | collective-permute-done | bytes 73760 | tf_op jit(solution)/shard_map/ppermute | solution.py:353
  16.5 0.1 collective-permute-start.5
  16.6 1.5 %collective-permute-done.5.rest_7_ = bf16[36,2,1536]{2,1,0:T(2,128)(2,1)S(1)} collective-permute-done((bf16[36,2,1536]{2,1,0:T(2,128)(2,1)S(1)}, bf16[36,2,1536]{2,1,0:T(2,128)(2,1)S(1)}, u32[]{:S(2)}, u32[]{:S(2)}) %collective-permute-start.5) | collective-permute-done | bytes 221216 | tf_op jit(solution)/shard_map/ppermute | solution.py:353
  18.0 3.1 %attend.1 = (f32[64,1664]{1,0:T(8,128)S(1)}, bf16[64,1664]{1,0:T(8,128)(2,1)S(1)}) custom-call(s32[1,192]{1,0:T(1,128)S(1)} %get-tuple-element.44.target_ref, f32[8,1024]{1,0:T(8,128)S(1)} %get-tuple-element.45.bias_ref, f32[8,16]{1,0:T(8,128)S(1)} %get-tuple-element.46.fresh_bias_ref, bf16[16,1536]{1,0:T(8,128)(2,1)S(1)} %get-tuple-element.47.fresh_key_ref, ...), custom_call_target="tpu_custom_call" | custom-call | flops 805306368 | bytes 6291456 | tf_op jit(solution)/shard_map/attend/pallas_call | solution.py:285
  21.1 0.2 collective-permute-start.6
  21.3 1.3 %collective-permute-done.6.other_ref = bf16[64,1664]{1,0:T(8,128)(2,1)S(1)} collective-permute-done((bf16[64,1664]{1,0:T(8,128)(2,1)S(1)}, bf16[64,1664]{1,0:T(8,128)(2,1)S(1)}, u32[]{:S(2)}, u32[]{:S(2)}) %collective-permute-start.6) | collective-permute-done | bytes 213024 | tf_op jit(solution)/shard_map/ppermute | solution.py:353
  22.6 0.4 %merge_cores.1 = bf16[8,8,1664]{2,1,0:T(8,128)(2,1)S(1)} custom-call(f32[64,1664]{1,0:T(8,128)S(1)} %get-tuple-element.57.keep_ref, bf16[64,1664]{1,0:T(8,128)(2,1)S(1)} %collective-permute-done.6.other_ref), custom_call_target="tpu_custom_call" | custom-call | tf_op jit(solution)/shard_map/merge_cores/pallas_call | solution.py:335
  23.1 13.0 %all_to_all.5.parts_ref = bf16[8,8,1664]{2,1,0:T(8,128)(2,1)S(1)} all-to-all(bf16[8,8,1664]{2,1,0:T(8,128)(2,1)S(1)} %merge_cores.1), channel_id=1, replica_groups={{0,2,4,6,8,10,12,14},{1,3,5,7,9,11,13,15},{16,18,20,22,24,26,28,30},{17..., dimensions={0} | all-to-all | bytes 425984 | tf_op jit(solution)/shard_map/all_to_all | solution.py:379
  36.1 0.9 %merge_chips.1 = bf16[2,4,1536]{2,1,0:T(4,128)(2,1)} custom-call(bf16[8,8,1664]{2,1,0:T(8,128)(2,1)S(1)} %all_to_all.5.parts_ref), custom_call_target="tpu_custom_call" | custom-call | tf_op jit(solution)/shard_map/merge_chips/pallas_call | solution.py:335
  (4 shorter events, 0.0 us)
Async XLA Ops:
  1.1 10.8 %copy-start = (s32[2,16]{1,0:T(2,128)S(1)}, s32[2,16]{1,0:T(2,128)}, u32[]{:S(2)}) copy-start(s32[2,16]{1,0:T(2,128)} %refs_1_) | copy-start | bytes 388
  1.1 10.8 %copy-start.1 = (s32[2,6]{1,0:T(2,128)S(1)}, s32[2,6]{1,0:T(2,128)}, u32[]{:S(2)}) copy-start(s32[2,6]{1,0:T(2,128)} %refs_2_) | copy-start | bytes 148
  1.1 7.1 %collective-permute-start = (bf16[6,2,1536]{2,1,0:T(2,128)(2,1)S(1)}, bf16[6,2,1536]{2,1,0:T(2,128)(2,1)S(1)}, u32[]{:S(2)}, u32[]{:S(2)}) collective-permute-start(bf16[6,2,1536]{2,1,0:T(2,128)(2,1)S(1)} %get-tuple-element.61.refs_0_), channel_id=1, source_target_pairs={{0,8},{1,5},{2,10},{3,7},{4,12},{5,1},{6,14},{7,3},{8,0},{9,13},{1... | collective-permute-start | bytes 110600 | tf_op jit(solution)/shard_map/ppermute | solution.py:353
  8.2 7.2 %collective-permute-start.4 = (bf16[12,2,1536]{2,1,0:T(2,128)(2,1)S(1)}, bf16[12,2,1536]{2,1,0:T(2,128)(2,1)S(1)}, u32[]{:S(2)}, u32[]{:S(2)}) collective-permute-start(bf16[12,2,1536]{2,1,0:T(2,128)(2,1)S(1)} %join.2.rest_4_), channel_id=1, source_target_pairs={{0,1},{1,0},{2,3},{3,2},{4,5},{5,4},{6,7},{7,6},{8,9},{9,8},{10,11... | collective-permute-start | bytes 221192 | tf_op jit(solution)/shard_map/ppermute | solution.py:353
  8.3 7.1 %collective-permute-start.3 = (bf16[12,2,1536]{2,1,0:T(2,128)(2,1)S(1)}, bf16[12,2,1536]{2,1,0:T(2,128)(2,1)S(1)}, u32[]{:S(2)}, u32[]{:S(2)}) collective-permute-start(bf16[12,2,1536]{2,1,0:T(2,128)(2,1)S(1)} %join.2.rest_4_), channel_id=1, source_target_pairs={{0,6},{1,11},{2,4},{3,9},{4,2},{5,15},{6,0},{7,13},{8,14},{9,3},{1... | collective-permute-start | bytes 221192 | tf_op jit(solution)/shard_map/ppermute | solution.py:353
  10.9 4.9 %collective-permute-start.2 = (bf16[12,2,1536]{2,1,0:T(2,128)(2,1)S(1)}, bf16[12,2,1536]{2,1,0:T(2,128)(2,1)S(1)}, u32[]{:S(2)}, u32[]{:S(2)}) collective-permute-start(bf16[12,2,1536]{2,1,0:T(2,128)(2,1)S(1)} %join.2.rest_4_), channel_id=1, source_target_pairs={{0,2},{1,9},{2,0},{3,11},{4,6},{5,13},{6,4},{7,15},{8,10},{9,1},{1... | collective-permute-start | bytes 221192 | tf_op jit(solution)/shard_map/ppermute | solution.py:353
  11.4 5.0 %collective-permute-start.1 = (bf16[12,2,1536]{2,1,0:T(2,128)(2,1)S(1)}, bf16[12,2,1536]{2,1,0:T(2,128)(2,1)S(1)}, u32[]{:S(2)}, u32[]{:S(2)}) collective-permute-start(bf16[12,2,1536]{2,1,0:T(2,128)(2,1)S(1)} %join.2.rest_4_), channel_id=1, source_target_pairs={{0,4},{1,3},{2,6},{3,1},{4,0},{5,7},{6,2},{7,5},{8,12},{9,11},{10,... | collective-permute-start | bytes 221192 | tf_op jit(solution)/shard_map/ppermute | solution.py:353
  16.5 1.5 %collective-permute-start.5 = (bf16[36,2,1536]{2,1,0:T(2,128)(2,1)S(1)}, bf16[36,2,1536]{2,1,0:T(2,128)(2,1)S(1)}, u32[]{:S(2)}, u32[]{:S(2)}) collective-permute-start(bf16[36,2,1536]{2,1,0:T(2,128)(2,1)S(1)} %join.3.rest_5_), channel_id=1, source_target_pairs={{0,1},{1,0},{2,3},{3,2},{4,5},{5,4},{6,7},{7,6},{8,9},{9,8},{10,11... | collective-permute-start | bytes 663560 | tf_op jit(solution)/shard_map/ppermute | solution.py:353
  21.1 1.5 %collective-permute-start.6 = (bf16[64,1664]{1,0:T(8,128)(2,1)S(1)}, bf16[64,1664]{1,0:T(8,128)(2,1)S(1)}, u32[]{:S(2)}, u32[]{:S(2)}) collective-permute-start(bf16[64,1664]{1,0:T(8,128)(2,1)S(1)} %get-tuple-element.58), channel_id=1, source_target_pairs={{0,1},{1,0},{2,3},{3,2},{4,5},{5,4},{6,7},{7,6},{8,9},{9,8},{10,11... | collective-permute-start | bytes 638984 | tf_op jit(solution)/shard_map/ppermute | solution.py:353
